TPU v7x, 32 devices: a whole 2x2x4 slice. The times are simulated.
32 devices in a mesh: dp: 4 (over y, x), sp: 8 (over z, core).
Axes of the slice: x: 2, y: 2, z: 4, core: 2. Of those that a mesh axis runs over, the one named last changes fastest.
Arguments:
- q_pre: bfloat16 [4, 256, 8192], P('dp', 'sp'), may hold values from -6 to 6
- attn_out: bfloat16 [4, 256, 8192], P('dp', 'sp'), may hold values from -6 to 6
- d_attn: bfloat16 [4, 256, 8192], P('dp', 'sp'), may hold values from -24 to 24
- k_pre: bfloat16 [4, 1024, 512], P('dp', 'sp'), may hold values from -6 to 6
- values: bfloat16 [4, 1024, 512], P('dp', 'sp'), may hold values from -6 to 6
- q_gain: float32 [128], replicated, may hold values from 0.5 to 1.5
- k_gain: float32 [128], replicated, may hold values from 0.5 to 1.5
- offsets: int32 [4], P('dp'), may hold values from 1 to 768, 2304 in all
- moe_in: bfloat16 [4, 256, 4096], P('dp', 'sp'), may hold values from -2.59375 to 2.59375
- router: bfloat16 [4096, 128], replicated, may hold values from -0.0074768066 to 0.0074768066
- expert_ids: int32 [4, 256, 8], P('dp', 'sp'), may hold values from 0 to 127, all different within a row; in each aligned block of 32 rows (0 to 31, 32 to 63, ..., all dimensions but the last counted through in order) at most 3 rows name the same one
- d_moe: bfloat16 [4, 256, 4096], P('dp', 'sp'), may hold values from -6 to 6
- expert_out: bfloat16 [4, 128, 8, 3, 4096], P('dp', 'sp'), may hold values from -0.3125 to 0.3125
Outputs:
- dq_pre: bfloat16 [4, 256, 8192], P('dp', 'sp')
- dk_pre: bfloat16 [4, 1024, 512], P('dp', 'sp')
- dv_out: bfloat16 [4, 1024, 512], P('dp', 'sp')
- batch_grad: bfloat16 [4, 128, 8, 3, 4096], P('dp', 'sp')
- router_grad: float32 [4096, 128], P('sp')
Inputs may be any that keep to these rules, and one draw needn't show every extreme that they name: `expert_ids`: within the rows of one device no expert is named more than 3 times; some expert is named exactly 3 times by the rows of some device. `offsets`: some group has its stretch at the end, offset 1024 - 256.
All inputs are finite; a program needn't handle non-finite values.
Results may differ from a plain program's by a relative error of at most 0.0075.
Values may be sent and summed in bfloat16 or wider, within the bound.
No kernel may reach another device: no remote copies, remote signals or barrier semaphores. Data moves between devices by JAX's collectives and lax.ppermute only.
A program may use at most 128 MiB of HBM per device.

v0:
```python
import math

import jax
import jax.numpy as jnp
from jax import lax
from jax.sharding import PartitionSpec as P

norm_eps = 1e-06


def normed(inputs, gain):
    inverse = lax.rsqrt(jnp.mean(inputs * inputs, axis=-1, keepdims=True) + norm_eps)
    unit_vals = inputs * inverse
    return (unit_vals, inverse, unit_vals * gain)


def norm_back(grad_hat, unit_vals, inverse, gain):
    grad_unit = grad_hat * gain
    return inverse * (
        grad_unit - unit_vals * jnp.mean(grad_unit * unit_vals, axis=-1, keepdims=True)
    )


def on_device(
    q_pre,
    attn_out,
    d_attn,
    k_pre,
    values,
    q_gain,
    k_gain,
    offsets,
    moe_in,
    router,
    expert_ids,
    d_moe,
    expert_out,
):
    head_dim = q_gain.shape[0]
    group_size = lax.axis_size("sp")
    key_dev = k_pre.shape[1]
    kv_heads = k_pre.shape[2] // head_dim
    repeat_count = group_size // kv_heads
    score_scale = head_dim ** (-0.5)
    q_local, out_local, dout_local = (
        lax.all_to_all(q_pre[0], "sp", split_axis=1, concat_axis=0, tiled=True),
        lax.all_to_all(attn_out[0], "sp", split_axis=1, concat_axis=0, tiled=True),
        lax.all_to_all(d_attn[0], "sp", split_axis=1, concat_axis=0, tiled=True),
    )
    stretch_len = q_local.shape[0]
    heads_here = q_local.shape[1] // head_dim
    q_unit, q_inv, q_hat32 = normed(
        q_local.astype(jnp.float32).reshape(stretch_len, heads_here, head_dim), q_gain
    )
    q_hat = q_hat32.astype(jnp.bfloat16)
    dout_three = dout_local.reshape(stretch_len, heads_here, head_dim)
    row_delta = jnp.einsum(
        "thd,thd->th",
        dout_three,
        out_local.reshape(stretch_len, heads_here, head_dim),
        preferred_element_type=jnp.float32,
    )
    k_unit, k_inv, k_hat32 = normed(
        k_pre[0].astype(jnp.float32).reshape(key_dev, kv_heads, head_dim), k_gain
    )
    k_hat = k_hat32.astype(jnp.bfloat16)
    value_local = values[0]
    key_copies = jnp.repeat(k_hat, repeat_count, axis=1).reshape(key_dev, group_size * head_dim)
    value_copies = jnp.repeat(
        value_local.reshape(key_dev, kv_heads, head_dim), repeat_count, axis=1
    ).reshape(key_dev, group_size * head_dim)
    key_full, value_full = (
        lax.all_to_all(key_copies, "sp", split_axis=1, concat_axis=0, tiled=True),
        lax.all_to_all(value_copies, "sp", split_axis=1, concat_axis=0, tiled=True),
    )
    key_count = key_full.shape[0]
    row_count = stretch_len * heads_here
    block_rows = math.gcd(row_count, 512)
    block_count = row_count // block_rows
    query_rows = q_hat.reshape(block_count, block_rows, head_dim)
    dout_rows = dout_three.reshape(block_count, block_rows, head_dim)
    delta_rows = row_delta.reshape(block_count, block_rows)
    limit_rows = (offsets[0] + jnp.arange(row_count, dtype=jnp.int32) // heads_here).reshape(
        block_count, block_rows
    )
    key_pos = jnp.arange(key_count, dtype=jnp.int32)

    def attend(totals, pieces):
        query_block, dout_block, delta_block, limit_block = pieces
        visible = key_pos[None, :] <= limit_block[:, None]
        scores = jnp.dot(query_block, key_full.T, preferred_element_type=jnp.float32) * score_scale
        lse = jnp.log(jnp.sum(jnp.where(visible, jnp.exp(scores), 0.0), axis=-1))
        probs = jnp.where(visible, jnp.exp(scores - lse[:, None]), 0.0)
        probs_b = probs.astype(jnp.bfloat16)
        dv_term = jnp.dot(probs_b.T, dout_block, preferred_element_type=jnp.float32)
        dprobs = jnp.dot(dout_block, value_full.T, preferred_element_type=jnp.float32)
        dscores = (probs * (dprobs - delta_block[:, None]) * score_scale).astype(jnp.bfloat16)
        dq_block = jnp.dot(dscores, key_full, preferred_element_type=jnp.float32)
        dk_term = jnp.dot(dscores.T, query_block, preferred_element_type=jnp.float32)
        return ((totals[0] + dk_term, totals[1] + dv_term), dq_block)

    zeros_kv = jnp.zeros((key_count, head_dim), jnp.float32)
    (dk_part, dv_part), dq_blocks = lax.scan(
        attend, (zeros_kv, zeros_kv), (query_rows, dout_rows, delta_rows, limit_rows)
    )
    dq_hat = dq_blocks.reshape(stretch_len, heads_here, head_dim)
    dq_local = (
        norm_back(dq_hat, q_unit, q_inv, q_gain)
        .astype(jnp.bfloat16)
        .reshape(stretch_len, heads_here * head_dim)
    )
    dq_back = lax.all_to_all(dq_local, "sp", split_axis=0, concat_axis=1, tiled=True)
    dk_terms, dv_terms = (
        lax.all_to_all(dk_part, "sp", split_axis=0, concat_axis=1, tiled=True),
        lax.all_to_all(dv_part, "sp", split_axis=0, concat_axis=1, tiled=True),
    )
    dk_hat = jnp.sum(dk_terms.reshape(key_dev, kv_heads, repeat_count, head_dim), axis=2)
    dv_sum = jnp.sum(dv_terms.reshape(key_dev, kv_heads, repeat_count, head_dim), axis=2)
    dk_local = (
        norm_back(dk_hat, k_unit, k_inv, k_gain)
        .astype(jnp.bfloat16)
        .reshape(key_dev, kv_heads * head_dim)
    )
    dv_local = dv_sum.astype(jnp.bfloat16).reshape(key_dev, kv_heads * head_dim)
    tokens_here = moe_in[0]
    chosen_ids = expert_ids[0]
    dmoe_here = d_moe[0]
    tok_dev = tokens_here.shape[0]
    top_count = chosen_ids.shape[1]
    expert_count = router.shape[1]
    capacity = expert_out.shape[3]
    model_width = tokens_here.shape[1]
    pairs = tok_dev * top_count
    logits_all = jnp.dot(tokens_here, router, preferred_element_type=jnp.float32)
    chosen = chosen_ids[:, :, None] == jnp.arange(expert_count, dtype=jnp.int32)[None, None, :]
    logits = jnp.sum(jnp.where(chosen, logits_all[:, None, :], 0.0), axis=-1)
    weights = jnp.exp(logits)
    gate_probs = weights / jnp.sum(weights, axis=-1, keepdims=True)
    gate_b = gate_probs.astype(jnp.bfloat16)
    chosen_flat = chosen.reshape(pairs, expert_count).astype(jnp.float32)
    pair_pos = jnp.arange(pairs, dtype=jnp.int32)
    earlier = (pair_pos[None, :] < pair_pos[:, None]).astype(jnp.float32)
    earlier_counts = jnp.dot(earlier, chosen_flat, precision=lax.Precision.HIGHEST)
    slot_index = jnp.sum(chosen_flat * earlier_counts, axis=-1).astype(jnp.int32)
    slot_key = chosen_ids.reshape(pairs) * capacity + slot_index
    slot_hit = jnp.arange(expert_count * capacity, dtype=jnp.int32)[:, None] == slot_key[None, :]
    token_hit = jnp.any(
        slot_hit.reshape(expert_count * capacity, tok_dev, top_count), axis=-1
    ).astype(jnp.bfloat16)
    send_rows = (
        jnp.dot(token_hit, dmoe_here, preferred_element_type=jnp.float32)
        .astype(jnp.bfloat16)
        .reshape(expert_count, 1, capacity, model_width)
    )
    send_gates = (
        jnp.dot(
            slot_hit.astype(jnp.float32),
            gate_b.reshape(pairs).astype(jnp.float32),
            precision=lax.Precision.HIGHEST,
        )
        .astype(jnp.bfloat16)
        .reshape(expert_count, 1, capacity)
    )
    rows_in, gates_in = (
        lax.all_to_all(send_rows, "sp", split_axis=0, concat_axis=1, tiled=True),
        lax.all_to_all(send_gates, "sp", split_axis=0, concat_axis=1, tiled=True),
    )
    batch_local = (gates_in.astype(jnp.float32)[..., None] * rows_in.astype(jnp.float32)).astype(
        jnp.bfloat16
    )
    slot_terms = jnp.einsum(
        "escd,escd->esc", rows_in, expert_out[0], preferred_element_type=jnp.float32
    )
    terms_back = lax.all_to_all(slot_terms, "sp", split_axis=1, concat_axis=0, tiled=True)
    dgate = jnp.take(terms_back.reshape(expert_count * capacity), slot_key).reshape(
        tok_dev, top_count
    )
    dlogit = gate_probs * (dgate - jnp.sum(gate_probs * dgate, axis=-1, keepdims=True))
    dense_grad = jnp.sum(jnp.where(chosen, dlogit[:, :, None], 0.0), axis=1)
    tokens_wide = tokens_here.astype(jnp.float32)
    rows_share = model_width // group_size
    partial_value = jnp.dot(tokens_wide.T, dense_grad, precision=lax.Precision.HIGHEST)
    summed = lax.psum(partial_value, ("dp", "sp"))
    router_local = lax.dynamic_slice_in_dim(
        summed, lax.axis_index("sp") * rows_share, rows_share, 0
    )
    return (dq_back[None], dk_local[None], dv_local[None], batch_local[None], router_local)


def solution(mesh):
    in_specs = (
        P("dp", "sp", None),
        P("dp", "sp", None),
        P("dp", "sp", None),
        P("dp", "sp", None),
        P("dp", "sp", None),
        P(),
        P(),
        P("dp"),
        P("dp", "sp", None),
        P(),
        P("dp", "sp", None),
        P("dp", "sp", None),
        P("dp", "sp", None, None, None),
    )
    out_specs = (
        P("dp", "sp", None),
        P("dp", "sp", None),
        P("dp", "sp", None),
        P("dp", "sp", None, None, None),
        P("sp", None),
    )
    return jax.shard_map(
        on_device, mesh=mesh, in_specs=in_specs, out_specs=out_specs, check_vma=False
    )
```

profile of v0, /device:TPU:0, one launch (start us, length us, event | category | flops | bytes accessed | tf_op | source)
XLA Modules:
  0.0 447.8 jit_solution(10066633710989468455)
XLA Ops:
  7.2 1.5 copy.167
  8.6 1.1 copy.135
  9.7 6.5 %all-to-all-start.4 = ((bf16[32,8,1024]{2,0,1:T(8,128)(2,1)}), bf16[32,8,1024]{2,0,1:T(8,128)(2,1)S(1)}, u32[]{:S(2)}, u32[]{:S(2)}) async-start(bf16[32,8,1024]{2,0,1:T(8,128)(2,1)} %copy.135), calls=%async_computation.4 | async-start | bytes 1048576 | tf_op jit(solution)/shard_map/all_to_all | solution.py:47
  16.5 1.1 copy.133
  17.6 14.0 %all-to-all-done.4 = bf16[32,8,1024]{2,0,1:T(8,128)(2,1)S(1)} async-done(((bf16[32,8,1024]{2,0,1:T(8,128)(2,1)}), bf16[32,8,1024]{2,0,1:T(8,128)(2,1)S(1)}, u32[]{:S(2)}, u32[]{:S(2)}) %all-to-all-start.4) | async-done | bytes 524320 | tf_op jit(solution)/shard_map/all_to_all | solution.py:47
  31.6 3.5 all-to-all-start.2
  35.4 1.1 copy.130
  36.5 13.9 %all-to-all-done.2 = bf16[32,8,1024]{2,0,1:T(8,128)(2,1)S(1)} async-done(((bf16[32,8,1024]{2,0,1:T(8,128)(2,1)}), bf16[32,8,1024]{2,0,1:T(8,128)(2,1)S(1)}, u32[]{:S(2)}, u32[]{:S(2)}) %all-to-all-start.2) | async-done | bytes 524320 | tf_op jit(solution)/shard_map/all_to_all | solution.py:48
  50.3 3.5 all-to-all-start
  58.8 10.3 %all-to-all-done = bf16[32,8,1024]{2,0,1:T(8,128)(2,1)S(1)} async-done(((bf16[32,8,1024]{2,0,1:T(8,128)(2,1)}), bf16[32,8,1024]{2,0,1:T(8,128)(2,1)S(1)}, u32[]{:S(2)}, u32[]{:S(2)}) %all-to-all-start) | async-done | bytes 524320 | tf_op jit(solution)/shard_map/all_to_all | solution.py:46
  69.1 1.6 broadcast_in_dim.54
  70.8 3.4 all-to-all-start.3
  74.2 1.1 convert_bitcast_fusion
  75.3 1.4 reshape.389
  76.8 1.2 copy.164
  78.0 1.6 reduce_sum.110
  79.5 4.3 all-to-all-done.3
  84.6 3.4 all-to-all-start.1
  89.9 7.8 %all-to-all-done.1 = bf16[128,8,128]{2,0,1:T(8,128)(2,1)S(1)} async-done(((bf16[128,8,128]{2,0,1:T(8,128)(2,1)}), bf16[128,8,128]{2,0,1:T(8,128)(2,1)S(1)}, u32[]{:S(2)}, u32[]{:S(2)}) %all-to-all-start.1) | async-done | bytes 262176 | tf_op jit(solution)/shard_map/all_to_all | solution.py:73
  97.7 27.0 %while.15 = (s32[]{:T(128)}, f32[1024,128]{1,0:T(8,128)}, f32[1024,128]{1,0:T(8,128)}, f32[4,512,128]{2,1,0:T(8,128)}, s32[4,512]{1,0:T(4,128)}, /*index=5*/bf16...) while((s32[]{:T(128)}, f32[1024,128]{1,0:T(8,128)}, ...), condition=%wide.region_4.5_spmd.clone, body=%wide.region_2.4_spmd.clone.sunk | while | flops 680525312 | bytes 20474132 | solution.py:103
  99.3 1.0 convolution_add_fusion.5
  101.2 1.3 convolution_add_fusion.4
  102.5 1.2 fusion.71
  105.3 1.0 convolution_add_fusion.5
  107.2 2.3 convolution_add_fusion.4
  109.6 1.2 fusion.71
  112.3 1.0 convolution_add_fusion.5
  114.2 2.3 convolution_add_fusion.4
  116.6 1.2 fusion.71
  119.3 1.0 convolution_add_fusion.5
  121.2 2.3 convolution_add_fusion.4
  123.6 1.2 fusion.71
  124.7 18.9 %all_to_all.170 = f32[8,128,128]{2,1,0:T(8,128)S(1)} all-to-all(f32[8,128,128]{2,1,0:T(8,128)} %bitcast.178), channel_id=1, replica_groups=mesh['dp'=4,'sp'=8] {'sp'}, dimensions={0} | all-to-all | bytes 1048576 | tf_op jit(solution)/shard_map/all_to_all | solution.py:115
  143.6 4.1 all-to-all-start.6
  148.5 3.6 convolution_convert_fusion
  152.2 7.1 %reshape.387 = bf16[128,1,3,4096]{3,2,0,1:T(4,128)(2,1)} reshape(bf16[384,4096]{1,0:T(8,128)(2,1)} %convolution_convert_fusion) | data formatting | bytes 6291456 | tf_op jit(solution)/shard_map/reshape | solution.py:153
  159.3 3.9 all-to-all-done.6
  163.1 4.9 %all-to-all-start.9 = ((bf16[128,1,3,4096]{3,2,1,0:T(4,128)(2,1)}), bf16[128,1,3,4096]{3,2,1,0:T(4,128)(2,1)}, u32[]{:S(2)}, u32[]{:S(2)}) async-start(bf16[128,1,3,4096]{3,2,1,0:T(4,128)(2,1)} %bitcast.160), calls=%async_computation.9 | async-start | bytes 8388608 | tf_op jit(solution)/shard_map/all_to_all | solution.py:165
  168.8 1.2 fusion.32
  172.5 1.3 mul.238
  173.8 2.4 mul.239
  176.2 2.4 reshape.383
  178.6 1.9 multiply_reduce_fusion.1
  180.6 1.3 mul.256
  181.9 2.4 mul.257
  184.3 2.8 multiply_convert_fusion.1
  187.1 74.8 %all-to-all-done.9 = bf16[128,1,3,4096]{3,2,1,0:T(4,128)(2,1)} async-done(((bf16[128,1,3,4096]{3,2,1,0:T(4,128)(2,1)}), bf16[128,1,3,4096]{3,2,1,0:T(4,128)(2,1)}, u32[]{:S(2)}, u32[]{:S(2)}) %all-to-all-start.9) | async-done | bytes 3145760 | tf_op jit(solution)/shard_map/all_to_all | solution.py:165
  261.8 3.5 all-to-all-start.5
  265.3 1.1 bitcast_reduce_fusion.1
  267.4 4.5 copy.145
  271.8 1.7 copy-done.1
  274.2 1.1 copy-done.3
  275.4 3.4 multiply_reduce_fusion
  279.5 1.1 all-to-all-done.5
  280.6 3.9 all-to-all-start.10
  286.9 1.0 broadcast_in_dim.55
  287.9 2.3 all-to-all-done.10
  290.5 2.1 gather_fusion
  294.3 3.4 all-to-all-start.8
  298.0 2.3 convolution_bitcast_fusion.1
  300.3 3.2 all-to-all-done.8
  303.8 2.9 fusion.23
  306.7 3.4 copy.150
  310.0 129.1 %all-reduce.2.cloned.1.call-done = f32[4096,128]{0,1:T(8,128)} async-done(((f32[4096,128]{0,1:T(8,128)}), f32[4096,128]{0,1:T(8,128)}) %all-reduce.2.cloned.1.call-update) | async-done | bytes 2097168 | tf_op jit(solution)/shard_map/psum | solution.py:183
  (179 shorter events, 30.2 us)
Async XLA Ops:
  7.2 161.6 %copy-start = (bf16[4096,128]{1,0:T(8,128)(2,1)S(1)}, bf16[4096,128]{1,0:T(8,128)(2,1)}, u32[]{:S(2)}) copy-start(bf16[4096,128]{1,0:T(8,128)(2,1)} %param.24) | copy-start | bytes 3145732
  7.2 9.0 %copy-start.10 = (bf16[1,32,8192]{2,1,0:T(8,128)(2,1)S(1)}, bf16[1,32,8192]{2,1,0:T(8,128)(2,1)}, u32[]{:S(2)}) copy-start(bf16[1,32,8192]{2,1,0:T(8,128)(2,1)} %param.17) | copy-start | bytes 1572868
  9.7 25.3 %copy-start.11 = (bf16[1,32,8192]{2,1,0:T(8,128)(2,1)S(1)}, bf16[1,32,8192]{2,1,0:T(8,128)(2,1)}, u32[]{:S(2)}) copy-start(bf16[1,32,8192]{2,1,0:T(8,128)(2,1)} %param.15) | copy-start | bytes 1572868
  9.7 21.8 %all-to-all-start.4 = ((bf16[32,8,1024]{2,0,1:T(8,128)(2,1)}), bf16[32,8,1024]{2,0,1:T(8,128)(2,1)S(1)}, u32[]{:S(2)}, u32[]{:S(2)}) async-start(bf16[32,8,1024]{2,0,1:T(8,128)(2,1)} %copy.135), calls=%async_computation.4 | async-start | bytes 1048576 | tf_op jit(solution)/shard_map/all_to_all | solution.py:47
  17.6 36.9 %copy-start.21 = (bf16[1,128,512]{2,1,0:T(8,128)(2,1)S(1)}, bf16[1,128,512]{2,1,0:T(8,128)(2,1)}, u32[]{:S(2)}) copy-start(bf16[1,128,512]{2,1,0:T(8,128)(2,1)} %param.18) | copy-start | bytes 393220
  17.6 37.1 %copy-start.22 = (bf16[1,128,512]{2,1,0:T(8,128)(2,1)S(1)}, bf16[1,128,512]{2,1,0:T(8,128)(2,1)}, u32[]{:S(2)}) copy-start(bf16[1,128,512]{2,1,0:T(8,128)(2,1)} %param.19) | copy-start | bytes 393220
  31.6 18.8 %all-to-all-start.2 = ((bf16[32,8,1024]{2,0,1:T(8,128)(2,1)}), bf16[32,8,1024]{2,0,1:T(8,128)(2,1)S(1)}, u32[]{:S(2)}, u32[]{:S(2)}) async-start(bf16[32,8,1024]{2,0,1:T(8,128)(2,1)} %copy.133), calls=%async_computation.2 | async-start | bytes 1048576 | tf_op jit(solution)/shard_map/all_to_all | solution.py:48
  35.1 21.2 %copy-start.30 = (f32[128]{0:T(128)S(1)}, f32[128]{0:T(128)}, u32[]{:S(2)}) copy-start(f32[128]{0:T(128)} %param.21) | copy-start | bytes 1540
  50.3 18.8 %all-to-all-start = ((bf16[32,8,1024]{2,0,1:T(8,128)(2,1)}), bf16[32,8,1024]{2,0,1:T(8,128)(2,1)S(1)}, u32[]{:S(2)}, u32[]{:S(2)}) async-start(bf16[32,8,1024]{2,0,1:T(8,128)(2,1)} %copy.130), calls=%async_computation | async-start | bytes 1048576 | tf_op jit(solution)/shard_map/all_to_all | solution.py:46
  55.5 3.2 copy-start.4
  56.3 0.8 copy-start.25
  70.8 13.1 %all-to-all-start.3 = ((bf16[128,8,128]{2,0,1:T(8,128)(2,1)}), bf16[128,8,128]{2,0,1:T(8,128)(2,1)S(1)}, u32[]{:S(2)}, u32[]{:S(2)}) async-start(bf16[128,8,128]{2,0,1:T(8,128)(2,1)} %bitcast.8), calls=%async_computation.3 | async-start | bytes 524288 | tf_op jit(solution)/shard_map/all_to_all | solution.py:74
  76.7 7.2 %copy-start.9 = (bf16[128,4,128]{2,0,1:T(8,128)(2,1)S(1)}, bf16[128,4,128]{2,0,1:T(8,128)(2,1)}, u32[]{:S(2)}) copy-start(bf16[128,4,128]{2,0,1:T(8,128)(2,1)} %multiply_convert_fusion.3) | copy-start | bytes 393220
  83.8 0.8 copy-start.19
  84.6 13.1 %all-to-all-start.1 = ((bf16[128,8,128]{2,0,1:T(8,128)(2,1)}), bf16[128,8,128]{2,0,1:T(8,128)(2,1)S(1)}, u32[]{:S(2)}, u32[]{:S(2)}) async-start(bf16[128,8,128]{2,0,1:T(8,128)(2,1)} %bitcast.4), calls=%async_computation.1 | async-start | bytes 524288 | tf_op jit(solution)/shard_map/all_to_all | solution.py:73
  88.1 0.7 copy-start.6
  88.9 8.9 %copy-start.23 = (f32[4,512]{1,0:T(4,128)}, f32[4,512]{1,0:T(4,128)S(1)}, u32[]{:S(2)}) copy-start(f32[4,512]{1,0:T(4,128)S(1)} %rsqrt.21) | copy-start | bytes 24580
  97.7 1.6 copy-start.12
  97.7 1.6 copy-start.13
  99.3 1.1 copy-start.20
  100.4 0.9 copy-start.14
  103.7 1.6 copy-start.12
  103.7 1.6 copy-start.13
  105.3 1.1 copy-start.20
  106.3 0.9 copy-start.14
  110.7 1.6 copy-start.12
  110.7 1.6 copy-start.13
  112.3 1.1 copy-start.20
  113.3 0.9 copy-start.14
  117.7 1.6 copy-start.12
  117.7 1.6 copy-start.13
  119.3 1.1 copy-start.20
  120.4 0.9 copy-start.14
  124.7 23.0 %copy-start.27 = (s32[1,32,8]{1,2,0:T(8,128)S(1)}, s32[1,32,8]{1,2,0:T(8,128)}, u32[]{:S(2)}) copy-start(s32[1,32,8]{1,2,0:T(8,128)} %param.25) | copy-start | bytes 3076
  143.6 19.5 %all-to-all-start.6 = ((f32[8,128,128]{2,1,0:T(8,128)}), f32[8,128,128]{2,1,0:T(8,128)}, u32[]{:S(2)}, u32[]{:S(2)}) async-start(f32[8,128,128]{2,1,0:T(8,128)} %bitcast.15), calls=%async_computation.6 | async-start | bytes 1048576 | tf_op jit(solution)/shard_map/all_to_all | solution.py:114
  148.3 11.0 %copy-start.15 = (s32[32,8]{1,0:T(8,128)}, s32[32,8]{1,0:T(8,128)S(1)}, u32[]{:S(2)}) copy-start(s32[32,8]{1,0:T(8,128)S(1)} %multiply_add_fusion) | copy-start | bytes 3076
  163.1 7.7 %copy-start.31 = (f32[128]{0:T(128)S(1)}, f32[128]{0:T(128)}, u32[]{:S(2)}) copy-start(f32[128]{0:T(128)} %param.21) | copy-start | bytes 1540
  163.1 8.8 %copy-start.29 = (f32[128]{0:T(128)S(1)}, f32[128]{0:T(128)}, u32[]{:S(2)}) copy-start(f32[128]{0:T(128)} %param.20) | copy-start | bytes 1540
  163.1 9.4 %copy-start.7 = (f32[256,8]{1,0:T(8,128)S(1)}, f32[256,8]{1,0:T(8,128)}, u32[]{:S(2)}) copy-start(f32[256,8]{1,0:T(8,128)} %copy-done.6) | copy-start | bytes 24580
  163.1 98.7 %all-to-all-start.9 = ((bf16[128,1,3,4096]{3,2,1,0:T(4,128)(2,1)}), bf16[128,1,3,4096]{3,2,1,0:T(4,128)(2,1)}, u32[]{:S(2)}, u32[]{:S(2)}) async-start(bf16[128,1,3,4096]{3,2,1,0:T(4,128)(2,1)} %bitcast.160), calls=%async_computation.9 | async-start | bytes 8388608 | tf_op jit(solution)/shard_map/all_to_all | solution.py:165
  170.2 8.3 %copy-start.17 = (f32[32,8]{1,0:T(8,128)}, f32[32,8]{1,0:T(8,128)S(1)}, u32[]{:S(2)}) copy-start(f32[32,8]{1,0:T(8,128)S(1)} %select_reduce_fusion.1) | copy-start | bytes 3076
  173.8 4.7 %copy-start.24 = (f32[4,512]{1,0:T(4,128)S(1)}, f32[4,512]{1,0:T(4,128)}, u32[]{:S(2)}) copy-start(f32[4,512]{1,0:T(4,128)} %copy-done.23) | copy-start | bytes 24580
  180.4 3.9 copy-start.2
  184.3 82.1 %copy-start.5 = (f32[128,4,128]{2,0,1:T(8,128)S(1)}, f32[128,4,128]{2,0,1:T(8,128)}, u32[]{:S(2)}) copy-start(f32[128,4,128]{2,0,1:T(8,128)} %copy-done.4) | copy-start | bytes 786436
  261.8 18.8 %all-to-all-start.5 = ((bf16[8,32,1024]{2,1,0:T(8,128)(2,1)}), bf16[8,32,1024]{2,1,0:T(8,128)(2,1)S(1)}, u32[]{:S(2)}, u32[]{:S(2)}) async-start(bf16[8,32,1024]{2,1,0:T(8,128)(2,1)} %multiply_convert_fusion.1), calls=%async_computation.5 | async-start | bytes 1048576 | tf_op jit(solution)/shard_map/all_to_all | solution.py:112
  271.8 1.7 copy-start.1
  273.5 1.9 copy-start.3
  275.4 10.2 %copy-start.26 = (f32[128,4]{0,1:T(4,128)S(1)}, f32[128,4]{0,1:T(4,128)}, u32[]{:S(2)}) copy-start(f32[128,4]{0,1:T(4,128)} %copy-done.25) | copy-start | bytes 6148
  275.4 10.2 %copy-start.28 = (f32[512]{0:T(512)S(1)}, f32[512]{0:T(512)}, u32[]{:S(2)}) copy-start(f32[512]{0:T(512)} %broadcast_bitcast_fusion.1) | copy-start | bytes 6148
  280.6 9.6 %all-to-all-start.10 = ((f32[16,8,3]{0,2,1:T(4,128)}), f32[16,8,3]{0,2,1:T(4,128)S(1)}, u32[]{:S(2)}, u32[]{:S(2)}) async-start(f32[16,8,3]{0,2,1:T(4,128)} %copy.160), calls=%async_computation.10 | async-start | bytes 32768 | tf_op jit(solution)/shard_map/all_to_all | solution.py:174
  285.6 7.1 %copy-start.16 = (s32[32,8]{1,0:T(8,128)S(1)}, s32[32,8]{1,0:T(8,128)}, u32[]{:S(2)}) copy-start(s32[32,8]{1,0:T(8,128)} %copy-done.15) | copy-start | bytes 3076
  285.6 7.1 %copy-start.18 = (f32[32,8]{1,0:T(8,128)S(1)}, f32[32,8]{1,0:T(8,128)}, u32[]{:S(2)}) copy-start(f32[32,8]{1,0:T(8,128)} %copy-done.17) | copy-start | bytes 3076
  285.6 7.1 %copy-start.32 = (f32[32]{0:T(128)S(1)}, f32[32]{0:T(128)}, u32[]{:S(2)}) copy-start(f32[32]{0:T(128)} %exponential_reduce_fusion) | copy-start | bytes 388
  285.6 7.6 %copy-start.33 = (s32[256]{0:T(256)S(1)}, s32[256]{0:T(256)}, u32[]{:S(2)}) copy-start(s32[256]{0:T(256)} %multiply_add_fusion.2) | copy-start | bytes 3076
  285.8 12.2 %copy-start.8 = (bf16[1,32,4096]{2,1,0:T(8,128)(2,1)S(1)}, bf16[1,32,4096]{2,1,0:T(8,128)(2,1)}, u32[]{:S(2)}) copy-start(bf16[1,32,4096]{2,1,0:T(8,128)(2,1)} %param.23) | copy-start | bytes 786436
  294.3 9.2 %all-to-all-start.8 = ((bf16[128,1,3]{2,1,0:T(2,128)(2,1)}), bf16[128,1,3]{2,1,0:T(2,128)(2,1)S(1)}, u32[]{:S(2)}, u32[]{:S(2)}) async-start(bf16[128,1,3]{2,1,0:T(2,128)(2,1)} %reshape.411), calls=%async_computation.8 | async-start | bytes 131072 | tf_op jit(solution)/shard_map/all_to_all | solution.py:166
  297.7 141.4 %all-reduce.2.cloned.1.call-start = ((), (), s32[]{:S(2)}) async-start(), calls=%async_computation.11 | async-start | bytes 4194304 | tf_op jit(solution)/shard_map/psum | solution.py:183
Sparse Core Ops, SparseCore 0:
  303.9 135.1 all-reduce.1
where the time goes:
time: 450 us; the launch traced here: 448 us
  waiting for transfers between devices  265 us (59%)
  local copies, waits for them, and re-layouts  55.1 us (12%)
  starting transfers between devices  40.3 us (9%)
  matrix products  31.1 us (7%)
  other arithmetic  22.2 us (5%)
  blocking collectives  18.9 us (4%)
  between operations  15.3 us (3%)
    psum x1, waiting for transfers between devices, on_device(): summed = lax.psum(partial_value, ('dp', 'sp'))  129 us
    all_to_all x1, waiting for transfers between devices, on_device(): lax.all_to_all(send_rows, 'sp', split_axis=0, concat_axis=1, tiled=True)  74.8 us
    all_to_all x1, blocking collectives, on_device(): lax.all_to_all(dv_part, 'sp', split_axis=0, concat_axis=1, tiled=True)  18.9 us
    all_to_all x1, waiting for transfers between devices, on_device(): lax.all_to_all(attn_out[0], 'sp', split_axis=1, concat_axis=0, tiled=True)  14 us
    all_to_all x1, waiting for transfers between devices, on_device(): lax.all_to_all(d_attn[0], 'sp', split_axis=1, concat_axis=0, tiled=True)  13.9 us
    unnamed x72, local copies, waits for them, and re-layouts  12.9 us
    all_to_all x1, waiting for transfers between devices, on_device(): lax.all_to_all(q_pre[0], 'sp', split_axis=1, concat_axis=0, tiled=True)  10.3 us
  transfers between devices with their start and end apart: 11, of which 11 were waited for; matrix products, arithmetic and copies ran while one was open for 15% of the time, Pallas kernels for 0%

commit v1 on v0

v1 whole, which is shorter than its diff:
```python
import functools
import math

import jax
import jax.numpy as jnp
import numpy as np
from jax import lax
from jax.experimental import pallas as pl
from jax.experimental.pallas import tpu as pltpu
from jax.sharding import PartitionSpec as P

norm_eps = 1e-06
f32 = jnp.float32
bf16 = jnp.bfloat16
vmem_limit = 56 * 1024 * 1024


def dot_nt(a, b):
    return lax.dot_general(a, b, (((1,), (1,)), ((), ())), preferred_element_type=f32)


def dot_nn(a, b):
    return lax.dot_general(a, b, (((1,), (0,)), ((), ())), preferred_element_type=f32)


def dot_tn(a, b):
    return lax.dot_general(a, b, (((0,), (0,)), ((), ())), preferred_element_type=f32)


def whole(shape):
    return pl.BlockSpec(shape, lambda *_: (0,) * len(shape))


def keys_kernel(k_ref, v_ref, gain_ref, kv_ref):
    hd = gain_ref.shape[1]
    gain = gain_ref[...]
    for g in range(k_ref.shape[1] // hd):
        k = k_ref[:, g * hd : (g + 1) * hd].astype(f32)
        inv = lax.rsqrt(jnp.mean(k * k, axis=-1, keepdims=True) + norm_eps)
        kv_ref[:, 2 * g * hd : (2 * g + 1) * hd] = ((k * inv) * gain).astype(bf16)
        kv_ref[:, (2 * g + 1) * hd : (2 * g + 2) * hd] = v_ref[:, g * hd : (g + 1) * hd]


def pack_keys(k_pre, values, k_gain):
    rows, width = k_pre.shape
    return pl.pallas_call(
        keys_kernel,
        out_shape=jax.ShapeDtypeStruct((rows, 2 * width), bf16),
        name="pack_keys",
    )(k_pre, values, k_gain)


def gates_kernel(moe_ref, router_ref, ids_ref, dmoe_ref, pack_ref, info_ref):
    tok, width = moe_ref.shape
    experts = router_ref.shape[1]
    logits = dot_nn(moe_ref[...], router_ref[...])
    lane = lax.broadcasted_iota(jnp.int32, (tok, experts), 1)
    chosen = lane == ids_ref[:, 0:1]
    for k in range(1, ids_ref.shape[1]):
        chosen = jnp.logical_or(chosen, lane == ids_ref[:, k : k + 1])
    weights = jnp.where(chosen, jnp.exp(logits), 0.0)
    probs = weights / jnp.sum(weights, axis=-1, keepdims=True)
    high = probs.astype(bf16)
    low = (probs - high.astype(f32)).astype(bf16)
    coded = jnp.where(chosen, high.astype(f32), -1.0).astype(bf16)
    pack_ref[:, :width] = dmoe_ref[...]
    pack_ref[:, width:] = coded
    info_ref[:, :experts] = coded
    info_ref[:, experts:] = low


def gates(moe_in, router, ids, d_moe):
    tok, width = moe_in.shape
    experts = router.shape[1]
    return pl.pallas_call(
        gates_kernel,
        out_shape=(
            jax.ShapeDtypeStruct((tok, width + experts), bf16),
            jax.ShapeDtypeStruct((tok, 2 * experts), bf16),
        ),
        compiler_params=pltpu.CompilerParams(vmem_limit_bytes=vmem_limit),
        name="gates",
    )(moe_in, router, ids, d_moe)


def attend_kernel(blocks, meta_ref, q_ref, o_ref, do_ref, gain_ref, *refs):
    kv_refs = refs[:blocks]
    dq_ref = refs[blocks]
    part_refs = refs[blocks + 1 : 2 * blocks + 1]
    tok = q_ref.shape[0]
    hd = gain_ref.shape[1]
    heads = q_ref.shape[1] // hd
    kb = kv_refs[0].shape[0]
    keys = kb * blocks
    scale = hd ** (-0.5)
    offset = meta_ref[0]
    gain = gain_ref[...]
    key = jnp.concatenate([r[:, :hd] for r in kv_refs], axis=0)
    val = jnp.concatenate([r[:, hd:] for r in kv_refs], axis=0)
    pos = jnp.concatenate(
        [
            meta_ref[1 + b] * kb + lax.broadcasted_iota(jnp.int32, (kb, 1), 0)
            for b in range(blocks)
        ],
        axis=0,
    )
    step_heads = min(heads, max(128 // tok, heads * 1024 // keys))
    rows = step_heads * tok
    limit = offset + lax.rem(lax.broadcasted_iota(jnp.int32, (1, rows), 1), tok)
    visible = pos <= limit
    dk = dv = None
    for h0 in range(0, heads, step_heads):

        def stack(ref):
            return jnp.concatenate(
                [ref[:, h * hd : (h + 1) * hd] for h in range(h0, h0 + step_heads)], axis=0
            )

        q = stack(q_ref).astype(f32)
        do = stack(do_ref)
        prod = do.astype(f32) * stack(o_ref).astype(f32)
        delta = jnp.sum(prod.T, axis=0, keepdims=True)
        inv = lax.rsqrt(jnp.mean(q * q, axis=-1, keepdims=True) + norm_eps)
        unit = q * inv
        q_hat = (unit * gain).astype(bf16)
        scores = dot_nt(key, q_hat)
        ex = jnp.where(visible, jnp.exp2(scores * (scale * math.log2(math.e))), 0.0)
        probs = ex * (1.0 / jnp.sum(ex, axis=0, keepdims=True))
        dv_one = dot_nn(probs.astype(bf16), do)
        dprobs = dot_nt(val, do)
        ds = ((probs * scale) * (dprobs - delta)).astype(bf16)
        dk_one = dot_nn(ds, q_hat)
        dq = dot_tn(key, ds).T
        c = dq * gain
        dq_pre = (inv * (c - unit * jnp.mean(c * unit, axis=-1, keepdims=True))).astype(bf16)
        for i in range(step_heads):
            h = h0 + i
            dq_ref[:, h * hd : (h + 1) * hd] = dq_pre[i * tok : (i + 1) * tok, :]
        dk = dk_one if dk is None else dk + dk_one
        dv = dv_one if dv is None else dv + dv_one
    for b in range(blocks):
        part_refs[b][:, :hd] = dk[b * kb : (b + 1) * kb, :].astype(part_refs[b].dtype)
        part_refs[b][:, hd:] = dv[b * kb : (b + 1) * kb, :].astype(part_refs[b].dtype)


def attend(meta, q, o, do, gain, kv_blocks, part_types):
    tok, width = q.shape
    hd = gain.shape[1]
    kb, kv_width = kv_blocks[0].shape
    kv_heads = kv_width // (2 * hd)
    blocks = len(kv_blocks)
    step = width // kv_heads
    row_spec = pl.BlockSpec((tok, step), lambda g, m: (0, g))
    kv_spec = pl.BlockSpec((kb, 2 * hd), lambda g, m: (0, g))
    return pl.pallas_call(
        functools.partial(attend_kernel, blocks),
        grid_spec=pltpu.PrefetchScalarGridSpec(
            num_scalar_prefetch=1,
            grid=(kv_heads,),
            in_specs=[row_spec] * 3 + [whole((1, hd))] + [kv_spec] * blocks,
            out_specs=[row_spec] + [kv_spec] * blocks,
        ),
        out_shape=[jax.ShapeDtypeStruct((tok, width), bf16)]
        + [jax.ShapeDtypeStruct((kb, kv_width), t) for t in part_types],
        compiler_params=pltpu.CompilerParams(vmem_limit_bytes=vmem_limit),
        name="attend",
    )(meta, q, o, do, gain, *kv_blocks)


def finish_kernel(k_ref, gain_ref, *refs):
    dk_ref, dv_ref = refs[-2:]
    hd = gain_ref.shape[1]
    gain = gain_ref[...]
    total = refs[0][...].astype(f32)
    for r in refs[1:-2]:
        total = total + r[...].astype(f32)
    for g in range(k_ref.shape[1] // hd):
        k = k_ref[:, g * hd : (g + 1) * hd].astype(f32)
        inv = lax.rsqrt(jnp.mean(k * k, axis=-1, keepdims=True) + norm_eps)
        unit = k * inv
        c = total[:, 2 * g * hd : (2 * g + 1) * hd] * gain
        dk = inv * (c - unit * jnp.mean(c * unit, axis=-1, keepdims=True))
        dk_ref[:, g * hd : (g + 1) * hd] = dk.astype(bf16)
        dv_ref[:, g * hd : (g + 1) * hd] = total[
            :, (2 * g + 1) * hd : (2 * g + 2) * hd
        ].astype(bf16)


def finish_keys(k_pre, k_gain, parts):
    out = jax.ShapeDtypeStruct(k_pre.shape, bf16)
    return pl.pallas_call(finish_kernel, out_shape=(out, out), name="finish_keys")(
        k_pre, k_gain, *parts
    )


def earlier_same_block(rows, block):
    i = lax.broadcasted_iota(jnp.int32, (rows, rows), 0)
    j = lax.broadcasted_iota(jnp.int32, (rows, rows), 1)
    same = lax.div(i, block) == lax.div(j, block)
    return jnp.where(jnp.logical_and(same, j < i), 1.0, 0.0).astype(bf16)


def slots_kernel(
    blocks, sp, cap, meta_ref, table_ref, lanes_ref, *refs
):
    d_refs = refs[:blocks]
    g_refs = refs[blocks : 2 * blocks]
    eout_ref, batch_ref, terms_ref, dm, gated, hit_scr, acc = refs[2 * blocks :]
    tok = d_refs[0].shape[0]
    experts = g_refs[0].shape[1]
    rows = eout_ref.shape[0]
    tokens = tok * blocks
    step = pl.program_id(0)

    def pick():
        expert = meta_ref[0] + table_ref[:, 0:1]
        return lax.broadcasted_iota(jnp.int32, (rows, experts), 1) == expert

    @pl.when(step == 0)
    def _():
        coded = jnp.concatenate([r[...] for r in g_refs], axis=0)
        chosen = (coded >= 0).astype(bf16)
        rank = dot_nn(earlier_same_block(tokens, tok), chosen)
        sel = jnp.where(pick(), 1.0, 0.0).astype(bf16)
        gate = dot_nt(sel, coded)
        place = dot_nt(sel, rank.astype(bf16))
        lane_block = lax.div(lax.broadcasted_iota(jnp.int32, (1, tokens), 1), tok)
        source = jnp.zeros((1, tokens), jnp.int32)
        for b in range(blocks):
            source = jnp.where(lane_block == b, meta_ref[1 + b], source)
        hit = jnp.logical_and(
            jnp.logical_and(gate >= 0.0, place == table_ref[:, 1:2].astype(f32)),
            source == table_ref[:, 2:3],
        )
        gated[...] = jnp.where(hit, gate, 0.0).astype(bf16)
        hit_scr[...] = jnp.where(hit, 1.0, 0.0)
        acc[...] = jnp.zeros_like(acc)

    for b in range(blocks):
        dm[b * tok : (b + 1) * tok, :] = d_refs[b][...]
    d_all = dm[...]
    batch_ref[...] = dot_nn(gated[...], d_all).astype(bf16)
    acc[...] += dot_nt(eout_ref[...], d_all)

    @pl.when(step == pl.num_programs(0) - 1)
    def _():
        terms = jnp.sum(acc[...] * hit_scr[...], axis=-1, keepdims=True)
        placed = jnp.where(pick(), terms, 0.0)
        want = lax.broadcasted_iota(jnp.int32, (cap * sp, rows), 0)
        fold = jnp.where(want == lanes_ref[...], 1.0, 0.0)
        terms_ref[...] = lax.dot_general(
            fold,
            placed,
            (((1,), (0,)), ((), ())),
            precision=lax.Precision.HIGHEST,
            preferred_element_type=f32,
        )


def slots(meta, packs, eout, experts_here, cap, sp):
    rows, width = eout.shape
    tok, packed = packs[0].shape
    experts = packed - width
    blocks = len(packs)
    r = np.arange(rows)
    e, c, s = r // (cap * sp), (r // sp) % cap, r % sp
    table = jnp.asarray(np.stack([e, c, s], axis=1), jnp.int32)
    lanes = jnp.asarray((c * sp + s)[None, :], jnp.int32)
    col = min(width, 1024)
    d_spec = pl.BlockSpec((tok, col), lambda i, m: (0, i))
    g_spec = pl.BlockSpec((tok, experts), lambda i, m: (0, width // experts))
    e_spec = pl.BlockSpec((rows, col), lambda i, m: (0, i))
    return pl.pallas_call(
        functools.partial(slots_kernel, blocks, sp, cap),
        grid_spec=pltpu.PrefetchScalarGridSpec(
            num_scalar_prefetch=1,
            grid=(width // col,),
            in_specs=[whole((rows, 3)), whole((1, rows))]
            + [d_spec] * blocks
            + [g_spec] * blocks
            + [e_spec],
            out_specs=[e_spec, whole((cap * sp, experts))],
            scratch_shapes=[
                pltpu.VMEM((tok * blocks, col), bf16),
                pltpu.VMEM((rows, tok * blocks), bf16),
                pltpu.VMEM((rows, tok * blocks), f32),
                pltpu.VMEM((rows, tok * blocks), f32),
            ],
        ),
        out_shape=[
            jax.ShapeDtypeStruct((rows, width), bf16),
            jax.ShapeDtypeStruct((cap * sp, experts), f32),
        ],
        compiler_params=pltpu.CompilerParams(vmem_limit_bytes=vmem_limit),
        name="slots",
    )(meta, table, lanes, *packs, *packs, eout)


def router_kernel(tok, sp, cap, info_ref, terms_ref, moe_ref, out_ref):
    tokens = moe_ref.shape[0]
    experts = out_ref.shape[1]

    @pl.when(pl.program_id(0) == 0)
    def _():
        out_ref[...] = jnp.zeros_like(out_ref)

    high = info_ref[:, :experts]
    chosen = high >= 0
    prob = jnp.where(chosen, high.astype(f32) + info_ref[:, experts:].astype(f32), 0.0)
    rank = dot_nn(earlier_same_block(tokens, tok), chosen.astype(bf16))
    terms = jnp.sum(terms_ref[...], axis=0)
    pieces = []
    for s in range(sp):
        place = rank[s * tok : (s + 1) * tok, :]
        one = jnp.zeros((tok, experts), f32)
        for c in range(cap):
            one = jnp.where(place == c, terms[c * sp + s : c * sp + s + 1, :], one)
        pieces.append(one)
    dgate = jnp.where(chosen, jnp.concatenate(pieces, axis=0), 0.0)
    dlogit = prob * (dgate - jnp.sum(prob * dgate, axis=-1, keepdims=True))
    a = dlogit.astype(bf16)
    rest = dlogit - a.astype(f32)
    b = rest.astype(bf16)
    c = (rest - b.astype(f32)).astype(bf16)
    wide = dot_tn(moe_ref[...], jnp.concatenate([a, b, c], axis=1))
    out_ref[...] += (
        wide[:, :experts] + wide[:, experts : 2 * experts] + wide[:, 2 * experts :]
    )


def router_grad(info, terms, moe, tok, dp, sp, cap):
    tokens = info.shape[0] // dp
    experts = info.shape[1] // 2
    share = moe.shape[1]
    return pl.pallas_call(
        functools.partial(router_kernel, tok, sp, cap),
        grid=(dp,),
        in_specs=[
            pl.BlockSpec((tokens, 2 * experts), lambda g: (g, 0)),
            pl.BlockSpec((sp, cap * sp, experts), lambda g: (g, 0, 0)),
            pl.BlockSpec((tokens, share), lambda g: (g, 0)),
        ],
        out_specs=whole((share, experts)),
        out_shape=jax.ShapeDtypeStruct((share, experts), f32),
        compiler_params=pltpu.CompilerParams(vmem_limit_bytes=vmem_limit),
        name="router_grad",
    )(info, terms, moe)


def on_device(
    q_pre,
    attn_out,
    d_attn,
    k_pre,
    values,
    q_gain,
    k_gain,
    offsets,
    moe_in,
    router,
    expert_ids,
    d_moe,
    expert_out,
):
    dp = lax.axis_size("dp")
    sp = lax.axis_size("sp")
    me = lax.axis_index("sp").astype(jnp.int32)
    other = jnp.bitwise_xor(me, 1)
    chips = sp // 2
    swap = [(i, i ^ 1) for i in range(sp)]

    def exchange(x):
        return lax.ppermute(x, "sp", swap)

    def ahead(x, k):
        return lax.ppermute(x, "sp", [(i, (i + 2 * k) % sp) for i in range(sp)])

    def back(x, k):
        return lax.ppermute(x, "sp", [(i, (i - 2 * k) % sp) for i in range(sp)])

    def gathered(x):
        mine = [x] + [ahead(x, k) for k in range(1, chips)]
        return mine + [exchange(m) for m in mine]

    steps = 2 * jnp.arange(chips, dtype=jnp.int32)
    owners = jnp.concatenate([lax.rem(me - steps + sp, sp), lax.rem(other - steps + sp, sp)])
    qg, kg = q_gain[None, :], k_gain[None, :]

    kv = pack_keys(k_pre[0], values[0], kg)
    kv_blocks = gathered(kv)
    pack, info = gates(moe_in[0], router, expert_ids[0], d_moe[0])
    packs = gathered(pack)

    moe_share = lax.all_to_all(moe_in[0], "sp", split_axis=1, concat_axis=0, tiled=True)
    moe_all = lax.all_gather(moe_share, "dp", axis=0, tiled=True)
    info_all = lax.all_gather(info, ("dp", "sp"), axis=0, tiled=True)

    meta = jnp.concatenate([offsets + me * q_pre.shape[1], owners])
    dq, *parts = attend(
        meta,
        q_pre[0],
        attn_out[0],
        d_attn[0],
        qg,
        kv_blocks,
        [f32] * chips + [bf16] * chips,
    )
    pairs = [keep + exchange(send).astype(f32) for keep, send in zip(parts[:chips], parts[chips:])]
    arrived = [back(pairs[k].astype(bf16), k) for k in range(1, chips)]
    dk, dv = finish_keys(k_pre[0], kg, [pairs[0]] + arrived)

    experts_here, _, cap, width = expert_out.shape[1:]
    eout = jnp.transpose(expert_out[0], (0, 2, 1, 3)).reshape(experts_here * cap * sp, width)
    slot_meta = jnp.concatenate([(me * experts_here)[None], owners])
    batch, terms = slots(slot_meta, packs, eout, experts_here, cap, sp)
    batch = jnp.transpose(batch.reshape(experts_here, cap, sp, width), (0, 2, 1, 3))
    terms_all = lax.all_to_all(
        jnp.broadcast_to(terms[None], (dp * sp,) + terms.shape),
        ("dp", "sp"),
        split_axis=0,
        concat_axis=0,
        tiled=True,
    )
    router_local = router_grad(info_all, terms_all, moe_all, moe_in.shape[1], dp, sp, cap)
    return (dq[None], dk[None], dv[None], batch[None], router_local)


def solution(mesh):
    in_specs = (
        P("dp", "sp", None),
        P("dp", "sp", None),
        P("dp", "sp", None),
        P("dp", "sp", None),
        P("dp", "sp", None),
        P(),
        P(),
        P("dp"),
        P("dp", "sp", None),
        P(),
        P("dp", "sp", None),
        P("dp", "sp", None),
        P("dp", "sp", None, None, None),
    )
    out_specs = (
        P("dp", "sp", None),
        P("dp", "sp", None),
        P("dp", "sp", None),
        P("dp", "sp", None, None, None),
        P("sp", None),
    )
    return jax.shard_map(
        on_device, mesh=mesh, in_specs=in_specs, out_specs=out_specs, check_vma=False
    )
```

time: 450 us -> 181 us (0.40)
  waiting for transfers between devices: 265 us -> 14.8 us
  local copies, waits for them, and re-layouts: 55.1 us -> 9.03 us
  blocking collectives: 18.9 us -> 63.1 us
  matrix products: 31.1 us -> 0 us
  Pallas kernels: 0 us -> 29.3 us
  other arithmetic: 22.2 us -> 2.65 us
  starting transfers between devices: 40.3 us -> 46.2 us
    psum x1 -> x0, waiting for transfers between devices: 129 us -> none  [on_device(): summed = lax.psum(partial_value, ('dp', 'sp'))]
    all_to_all x10 -> x2, waiting for transfers between devices: 136 us -> 9.68 us  [the longest x1 9.68 us: on_device(): lax.all_to_all(moe_in[0], 'sp', split_axis=1, concat_axis=0, tiled=True)]
    all_gather x0 -> x1, blocking collectives: none -> 63.1 us  [on_device(): info_all = lax.all_gather(info, ('dp', 'sp'), axis=0, tiled=True)]
    ppermute x0 -> x21, starting transfers between devices: none -> 33.2 us  [the longest x6 25.7 us: ahead(): return lax.ppermute(x, 'sp', [(i, (i + 2 * k) % sp) for i in range(sp)])]
    dot_general x25 -> x0, matrix products: 31.1 us -> none  [the longest x4 8.25 us: attend(): jnp.dot(dscores.T, query_block, preferred_element_type=jnp.float32)]
    pallas_call x0 -> x6, Pallas kernels: none -> 29.3 us  [the longest x1 10.2 us: attend(): pl.pallas_call(functools.partial(attend_kernel, blocks), grid_spec=pltpu....]
    all_to_all x10 -> x2, starting transfers between devices: 40 us -> 13 us  [the longest x1 9.56 us: on_device(): lax.all_to_all(jnp.broadcast_to(terms[None], (dp * sp,) + terms.shape), (...]
    all_to_all x1 -> x0, blocking collectives: 18.9 us -> none  [on_device(): lax.all_to_all(dv_part, 'sp', split_axis=0, concat_axis=1, tiled=True)]
  transfers between devices with their start and end apart: 11 -> 24, of which waited for: 11 -> 2; matrix products, arithmetic and copies ran while one was open for 15% -> 4% of each run, Pallas kernels for 0% -> 13%
where the time goes in v1:
time: 181 us; the launch traced here: 180 us
  blocking collectives  63.1 us (35%)
  starting transfers between devices  46.2 us (26%)
  Pallas kernels  29.3 us (16%)
  between operations  15 us (8%)
  waiting for transfers between devices  14.8 us (8%)
  local copies, waits for them, and re-layouts  9.03 us (5%)
  other arithmetic  2.65 us (1%)
    all_gather x1, blocking collectives, on_device(): info_all = lax.all_gather(info, ('dp', 'sp'), axis=0, tiled=True)  63.1 us
    ppermute x6, starting transfers between devices, ahead(): return lax.ppermute(x, 'sp', [(i, (i + 2 * k) % sp) for i in range(sp)])  25.7 us
    pallas_call x1, Pallas kernels, attend(): pl.pallas_call(functools.partial(attend_kernel, blocks), grid_spec=pltpu....  10.2 us
    all_to_all x1, waiting for transfers between devices, on_device(): lax.all_to_all(moe_in[0], 'sp', split_axis=1, concat_axis=0, tiled=True)  9.68 us
    all_to_all x1, starting transfers between devices, on_device(): lax.all_to_all(jnp.broadcast_to(terms[None], (dp * sp,) + terms.shape), (...  9.56 us
    pallas_call x1, Pallas kernels, slots(): pl.pallas_call(functools.partial(slots_kernel, blocks, sp, cap), grid_spe...  7.91 us
    unnamed x48, local copies, waits for them, and re-layouts  6.67 us
    ppermute x6, waiting for transfers between devices, ahead(): return lax.ppermute(x, 'sp', [(i, (i + 2 * k) % sp) for i in range(sp)])  5.07 us
  transfers between devices with their start and end apart: 24, of which 2 were waited for; matrix products, arithmetic and copies ran while one was open for 4% of the time, Pallas kernels for 13%

profile of v1, /device:TPU:0, one launch (start us, length us, event | category | flops | bytes accessed | tf_op | source)
XLA Modules:
  0.0 180.2 jit_solution(13494825557843508179)
XLA Ops:
  7.2 1.8 %pack_keys.1.refs_0_ = bf16[128,1024]{1,0:T(8,128)(2,1)} custom-call(bf16[128,512]{1,0:T(8,128)(2,1)} %bitcast.39, bf16[128,512]{1,0:T(8,128)(2,1)} %bitcast.42, f32[1,128]{1,0:T(1,128)} %bitcast.44), custom_call_target="tpu_custom_call" | custom-call | tf_op jit(solution)/shard_map/pack_keys/pallas_call | solution.py:46
  9.0 3.0 %collective-permute-start = (bf16[128,1024]{1,0:T(8,128)(2,1)}, bf16[128,1024]{1,0:T(8,128)(2,1)S(1)}, u32[]{:S(2)}, u32[]{:S(2)}) collective-permute-start(bf16[128,1024]{1,0:T(8,128)(2,1)} %pack_keys.1.refs_0_), channel_id=1, source_target_pairs={{0,2},{1,3},{2,4},{3,5},{4,6},{5,7},{6,0},{7,1},{8,10},{9,11},{10,... | collective-permute-start | bytes 786440 | tf_op jit(solution)/shard_map/ppermute | solution.py:376
  12.0 2.6 %collective-permute-start.1 = (bf16[128,1024]{1,0:T(8,128)(2,1)}, bf16[128,1024]{1,0:T(8,128)(2,1)S(1)}, u32[]{:S(2)}, u32[]{:S(2)}) collective-permute-start(bf16[128,1024]{1,0:T(8,128)(2,1)} %pack_keys.1.refs_0_), channel_id=1, source_target_pairs={{0,4},{1,5},{2,6},{3,7},{4,0},{5,1},{6,2},{7,3},{8,12},{9,13},{10,... | collective-permute-start | bytes 786440 | tf_op jit(solution)/shard_map/ppermute | solution.py:376
  14.6 1.3 collective-permute-start.2
  16.0 0.0 collective-permute-start.3
  16.0 1.0 copy.22
  17.0 0.8 copy.21
  17.8 3.4 %all-to-all-start.1 = ((bf16[32,8,512]{2,0,1:T(8,128)(2,1)}), bf16[32,8,512]{2,0,1:T(8,128)(2,1)S(1)}, u32[]{:S(2)}, u32[]{:S(2)}) async-start(bf16[32,8,512]{2,0,1:T(8,128)(2,1)} %copy.21), calls=%async_computation.1 | async-start | bytes 524288 | tf_op jit(solution)/shard_map/all_to_all | solution.py:394
  21.2 0.0 all-gather.2.cloned.1.call-start
  21.3 1.4 copy.20
  22.6 2.4 %gates.1 = (bf16[32,4224]{1,0:T(8,128)(2,1)}, bf16[32,256]{1,0:T(8,128)(2,1)}) custom-call(bf16[32,4096]{1,0:T(8,128)(2,1)} %bitcast.33, bf16[4096,128]{1,0:T(8,128)(2,1)} %router_ref.1, s32[32,8]{1,0:T(8,128)} %bitcast.43, bf16[32,4096]{1,0:T(8,128)(2,1)} %bitcast.41), custom_call_target="tpu_custom_call" | custom-call | tf_op jit(solution)/shard_map/gates/pallas_call | solution.py:75
  25.1 1.9 %collective-permute-start.14 = (bf16[32,4224]{1,0:T(8,128)(2,1)}, bf16[32,4224]{1,0:T(8,128)(2,1)S(1)}, u32[]{:S(2)}, u32[]{:S(2)}) collective-permute-start(bf16[32,4224]{1,0:T(8,128)(2,1)} %get-tuple-element.31.refs_0_.refs_8_), channel_id=1, source_target_pairs={{0,2},{1,3},{2,4},{3,5},{4,6},{5,7},{6,0},{7,1},{8,10},{9,11},{10,... | collective-permute-start | bytes 811016 | tf_op jit(solution)/shard_map/ppermute | solution.py:376
  26.9 0.0 collective-permute-done.refs_1_
  26.9 8.9 %collective-permute-start.15 = (bf16[32,4224]{1,0:T(8,128)(2,1)}, bf16[32,4224]{1,0:T(8,128)(2,1)S(1)}, u32[]{:S(2)}, u32[]{:S(2)}) collective-permute-start(bf16[32,4224]{1,0:T(8,128)(2,1)} %get-tuple-element.31.refs_0_.refs_8_), channel_id=1, source_target_pairs={{0,4},{1,5},{2,6},{3,7},{4,0},{5,1},{6,2},{7,3},{8,12},{9,13},{10,... | collective-permute-start | bytes 811016 | tf_op jit(solution)/shard_map/ppermute | solution.py:376
  35.8 0.0 collective-permute-done.1.refs_2_
  35.8 8.0 %collective-permute-start.16 = (bf16[32,4224]{1,0:T(8,128)(2,1)}, bf16[32,4224]{1,0:T(8,128)(2,1)S(1)}, u32[]{:S(2)}, u32[]{:S(2)}) collective-permute-start(bf16[32,4224]{1,0:T(8,128)(2,1)} %get-tuple-element.31.refs_0_.refs_8_), channel_id=1, source_target_pairs={{0,6},{1,7},{2,0},{3,1},{4,2},{5,3},{6,4},{7,5},{8,14},{9,15},{10,... | collective-permute-start | bytes 811016 | tf_op jit(solution)/shard_map/ppermute | solution.py:376
  43.8 0.0 collective-permute-done.2.refs_3_
  43.8 0.0 collective-permute-start.4
  43.9 0.5 collective-permute-start.5
  44.3 0.1 collective-permute-start.6
  45.1 9.7 %all-to-all-done.1 = bf16[32,8,512]{2,0,1:T(8,128)(2,1)S(1)} async-done(((bf16[32,8,512]{2,0,1:T(8,128)(2,1)}), bf16[32,8,512]{2,0,1:T(8,128)(2,1)S(1)}, u32[]{:S(2)}, u32[]{:S(2)}) %all-to-all-start.1) | async-done | bytes 262176 | tf_op jit(solution)/shard_map/all_to_all | solution.py:394
  54.8 0.7 copy-done.8
  55.5 0.0 all-gather.2.cloned.1.call-update
  55.5 5.1 %collective-permute-done.15.refs_2_.refs_10_ = bf16[32,4224]{1,0:T(8,128)(2,1)S(1)} collective-permute-done((bf16[32,4224]{1,0:T(8,128)(2,1)}, bf16[32,4224]{1,0:T(8,128)(2,1)S(1)}, u32[]{:S(2)}, u32[]{:S(2)}) %collective-permute-start.15) | collective-permute-done | bytes 270368 | tf_op jit(solution)/shard_map/ppermute | solution.py:376
  60.6 0.0 collective-permute-start.17
  60.6 0.0 collective-permute-done.16.refs_3_.refs_11_
  60.6 0.5 collective-permute-start.18
  61.1 0.0 collective-permute-done.4.refs_5_
  61.1 0.1 collective-permute-start.19
  61.2 0.0 collective-permute-done.5.refs_6_
  61.2 0.4 collective-permute-start.20
  61.6 0.7 add_add_fusion.1
  62.3 0.0 collective-permute-done.6.refs_7_
  62.4 0.6 copy-done.22
  63.0 10.2 %attend.1 = (bf16[32,8192]{1,0:T(8,128)(2,1)}, f32[128,1024]{1,0:T(8,128)}, f32[128,1024]{1,0:T(8,128)}, f32[128,1024]{1,0:T(8,128)}, f32[128,1024]{1,0:T(8,128)...) custom-call(s32[9]{0:T(128)} %get-tuple-element.36.meta_ref, ...), custom_call_target="tpu_custom_call" | custom-call | tf_op jit(solution)/shard_map/attend/pallas_call | solution.py:155
  73.2 0.1 collective-permute-start.8
  73.4 0.0 collective-permute-done.17.refs_4_.refs_12_
  73.4 0.4 collective-permute-start.10
  73.8 0.1 collective-permute-start.7
  73.9 0.4 collective-permute-start.12
  74.4 0.0 collective-permute-done.20.refs_7_.refs_15_
  74.4 0.2 copy-done.5
  74.6 0.1 copy-done.6
  74.6 0.4 copy-done.7
  75.1 7.9 %slots.1 = (bf16[384,4096]{1,0:T(8,128)(2,1)}, f32[24,128]{1,0:T(8,128)}) custom-call(s32[9]{0:T(128)} %get-tuple-element.35.meta_ref, s32[384,3]{1,0:T(8,128)} %constant.24.clone.table_ref, s32[1,384]{1,0:T(1,128)} %constant.25.clone.lanes_ref, bf16[32,4224]{1,0:T(8,128)(2,1)} %get-tuple-element.31.refs_0_.refs_8_, bf16[32,4224]{1,0:T(8,128)(2,1)} %copy-done.1, ...), custom_call_target="tpu_custom_call" | custom-call | tf_op jit(solution)/shard_map/slots/pallas_call | solution.py:273
  83.0 1.6 broadcast_in_dim.34
  84.6 9.6 %all-to-all-start = ((f32[32,24,128]{2,1,0:T(8,128)}), f32[32,24,128]{2,1,0:T(8,128)S(1)}, u32[]{:S(2)}, u32[]{:S(2)}) async-start(f32[32,24,128]{2,1,0:T(8,128)} %broadcast_in_dim.34), calls=%async_computation | async-start | bytes 786432 | tf_op jit(solution)/shard_map/all_to_all | solution.py:417
  94.1 0.0 collective-permute-done.8
  94.2 1.0 add_convert_fusion.2
  95.2 3.7 %collective-permute-start.9 = (bf16[128,1024]{1,0:T(8,128)(2,1)S(1)}, bf16[128,1024]{1,0:T(8,128)(2,1)S(1)}, u32[]{:S(2)}, u32[]{:S(2)}) collective-permute-start(bf16[128,1024]{1,0:T(8,128)(2,1)S(1)} %add_convert_fusion.2), channel_id=1, source_target_pairs={{0,6},{1,7},{2,0},{3,1},{4,2},{5,3},{6,4},{7,5},{8,14},{9,15},{10,... | collective-permute-start | bytes 786440 | tf_op jit(solution)/shard_map/ppermute | solution.py:379
  98.8 0.0 collective-permute-done.10
  98.8 0.1 add_convert_fusion.1
  98.9 0.1 collective-permute-start.11
  99.0 0.1 add_convert_fusion
  99.1 1.1 collective-permute-start.13
  100.2 63.1 %all_gather.6.info_ref = bf16[1024,256]{1,0:T(8,128)(2,1)} all-gather(bf16[32,256]{1,0:T(8,128)(2,1)} %get-tuple-element.33), channel_id=1, replica_groups=mesh['dp'=4,'sp'=8] {'dp','sp'}, dimensions={0}, use_global_device_ids=true | all-gather | bytes 540672 | tf_op jit(solution)/shard_map/all_gather | solution.py:396
  163.3 0.9 convert_add_fusion.refs_0_
  164.2 0.7 copy-done.13
  164.9 0.1 copy-done.14
  165.0 0.7 copy-done.15
  165.7 2.3 %finish_keys.1 = (bf16[128,512]{1,0:T(8,128)(2,1)}, bf16[128,512]{1,0:T(8,128)(2,1)}) custom-call(bf16[128,512]{1,0:T(8,128)(2,1)} %bitcast.40, f32[1,128]{1,0:T(1,128)} %bitcast.45, f32[128,1024]{1,0:T(8,128)} %convert_add_fusion.refs_0_, bf16[128,1024]{1,0:T(8,128)(2,1)} %copy-done.13, bf16[128,1024]{1,0:T(8,128)(2,1)} %copy-done.14, ...), custom_call_target="tpu_custom_call" | custom-call | tf_op jit(solution)/shard_map/finish_keys/pallas_call | solution.py:191
  168.0 0.0 all-gather.2.cloned.1.call-done.moe_ref
  168.0 0.7 copy-done
  168.7 4.6 %router_grad.1 = f32[512,128]{1,0:T(8,128)} custom-call(bf16[1024,256]{1,0:T(8,128)(2,1)} %all_gather.6.info_ref, f32[32,24,128]{2,1,0:T(8,128)} %copy-done, bf16[1024,512]{1,0:T(8,128)(2,1)} %all-gather.2.cloned.1.call-done.moe_ref), custom_call_target="tpu_custom_call" | custom-call | tf_op jit(solution)/shard_map/router_grad/pallas_call | solution.py:335
  (48 shorter events, 0.1 us)
Async XLA Ops:
  9.0 17.9 %collective-permute-start = (bf16[128,1024]{1,0:T(8,128)(2,1)}, bf16[128,1024]{1,0:T(8,128)(2,1)S(1)}, u32[]{:S(2)}, u32[]{:S(2)}) collective-permute-start(bf16[128,1024]{1,0:T(8,128)(2,1)} %pack_keys.1.refs_0_), channel_id=1, source_target_pairs={{0,2},{1,3},{2,4},{3,5},{4,6},{5,7},{6,0},{7,1},{8,10},{9,11},{10,... | collective-permute-start | bytes 786440 | tf_op jit(solution)/shard_map/ppermute | solution.py:376
  12.0 23.8 %collective-permute-start.1 = (bf16[128,1024]{1,0:T(8,128)(2,1)}, bf16[128,1024]{1,0:T(8,128)(2,1)S(1)}, u32[]{:S(2)}, u32[]{:S(2)}) collective-permute-start(bf16[128,1024]{1,0:T(8,128)(2,1)} %pack_keys.1.refs_0_), channel_id=1, source_target_pairs={{0,4},{1,5},{2,6},{3,7},{4,0},{5,1},{6,2},{7,3},{8,12},{9,13},{10,... | collective-permute-start | bytes 786440 | tf_op jit(solution)/shard_map/ppermute | solution.py:376
  14.6 29.2 %collective-permute-start.2 = (bf16[128,1024]{1,0:T(8,128)(2,1)}, bf16[128,1024]{1,0:T(8,128)(2,1)S(1)}, u32[]{:S(2)}, u32[]{:S(2)}) collective-permute-start(bf16[128,1024]{1,0:T(8,128)(2,1)} %pack_keys.1.refs_0_), channel_id=1, source_target_pairs={{0,6},{1,7},{2,0},{3,1},{4,2},{5,3},{6,4},{7,5},{8,14},{9,15},{10,... | collective-permute-start | bytes 786440 | tf_op jit(solution)/shard_map/ppermute | solution.py:376
  16.0 27.9 %collective-permute-start.3 = (bf16[128,1024]{1,0:T(8,128)(2,1)}, bf16[128,1024]{1,0:T(8,128)(2,1)S(1)}, u32[]{:S(2)}, u32[]{:S(2)}) collective-permute-start(bf16[128,1024]{1,0:T(8,128)(2,1)} %pack_keys.1.refs_0_), channel_id=1, source_target_pairs={{0,1},{1,0},{2,3},{3,2},{4,5},{5,4},{6,7},{7,6},{8,9},{9,8},{10,11... | collective-permute-start | bytes 786440 | tf_op jit(solution)/shard_map/ppermute | solution.py:373
  17.8 37.0 %all-to-all-start.1 = ((bf16[32,8,512]{2,0,1:T(8,128)(2,1)}), bf16[32,8,512]{2,0,1:T(8,128)(2,1)S(1)}, u32[]{:S(2)}, u32[]{:S(2)}) async-start(bf16[32,8,512]{2,0,1:T(8,128)(2,1)} %copy.21), calls=%async_computation.1 | async-start | bytes 524288 | tf_op jit(solution)/shard_map/all_to_all | solution.py:394
  21.2 146.8 %all-gather.2.cloned.1.call-start = ((), (), s32[]{:S(2)}) async-start(), calls=%async_computation.2 | async-start | bytes 1310720 | tf_op jit(solution)/shard_map/all_gather | solution.py:395
  25.1 19.3 %collective-permute-start.14 = (bf16[32,4224]{1,0:T(8,128)(2,1)}, bf16[32,4224]{1,0:T(8,128)(2,1)S(1)}, u32[]{:S(2)}, u32[]{:S(2)}) collective-permute-start(bf16[32,4224]{1,0:T(8,128)(2,1)} %get-tuple-element.31.refs_0_.refs_8_), channel_id=1, source_target_pairs={{0,2},{1,3},{2,4},{3,5},{4,6},{5,7},{6,0},{7,1},{8,10},{9,11},{10,... | collective-permute-start | bytes 811016 | tf_op jit(solution)/shard_map/ppermute | solution.py:376
  26.9 35.4 %copy-start.16 = (bf16[128,1024]{1,0:T(8,128)(2,1)}, bf16[128,1024]{1,0:T(8,128)(2,1)S(1)}, u32[]{:S(2)}) copy-start(bf16[128,1024]{1,0:T(8,128)(2,1)S(1)} %collective-permute-done.refs_1_) | copy-start | bytes 786436
  26.9 33.7 %collective-permute-start.15 = (bf16[32,4224]{1,0:T(8,128)(2,1)}, bf16[32,4224]{1,0:T(8,128)(2,1)S(1)}, u32[]{:S(2)}, u32[]{:S(2)}) collective-permute-start(bf16[32,4224]{1,0:T(8,128)(2,1)} %get-tuple-element.31.refs_0_.refs_8_), channel_id=1, source_target_pairs={{0,4},{1,5},{2,6},{3,7},{4,0},{5,1},{6,2},{7,3},{8,12},{9,13},{10,... | collective-permute-start | bytes 811016 | tf_op jit(solution)/shard_map/ppermute | solution.py:376
  35.8 26.5 %copy-start.17 = (bf16[128,1024]{1,0:T(8,128)(2,1)}, bf16[128,1024]{1,0:T(8,128)(2,1)S(1)}, u32[]{:S(2)}) copy-start(bf16[128,1024]{1,0:T(8,128)(2,1)S(1)} %collective-permute-done.1.refs_2_) | copy-start | bytes 786436
  35.8 24.8 %collective-permute-start.16 = (bf16[32,4224]{1,0:T(8,128)(2,1)}, bf16[32,4224]{1,0:T(8,128)(2,1)S(1)}, u32[]{:S(2)}, u32[]{:S(2)}) collective-permute-start(bf16[32,4224]{1,0:T(8,128)(2,1)} %get-tuple-element.31.refs_0_.refs_8_), channel_id=1, source_target_pairs={{0,6},{1,7},{2,0},{3,1},{4,2},{5,3},{6,4},{7,5},{8,14},{9,15},{10,... | collective-permute-start | bytes 811016 | tf_op jit(solution)/shard_map/ppermute | solution.py:376
  43.8 18.5 %copy-start.18 = (bf16[128,1024]{1,0:T(8,128)(2,1)}, bf16[128,1024]{1,0:T(8,128)(2,1)S(1)}, u32[]{:S(2)}) copy-start(bf16[128,1024]{1,0:T(8,128)(2,1)S(1)} %collective-permute-done.2.refs_3_) | copy-start | bytes 786436
  43.8 17.3 %collective-permute-start.4 = (bf16[128,1024]{1,0:T(8,128)(2,1)S(1)}, bf16[128,1024]{1,0:T(8,128)(2,1)S(1)}, u32[]{:S(2)}, u32[]{:S(2)}) collective-permute-start(bf16[128,1024]{1,0:T(8,128)(2,1)S(1)} %collective-permute-done.refs_1_), channel_id=1, source_target_pairs={{0,1},{1,0},{2,3},{3,2},{4,5},{5,4},{6,7},{7,6},{8,9},{9,8},{10,11... | collective-permute-start | bytes 786440 | tf_op jit(solution)/shard_map/ppermute | solution.py:373
  43.8 18.5 %copy-start.19 = (bf16[128,1024]{1,0:T(8,128)(2,1)}, bf16[128,1024]{1,0:T(8,128)(2,1)S(1)}, u32[]{:S(2)}) copy-start(bf16[128,1024]{1,0:T(8,128)(2,1)S(1)} %collective-permute-done.3.refs_4_) | copy-start | bytes 786436
  43.9 17.4 %collective-permute-start.5 = (bf16[128,1024]{1,0:T(8,128)(2,1)S(1)}, bf16[128,1024]{1,0:T(8,128)(2,1)S(1)}, u32[]{:S(2)}, u32[]{:S(2)}) collective-permute-start(bf16[128,1024]{1,0:T(8,128)(2,1)S(1)} %collective-permute-done.1.refs_2_), channel_id=1, source_target_pairs={{0,1},{1,0},{2,3},{3,2},{4,5},{5,4},{6,7},{7,6},{8,9},{9,8},{10,11... | collective-permute-start | bytes 786440 | tf_op jit(solution)/shard_map/ppermute | solution.py:373
  44.3 30.0 %copy-start.1 = (bf16[32,4224]{1,0:T(8,128)(2,1)}, bf16[32,4224]{1,0:T(8,128)(2,1)S(1)}, u32[]{:S(2)}) copy-start(bf16[32,4224]{1,0:T(8,128)(2,1)S(1)} %collective-permute-done.14.refs_1_.refs_9_) | copy-start | bytes 811012
  44.3 17.9 %collective-permute-start.6 = (bf16[128,1024]{1,0:T(8,128)(2,1)S(1)}, bf16[128,1024]{1,0:T(8,128)(2,1)S(1)}, u32[]{:S(2)}, u32[]{:S(2)}) collective-permute-start(bf16[128,1024]{1,0:T(8,128)(2,1)S(1)} %collective-permute-done.2.refs_3_), channel_id=1, source_target_pairs={{0,1},{1,0},{2,3},{3,2},{4,5},{5,4},{6,7},{7,6},{8,9},{9,8},{10,11... | collective-permute-start | bytes 786440 | tf_op jit(solution)/shard_map/ppermute | solution.py:373
  54.8 0.7 copy-start.8
  60.6 13.8 %copy-start.2 = (bf16[32,4224]{1,0:T(8,128)(2,1)}, bf16[32,4224]{1,0:T(8,128)(2,1)S(1)}, u32[]{:S(2)}) copy-start(bf16[32,4224]{1,0:T(8,128)(2,1)S(1)} %collective-permute-done.15.refs_2_.refs_10_) | copy-start | bytes 811012
  60.6 12.8 %collective-permute-start.17 = (bf16[32,4224]{1,0:T(8,128)(2,1)}, bf16[32,4224]{1,0:T(8,128)(2,1)S(1)}, u32[]{:S(2)}, u32[]{:S(2)}) collective-permute-start(bf16[32,4224]{1,0:T(8,128)(2,1)} %get-tuple-element.31.refs_0_.refs_8_), channel_id=1, source_target_pairs={{0,1},{1,0},{2,3},{3,2},{4,5},{5,4},{6,7},{7,6},{8,9},{9,8},{10,11... | collective-permute-start | bytes 811016 | tf_op jit(solution)/shard_map/ppermute | solution.py:373
  60.6 13.8 %copy-start.3 = (bf16[32,4224]{1,0:T(8,128)(2,1)}, bf16[32,4224]{1,0:T(8,128)(2,1)S(1)}, u32[]{:S(2)}) copy-start(bf16[32,4224]{1,0:T(8,128)(2,1)S(1)} %collective-permute-done.16.refs_3_.refs_11_) | copy-start | bytes 811012
  60.6 13.2 %collective-permute-start.18 = (bf16[32,4224]{1,0:T(8,128)(2,1)S(1)}, bf16[32,4224]{1,0:T(8,128)(2,1)S(1)}, u32[]{:S(2)}, u32[]{:S(2)}) collective-permute-start(bf16[32,4224]{1,0:T(8,128)(2,1)S(1)} %collective-permute-done.14.refs_1_.refs_9_), channel_id=1, source_target_pairs={{0,1},{1,0},{2,3},{3,2},{4,5},{5,4},{6,7},{7,6},{8,9},{9,8},{10,11... | collective-permute-start | bytes 811016 | tf_op jit(solution)/shard_map/ppermute | solution.py:373
  61.1 1.2 copy-start.20
  61.1 12.8 %collective-permute-start.19 = (bf16[32,4224]{1,0:T(8,128)(2,1)S(1)}, bf16[32,4224]{1,0:T(8,128)(2,1)S(1)}, u32[]{:S(2)}, u32[]{:S(2)}) collective-permute-start(bf16[32,4224]{1,0:T(8,128)(2,1)S(1)} %collective-permute-done.15.refs_2_.refs_10_), channel_id=1, source_target_pairs={{0,1},{1,0},{2,3},{3,2},{4,5},{5,4},{6,7},{7,6},{8,9},{9,8},{10,11... | collective-permute-start | bytes 811016 | tf_op jit(solution)/shard_map/ppermute | solution.py:373
  61.2 1.1 copy-start.21
  61.2 13.1 %collective-permute-start.20 = (bf16[32,4224]{1,0:T(8,128)(2,1)S(1)}, bf16[32,4224]{1,0:T(8,128)(2,1)S(1)}, u32[]{:S(2)}, u32[]{:S(2)}) collective-permute-start(bf16[32,4224]{1,0:T(8,128)(2,1)S(1)} %collective-permute-done.16.refs_3_.refs_11_), channel_id=1, source_target_pairs={{0,1},{1,0},{2,3},{3,2},{4,5},{5,4},{6,7},{7,6},{8,9},{9,8},{10,11... | collective-permute-start | bytes 811016 | tf_op jit(solution)/shard_map/ppermute | solution.py:373
  62.3 0.7 copy-start.22
  73.2 20.9 %collective-permute-start.8 = (bf16[128,1024]{1,0:T(8,128)(2,1)}, bf16[128,1024]{1,0:T(8,128)(2,1)}, u32[]{:S(2)}, u32[]{:S(2)}) collective-permute-start(bf16[128,1024]{1,0:T(8,128)(2,1)} %get-tuple-element.24), channel_id=1, source_target_pairs={{0,1},{1,0},{2,3},{3,2},{4,5},{5,4},{6,7},{7,6},{8,9},{9,8},{10,11... | collective-permute-start | bytes 786440 | tf_op jit(solution)/shard_map/ppermute | solution.py:373
  73.4 1.0 copy-start.4
  73.4 25.4 %collective-permute-start.10 = (bf16[128,1024]{1,0:T(8,128)(2,1)}, bf16[128,1024]{1,0:T(8,128)(2,1)S(1)}, u32[]{:S(2)}, u32[]{:S(2)}) collective-permute-start(bf16[128,1024]{1,0:T(8,128)(2,1)} %get-tuple-element.26), channel_id=1, source_target_pairs={{0,1},{1,0},{2,3},{3,2},{4,5},{5,4},{6,7},{7,6},{8,9},{9,8},{10,11... | collective-permute-start | bytes 786440 | tf_op jit(solution)/shard_map/ppermute | solution.py:373
  73.8 0.7 copy-start.5
  73.8 89.5 %collective-permute-start.7 = (bf16[128,1024]{1,0:T(8,128)(2,1)}, bf16[128,1024]{1,0:T(8,128)(2,1)S(1)}, u32[]{:S(2)}, u32[]{:S(2)}) collective-permute-start(bf16[128,1024]{1,0:T(8,128)(2,1)} %get-tuple-element.22), channel_id=1, source_target_pairs={{0,1},{1,0},{2,3},{3,2},{4,5},{5,4},{6,7},{7,6},{8,9},{9,8},{10,11... | collective-permute-start | bytes 786440 | tf_op jit(solution)/shard_map/ppermute | solution.py:373
  73.9 0.7 copy-start.6
  73.9 25.1 %collective-permute-start.12 = (bf16[128,1024]{1,0:T(8,128)(2,1)}, bf16[128,1024]{1,0:T(8,128)(2,1)S(1)}, u32[]{:S(2)}, u32[]{:S(2)}) collective-permute-start(bf16[128,1024]{1,0:T(8,128)(2,1)} %get-tuple-element.28), channel_id=1, source_target_pairs={{0,1},{1,0},{2,3},{3,2},{4,5},{5,4},{6,7},{7,6},{8,9},{9,8},{10,11... | collective-permute-start | bytes 786440 | tf_op jit(solution)/shard_map/ppermute | solution.py:373
  74.4 0.7 copy-start.7
  75.1 19.1 %copy-start.12 = (f32[128,1024]{1,0:T(8,128)S(1)}, f32[128,1024]{1,0:T(8,128)}, u32[]{:S(2)}) copy-start(f32[128,1024]{1,0:T(8,128)} %get-tuple-element.23) | copy-start | bytes 1572868
  75.1 23.8 %copy-start.11 = (f32[128,1024]{1,0:T(8,128)S(1)}, f32[128,1024]{1,0:T(8,128)}, u32[]{:S(2)}) copy-start(f32[128,1024]{1,0:T(8,128)} %get-tuple-element.25) | copy-start | bytes 1572868
  83.0 16.0 %copy-start.10 = (f32[128,1024]{1,0:T(8,128)S(1)}, f32[128,1024]{1,0:T(8,128)}, u32[]{:S(2)}) copy-start(f32[128,1024]{1,0:T(8,128)} %get-tuple-element.27) | copy-start | bytes 1572868
  83.0 80.3 %copy-start.9 = (f32[128,1024]{1,0:T(8,128)S(1)}, f32[128,1024]{1,0:T(8,128)}, u32[]{:S(2)}) copy-start(f32[128,1024]{1,0:T(8,128)} %get-tuple-element.21) | copy-start | bytes 1572868
  84.6 83.4 %all-to-all-start = ((f32[32,24,128]{2,1,0:T(8,128)}), f32[32,24,128]{2,1,0:T(8,128)S(1)}, u32[]{:S(2)}, u32[]{:S(2)}) async-start(f32[32,24,128]{2,1,0:T(8,128)} %broadcast_in_dim.34), calls=%async_computation | async-start | bytes 786432 | tf_op jit(solution)/shard_map/all_to_all | solution.py:417
  95.2 69.0 %collective-permute-start.9 = (bf16[128,1024]{1,0:T(8,128)(2,1)S(1)}, bf16[128,1024]{1,0:T(8,128)(2,1)S(1)}, u32[]{:S(2)}, u32[]{:S(2)}) collective-permute-start(bf16[128,1024]{1,0:T(8,128)(2,1)S(1)} %add_convert_fusion.2), channel_id=1, source_target_pairs={{0,6},{1,7},{2,0},{3,1},{4,2},{5,3},{6,4},{7,5},{8,14},{9,15},{10,... | collective-permute-start | bytes 786440 | tf_op jit(solution)/shard_map/ppermute | solution.py:379
  98.9 65.3 %collective-permute-start.11 = (bf16[128,1024]{1,0:T(8,128)(2,1)S(1)}, bf16[128,1024]{1,0:T(8,128)(2,1)S(1)}, u32[]{:S(2)}, u32[]{:S(2)}) collective-permute-start(bf16[128,1024]{1,0:T(8,128)(2,1)S(1)} %add_convert_fusion.1), channel_id=1, source_target_pairs={{0,4},{1,5},{2,6},{3,7},{4,0},{5,1},{6,2},{7,3},{8,12},{9,13},{10,... | collective-permute-start | bytes 786440 | tf_op jit(solution)/shard_map/ppermute | solution.py:379
  99.1 65.1 %collective-permute-start.13 = (bf16[128,1024]{1,0:T(8,128)(2,1)S(1)}, bf16[128,1024]{1,0:T(8,128)(2,1)S(1)}, u32[]{:S(2)}, u32[]{:S(2)}) collective-permute-start(bf16[128,1024]{1,0:T(8,128)(2,1)S(1)} %add_convert_fusion), channel_id=1, source_target_pairs={{0,2},{1,3},{2,4},{3,5},{4,6},{5,7},{6,0},{7,1},{8,10},{9,11},{10,... | collective-permute-start | bytes 786440 | tf_op jit(solution)/shard_map/ppermute | solution.py:379
  164.2 0.7 copy-start.13
  164.2 0.8 copy-start.14
  165.0 0.7 copy-start.15
  168.0 0.8 copy-start
Sparse Core Ops, SparseCore 0:
  55.7 32.6 all-gather.1

commit v2 on v1

--- a/solution.py
+++ b/solution.py
@@ -31,26 +31,28 @@
     return pl.BlockSpec(shape, lambda *_: (0,) * len(shape))
 
 
-def keys_kernel(k_ref, v_ref, gain_ref, kv_ref):
+def keys_kernel(k_ref, v_ref, gain_ref, *kv_refs):
     hd = gain_ref.shape[1]
     gain = gain_ref[...]
+    each = k_ref.shape[1] // hd // len(kv_refs)
     for g in range(k_ref.shape[1] // hd):
+        kv_ref, i = kv_refs[g // each], g % each
         k = k_ref[:, g * hd : (g + 1) * hd].astype(f32)
         inv = lax.rsqrt(jnp.mean(k * k, axis=-1, keepdims=True) + norm_eps)
-        kv_ref[:, 2 * g * hd : (2 * g + 1) * hd] = ((k * inv) * gain).astype(bf16)
-        kv_ref[:, (2 * g + 1) * hd : (2 * g + 2) * hd] = v_ref[:, g * hd : (g + 1) * hd]
-
-
-def pack_keys(k_pre, values, k_gain):
+        kv_ref[:, 2 * i * hd : (2 * i + 1) * hd] = ((k * inv) * gain).astype(bf16)
+        kv_ref[:, (2 * i + 1) * hd : (2 * i + 2) * hd] = v_ref[:, g * hd : (g + 1) * hd]
+
+
+def pack_keys(k_pre, values, k_gain, parts):
     rows, width = k_pre.shape
     return pl.pallas_call(
         keys_kernel,
-        out_shape=jax.ShapeDtypeStruct((rows, 2 * width), bf16),
+        out_shape=[jax.ShapeDtypeStruct((rows, 2 * width // parts), bf16)] * parts,
         name="pack_keys",
     )(k_pre, values, k_gain)
 
 
-def gates_kernel(moe_ref, router_ref, ids_ref, dmoe_ref, pack_ref, info_ref):
+def gates_kernel(chips, meta_ref, moe_ref, router_ref, ids_ref, dmoe_ref, pack_ref, *share_refs):
     tok, width = moe_ref.shape
     experts = router_ref.shape[1]
     logits = dot_nn(moe_ref[...], router_ref[...])
@@ -62,29 +64,35 @@
     probs = weights / jnp.sum(weights, axis=-1, keepdims=True)
     high = probs.astype(bf16)
     low = (probs - high.astype(f32)).astype(bf16)
-    coded = jnp.where(chosen, high.astype(f32), -1.0).astype(bf16)
     pack_ref[:, :width] = dmoe_ref[...]
-    pack_ref[:, width:] = coded
-    info_ref[:, :experts] = coded
-    info_ref[:, experts:] = low
-
-
-def gates(moe_in, router, ids, d_moe):
+    pack_ref[:, width : width + experts] = jnp.where(chosen, high.astype(f32), -1.0).astype(bf16)
+    pack_ref[:, width + experts :] = low
+    share = width // (2 * chips)
+    chip, core = meta_ref[0], meta_ref[1]
+    for k in range(chips):
+        to = lax.rem(chip + k, chips) * 2
+        for i in range(2):
+            at = pl.multiple_of((to + lax.rem(core + i, 2)) * share, 128)
+            share_refs[k][:, i * share : (i + 1) * share] = moe_ref[:, pl.ds(at, share)]
+
+
+def gates(meta, moe_in, router, ids, d_moe, chips):
     tok, width = moe_in.shape
     experts = router.shape[1]
-    return pl.pallas_call(
-        gates_kernel,
-        out_shape=(
-            jax.ShapeDtypeStruct((tok, width + experts), bf16),
-            jax.ShapeDtypeStruct((tok, 2 * experts), bf16),
-        ),
+    vm = pl.BlockSpec(memory_space=pltpu.VMEM)
+    return pl.pallas_call(
+        functools.partial(gates_kernel, chips),
+        in_specs=[pl.BlockSpec(memory_space=pltpu.SMEM)] + [vm] * 4,
+        out_shape=[jax.ShapeDtypeStruct((tok, width + 2 * experts), bf16)]
+        + [jax.ShapeDtypeStruct((tok, width // chips), bf16)] * chips,
         compiler_params=pltpu.CompilerParams(vmem_limit_bytes=vmem_limit),
         name="gates",
-    )(moe_in, router, ids, d_moe)
-
-
-def attend_kernel(blocks, meta_ref, q_ref, o_ref, do_ref, gain_ref, *refs):
+    )(meta, moe_in, router, ids, d_moe)
+
+
+def attend_kernel(blocks, first, meta_ref, q_ref, o_ref, do_ref, gain_ref, *refs):
     kv_refs = refs[:blocks]
+    refs = refs[:blocks] + refs[blocks + (first > 0) :]
     dq_ref = refs[blocks]
     part_refs = refs[blocks + 1 : 2 * blocks + 1]
     tok = q_ref.shape[0]
@@ -143,54 +151,64 @@
         part_refs[b][:, hd:] = dv[b * kb : (b + 1) * kb, :].astype(part_refs[b].dtype)
 
 
-def attend(meta, q, o, do, gain, kv_blocks, part_types):
+def attend(meta, q, o, do, gain, kv_blocks, part_types, kv_heads, first, dq):
     tok, width = q.shape
     hd = gain.shape[1]
     kb, kv_width = kv_blocks[0].shape
-    kv_heads = kv_width // (2 * hd)
     blocks = len(kv_blocks)
     step = width // kv_heads
-    row_spec = pl.BlockSpec((tok, step), lambda g, m: (0, g))
+    row_spec = pl.BlockSpec((tok, step), lambda g, m: (0, g + first))
+    filled = [] if dq is None else [dq]
     kv_spec = pl.BlockSpec((kb, 2 * hd), lambda g, m: (0, g))
     return pl.pallas_call(
-        functools.partial(attend_kernel, blocks),
+        functools.partial(attend_kernel, blocks, first),
         grid_spec=pltpu.PrefetchScalarGridSpec(
             num_scalar_prefetch=1,
-            grid=(kv_heads,),
-            in_specs=[row_spec] * 3 + [whole((1, hd))] + [kv_spec] * blocks,
+            grid=(kv_width // (2 * hd),),
+            in_specs=[row_spec] * 3
+            + [whole((1, hd))]
+            + [kv_spec] * blocks
+            + [pl.BlockSpec(memory_space=pl.ANY)] * len(filled),
             out_specs=[row_spec] + [kv_spec] * blocks,
         ),
         out_shape=[jax.ShapeDtypeStruct((tok, width), bf16)]
         + [jax.ShapeDtypeStruct((kb, kv_width), t) for t in part_types],
         compiler_params=pltpu.CompilerParams(vmem_limit_bytes=vmem_limit),
+        input_output_aliases={5 + blocks: 0} if filled else {},
         name="attend",
-    )(meta, q, o, do, gain, *kv_blocks)
-
-
-def finish_kernel(k_ref, gain_ref, *refs):
+    )(meta, q, o, do, gain, *kv_blocks, *filled)
+
+
+def finish_kernel(parts, k_ref, gain_ref, *refs):
     dk_ref, dv_ref = refs[-2:]
     hd = gain_ref.shape[1]
     gain = gain_ref[...]
-    total = refs[0][...].astype(f32)
-    for r in refs[1:-2]:
-        total = total + r[...].astype(f32)
-    for g in range(k_ref.shape[1] // hd):
-        k = k_ref[:, g * hd : (g + 1) * hd].astype(f32)
-        inv = lax.rsqrt(jnp.mean(k * k, axis=-1, keepdims=True) + norm_eps)
-        unit = k * inv
-        c = total[:, 2 * g * hd : (2 * g + 1) * hd] * gain
-        dk = inv * (c - unit * jnp.mean(c * unit, axis=-1, keepdims=True))
-        dk_ref[:, g * hd : (g + 1) * hd] = dk.astype(bf16)
-        dv_ref[:, g * hd : (g + 1) * hd] = total[
-            :, (2 * g + 1) * hd : (2 * g + 2) * hd
-        ].astype(bf16)
-
-
-def finish_keys(k_pre, k_gain, parts):
+    each = (len(refs) - 2) // parts
+    heads = k_ref.shape[1] // hd
+    for p in range(parts):
+        total = refs[p * each][...].astype(f32)
+        for r in refs[p * each + 1 : (p + 1) * each]:
+            total = total + r[...].astype(f32)
+        for i in range(heads // parts):
+            g = p * (heads // parts) + i
+            k = k_ref[:, g * hd : (g + 1) * hd].astype(f32)
+            inv = lax.rsqrt(jnp.mean(k * k, axis=-1, keepdims=True) + norm_eps)
+            unit = k * inv
+            c = total[:, 2 * i * hd : (2 * i + 1) * hd] * gain
+            dk = inv * (c - unit * jnp.mean(c * unit, axis=-1, keepdims=True))
+            dk_ref[:, g * hd : (g + 1) * hd] = dk.astype(bf16)
+            dv = total[:, (2 * i + 1) * hd : (2 * i + 2) * hd]
+            dv_ref[:, g * hd : (g + 1) * hd] = dv.astype(bf16)
+
+
+def finish_keys(k_pre, k_gain, sums):
     out = jax.ShapeDtypeStruct(k_pre.shape, bf16)
-    return pl.pallas_call(finish_kernel, out_shape=(out, out), name="finish_keys")(
-        k_pre, k_gain, *parts
-    )
+    return pl.pallas_call(
+        functools.partial(finish_kernel, len(sums)),
+        out_shape=(out, out),
+        compiler_params=pltpu.CompilerParams(vmem_limit_bytes=vmem_limit),
+        name="finish_keys",
+    )(k_pre, k_gain, *[x for part in sums for x in part])
 
 
 def earlier_same_block(rows, block):
@@ -260,7 +278,7 @@
 def slots(meta, packs, eout, experts_here, cap, sp):
     rows, width = eout.shape
     tok, packed = packs[0].shape
-    experts = packed - width
+    experts = (packed - width) // 2
     blocks = len(packs)
     r = np.arange(rows)
     e, c, s = r // (cap * sp), (r // sp) % cap, r % sp
@@ -296,25 +314,32 @@
     )(meta, table, lanes, *packs, *packs, eout)
 
 
-def router_kernel(tok, sp, cap, info_ref, terms_ref, moe_ref, out_ref):
-    tokens = moe_ref.shape[0]
-    experts = out_ref.shape[1]
-
-    @pl.when(pl.program_id(0) == 0)
-    def _():
-        out_ref[...] = jnp.zeros_like(out_ref)
-
-    high = info_ref[:, :experts]
+def router_kernel(sp, cap, meta_ref, *refs):
+    blocks = sp
+    half = sp // 2
+    info_refs = refs[:blocks]
+    term_refs = refs[blocks : blocks + half]
+    mine_refs = refs[blocks + half : blocks + 2 * half]
+    sent_ref, out_ref, terms_scr = refs[blocks + 2 * half :]
+    share, experts = out_ref.shape
+    tok = info_refs[0].shape[0]
+    info = jnp.concatenate([r[...] for r in info_refs], axis=0)
+    moe = jnp.concatenate([r[:, :share] for r in mine_refs] + [sent_ref[...]], axis=0)
+    terms = term_refs[0][...]
+    for r in term_refs[1:]:
+        terms = terms + r[...]
+    terms_scr[...] = terms
+    high = info[:, :experts]
     chosen = high >= 0
-    prob = jnp.where(chosen, high.astype(f32) + info_ref[:, experts:].astype(f32), 0.0)
-    rank = dot_nn(earlier_same_block(tokens, tok), chosen.astype(bf16))
-    terms = jnp.sum(terms_ref[...], axis=0)
+    prob = jnp.where(chosen, high.astype(f32) + info[:, experts:].astype(f32), 0.0)
+    rank = dot_nn(earlier_same_block(tok * blocks, tok), chosen.astype(bf16))
     pieces = []
-    for s in range(sp):
-        place = rank[s * tok : (s + 1) * tok, :]
+    for b in range(blocks):
+        place = rank[b * tok : (b + 1) * tok, :]
         one = jnp.zeros((tok, experts), f32)
         for c in range(cap):
-            one = jnp.where(place == c, terms[c * sp + s : c * sp + s + 1, :], one)
+            row = terms_scr[pl.ds(c * sp + meta_ref[1 + b], 1), :]
+            one = jnp.where(place == c, row, one)
         pieces.append(one)
     dgate = jnp.where(chosen, jnp.concatenate(pieces, axis=0), 0.0)
     dlogit = prob * (dgate - jnp.sum(prob * dgate, axis=-1, keepdims=True))
@@ -322,29 +347,32 @@
     rest = dlogit - a.astype(f32)
     b = rest.astype(bf16)
     c = (rest - b.astype(f32)).astype(bf16)
-    wide = dot_tn(moe_ref[...], jnp.concatenate([a, b, c], axis=1))
-    out_ref[...] += (
-        wide[:, :experts] + wide[:, experts : 2 * experts] + wide[:, 2 * experts :]
-    )
-
-
-def router_grad(info, terms, moe, tok, dp, sp, cap):
-    tokens = info.shape[0] // dp
-    experts = info.shape[1] // 2
-    share = moe.shape[1]
-    return pl.pallas_call(
-        functools.partial(router_kernel, tok, sp, cap),
-        grid=(dp,),
-        in_specs=[
-            pl.BlockSpec((tokens, 2 * experts), lambda g: (g, 0)),
-            pl.BlockSpec((sp, cap * sp, experts), lambda g: (g, 0, 0)),
-            pl.BlockSpec((tokens, share), lambda g: (g, 0)),
-        ],
-        out_specs=whole((share, experts)),
+    wide = dot_tn(moe, jnp.concatenate([a, b, c], axis=1))
+    out_ref[...] = wide[:, :experts] + wide[:, experts : 2 * experts] + wide[:, 2 * experts :]
+
+
+def router_grad(meta, packs, terms, mine, sent, width, cap):
+    sp = len(packs)
+    tok, packed = packs[0].shape
+    experts = (packed - width) // 2
+    share = sent.shape[1]
+    info_spec = pl.BlockSpec((tok, 2 * experts), lambda i, m: (0, width // (2 * experts)))
+    return pl.pallas_call(
+        functools.partial(router_kernel, sp, cap),
+        grid_spec=pltpu.PrefetchScalarGridSpec(
+            num_scalar_prefetch=1,
+            grid=(1,),
+            in_specs=[info_spec] * sp
+            + [whole(terms[0].shape)] * len(terms)
+            + [whole(mine[0].shape)] * len(mine)
+            + [whole(sent.shape)],
+            out_specs=whole((share, experts)),
+            scratch_shapes=[pltpu.VMEM((cap * sp, experts), f32)],
+        ),
         out_shape=jax.ShapeDtypeStruct((share, experts), f32),
         compiler_params=pltpu.CompilerParams(vmem_limit_bytes=vmem_limit),
         name="router_grad",
-    )(info, terms, moe)
+    )(meta, *packs, *terms, *mine, sent)
 
 
 def on_device(
@@ -385,43 +413,54 @@
     steps = 2 * jnp.arange(chips, dtype=jnp.int32)
     owners = jnp.concatenate([lax.rem(me - steps + sp, sp), lax.rem(other - steps + sp, sp)])
     qg, kg = q_gain[None, :], k_gain[None, :]
-
-    kv = pack_keys(k_pre[0], values[0], kg)
-    kv_blocks = gathered(kv)
-    pack, info = gates(moe_in[0], router, expert_ids[0], d_moe[0])
+    kv_heads = k_pre.shape[2] // q_gain.shape[0]
+    parts = 2
+    width = moe_in.shape[2]
+    place = jnp.stack([me // 2, jnp.bitwise_and(me, 1)])
+
+    pack, *shares = gates(place, moe_in[0], router, expert_ids[0], d_moe[0], chips)
     packs = gathered(pack)
-
-    moe_share = lax.all_to_all(moe_in[0], "sp", split_axis=1, concat_axis=0, tiled=True)
-    moe_all = lax.all_gather(moe_share, "dp", axis=0, tiled=True)
-    info_all = lax.all_gather(info, ("dp", "sp"), axis=0, tiled=True)
+    kv_parts = [gathered(kv) for kv in pack_keys(k_pre[0], values[0], kg, parts)]
+    mine = [shares[0]] + [ahead(shares[k], k) for k in range(1, chips)]
+    share = width // sp
+    sent = exchange(jnp.concatenate([m[:, share:] for m in mine], axis=0))
 
     meta = jnp.concatenate([offsets + me * q_pre.shape[1], owners])
-    dq, *parts = attend(
-        meta,
-        q_pre[0],
-        attn_out[0],
-        d_attn[0],
-        qg,
-        kv_blocks,
-        [f32] * chips + [bf16] * chips,
-    )
-    pairs = [keep + exchange(send).astype(f32) for keep, send in zip(parts[:chips], parts[chips:])]
-    arrived = [back(pairs[k].astype(bf16), k) for k in range(1, chips)]
-    dk, dv = finish_keys(k_pre[0], kg, [pairs[0]] + arrived)
-
-    experts_here, _, cap, width = expert_out.shape[1:]
+    dq, sums = None, []
+    for p in range(parts):
+        dq, *terms = attend(
+            meta,
+            q_pre[0],
+            attn_out[0],
+            d_attn[0],
+            qg,
+            kv_parts[p],
+            [f32] * chips + [bf16] * chips,
+            kv_heads,
+            p * (kv_heads // parts),
+            dq,
+        )
+        pairs = [
+            keep + exchange(send).astype(f32) for keep, send in zip(terms[:chips], terms[chips:])
+        ]
+        sums.append([pairs[0]] + [back(pairs[k].astype(bf16), k) for k in range(1, chips)])
+    dk, dv = finish_keys(k_pre[0], kg, sums)
+
+    experts_here, _, cap, _ = expert_out.shape[1:]
     eout = jnp.transpose(expert_out[0], (0, 2, 1, 3)).reshape(experts_here * cap * sp, width)
     slot_meta = jnp.concatenate([(me * experts_here)[None], owners])
     batch, terms = slots(slot_meta, packs, eout, experts_here, cap, sp)
     batch = jnp.transpose(batch.reshape(experts_here, cap, sp, width), (0, 2, 1, 3))
-    terms_all = lax.all_to_all(
-        jnp.broadcast_to(terms[None], (dp * sp,) + terms.shape),
-        ("dp", "sp"),
-        split_axis=0,
-        concat_axis=0,
-        tiled=True,
-    )
-    router_local = router_grad(info_all, terms_all, moe_all, moe_in.shape[1], dp, sp, cap)
+    terms = terms + exchange(terms)
+    terms = [terms] + [ahead(terms, k) for k in range(1, chips)]
+    partial_sum = router_grad(slot_meta, packs, terms, mine, sent, width, cap)
+    router_local = partial_sum
+    for k in range(1, dp):
+        if dp & (dp - 1):
+            perm = [(i, (i + k) % dp) for i in range(dp)]
+        else:
+            perm = [(i, i ^ k) for i in range(dp)]
+        router_local = router_local + lax.ppermute(partial_sum, "dp", perm)
     return (dq[None], dk[None], dv[None], batch[None], router_local)
 
 

time: 181 us -> 125 us (0.69)
  blocking collectives: 63.1 us -> 0 us
  waiting for transfers between devices: 14.8 us -> 33.4 us
  between operations: 15 us -> 1.89 us
  local copies, waits for them, and re-layouts: 9.03 us -> 5.2 us
  other arithmetic: 2.65 us -> 5.33 us
  starting transfers between devices: 46.2 us -> 48.8 us
    all_gather x1 -> x0, blocking collectives: 63.1 us -> none  [on_device(): info_all = lax.all_gather(info, ('dp', 'sp'), axis=0, tiled=True)]
    ppermute x6 -> x15, waiting for transfers between devices: 5.07 us -> 23.9 us  [ahead(): return lax.ppermute(x, 'sp', [(i, (i + 2 * k) % sp) for i in range(sp)])]
    all_to_all x2 -> x0, starting transfers between devices: 13 us -> none  [the longest x1 9.56 us: on_device(): lax.all_to_all(jnp.broadcast_to(terms[None], (dp * sp,) + terms.shape), (...]
    all_to_all x2 -> x0, waiting for transfers between devices: 9.68 us -> none  [the longest x1 9.68 us: on_device(): lax.all_to_all(moe_in[0], 'sp', split_axis=1, concat_axis=0, tiled=True)]
    ppermute x3 -> x6, waiting for transfers between devices: 0.01 us -> 7.58 us  [back(): return lax.ppermute(x, 'sp', [(i, (i - 2 * k) % sp) for i in range(sp)])]
    ppermute x6 -> x15, starting transfers between devices: 25.7 us -> 31.5 us  [ahead(): return lax.ppermute(x, 'sp', [(i, (i + 2 * k) % sp) for i in range(sp)])]
    ppermute x3 -> x6, starting transfers between devices: 4.85 us -> 9.66 us  [back(): return lax.ppermute(x, 'sp', [(i, (i - 2 * k) % sp) for i in range(sp)])]
    ppermute x0 -> x3, starting transfers between devices: none -> 3.49 us  [on_device(): router_local = router_local + lax.ppermute(partial_sum, 'dp', perm)]
  transfers between devices with their start and end apart: 24 -> 46, of which waited for: 2 -> 13; matrix products, arithmetic and copies ran while one was open for 4% -> 5% of each run, Pallas kernels for 13% -> 23%
where the time goes in v2:
time: 125 us
  starting transfers between devices  48.8 us (39%)
  waiting for transfers between devices  33.4 us (27%)
  Pallas kernels  30.3 us (24%)
  other arithmetic  5.33 us (4%)
  local copies, waits for them, and re-layouts  5.2 us (4%)
  between operations  1.89 us (2%)
    ppermute x15, starting transfers between devices, ahead(): return lax.ppermute(x, 'sp', [(i, (i + 2 * k) % sp) for i in range(sp)])  31.5 us
    ppermute x15, waiting for transfers between devices, ahead(): return lax.ppermute(x, 'sp', [(i, (i + 2 * k) % sp) for i in range(sp)])  23.9 us
    pallas_call x2, Pallas kernels, attend(): pl.pallas_call(functools.partial(attend_kernel, blocks, first), grid_spec...  12.8 us
    ppermute x6, starting transfers between devices, back(): return lax.ppermute(x, 'sp', [(i, (i - 2 * k) % sp) for i in range(sp)])  9.66 us
    pallas_call x1, Pallas kernels, slots(): pl.pallas_call(functools.partial(slots_kernel, blocks, sp, cap), grid_spe...  7.78 us
    ppermute x6, waiting for transfers between devices, back(): return lax.ppermute(x, 'sp', [(i, (i - 2 * k) % sp) for i in range(sp)])  7.58 us
    unnamed x97, local copies, waits for them, and re-layouts  4.31 us
    ppermute x22, starting transfers between devices, exchange(): return lax.ppermute(x, 'sp', swap)  4.16 us
  transfers between devices with their start and end apart: 46, of which 13 were waited for; matrix products, arithmetic and copies ran while one was open for 5% of the time, Pallas kernels for 23%

profile of v2, /device:TPU:0, one launch (start us, length us, event | category | flops | bytes accessed | tf_op | source)
XLA Modules:
  0.0 124.9 jit_solution(17946851555612859184)
XLA Ops:
  0.6 1.8 %pack_keys.1 = (bf16[128,512]{1,0:T(8,128)(2,1)}, bf16[128,512]{1,0:T(8,128)(2,1)}) custom-call(bf16[128,512]{1,0:T(8,128)(2,1)} %bitcast.35, bf16[128,512]{1,0:T(8,128)(2,1)} %bitcast.39, f32[1,128]{1,0:T(1,128)} %bitcast.43), custom_call_target="tpu_custom_call" | custom-call | tf_op jit(solution)/shard_map/pack_keys/pallas_call | solution.py:48
  2.4 3.0 %collective-permute-start = (bf16[128,512]{1,0:T(8,128)(2,1)}, bf16[128,512]{1,0:T(8,128)(2,1)S(1)}, u32[]{:S(2)}, u32[]{:S(2)}) collective-permute-start(bf16[128,512]{1,0:T(8,128)(2,1)} %get-tuple-element.34.refs_0_), channel_id=1, source_target_pairs={{0,2},{1,3},{2,4},{3,5},{4,6},{5,7},{6,0},{7,1},{8,10},{9,11},{10,... | collective-permute-start | bytes 393224 | tf_op jit(solution)/shard_map/ppermute | solution.py:404
  5.5 2.6 %collective-permute-start.1 = (bf16[128,512]{1,0:T(8,128)(2,1)}, bf16[128,512]{1,0:T(8,128)(2,1)S(1)}, u32[]{:S(2)}, u32[]{:S(2)}) collective-permute-start(bf16[128,512]{1,0:T(8,128)(2,1)} %get-tuple-element.34.refs_0_), channel_id=1, source_target_pairs={{0,4},{1,5},{2,6},{3,7},{4,0},{5,1},{6,2},{7,3},{8,12},{9,13},{10,... | collective-permute-start | bytes 393224 | tf_op jit(solution)/shard_map/ppermute | solution.py:404
  8.0 0.6 pad_add_fusion.meta_ref
  8.7 1.4 %copy.21 = s32[1,32,8]{2,1,0:T(8,128)} copy(s32[1,32,8]{1,2,0:T(8,128)} %param.25) | data formatting | bytes 2048 | tf_op args[10]
  10.0 2.4 %gates.1 = (bf16[32,4352]{1,0:T(8,128)(2,1)}, bf16[32,1024]{1,0:T(8,128)(2,1)}, bf16[32,1024]{1,0:T(8,128)(2,1)}, bf16[32,1024]{1,0:T(8,128)(2,1)}, bf16[32,1024]{1,0:T(8,128)(2,1)}) custom-call(s32[2]{0:T(128)} %pad_add_fusion.meta_ref, bf16[32,4096]{1,0:T(8,128)(2,1)} %bitcast.37, bf16[4096,128]{1,0:T(8,128)(2,1)} %router_ref.1, s32[32,8]{1,0:T(8,128)} %bitcast.40, ...), custom_call_target="tpu_custom_call" | custom-call | tf_op jit(solution)/shard_map/gates/pallas_call | solution.py:83
  12.5 0.9 collective-permute-start.39
  13.4 3.5 %collective-permute-start.40 = (bf16[32,1024]{1,0:T(8,128)(2,1)}, bf16[32,1024]{1,0:T(8,128)(2,1)S(1)}, u32[]{:S(2)}, u32[]{:S(2)}) collective-permute-start(bf16[32,1024]{1,0:T(8,128)(2,1)} %get-tuple-element.61), channel_id=1, source_target_pairs={{0,4},{1,5},{2,6},{3,7},{4,0},{5,1},{6,2},{7,3},{8,12},{9,13},{10,... | collective-permute-start | bytes 196616 | tf_op jit(solution)/shard_map/ppermute | solution.py:404
  16.8 2.2 %collective-permute-done.39.refs_13_ = bf16[32,1024]{1,0:T(8,128)(2,1)S(1)} collective-permute-done((bf16[32,1024]{1,0:T(8,128)(2,1)}, bf16[32,1024]{1,0:T(8,128)(2,1)S(1)}, u32[]{:S(2)}, u32[]{:S(2)}) %collective-permute-start.39) | collective-permute-done | bytes 65568 | tf_op jit(solution)/shard_map/ppermute | solution.py:404
  19.0 5.3 %collective-permute-start.8 = (bf16[128,512]{1,0:T(8,128)(2,1)}, bf16[128,512]{1,0:T(8,128)(2,1)S(1)}, u32[]{:S(2)}, u32[]{:S(2)}) collective-permute-start(bf16[128,512]{1,0:T(8,128)(2,1)} %get-tuple-element.35.refs_0_), channel_id=1, source_target_pairs={{0,4},{1,5},{2,6},{3,7},{4,0},{5,1},{6,2},{7,3},{8,12},{9,13},{10,... | collective-permute-start | bytes 393224 | tf_op jit(solution)/shard_map/ppermute | solution.py:404
  24.3 1.0 collective-permute-done.40.refs_14_
  25.3 2.7 %collective-permute-start.2 = (bf16[128,512]{1,0:T(8,128)(2,1)}, bf16[128,512]{1,0:T(8,128)(2,1)S(1)}, u32[]{:S(2)}, u32[]{:S(2)}) collective-permute-start(bf16[128,512]{1,0:T(8,128)(2,1)} %get-tuple-element.34.refs_0_), channel_id=1, source_target_pairs={{0,6},{1,7},{2,0},{3,1},{4,2},{5,3},{6,4},{7,5},{8,14},{9,15},{10,... | collective-permute-start | bytes 393224 | tf_op jit(solution)/shard_map/ppermute | solution.py:404
  28.1 0.5 collective-permute-start.11
  28.6 1.7 %collective-permute-done.8.refs_2_ = bf16[128,512]{1,0:T(8,128)(2,1)S(1)} collective-permute-done((bf16[128,512]{1,0:T(8,128)(2,1)}, bf16[128,512]{1,0:T(8,128)(2,1)S(1)}, u32[]{:S(2)}, u32[]{:S(2)}) %collective-permute-start.8) | collective-permute-done | bytes 131104 | tf_op jit(solution)/shard_map/ppermute | solution.py:404
  30.3 2.2 %collective-permute-done.2.refs_3_ = bf16[128,512]{1,0:T(8,128)(2,1)S(1)} collective-permute-done((bf16[128,512]{1,0:T(8,128)(2,1)}, bf16[128,512]{1,0:T(8,128)(2,1)S(1)}, u32[]{:S(2)}, u32[]{:S(2)}) %collective-permute-start.2) | collective-permute-done | bytes 131104 | tf_op jit(solution)/shard_map/ppermute | solution.py:404
  32.5 2.1 %collective-permute-done.9.refs_3_ = bf16[128,512]{1,0:T(8,128)(2,1)S(1)} collective-permute-done((bf16[128,512]{1,0:T(8,128)(2,1)}, bf16[128,512]{1,0:T(8,128)(2,1)S(1)}, u32[]{:S(2)}, u32[]{:S(2)}) %collective-permute-start.9) | collective-permute-done | bytes 131104 | tf_op jit(solution)/shard_map/ppermute | solution.py:404
  34.6 0.5 collective-permute-start.5
  35.9 2.3 %collective-permute-start.41 = (bf16[32,1024]{1,0:T(8,128)(2,1)}, bf16[32,1024]{1,0:T(8,128)(2,1)S(1)}, u32[]{:S(2)}, u32[]{:S(2)}) collective-permute-start(bf16[32,1024]{1,0:T(8,128)(2,1)} %get-tuple-element.62), channel_id=1, source_target_pairs={{0,6},{1,7},{2,0},{3,1},{4,2},{5,3},{6,4},{7,5},{8,14},{9,15},{10,... | collective-permute-start | bytes 196616 | tf_op jit(solution)/shard_map/ppermute | solution.py:404
  38.2 0.7 add_add_fusion.2
  38.9 0.2 collective-permute-start.6
  39.1 0.5 copy-done.33
  39.6 6.4 %attend.2 = (bf16[32,8192]{1,0:T(8,128)(2,1)}, f32[128,512]{1,0:T(8,128)}, f32[128,512]{1,0:T(8,128)}, f32[128,512]{1,0:T(8,128)}, f32[128,512]{1,0:T(8,128)}, /...) custom-call(s32[9]{0:T(128)} %get-tuple-element.64.meta_ref, ...), custom_call_target="tpu_custom_call" | custom-call | tf_op jit(solution)/shard_map/attend/pallas_call | solution.py:163
  46.0 0.2 collective-permute-start.14
  46.3 0.9 slice.12
  47.3 0.7 collective-permute-start.29
  48.0 3.2 %collective-permute-start.30 = (bf16[32,4352]{1,0:T(8,128)(2,1)}, bf16[32,4352]{1,0:T(8,128)(2,1)S(1)}, u32[]{:S(2)}, u32[]{:S(2)}) collective-permute-start(bf16[32,4352]{1,0:T(8,128)(2,1)} %get-tuple-element.56.refs_0_.refs_8_), channel_id=1, source_target_pairs={{0,6},{1,7},{2,0},{3,1},{4,2},{5,3},{6,4},{7,5},{8,14},{9,15},{10,... | collective-permute-start | bytes 835592 | tf_op jit(solution)/shard_map/ppermute | solution.py:404
  51.3 0.5 copy-done.31
  51.8 6.4 %attend.3 = (bf16[32,8192]{1,0:T(8,128)(2,1)}, f32[128,512]{1,0:T(8,128)}, f32[128,512]{1,0:T(8,128)}, f32[128,512]{1,0:T(8,128)}, f32[128,512]{1,0:T(8,128)}, /...) custom-call(s32[9]{0:T(128)} %get-tuple-element.64.meta_ref, ...), custom_call_target="tpu_custom_call", output_to_operand_aliasing={{0}: (13, {})} | custom-call | tf_op jit(solution)/shard_map/attend/pallas_call | solution.py:163
  58.4 0.7 convert_add_fusion.1.refs_0_
  59.1 0.5 collective-permute-start.17
  59.7 10.2 %collective-permute-done.29.refs_2_.refs_10_ = bf16[32,4352]{1,0:T(8,128)(2,1)S(1)} collective-permute-done((bf16[32,4352]{1,0:T(8,128)(2,1)}, bf16[32,4352]{1,0:T(8,128)(2,1)S(1)}, u32[]{:S(2)}, u32[]{:S(2)}) %collective-permute-start.29) | collective-permute-done | bytes 278560 | tf_op jit(solution)/shard_map/ppermute | solution.py:404
  69.9 0.5 collective-permute-start.33
  70.6 0.5 collective-permute-start.19
  71.3 0.2 collective-permute-done.32.refs_5_.refs_13_
  71.5 0.2 collective-permute-start.21
  71.7 0.2 collective-permute-done.33.refs_6_.refs_14_
  72.0 0.3 collective-permute-done.34.refs_7_.refs_15_
  72.4 0.2 copy-done.6
  72.6 0.4 copy-done.7
  73.0 7.8 %slots.1 = (bf16[384,4096]{1,0:T(8,128)(2,1)}, f32[24,128]{1,0:T(8,128)}) custom-call(s32[9]{0:T(128)} %get-tuple-element.63.meta_ref, s32[384,3]{1,0:T(8,128)} %constant.36.clone.table_ref, s32[1,384]{1,0:T(1,128)} %constant.37.clone.lanes_ref, bf16[32,4352]{1,0:T(8,128)(2,1)} %get-tuple-element.56.refs_0_.refs_8_, bf16[32,4352]{1,0:T(8,128)(2,1)} %copy-done.1, ...), custom_call_target="tpu_custom_call" | custom-call | tf_op jit(solution)/shard_map/slots/pallas_call | solution.py:291
  80.8 0.2 collective-permute-start.35
  81.0 1.2 collective-permute-done.35
  82.3 0.7 add.61.refs_8_
  83.0 5.4 %collective-permute-start.36 = (f32[24,128]{1,0:T(8,128)S(1)}, f32[24,128]{1,0:T(8,128)S(1)}, u32[]{:S(2)}, u32[]{:S(2)}) collective-permute-start(f32[24,128]{1,0:T(8,128)S(1)} %add.61.refs_8_), channel_id=1, source_target_pairs={{0,2},{1,3},{2,4},{3,5},{4,6},{5,7},{6,0},{7,1},{8,10},{9,11},{10,... | collective-permute-start | bytes 36872 | tf_op jit(solution)/shard_map/ppermute | solution.py:404
  88.4 0.4 collective-permute-start.37
  89.0 2.0 %collective-permute-start.16 = (bf16[128,512]{1,0:T(8,128)(2,1)S(1)}, bf16[128,512]{1,0:T(8,128)(2,1)S(1)}, u32[]{:S(2)}, u32[]{:S(2)}) collective-permute-start(bf16[128,512]{1,0:T(8,128)(2,1)S(1)} %add_convert_fusion.5), channel_id=1, source_target_pairs={{0,6},{1,7},{2,0},{3,1},{4,2},{5,3},{6,4},{7,5},{8,14},{9,15},{10,... | collective-permute-start | bytes 393224 | tf_op jit(solution)/shard_map/ppermute | solution.py:407
  91.1 0.6 collective-permute-start.18
  91.7 1.5 %collective-permute-done.37.refs_10_ = f32[24,128]{1,0:T(8,128)S(1)} collective-permute-done((f32[24,128]{1,0:T(8,128)S(1)}, f32[24,128]{1,0:T(8,128)S(1)}, u32[]{:S(2)}, u32[]{:S(2)}) %collective-permute-start.37) | collective-permute-done | bytes 12320 | tf_op jit(solution)/shard_map/ppermute | solution.py:404
  93.2 1.3 %collective-permute-start.38 = (f32[24,128]{1,0:T(8,128)S(1)}, f32[24,128]{1,0:T(8,128)S(1)}, u32[]{:S(2)}, u32[]{:S(2)}) collective-permute-start(f32[24,128]{1,0:T(8,128)S(1)} %add.61.refs_8_), channel_id=1, source_target_pairs={{0,6},{1,7},{2,0},{3,1},{4,2},{5,3},{6,4},{7,5},{8,14},{9,15},{10,... | collective-permute-start | bytes 36872 | tf_op jit(solution)/shard_map/ppermute | solution.py:404
  94.5 3.0 %collective-permute-done.38.refs_11_ = f32[24,128]{1,0:T(8,128)S(1)} collective-permute-done((f32[24,128]{1,0:T(8,128)S(1)}, f32[24,128]{1,0:T(8,128)S(1)}, u32[]{:S(2)}, u32[]{:S(2)}) %collective-permute-start.38) | collective-permute-done | bytes 12320 | tf_op jit(solution)/shard_map/ppermute | solution.py:404
  97.5 4.7 %collective-permute-start.20 = (bf16[128,512]{1,0:T(8,128)(2,1)S(1)}, bf16[128,512]{1,0:T(8,128)(2,1)S(1)}, u32[]{:S(2)}, u32[]{:S(2)}) collective-permute-start(bf16[128,512]{1,0:T(8,128)(2,1)S(1)} %add_convert_fusion.3), channel_id=1, source_target_pairs={{0,2},{1,3},{2,4},{3,5},{4,6},{5,7},{6,0},{7,1},{8,10},{9,11},{10,... | collective-permute-start | bytes 393224 | tf_op jit(solution)/shard_map/ppermute | solution.py:407
  102.3 3.1 %router_grad.1 = f32[512,128]{1,0:T(8,128)} custom-call(s32[9]{0:T(128)} %get-tuple-element.63.meta_ref, bf16[32,4352]{1,0:T(8,128)(2,1)} %get-tuple-element.56.refs_0_.refs_8_, bf16[32,4352]{1,0:T(8,128)(2,1)} %copy-done.1, bf16[32,4352]{1,0:T(8,128)(2,1)} %copy-done.2, bf16[32,4352]{1,0:T(8,128)(2,1)} %copy-done.3, bf16[32,4352]{1,0:T(8,128)(2,1)} %copy-done.4, ...), custom_call_target="tpu_custom_call" | custom-call | tf_op jit(solution)/shard_map/router_grad/pallas_call | solution.py:360
  105.4 0.2 collective-permute-start.23
  105.6 2.4 %collective-permute-start.45 = (f32[512,128]{1,0:T(8,128)}, f32[512,128]{1,0:T(8,128)S(1)}, u32[]{:S(2)}, u32[]{:S(2)}) collective-permute-start(f32[512,128]{1,0:T(8,128)} %router_grad.1), channel_id=1, source_target_pairs={{0,24},{8,16},{16,8},{24,0},{1,25},{9,17},{17,9},{25,1},{2,26},{10... | collective-permute-start | bytes 786440 | tf_op jit(solution)/shard_map/ppermute | solution.py:463
  108.1 0.5 collective-permute-start.44
  108.6 0.5 collective-permute-start.43
  109.2 1.9 %collective-permute-start.25 = (bf16[128,512]{1,0:T(8,128)(2,1)S(1)}, bf16[128,512]{1,0:T(8,128)(2,1)S(1)}, u32[]{:S(2)}, u32[]{:S(2)}) collective-permute-start(bf16[128,512]{1,0:T(8,128)(2,1)S(1)} %add_convert_fusion.1), channel_id=1, source_target_pairs={{0,4},{1,5},{2,6},{3,7},{4,0},{5,1},{6,2},{7,3},{8,12},{9,13},{10,... | collective-permute-start | bytes 393224 | tf_op jit(solution)/shard_map/ppermute | solution.py:407
  111.1 0.2 collective-permute-start.27
  111.3 0.7 convert_add_fusion.refs_4_
  112.0 7.6 %collective-permute-done.25.refs_6_ = bf16[128,512]{1,0:T(8,128)(2,1)S(1)} collective-permute-done((bf16[128,512]{1,0:T(8,128)(2,1)S(1)}, bf16[128,512]{1,0:T(8,128)(2,1)S(1)}, u32[]{:S(2)}, u32[]{:S(2)}) %collective-permute-start.25) | collective-permute-done | bytes 131104 | tf_op jit(solution)/shard_map/ppermute | solution.py:407
  119.6 0.6 copy-done.38
  120.2 0.6 copy-done.39
  120.9 2.3 %finish_keys.1 = (bf16[128,512]{1,0:T(8,128)(2,1)}, bf16[128,512]{1,0:T(8,128)(2,1)}) custom-call(bf16[128,512]{1,0:T(8,128)(2,1)} %bitcast.36, f32[1,128]{1,0:T(1,128)} %bitcast.44, f32[128,512]{1,0:T(8,128)} %convert_add_fusion.1.refs_0_, bf16[128,512]{1,0:T(8,128)(2,1)} %copy-done.34, bf16[128,512]{1,0:T(8,128)(2,1)} %copy-done.35, ...), custom_call_target="tpu_custom_call" | custom-call | tf_op jit(solution)/shard_map/finish_keys/pallas_call | solution.py:206
  123.2 1.7 %add_add_fusion = f32[512,128]{1,0:T(8,128)} fusion(f32[512,128]{1,0:T(8,128)S(1)} %collective-permute-done.45, f32[512,128]{1,0:T(8,128)S(1)} %collective-permute-done.44, f32[512,128]{1,0:T(8,128)} %router_grad.1, f32[512,128]{1,0:T(8,128)S(1)} %collective-permute-done.43), kind=kLoop, calls=%fused_computation | loop fusion | flops 196608 | bytes 1310720 | tf_op jit(solution)/shard_map/add | solution.py:463
  (150 shorter events, 1.4 us)
Async XLA Ops:
  2.4 25.6 %collective-permute-start = (bf16[128,512]{1,0:T(8,128)(2,1)}, bf16[128,512]{1,0:T(8,128)(2,1)S(1)}, u32[]{:S(2)}, u32[]{:S(2)}) collective-permute-start(bf16[128,512]{1,0:T(8,128)(2,1)} %get-tuple-element.34.refs_0_), channel_id=1, source_target_pairs={{0,2},{1,3},{2,4},{3,5},{4,6},{5,7},{6,0},{7,1},{8,10},{9,11},{10,... | collective-permute-start | bytes 393224 | tf_op jit(solution)/shard_map/ppermute | solution.py:404
  5.5 22.6 %collective-permute-start.1 = (bf16[128,512]{1,0:T(8,128)(2,1)}, bf16[128,512]{1,0:T(8,128)(2,1)S(1)}, u32[]{:S(2)}, u32[]{:S(2)}) collective-permute-start(bf16[128,512]{1,0:T(8,128)(2,1)} %get-tuple-element.34.refs_0_), channel_id=1, source_target_pairs={{0,4},{1,5},{2,6},{3,7},{4,0},{5,1},{6,2},{7,3},{8,12},{9,13},{10,... | collective-permute-start | bytes 393224 | tf_op jit(solution)/shard_map/ppermute | solution.py:404
  8.0 20.1 %collective-permute-start.7 = (bf16[128,512]{1,0:T(8,128)(2,1)}, bf16[128,512]{1,0:T(8,128)(2,1)S(1)}, u32[]{:S(2)}, u32[]{:S(2)}) collective-permute-start(bf16[128,512]{1,0:T(8,128)(2,1)} %get-tuple-element.35.refs_0_), channel_id=1, source_target_pairs={{0,2},{1,3},{2,4},{3,5},{4,6},{5,7},{6,0},{7,1},{8,10},{9,11},{10,... | collective-permute-start | bytes 393224 | tf_op jit(solution)/shard_map/ppermute | solution.py:404
  12.5 38.7 %copy-start = (bf16[32,4352]{1,0:T(8,128)(2,1)S(1)}, bf16[32,4352]{1,0:T(8,128)(2,1)}, u32[]{:S(2)}) copy-start(bf16[32,4352]{1,0:T(8,128)(2,1)} %get-tuple-element.56.refs_0_.refs_8_) | copy-start | bytes 835588
  12.5 6.5 %collective-permute-start.39 = (bf16[32,1024]{1,0:T(8,128)(2,1)}, bf16[32,1024]{1,0:T(8,128)(2,1)S(1)}, u32[]{:S(2)}, u32[]{:S(2)}) collective-permute-start(bf16[32,1024]{1,0:T(8,128)(2,1)} %get-tuple-element.60), channel_id=1, source_target_pairs={{0,2},{1,3},{2,4},{3,5},{4,6},{5,7},{6,0},{7,1},{8,10},{9,11},{10,... | collective-permute-start | bytes 196616 | tf_op jit(solution)/shard_map/ppermute | solution.py:404
  13.4 12.0 %collective-permute-start.40 = (bf16[32,1024]{1,0:T(8,128)(2,1)}, bf16[32,1024]{1,0:T(8,128)(2,1)S(1)}, u32[]{:S(2)}, u32[]{:S(2)}) collective-permute-start(bf16[32,1024]{1,0:T(8,128)(2,1)} %get-tuple-element.61), channel_id=1, source_target_pairs={{0,4},{1,5},{2,6},{3,7},{4,0},{5,1},{6,2},{7,3},{8,12},{9,13},{10,... | collective-permute-start | bytes 196616 | tf_op jit(solution)/shard_map/ppermute | solution.py:404
  19.0 39.2 %copy-start.16 = (bf16[32,1024]{1,0:T(8,128)(2,1)}, bf16[32,1024]{1,0:T(8,128)(2,1)S(1)}, u32[]{:S(2)}) copy-start(bf16[32,1024]{1,0:T(8,128)(2,1)S(1)} %collective-permute-done.39.refs_13_) | copy-start | bytes 196612
  19.0 11.3 %collective-permute-start.8 = (bf16[128,512]{1,0:T(8,128)(2,1)}, bf16[128,512]{1,0:T(8,128)(2,1)S(1)}, u32[]{:S(2)}, u32[]{:S(2)}) collective-permute-start(bf16[128,512]{1,0:T(8,128)(2,1)} %get-tuple-element.35.refs_0_), channel_id=1, source_target_pairs={{0,4},{1,5},{2,6},{3,7},{4,0},{5,1},{6,2},{7,3},{8,12},{9,13},{10,... | collective-permute-start | bytes 393224 | tf_op jit(solution)/shard_map/ppermute | solution.py:404
  25.3 32.9 %copy-start.17 = (bf16[32,1024]{1,0:T(8,128)(2,1)}, bf16[32,1024]{1,0:T(8,128)(2,1)S(1)}, u32[]{:S(2)}) copy-start(bf16[32,1024]{1,0:T(8,128)(2,1)S(1)} %collective-permute-done.40.refs_14_) | copy-start | bytes 196612
  25.3 7.2 %collective-permute-start.2 = (bf16[128,512]{1,0:T(8,128)(2,1)}, bf16[128,512]{1,0:T(8,128)(2,1)S(1)}, u32[]{:S(2)}, u32[]{:S(2)}) collective-permute-start(bf16[128,512]{1,0:T(8,128)(2,1)} %get-tuple-element.34.refs_0_), channel_id=1, source_target_pairs={{0,6},{1,7},{2,0},{3,1},{4,2},{5,3},{6,4},{7,5},{8,14},{9,15},{10,... | collective-permute-start | bytes 393224 | tf_op jit(solution)/shard_map/ppermute | solution.py:404
  28.0 23.3 %copy-start.19 = (bf16[128,512]{1,0:T(8,128)(2,1)}, bf16[128,512]{1,0:T(8,128)(2,1)S(1)}, u32[]{:S(2)}) copy-start(bf16[128,512]{1,0:T(8,128)(2,1)S(1)} %collective-permute-done.refs_1_) | copy-start | bytes 393220
  28.0 6.6 %collective-permute-start.9 = (bf16[128,512]{1,0:T(8,128)(2,1)}, bf16[128,512]{1,0:T(8,128)(2,1)S(1)}, u32[]{:S(2)}, u32[]{:S(2)}) collective-permute-start(bf16[128,512]{1,0:T(8,128)(2,1)} %get-tuple-element.35.refs_0_), channel_id=1, source_target_pairs={{0,6},{1,7},{2,0},{3,1},{4,2},{5,3},{6,4},{7,5},{8,14},{9,15},{10,... | collective-permute-start | bytes 393224 | tf_op jit(solution)/shard_map/ppermute | solution.py:404
  28.1 23.2 %copy-start.20 = (bf16[128,512]{1,0:T(8,128)(2,1)}, bf16[128,512]{1,0:T(8,128)(2,1)S(1)}, u32[]{:S(2)}) copy-start(bf16[128,512]{1,0:T(8,128)(2,1)S(1)} %collective-permute-done.1.refs_2_) | copy-start | bytes 393220
  28.1 6.5 %collective-permute-start.10 = (bf16[128,512]{1,0:T(8,128)(2,1)}, bf16[128,512]{1,0:T(8,128)(2,1)S(1)}, u32[]{:S(2)}, u32[]{:S(2)}) collective-permute-start(bf16[128,512]{1,0:T(8,128)(2,1)} %get-tuple-element.35.refs_0_), channel_id=1, source_target_pairs={{0,1},{1,0},{2,3},{3,2},{4,5},{5,4},{6,7},{7,6},{8,9},{9,8},{10,11... | collective-permute-start | bytes 393224 | tf_op jit(solution)/shard_map/ppermute | solution.py:401
  28.1 7.0 %collective-permute-start.11 = (bf16[128,512]{1,0:T(8,128)(2,1)S(1)}, bf16[128,512]{1,0:T(8,128)(2,1)S(1)}, u32[]{:S(2)}, u32[]{:S(2)}) collective-permute-start(bf16[128,512]{1,0:T(8,128)(2,1)S(1)} %collective-permute-done.7.refs_1_), channel_id=1, source_target_pairs={{0,1},{1,0},{2,3},{3,2},{4,5},{5,4},{6,7},{7,6},{8,9},{9,8},{10,11... | collective-permute-start | bytes 393224 | tf_op jit(solution)/shard_map/ppermute | solution.py:401
  30.3 5.6 %collective-permute-start.12 = (bf16[128,512]{1,0:T(8,128)(2,1)S(1)}, bf16[128,512]{1,0:T(8,128)(2,1)S(1)}, u32[]{:S(2)}, u32[]{:S(2)}) collective-permute-start(bf16[128,512]{1,0:T(8,128)(2,1)S(1)} %collective-permute-done.8.refs_2_), channel_id=1, source_target_pairs={{0,1},{1,0},{2,3},{3,2},{4,5},{5,4},{6,7},{7,6},{8,9},{9,8},{10,11... | collective-permute-start | bytes 393224 | tf_op jit(solution)/shard_map/ppermute | solution.py:401
  32.5 18.8 %copy-start.22 = (bf16[128,512]{1,0:T(8,128)(2,1)}, bf16[128,512]{1,0:T(8,128)(2,1)S(1)}, u32[]{:S(2)}) copy-start(bf16[128,512]{1,0:T(8,128)(2,1)S(1)} %collective-permute-done.2.refs_3_) | copy-start | bytes 393220
  32.5 14.6 %collective-permute-start.3 = (bf16[128,512]{1,0:T(8,128)(2,1)}, bf16[128,512]{1,0:T(8,128)(2,1)S(1)}, u32[]{:S(2)}, u32[]{:S(2)}) collective-permute-start(bf16[128,512]{1,0:T(8,128)(2,1)} %get-tuple-element.34.refs_0_), channel_id=1, source_target_pairs={{0,1},{1,0},{2,3},{3,2},{4,5},{5,4},{6,7},{7,6},{8,9},{9,8},{10,11... | collective-permute-start | bytes 393224 | tf_op jit(solution)/shard_map/ppermute | solution.py:401
  34.6 12.6 %collective-permute-start.4 = (bf16[128,512]{1,0:T(8,128)(2,1)S(1)}, bf16[128,512]{1,0:T(8,128)(2,1)S(1)}, u32[]{:S(2)}, u32[]{:S(2)}) collective-permute-start(bf16[128,512]{1,0:T(8,128)(2,1)S(1)} %collective-permute-done.refs_1_), channel_id=1, source_target_pairs={{0,1},{1,0},{2,3},{3,2},{4,5},{5,4},{6,7},{7,6},{8,9},{9,8},{10,11... | collective-permute-start | bytes 393224 | tf_op jit(solution)/shard_map/ppermute | solution.py:401
  34.6 13.3 %collective-permute-start.5 = (bf16[128,512]{1,0:T(8,128)(2,1)S(1)}, bf16[128,512]{1,0:T(8,128)(2,1)S(1)}, u32[]{:S(2)}, u32[]{:S(2)}) collective-permute-start(bf16[128,512]{1,0:T(8,128)(2,1)S(1)} %collective-permute-done.1.refs_2_), channel_id=1, source_target_pairs={{0,1},{1,0},{2,3},{3,2},{4,5},{5,4},{6,7},{7,6},{8,9},{9,8},{10,11... | collective-permute-start | bytes 393224 | tf_op jit(solution)/shard_map/ppermute | solution.py:401
  35.1 3.8 %collective-permute-start.13 = (bf16[128,512]{1,0:T(8,128)(2,1)S(1)}, bf16[128,512]{1,0:T(8,128)(2,1)S(1)}, u32[]{:S(2)}, u32[]{:S(2)}) collective-permute-start(bf16[128,512]{1,0:T(8,128)(2,1)S(1)} %collective-permute-done.9.refs_3_), channel_id=1, source_target_pairs={{0,1},{1,0},{2,3},{3,2},{4,5},{5,4},{6,7},{7,6},{8,9},{9,8},{10,11... | collective-permute-start | bytes 393224 | tf_op jit(solution)/shard_map/ppermute | solution.py:401
  35.9 10.1 %collective-permute-start.41 = (bf16[32,1024]{1,0:T(8,128)(2,1)}, bf16[32,1024]{1,0:T(8,128)(2,1)S(1)}, u32[]{:S(2)}, u32[]{:S(2)}) collective-permute-start(bf16[32,1024]{1,0:T(8,128)(2,1)} %get-tuple-element.62), channel_id=1, source_target_pairs={{0,6},{1,7},{2,0},{3,1},{4,2},{5,3},{6,4},{7,5},{8,14},{9,15},{10,... | collective-permute-start | bytes 196616 | tf_op jit(solution)/shard_map/ppermute | solution.py:404
  38.9 12.2 %collective-permute-start.6 = (bf16[128,512]{1,0:T(8,128)(2,1)S(1)}, bf16[128,512]{1,0:T(8,128)(2,1)S(1)}, u32[]{:S(2)}, u32[]{:S(2)}) collective-permute-start(bf16[128,512]{1,0:T(8,128)(2,1)S(1)} %collective-permute-done.2.refs_3_), channel_id=1, source_target_pairs={{0,1},{1,0},{2,3},{3,2},{4,5},{5,4},{6,7},{7,6},{8,9},{9,8},{10,11... | collective-permute-start | bytes 393224 | tf_op jit(solution)/shard_map/ppermute | solution.py:401
  46.0 24.5 %copy-start.14 = (f32[128,512]{1,0:T(8,128)S(1)}, f32[128,512]{1,0:T(8,128)}, u32[]{:S(2)}) copy-start(f32[128,512]{1,0:T(8,128)} %get-tuple-element.40) | copy-start | bytes 786436
  46.0 24.6 %copy-start.45 = (bf16[128,512]{1,0:T(8,128)(2,1)S(1)}, bf16[128,512]{1,0:T(8,128)(2,1)}, u32[]{:S(2)}) copy-start(bf16[128,512]{1,0:T(8,128)(2,1)} %get-tuple-element.45) | copy-start | bytes 393220
  46.0 25.1 %copy-start.13 = (f32[128,512]{1,0:T(8,128)S(1)}, f32[128,512]{1,0:T(8,128)}, u32[]{:S(2)}) copy-start(f32[128,512]{1,0:T(8,128)} %get-tuple-element.42) | copy-start | bytes 786436
  46.0 34.7 %copy-start.18 = (bf16[32,1024]{1,0:T(8,128)(2,1)}, bf16[32,1024]{1,0:T(8,128)(2,1)S(1)}, u32[]{:S(2)}) copy-start(bf16[32,1024]{1,0:T(8,128)(2,1)S(1)} %collective-permute-done.41.refs_15_) | copy-start | bytes 196612
  46.0 12.2 %collective-permute-start.14 = (bf16[128,512]{1,0:T(8,128)(2,1)}, bf16[128,512]{1,0:T(8,128)(2,1)S(1)}, u32[]{:S(2)}, u32[]{:S(2)}) collective-permute-start(bf16[128,512]{1,0:T(8,128)(2,1)} %get-tuple-element.39), channel_id=1, source_target_pairs={{0,1},{1,0},{2,3},{3,2},{4,5},{5,4},{6,7},{7,6},{8,9},{9,8},{10,11... | collective-permute-start | bytes 393224 | tf_op jit(solution)/shard_map/ppermute | solution.py:401
  47.2 11.9 %collective-permute-start.28 = (bf16[32,4352]{1,0:T(8,128)(2,1)}, bf16[32,4352]{1,0:T(8,128)(2,1)S(1)}, u32[]{:S(2)}, u32[]{:S(2)}) collective-permute-start(bf16[32,4352]{1,0:T(8,128)(2,1)} %get-tuple-element.56.refs_0_.refs_8_), channel_id=1, source_target_pairs={{0,2},{1,3},{2,4},{3,5},{4,6},{5,7},{6,0},{7,1},{8,10},{9,11},{10,... | collective-permute-start | bytes 835592 | tf_op jit(solution)/shard_map/ppermute | solution.py:404
  47.3 22.6 %collective-permute-start.29 = (bf16[32,4352]{1,0:T(8,128)(2,1)}, bf16[32,4352]{1,0:T(8,128)(2,1)S(1)}, u32[]{:S(2)}, u32[]{:S(2)}) collective-permute-start(bf16[32,4352]{1,0:T(8,128)(2,1)} %get-tuple-element.56.refs_0_.refs_8_), channel_id=1, source_target_pairs={{0,4},{1,5},{2,6},{3,7},{4,0},{5,1},{6,2},{7,3},{8,12},{9,13},{10,... | collective-permute-start | bytes 835592 | tf_op jit(solution)/shard_map/ppermute | solution.py:404
  48.0 21.9 %collective-permute-start.30 = (bf16[32,4352]{1,0:T(8,128)(2,1)}, bf16[32,4352]{1,0:T(8,128)(2,1)S(1)}, u32[]{:S(2)}, u32[]{:S(2)}) collective-permute-start(bf16[32,4352]{1,0:T(8,128)(2,1)} %get-tuple-element.56.refs_0_.refs_8_), channel_id=1, source_target_pairs={{0,6},{1,7},{2,0},{3,1},{4,2},{5,3},{6,4},{7,5},{8,14},{9,15},{10,... | collective-permute-start | bytes 835592 | tf_op jit(solution)/shard_map/ppermute | solution.py:404
  51.2 19.9 %collective-permute-start.31 = (bf16[32,4352]{1,0:T(8,128)(2,1)S(1)}, bf16[32,4352]{1,0:T(8,128)(2,1)S(1)}, u32[]{:S(2)}, u32[]{:S(2)}) collective-permute-start(bf16[32,4352]{1,0:T(8,128)(2,1)S(1)} %copy-done), channel_id=1, source_target_pairs={{0,1},{1,0},{2,3},{3,2},{4,5},{5,4},{6,7},{7,6},{8,9},{9,8},{10,11... | collective-permute-start | bytes 835592 | tf_op jit(solution)/shard_map/ppermute | solution.py:401
  58.3 12.1 %collective-permute-start.15 = (bf16[128,512]{1,0:T(8,128)(2,1)S(1)}, bf16[128,512]{1,0:T(8,128)(2,1)S(1)}, u32[]{:S(2)}, u32[]{:S(2)}) collective-permute-start(bf16[128,512]{1,0:T(8,128)(2,1)S(1)} %copy-done.47), channel_id=1, source_target_pairs={{0,1},{1,0},{2,3},{3,2},{4,5},{5,4},{6,7},{7,6},{8,9},{9,8},{10,11... | collective-permute-start | bytes 393224 | tf_op jit(solution)/shard_map/ppermute | solution.py:401
  59.1 13.3 %copy-start.1 = (bf16[32,4352]{1,0:T(8,128)(2,1)}, bf16[32,4352]{1,0:T(8,128)(2,1)S(1)}, u32[]{:S(2)}) copy-start(bf16[32,4352]{1,0:T(8,128)(2,1)S(1)} %collective-permute-done.28.refs_1_.refs_9_) | copy-start | bytes 835588
  59.1 11.4 %collective-permute-start.17 = (bf16[128,512]{1,0:T(8,128)(2,1)S(1)}, bf16[128,512]{1,0:T(8,128)(2,1)S(1)}, u32[]{:S(2)}, u32[]{:S(2)}) collective-permute-start(bf16[128,512]{1,0:T(8,128)(2,1)S(1)} %copy-done.46), channel_id=1, source_target_pairs={{0,1},{1,0},{2,3},{3,2},{4,5},{5,4},{6,7},{7,6},{8,9},{9,8},{10,11... | collective-permute-start | bytes 393224 | tf_op jit(solution)/shard_map/ppermute | solution.py:401
  69.9 1.6 %collective-permute-start.32 = (bf16[32,4352]{1,0:T(8,128)(2,1)S(1)}, bf16[32,4352]{1,0:T(8,128)(2,1)S(1)}, u32[]{:S(2)}, u32[]{:S(2)}) collective-permute-start(bf16[32,4352]{1,0:T(8,128)(2,1)S(1)} %collective-permute-done.28.refs_1_.refs_9_), channel_id=1, source_target_pairs={{0,1},{1,0},{2,3},{3,2},{4,5},{5,4},{6,7},{7,6},{8,9},{9,8},{10,11... | collective-permute-start | bytes 835592 | tf_op jit(solution)/shard_map/ppermute | solution.py:401
  69.9 1.9 %collective-permute-start.33 = (bf16[32,4352]{1,0:T(8,128)(2,1)S(1)}, bf16[32,4352]{1,0:T(8,128)(2,1)S(1)}, u32[]{:S(2)}, u32[]{:S(2)}) collective-permute-start(bf16[32,4352]{1,0:T(8,128)(2,1)S(1)} %collective-permute-done.29.refs_2_.refs_10_), channel_id=1, source_target_pairs={{0,1},{1,0},{2,3},{3,2},{4,5},{5,4},{6,7},{7,6},{8,9},{9,8},{10,11... | collective-permute-start | bytes 835592 | tf_op jit(solution)/shard_map/ppermute | solution.py:401
  70.4 1.8 %collective-permute-start.34 = (bf16[32,4352]{1,0:T(8,128)(2,1)S(1)}, bf16[32,4352]{1,0:T(8,128)(2,1)S(1)}, u32[]{:S(2)}, u32[]{:S(2)}) collective-permute-start(bf16[32,4352]{1,0:T(8,128)(2,1)S(1)} %collective-permute-done.30.refs_3_.refs_11_), channel_id=1, source_target_pairs={{0,1},{1,0},{2,3},{3,2},{4,5},{5,4},{6,7},{7,6},{8,9},{9,8},{10,11... | collective-permute-start | bytes 835592 | tf_op jit(solution)/shard_map/ppermute | solution.py:401
  70.6 10.2 %collective-permute-start.19 = (bf16[128,512]{1,0:T(8,128)(2,1)S(1)}, bf16[128,512]{1,0:T(8,128)(2,1)S(1)}, u32[]{:S(2)}, u32[]{:S(2)}) collective-permute-start(bf16[128,512]{1,0:T(8,128)(2,1)S(1)} %copy-done.45), channel_id=1, source_target_pairs={{0,1},{1,0},{2,3},{3,2},{4,5},{5,4},{6,7},{7,6},{8,9},{9,8},{10,11... | collective-permute-start | bytes 393224 | tf_op jit(solution)/shard_map/ppermute | solution.py:401
  71.1 17.8 %collective-permute-start.42 = (bf16[128,512]{1,0:T(8,128)(2,1)S(1)}, bf16[128,512]{1,0:T(8,128)(2,1)S(1)}, u32[]{:S(2)}, u32[]{:S(2)}) collective-permute-start(bf16[128,512]{1,0:T(8,128)(2,1)S(1)} %pad_maximum_fusion), channel_id=1, source_target_pairs={{0,1},{1,0},{2,3},{3,2},{4,5},{5,4},{6,7},{7,6},{8,9},{9,8},{10,11... | collective-permute-start | bytes 393224 | tf_op jit(solution)/shard_map/ppermute | solution.py:401
  71.5 33.9 %collective-permute-start.21 = (bf16[128,512]{1,0:T(8,128)(2,1)}, bf16[128,512]{1,0:T(8,128)(2,1)S(1)}, u32[]{:S(2)}, u32[]{:S(2)}) collective-permute-start(bf16[128,512]{1,0:T(8,128)(2,1)} %get-tuple-element.47), channel_id=1, source_target_pairs={{0,1},{1,0},{2,3},{3,2},{4,5},{5,4},{6,7},{7,6},{8,9},{9,8},{10,11... | collective-permute-start | bytes 393224 | tf_op jit(solution)/shard_map/ppermute | solution.py:401
  71.9 16.5 %collective-permute-start.22 = (bf16[128,512]{1,0:T(8,128)(2,1)}, bf16[128,512]{1,0:T(8,128)(2,1)S(1)}, u32[]{:S(2)}, u32[]{:S(2)}) collective-permute-start(bf16[128,512]{1,0:T(8,128)(2,1)} %get-tuple-element.49), channel_id=1, source_target_pairs={{0,1},{1,0},{2,3},{3,2},{4,5},{5,4},{6,7},{7,6},{8,9},{9,8},{10,11... | collective-permute-start | bytes 393224 | tf_op jit(solution)/shard_map/ppermute | solution.py:401
  72.3 16.7 %collective-permute-start.24 = (bf16[128,512]{1,0:T(8,128)(2,1)}, bf16[128,512]{1,0:T(8,128)(2,1)S(1)}, u32[]{:S(2)}, u32[]{:S(2)}) collective-permute-start(bf16[128,512]{1,0:T(8,128)(2,1)} %get-tuple-element.51), channel_id=1, source_target_pairs={{0,1},{1,0},{2,3},{3,2},{4,5},{5,4},{6,7},{7,6},{8,9},{9,8},{10,11... | collective-permute-start | bytes 393224 | tf_op jit(solution)/shard_map/ppermute | solution.py:401
  73.0 15.9 %copy-start.12 = (f32[128,512]{1,0:T(8,128)S(1)}, f32[128,512]{1,0:T(8,128)}, u32[]{:S(2)}) copy-start(f32[128,512]{1,0:T(8,128)} %get-tuple-element.48) | copy-start | bytes 786436
  73.0 15.9 %copy-start.44 = (bf16[128,512]{1,0:T(8,128)(2,1)S(1)}, bf16[128,512]{1,0:T(8,128)(2,1)}, u32[]{:S(2)}) copy-start(bf16[128,512]{1,0:T(8,128)(2,1)} %get-tuple-element.53) | copy-start | bytes 393220
  73.0 21.5 %copy-start.11 = (f32[128,512]{1,0:T(8,128)S(1)}, f32[128,512]{1,0:T(8,128)}, u32[]{:S(2)}) copy-start(f32[128,512]{1,0:T(8,128)} %get-tuple-element.50) | copy-start | bytes 786436
  80.8 28.3 %copy-start.9 = (f32[128,512]{1,0:T(8,128)S(1)}, f32[128,512]{1,0:T(8,128)}, u32[]{:S(2)}) copy-start(f32[128,512]{1,0:T(8,128)} %get-tuple-element.52) | copy-start | bytes 786436
  80.8 30.5 %copy-start.8 = (f32[128,512]{1,0:T(8,128)S(1)}, f32[128,512]{1,0:T(8,128)}, u32[]{:S(2)}) copy-start(f32[128,512]{1,0:T(8,128)} %get-tuple-element.46) | copy-start | bytes 786436
  80.8 1.5 %collective-permute-start.35 = (f32[24,128]{1,0:T(8,128)}, f32[24,128]{1,0:T(8,128)S(1)}, u32[]{:S(2)}, u32[]{:S(2)}) collective-permute-start(f32[24,128]{1,0:T(8,128)} %get-tuple-element.58), channel_id=1, source_target_pairs={{0,1},{1,0},{2,3},{3,2},{4,5},{5,4},{6,7},{7,6},{8,9},{9,8},{10,11... | collective-permute-start | bytes 36872 | tf_op jit(solution)/shard_map/ppermute | solution.py:401
  83.0 19.3 %copy-start.40 = (f32[24,128]{1,0:T(8,128)}, f32[24,128]{1,0:T(8,128)S(1)}, u32[]{:S(2)}) copy-start(f32[24,128]{1,0:T(8,128)S(1)} %add.61.refs_8_) | copy-start | bytes 36868
  83.0 8.1 %collective-permute-start.36 = (f32[24,128]{1,0:T(8,128)S(1)}, f32[24,128]{1,0:T(8,128)S(1)}, u32[]{:S(2)}, u32[]{:S(2)}) collective-permute-start(f32[24,128]{1,0:T(8,128)S(1)} %add.61.refs_8_), channel_id=1, source_target_pairs={{0,2},{1,3},{2,4},{3,5},{4,6},{5,7},{6,0},{7,1},{8,10},{9,11},{10,... | collective-permute-start | bytes 36872 | tf_op jit(solution)/shard_map/ppermute | solution.py:404
  88.4 4.7 %collective-permute-start.37 = (f32[24,128]{1,0:T(8,128)S(1)}, f32[24,128]{1,0:T(8,128)S(1)}, u32[]{:S(2)}, u32[]{:S(2)}) collective-permute-start(f32[24,128]{1,0:T(8,128)S(1)} %add.61.refs_8_), channel_id=1, source_target_pairs={{0,4},{1,5},{2,6},{3,7},{4,0},{5,1},{6,2},{7,3},{8,12},{9,13},{10,... | collective-permute-start | bytes 36872 | tf_op jit(solution)/shard_map/ppermute | solution.py:404
  88.9 13.3 %copy-start.26 = (bf16[128,512]{1,0:T(8,128)(2,1)}, bf16[128,512]{1,0:T(8,128)(2,1)S(1)}, u32[]{:S(2)}) copy-start(bf16[128,512]{1,0:T(8,128)(2,1)S(1)} %collective-permute-done.42.refs_16_) | copy-start | bytes 393220
  88.9 16.7 %collective-permute-start.26 = (bf16[128,512]{1,0:T(8,128)(2,1)S(1)}, bf16[128,512]{1,0:T(8,128)(2,1)S(1)}, u32[]{:S(2)}, u32[]{:S(2)}) collective-permute-start(bf16[128,512]{1,0:T(8,128)(2,1)S(1)} %copy-done.44), channel_id=1, source_target_pairs={{0,1},{1,0},{2,3},{3,2},{4,5},{5,4},{6,7},{7,6},{8,9},{9,8},{10,11... | collective-permute-start | bytes 393224 | tf_op jit(solution)/shard_map/ppermute | solution.py:401
  89.0 19.0 %collective-permute-start.16 = (bf16[128,512]{1,0:T(8,128)(2,1)S(1)}, bf16[128,512]{1,0:T(8,128)(2,1)S(1)}, u32[]{:S(2)}, u32[]{:S(2)}) collective-permute-start(bf16[128,512]{1,0:T(8,128)(2,1)S(1)} %add_convert_fusion.5), channel_id=1, source_target_pairs={{0,6},{1,7},{2,0},{3,1},{4,2},{5,3},{6,4},{7,5},{8,14},{9,15},{10,... | collective-permute-start | bytes 393224 | tf_op jit(solution)/shard_map/ppermute | solution.py:407
  91.1 17.5 %collective-permute-start.18 = (bf16[128,512]{1,0:T(8,128)(2,1)S(1)}, bf16[128,512]{1,0:T(8,128)(2,1)S(1)}, u32[]{:S(2)}, u32[]{:S(2)}) collective-permute-start(bf16[128,512]{1,0:T(8,128)(2,1)S(1)} %add_convert_fusion.4), channel_id=1, source_target_pairs={{0,4},{1,5},{2,6},{3,7},{4,0},{5,1},{6,2},{7,3},{8,12},{9,13},{10,... | collective-permute-start | bytes 393224 | tf_op jit(solution)/shard_map/ppermute | solution.py:407
  93.2 4.4 %collective-permute-start.38 = (f32[24,128]{1,0:T(8,128)S(1)}, f32[24,128]{1,0:T(8,128)S(1)}, u32[]{:S(2)}, u32[]{:S(2)}) collective-permute-start(f32[24,128]{1,0:T(8,128)S(1)} %add.61.refs_8_), channel_id=1, source_target_pairs={{0,6},{1,7},{2,0},{3,1},{4,2},{5,3},{6,4},{7,5},{8,14},{9,15},{10,... | collective-permute-start | bytes 36872 | tf_op jit(solution)/shard_map/ppermute | solution.py:404
  97.5 11.6 %collective-permute-start.20 = (bf16[128,512]{1,0:T(8,128)(2,1)S(1)}, bf16[128,512]{1,0:T(8,128)(2,1)S(1)}, u32[]{:S(2)}, u32[]{:S(2)}) collective-permute-start(bf16[128,512]{1,0:T(8,128)(2,1)S(1)} %add_convert_fusion.3), channel_id=1, source_target_pairs={{0,2},{1,3},{2,4},{3,5},{4,6},{5,7},{6,0},{7,1},{8,10},{9,11},{10,... | collective-permute-start | bytes 393224 | tf_op jit(solution)/shard_map/ppermute | solution.py:407
  105.4 5.7 %collective-permute-start.23 = (bf16[128,512]{1,0:T(8,128)(2,1)S(1)}, bf16[128,512]{1,0:T(8,128)(2,1)S(1)}, u32[]{:S(2)}, u32[]{:S(2)}) collective-permute-start(bf16[128,512]{1,0:T(8,128)(2,1)S(1)} %add_convert_fusion.2), channel_id=1, source_target_pairs={{0,6},{1,7},{2,0},{3,1},{4,2},{5,3},{6,4},{7,5},{8,14},{9,15},{10,... | collective-permute-start | bytes 393224 | tf_op jit(solution)/shard_map/ppermute | solution.py:407
  105.6 17.6 %collective-permute-start.45 = (f32[512,128]{1,0:T(8,128)}, f32[512,128]{1,0:T(8,128)S(1)}, u32[]{:S(2)}, u32[]{:S(2)}) collective-permute-start(f32[512,128]{1,0:T(8,128)} %router_grad.1), channel_id=1, source_target_pairs={{0,24},{8,16},{16,8},{24,0},{1,25},{9,17},{17,9},{25,1},{2,26},{10... | collective-permute-start | bytes 786440 | tf_op jit(solution)/shard_map/ppermute | solution.py:463
  108.1 15.1 %collective-permute-start.44 = (f32[512,128]{1,0:T(8,128)}, f32[512,128]{1,0:T(8,128)S(1)}, u32[]{:S(2)}, u32[]{:S(2)}) collective-permute-start(f32[512,128]{1,0:T(8,128)} %router_grad.1), channel_id=1, source_target_pairs={{0,16},{8,24},{16,0},{24,8},{1,17},{9,25},{17,1},{25,9},{2,18},{10... | collective-permute-start | bytes 786440 | tf_op jit(solution)/shard_map/ppermute | solution.py:463
  108.6 14.6 %collective-permute-start.43 = (f32[512,128]{1,0:T(8,128)}, f32[512,128]{1,0:T(8,128)S(1)}, u32[]{:S(2)}, u32[]{:S(2)}) collective-permute-start(f32[512,128]{1,0:T(8,128)} %router_grad.1), channel_id=1, source_target_pairs={{0,8},{8,0},{16,24},{24,16},{1,9},{9,1},{17,25},{25,17},{2,10},{10... | collective-permute-start | bytes 786440 | tf_op jit(solution)/shard_map/ppermute | solution.py:463
  109.2 10.4 %collective-permute-start.25 = (bf16[128,512]{1,0:T(8,128)(2,1)S(1)}, bf16[128,512]{1,0:T(8,128)(2,1)S(1)}, u32[]{:S(2)}, u32[]{:S(2)}) collective-permute-start(bf16[128,512]{1,0:T(8,128)(2,1)S(1)} %add_convert_fusion.1), channel_id=1, source_target_pairs={{0,4},{1,5},{2,6},{3,7},{4,0},{5,1},{6,2},{7,3},{8,12},{9,13},{10,... | collective-permute-start | bytes 393224 | tf_op jit(solution)/shard_map/ppermute | solution.py:407
  111.1 8.5 %collective-permute-start.27 = (bf16[128,512]{1,0:T(8,128)(2,1)S(1)}, bf16[128,512]{1,0:T(8,128)(2,1)S(1)}, u32[]{:S(2)}, u32[]{:S(2)}) collective-permute-start(bf16[128,512]{1,0:T(8,128)(2,1)S(1)} %add_convert_fusion), channel_id=1, source_target_pairs={{0,2},{1,3},{2,4},{3,5},{4,6},{5,7},{6,0},{7,1},{8,10},{9,11},{10,... | collective-permute-start | bytes 393224 | tf_op jit(solution)/shard_map/ppermute | solution.py:407
  (30 other events, 171.0 us)

commit v3 on v1

v3 whole, which is shorter than its diff:
```python
import functools
import math

import jax
import jax.numpy as jnp
import numpy as np
from jax import lax
from jax.experimental import pallas as pl
from jax.experimental.pallas import tpu as pltpu
from jax.sharding import PartitionSpec as P

norm_eps = 1e-06
f32 = jnp.float32
bf16 = jnp.bfloat16
vmem_limit = 56 * 1024 * 1024


def takes(us):
    flops = int(us * 1.15e9)
    return pl.CostEstimate(flops=flops, transcendentals=0, bytes_accessed=int(us * 3.6e6))


def dot_nt(a, b):
    return lax.dot_general(a, b, (((1,), (1,)), ((), ())), preferred_element_type=f32)


def dot_nn(a, b):
    return lax.dot_general(a, b, (((1,), (0,)), ((), ())), preferred_element_type=f32)


def dot_tn(a, b):
    return lax.dot_general(a, b, (((0,), (0,)), ((), ())), preferred_element_type=f32)


def whole(shape):
    return pl.BlockSpec(shape, lambda *_: (0,) * len(shape))


def keys_kernel(k_ref, v_ref, gain_ref, kv_ref):
    hd = gain_ref.shape[1]
    gain = gain_ref[...]
    for g in range(k_ref.shape[1] // hd):
        k = k_ref[:, g * hd : (g + 1) * hd].astype(f32)
        inv = lax.rsqrt(jnp.mean(k * k, axis=-1, keepdims=True) + norm_eps)
        kv_ref[:, 2 * g * hd : (2 * g + 1) * hd] = ((k * inv) * gain).astype(bf16)
        kv_ref[:, (2 * g + 1) * hd : (2 * g + 2) * hd] = v_ref[:, g * hd : (g + 1) * hd]


def pack_keys(k_pre, values, k_gain):
    rows, width = k_pre.shape
    return pl.pallas_call(
        keys_kernel,
        out_shape=jax.ShapeDtypeStruct((rows, 2 * width), bf16),
        cost_estimate=takes(1.8),
        name="pack_keys",
    )(k_pre, values, k_gain)


def gates_kernel(meta_ref, moe_ref, router_ref, ids_ref, dmoe_ref, *pack_refs):
    tok, width = moe_ref.shape
    experts = router_ref.shape[1]
    chips = len(pack_refs)
    logits = dot_nn(moe_ref[...], router_ref[...])
    lane = lax.broadcasted_iota(jnp.int32, (tok, experts), 1)
    chosen = lane == ids_ref[:, 0:1]
    for k in range(1, ids_ref.shape[1]):
        chosen = jnp.logical_or(chosen, lane == ids_ref[:, k : k + 1])
    weights = jnp.where(chosen, jnp.exp(logits), 0.0)
    probs = weights / jnp.sum(weights, axis=-1, keepdims=True)
    high = probs.astype(bf16)
    low = (probs - high.astype(f32)).astype(bf16)
    coded = jnp.where(chosen, high.astype(f32), -1.0).astype(bf16)
    share = width // (2 * chips)
    chip, core = meta_ref[0], meta_ref[1]
    d_all = dmoe_ref[...]
    for k in range(chips):
        to = lax.rem(chip + k, chips) * 2
        pack_refs[k][:, :width] = d_all
        for i in range(2):
            at = pl.multiple_of((to + lax.rem(core + i, 2)) * share, 128)
            pack_refs[k][:, width + i * share : width + (i + 1) * share] = moe_ref[
                :, pl.ds(at, share)
            ]
        pack_refs[k][:, width + 2 * share : width + 2 * share + experts] = coded
        pack_refs[k][:, width + 2 * share + experts :] = low


def gates(meta, moe_in, router, ids, d_moe, chips):
    tok, width = moe_in.shape
    experts = router.shape[1]
    vm = pl.BlockSpec(memory_space=pltpu.VMEM)
    packed = width + width // chips + 2 * experts
    return pl.pallas_call(
        gates_kernel,
        in_specs=[pl.BlockSpec(memory_space=pltpu.SMEM)] + [vm] * 4,
        out_shape=[jax.ShapeDtypeStruct((tok, packed), bf16)] * chips,
        compiler_params=pltpu.CompilerParams(vmem_limit_bytes=vmem_limit),
        cost_estimate=takes(2.8),
        name="gates",
    )(meta, moe_in, router, ids, d_moe)


def attend_kernel(blocks, meta_ref, q_ref, o_ref, do_ref, gain_ref, *refs):
    kv_refs = refs[:2]
    dq_ref = refs[-3]
    part_refs = refs[-2:]
    tok = q_ref.shape[0]
    hd = gain_ref.shape[1]
    heads = q_ref.shape[1] // hd
    kb = 2 * kv_refs[0].shape[0] // blocks
    keys = kb * blocks
    scale = hd ** (-0.5)
    offset = meta_ref[0]
    gain = gain_ref[...]
    key = jnp.concatenate([r[:, :hd] for r in kv_refs], axis=0)
    val = jnp.concatenate([r[:, hd:] for r in kv_refs], axis=0)
    pos = jnp.concatenate(
        [
            meta_ref[1 + b] * kb + lax.broadcasted_iota(jnp.int32, (kb, 1), 0)
            for b in range(blocks)
        ],
        axis=0,
    )
    step_heads = min(heads, max(128 // tok, heads * 1024 // keys))
    rows = step_heads * tok
    limit = offset + lax.rem(lax.broadcasted_iota(jnp.int32, (1, rows), 1), tok)
    visible = pos <= limit
    dk = dv = None
    for h0 in range(0, heads, step_heads):

        def stack(ref):
            return jnp.concatenate(
                [ref[:, h * hd : (h + 1) * hd] for h in range(h0, h0 + step_heads)], axis=0
            )

        q = stack(q_ref).astype(f32)
        do = stack(do_ref)
        prod = do.astype(f32) * stack(o_ref).astype(f32)
        delta = jnp.sum(prod.T, axis=0, keepdims=True)
        inv = lax.rsqrt(jnp.mean(q * q, axis=-1, keepdims=True) + norm_eps)
        unit = q * inv
        q_hat = (unit * gain).astype(bf16)
        scores = dot_nt(key, q_hat)
        ex = jnp.where(visible, jnp.exp2(scores * (scale * math.log2(math.e))), 0.0)
        probs = ex * (1.0 / jnp.sum(ex, axis=0, keepdims=True))
        dv_one = dot_nn(probs.astype(bf16), do)
        dprobs = dot_nt(val, do)
        ds = ((probs * scale) * (dprobs - delta)).astype(bf16)
        dk_one = dot_nn(ds, q_hat)
        dq = dot_tn(key, ds).T
        c = dq * gain
        dq_pre = (inv * (c - unit * jnp.mean(c * unit, axis=-1, keepdims=True))).astype(bf16)
        for i in range(step_heads):
            h = h0 + i
            dq_ref[:, h * hd : (h + 1) * hd] = dq_pre[i * tok : (i + 1) * tok, :]
        dk = dk_one if dk is None else dk + dk_one
        dv = dv_one if dv is None else dv + dv_one
    half = keys // 2
    for i, ref in enumerate(part_refs):
        ref[:, :hd] = dk[i * half : (i + 1) * half, :].astype(ref.dtype)
        ref[:, hd:] = dv[i * half : (i + 1) * half, :].astype(ref.dtype)


def attend(meta, q, o, do, gain, kv_halves, blocks, kv_heads):
    tok, width = q.shape
    hd = gain.shape[1]
    half, kv_width = kv_halves[0].shape
    step = width // kv_heads
    row_spec = pl.BlockSpec((tok, step), lambda g, m: (0, g))
    part_spec = pl.BlockSpec((half, 2 * hd), lambda g, m: (0, g))
    return pl.pallas_call(
        functools.partial(attend_kernel, blocks),
        grid_spec=pltpu.PrefetchScalarGridSpec(
            num_scalar_prefetch=1,
            grid=(kv_width // (2 * hd),),
            in_specs=[row_spec] * 3
            + [whole((1, hd))]
            + [part_spec] * 2,
            out_specs=[row_spec, part_spec, part_spec],
        ),
        out_shape=[
            jax.ShapeDtypeStruct((tok, width), bf16),
            jax.ShapeDtypeStruct((half, kv_width), f32),
            jax.ShapeDtypeStruct((half, kv_width), bf16),
        ],
        compiler_params=pltpu.CompilerParams(vmem_limit_bytes=vmem_limit),
        cost_estimate=takes(10),
        name="attend",
    )(meta, q, o, do, gain, *kv_halves)


def finish_kernel(k_ref, gain_ref, *refs):
    dk_ref, dv_ref = refs[-2:]
    hd = gain_ref.shape[1]
    gain = gain_ref[...]
    total = refs[0][...].astype(f32)
    for r in refs[1:-2]:
        total = total + r[...].astype(f32)
    for g in range(k_ref.shape[1] // hd):
        k = k_ref[:, g * hd : (g + 1) * hd].astype(f32)
        inv = lax.rsqrt(jnp.mean(k * k, axis=-1, keepdims=True) + norm_eps)
        unit = k * inv
        c = total[:, 2 * g * hd : (2 * g + 1) * hd] * gain
        dk = inv * (c - unit * jnp.mean(c * unit, axis=-1, keepdims=True))
        dk_ref[:, g * hd : (g + 1) * hd] = dk.astype(bf16)
        dv_ref[:, g * hd : (g + 1) * hd] = total[
            :, (2 * g + 1) * hd : (2 * g + 2) * hd
        ].astype(bf16)


def finish_keys(k_pre, k_gain, sums):
    out = jax.ShapeDtypeStruct(k_pre.shape, bf16)
    return pl.pallas_call(
        finish_kernel,
        out_shape=(out, out),
        compiler_params=pltpu.CompilerParams(vmem_limit_bytes=vmem_limit),
        cost_estimate=takes(2.2),
        name="finish_keys",
    )(k_pre, k_gain, *sums)


def earlier_same_block(rows, block):
    i = lax.broadcasted_iota(jnp.int32, (rows, rows), 0)
    j = lax.broadcasted_iota(jnp.int32, (rows, rows), 1)
    same = lax.div(i, block) == lax.div(j, block)
    return jnp.where(jnp.logical_and(same, j < i), 1.0, 0.0).astype(bf16)


def terms_kernel(blocks, sp, cap, meta_ref, table_ref, lanes_ref, *refs):
    d_refs = refs[:2]
    g_refs = refs[2:4]
    eout_ref, gated_ref, terms_ref, dm, hit_scr, acc = refs[4:]
    half = d_refs[0].shape[0]
    tokens = 2 * half
    tok = tokens // blocks
    experts = g_refs[0].shape[1]
    rows = eout_ref.shape[0]
    step = pl.program_id(0)

    def pick():
        expert = meta_ref[0] + table_ref[:, 0:1]
        return lax.broadcasted_iota(jnp.int32, (rows, experts), 1) == expert

    @pl.when(step == 0)
    def _():
        coded = jnp.concatenate([r[...] for r in g_refs], axis=0)
        chosen = (coded >= 0).astype(bf16)
        rank = dot_nn(earlier_same_block(tokens, tok), chosen)
        sel = jnp.where(pick(), 1.0, 0.0).astype(bf16)
        gate = dot_nt(sel, coded)
        place = dot_nt(sel, rank.astype(bf16))
        lane_block = lax.div(lax.broadcasted_iota(jnp.int32, (1, tokens), 1), tok)
        source = jnp.zeros((1, tokens), jnp.int32)
        for b in range(blocks):
            source = jnp.where(lane_block == b, meta_ref[1 + b], source)
        hit = jnp.logical_and(
            jnp.logical_and(gate >= 0.0, place == table_ref[:, 1:2].astype(f32)),
            source == table_ref[:, 2:3],
        )
        gated_ref[...] = jnp.where(hit, gate, 0.0).astype(bf16)
        hit_scr[...] = jnp.where(hit, 1.0, 0.0)
        acc[...] = jnp.zeros_like(acc)

    for i in range(2):
        dm[i * half : (i + 1) * half, :] = d_refs[i][...]
    acc[...] += dot_nt(eout_ref[...], dm[...])

    @pl.when(step == pl.num_programs(0) - 1)
    def _():
        terms = jnp.sum(acc[...] * hit_scr[...], axis=-1, keepdims=True)
        placed = jnp.where(pick(), terms, 0.0)
        want = lax.broadcasted_iota(jnp.int32, (cap * sp, rows), 0)
        fold = jnp.where(want == lanes_ref[...], 1.0, 0.0)
        terms_ref[...] = lax.dot_general(
            fold,
            placed,
            (((1,), (0,)), ((), ())),
            precision=lax.Precision.HIGHEST,
            preferred_element_type=f32,
        )


def slot_terms(meta, packs, eout, experts, cap, sp):
    rows, width = eout.shape
    half, packed = packs[0].shape
    blocks = sp
    r = np.arange(rows)
    e, c, s = r // (cap * sp), (r // sp) % cap, r % sp
    table = jnp.asarray(np.stack([e, c, s], axis=1), jnp.int32)
    lanes = jnp.asarray((c * sp + s)[None, :], jnp.int32)
    col = min(width, 1024)
    tokens = 2 * half
    gate_at = (packed - 2 * experts) // experts
    d_spec = pl.BlockSpec((half, col), lambda i, m: (0, i))
    g_spec = pl.BlockSpec((half, experts), lambda i, m: (0, gate_at))
    e_spec = pl.BlockSpec((rows, col), lambda i, m: (0, i))
    return pl.pallas_call(
        functools.partial(terms_kernel, blocks, sp, cap),
        grid_spec=pltpu.PrefetchScalarGridSpec(
            num_scalar_prefetch=1,
            grid=(width // col,),
            in_specs=[whole((rows, 3)), whole((1, rows))]
            + [d_spec] * 2
            + [g_spec] * 2
            + [e_spec],
            out_specs=[whole((rows, tokens)), whole((cap * sp, experts))],
            scratch_shapes=[
                pltpu.VMEM((tokens, col), bf16),
                pltpu.VMEM((rows, tokens), f32),
                pltpu.VMEM((rows, tokens), f32),
            ],
        ),
        out_shape=[
            jax.ShapeDtypeStruct((rows, tokens), bf16),
            jax.ShapeDtypeStruct((cap * sp, experts), f32),
        ],
        compiler_params=pltpu.CompilerParams(vmem_limit_bytes=vmem_limit),
        cost_estimate=takes(6.2),
        name="slot_terms",
    )(meta, table, lanes, *packs, *packs, eout)


def batch_kernel(gated_ref, *refs):
    batch_ref, dm = refs[-2:]
    tok = refs[0].shape[0]
    for b, r in enumerate(refs[:-2]):
        dm[b * tok : (b + 1) * tok, :] = r[...]
    batch_ref[...] = dot_nn(gated_ref[...], dm[...]).astype(bf16)


def batch_grad(gated, packs, width):
    rows, tokens = gated.shape
    tok = packs[0].shape[0]
    col = min(width, 1024)
    return pl.pallas_call(
        batch_kernel,
        grid=(width // col,),
        in_specs=[whole((rows, tokens))]
        + [pl.BlockSpec((tok, col), lambda i: (0, i))] * len(packs),
        out_specs=pl.BlockSpec((rows, col), lambda i: (0, i)),
        out_shape=jax.ShapeDtypeStruct((rows, width), bf16),
        scratch_shapes=[pltpu.VMEM((tokens, col), bf16)],
        compiler_params=pltpu.CompilerParams(vmem_limit_bytes=vmem_limit),
        cost_estimate=takes(4.6),
        name="batch_grad",
    )(gated, *packs)


def router_kernel(sp, cap, meta_ref, *refs):
    info_refs, moe_refs = refs[:2], refs[2:4]
    terms_in, out_ref, terms_ref = refs[4:]
    terms_ref[...] = jnp.sum(terms_in[...], axis=0)
    share, experts = out_ref.shape
    tok = 2 * info_refs[0].shape[0] // sp
    info = jnp.concatenate([r[...] for r in info_refs], axis=0)
    moe = jnp.concatenate([r[...] for r in moe_refs], axis=0)
    high = info[:, :experts]
    chosen = high >= 0
    prob = jnp.where(chosen, high.astype(f32) + info[:, experts:].astype(f32), 0.0)
    rank = dot_nn(earlier_same_block(tok * sp, tok), chosen.astype(bf16))
    pieces = []
    for b in range(sp):
        place = rank[b * tok : (b + 1) * tok, :]
        one = jnp.zeros((tok, experts), f32)
        for c in range(cap):
            row = terms_ref[pl.ds(c * sp + meta_ref[1 + b], 1), :]
            one = jnp.where(place == c, row, one)
        pieces.append(one)
    dgate = jnp.where(chosen, jnp.concatenate(pieces, axis=0), 0.0)
    dlogit = prob * (dgate - jnp.sum(prob * dgate, axis=-1, keepdims=True))
    a = dlogit.astype(bf16)
    rest = dlogit - a.astype(f32)
    b = rest.astype(bf16)
    c = (rest - b.astype(f32)).astype(bf16)
    wide = dot_tn(moe, jnp.concatenate([a, b, c], axis=1))
    total = wide[:, :experts] + wide[:, experts : 2 * experts] + wide[:, 2 * experts :]
    out_ref[...] = total.astype(bf16)


def router_grad(meta, packs, terms, width, experts, cap, sp):
    half, packed = packs[0].shape
    share = width // sp
    info_at = packed // (2 * experts) - 1
    info_spec = pl.BlockSpec((half, 2 * experts), lambda i, m: (0, info_at))
    moe_specs = [pl.BlockSpec((half, share), lambda i, m, c=c: (0, sp + c)) for c in range(2)]
    return pl.pallas_call(
        functools.partial(router_kernel, sp, cap),
        grid_spec=pltpu.PrefetchScalarGridSpec(
            num_scalar_prefetch=1,
            grid=(1,),
            in_specs=[info_spec] * 2 + moe_specs + [whole(terms.shape)],
            out_specs=whole((share, experts)),
            scratch_shapes=[pltpu.VMEM((cap * sp, experts), f32)],
        ),
        out_shape=jax.ShapeDtypeStruct((share, experts), bf16),
        compiler_params=pltpu.CompilerParams(vmem_limit_bytes=vmem_limit),
        cost_estimate=takes(3),
        name="router_grad",
    )(meta, *packs, *packs, terms)


def flipped(x, axis, size, k):
    return lax.ppermute(x, axis, [(i, i ^ k) for i in range(size)])


def sent_over(axis, size, x):
    if size & (size - 1):
        return [lax.psum(x.astype(f32), axis)]
    return [x] + [flipped(x, axis, size, k) for k in range(1, size)]


def tree_sum(terms):
    terms = [x.astype(f32) for x in terms]
    while len(terms) > 1:
        terms = [a + b for a, b in zip(terms[0::2], terms[1::2])]
    return terms[0]


def together(*arrays):
    return lax.optimization_barrier(arrays)


def on_device(
    q_pre,
    attn_out,
    d_attn,
    k_pre,
    values,
    q_gain,
    k_gain,
    offsets,
    moe_in,
    router,
    expert_ids,
    d_moe,
    expert_out,
):
    dp = lax.axis_size("dp")
    sp = lax.axis_size("sp")
    me = lax.axis_index("sp").astype(jnp.int32)
    other = jnp.bitwise_xor(me, 1)
    chips = sp // 2
    swap = [(i, i ^ 1) for i in range(sp)]

    def exchange(x):
        return lax.ppermute(x, "sp", swap)

    def ahead(x, k):
        return lax.ppermute(x, "sp", [(i, (i + 2 * k) % sp) for i in range(sp)])

    def back(x, k):
        return lax.ppermute(x, "sp", [(i, (i - 2 * k) % sp) for i in range(sp)])

    def both(mine):
        mine = jnp.concatenate(mine, axis=0)
        return [mine, exchange(mine)]

    steps = 2 * jnp.arange(chips, dtype=jnp.int32)
    owners = jnp.concatenate([lax.rem(me - steps + sp, sp), lax.rem(other - steps + sp, sp)])
    qg, kg = q_gain[None, :], k_gain[None, :]
    kv_heads = k_pre.shape[2] // q_gain.shape[0]
    width = moe_in.shape[2]
    experts = router.shape[1]
    place = jnp.stack([me // 2, jnp.bitwise_and(me, 1)])

    experts_here, _, cap, _ = expert_out.shape[1:]
    eout = jnp.transpose(expert_out[0], (0, 2, 1, 3)).reshape(experts_here * cap * sp, width)
    slot_meta = jnp.concatenate([(me * experts_here)[None], owners])
    meta = jnp.concatenate([offsets + me * q_pre.shape[1], owners])

    kv = pack_keys(k_pre[0], values[0], kg)
    kv = [kv] + [ahead(kv, k) for k in range(1, chips)]
    packs = gates(place, moe_in[0], router, expert_ids[0], d_moe[0], chips)
    kv, packs = together(kv, packs)

    packs = [packs[0]] + [ahead(packs[k], k) for k in range(1, chips)]
    dq, keep, send = attend(
        meta, q_pre[0], attn_out[0], d_attn[0], qg, both(kv), sp, kv_heads
    )
    packs, keep, send = together(packs, keep, send)

    rows = k_pre.shape[1]
    arrived = exchange(send)
    sums = [
        keep[k * rows : (k + 1) * rows] + arrived[k * rows : (k + 1) * rows].astype(f32)
        for k in range(chips)
    ]
    sums = [sums[0]] + [x.astype(bf16) for x in sums[1:]]
    packs, sums = together(packs, sums)

    sums = [sums[0]] + [back(sums[k], k) for k in range(1, chips)]
    packs = both(packs)
    gated, terms = slot_terms(slot_meta, packs, eout, experts, cap, sp)
    terms = lax.all_to_all(
        jnp.broadcast_to(terms[None], (sp,) + terms.shape),
        "sp",
        split_axis=0,
        concat_axis=0,
        tiled=True,
    )
    batch = batch_grad(gated, packs, width)
    sums, terms, batch = together(sums, terms, batch)

    routed = router_grad(slot_meta, packs, terms, width, experts, cap, sp)
    routed = sent_over("dp", dp, routed)
    dk, dv = finish_keys(k_pre[0], kg, sums)
    batch = jnp.transpose(batch.reshape(experts_here, cap, sp, width), (0, 2, 1, 3))
    return (dq[None], dk[None], dv[None], batch[None], tree_sum(routed))


def solution(mesh):
    in_specs = (
        P("dp", "sp", None),
        P("dp", "sp", None),
        P("dp", "sp", None),
        P("dp", "sp", None),
        P("dp", "sp", None),
        P(),
        P(),
        P("dp"),
        P("dp", "sp", None),
        P(),
        P("dp", "sp", None),
        P("dp", "sp", None),
        P("dp", "sp", None, None, None),
    )
    out_specs = (
        P("dp", "sp", None),
        P("dp", "sp", None),
        P("dp", "sp", None),
        P("dp", "sp", None, None, None),
        P("sp", None),
    )
    return jax.shard_map(
        on_device, mesh=mesh, in_specs=in_specs, out_specs=out_specs, check_vma=False
    )
```

time: 181 us -> 114 us (0.63)
  blocking collectives: 63.1 us -> 0 us
  waiting for transfers between devices: 14.8 us -> 40.9 us
  starting transfers between devices: 46.2 us -> 29.9 us
  between operations: 15 us -> 1.47 us
  local copies, waits for them, and re-layouts: 9.03 us -> 4.94 us
  other arithmetic: 2.65 us -> 4.69 us
  Pallas kernels: 29.3 us -> 31.2 us
    all_gather x1 -> x0, blocking collectives: 63.1 us -> none  [on_device(): info_all = lax.all_gather(info, ('dp', 'sp'), axis=0, tiled=True)]
    ppermute x6, waiting for transfers between devices: 5.07 us -> 27.7 us  [ahead(): return lax.ppermute(x, 'sp', [(i, (i + 2 * k) % sp) for i in range(sp)])]
    ppermute x6, starting transfers between devices: 25.7 us -> 11.8 us  [ahead(): return lax.ppermute(x, 'sp', [(i, (i + 2 * k) % sp) for i in range(sp)])]
    all_to_all x2 -> x1, waiting for transfers between devices: 9.68 us -> 0.52 us  [on_device(): lax.all_to_all(jnp.broadcast_to(terms[None], (sp,) + terms.shape), 'sp',...]
    all_to_all x2 -> x1, starting transfers between devices: 13 us -> 4.53 us  [on_device(): lax.all_to_all(jnp.broadcast_to(terms[None], (sp,) + terms.shape), 'sp',...]
    ppermute x3, waiting for transfers between devices: 0.01 us -> 6.43 us  [back(): return lax.ppermute(x, 'sp', [(i, (i - 2 * k) % sp) for i in range(sp)])]
    ppermute x3, starting transfers between devices: 4.85 us -> 9.72 us  [back(): return lax.ppermute(x, 'sp', [(i, (i - 2 * k) % sp) for i in range(sp)])]
    ppermute x0 -> x3, starting transfers between devices: none -> 3.55 us  [flipped(): return lax.ppermute(x, axis, [(i, i ^ k) for i in range(size)])]
  transfers between devices with their start and end apart: 24 -> 16, of which waited for: 2 -> 9; matrix products, arithmetic and copies ran while one was open for 4% -> 3% of each run, Pallas kernels for 13% -> 23%
where the time goes in v3:
time: 114 us; the launch traced here: 113 us
  waiting for transfers between devices  40.9 us (36%)
  Pallas kernels  31.2 us (27%)
  starting transfers between devices  29.9 us (26%)
  local copies, waits for them, and re-layouts  4.94 us (4%)
  other arithmetic  4.69 us (4%)
  between operations  1.47 us (1%)
    ppermute x6, waiting for transfers between devices, ahead(): return lax.ppermute(x, 'sp', [(i, (i + 2 * k) % sp) for i in range(sp)])  27.7 us
    ppermute x6, starting transfers between devices, ahead(): return lax.ppermute(x, 'sp', [(i, (i + 2 * k) % sp) for i in range(sp)])  11.8 us
    pallas_call x1, Pallas kernels, attend(): pl.pallas_call(functools.partial(attend_kernel, blocks), grid_spec=pltpu....  10.3 us
    ppermute x3, starting transfers between devices, back(): return lax.ppermute(x, 'sp', [(i, (i - 2 * k) % sp) for i in range(sp)])  9.72 us
    ppermute x3, waiting for transfers between devices, back(): return lax.ppermute(x, 'sp', [(i, (i - 2 * k) % sp) for i in range(sp)])  6.43 us
    pallas_call x1, Pallas kernels, slot_terms(): pl.pallas_call(functools.partial(terms_kernel, blocks, sp, cap), grid_spe...  6.29 us
    pallas_call x1, Pallas kernels, batch_grad(): pl.pallas_call(batch_kernel, grid=(width // col,), in_specs=[whole((rows,...  4.68 us
    all_to_all x1, starting transfers between devices, on_device(): lax.all_to_all(jnp.broadcast_to(terms[None], (sp,) + terms.shape), 'sp',...  4.53 us
  transfers between devices with their start and end apart: 16, of which 9 were waited for; matrix products, arithmetic and copies ran while one was open for 3% of the time, Pallas kernels for 23%

profile of v3, /device:TPU:0, one launch (start us, length us, event | category | flops | bytes accessed | tf_op | source)
XLA Modules:
  0.0 113.0 jit_solution(641673207576795380)
XLA Ops:
  0.6 0.0 copy-start.6
  0.6 1.8 %pack_keys.1 = bf16[128,1024]{1,0:T(8,128)(2,1)} custom-call(bf16[128,512]{1,0:T(8,128)(2,1)} %bitcast.35, bf16[128,512]{1,0:T(8,128)(2,1)} %bitcast.34, f32[1,128]{1,0:T(1,128)} %bitcast.38), custom_call_target="tpu_custom_call" | custom-call | flops 2070000000 | bytes 6480000 | tf_op jit(solution)/shard_map/pack_keys/pallas_call | solution.py:51
  2.5 5.0 %collective-permute-start.2 = (bf16[128,1024]{1,0:T(8,128)(2,1)}, bf16[128,1024]{1,0:T(8,128)(2,1)S(1)}, u32[]{:S(2)}, u32[]{:S(2)}) collective-permute-start(bf16[128,1024]{1,0:T(8,128)(2,1)} %pack_keys.1), channel_id=1, source_target_pairs={{0,6},{1,7},{2,0},{3,1},{4,2},{5,3},{6,4},{7,5},{8,14},{9,15},{10,... | collective-permute-start | bytes 786440 | tf_op jit(solution)/shard_map/ppermute | solution.py:449
  7.5 0.0 collective-permute-start.1
  7.5 1.0 collective-permute-start
  8.5 0.0 copy-done.6
  8.6 0.7 copy.20
  9.2 0.6 pad_add_fusion.meta_ref
  9.8 0.0 copy-start.1
  9.8 2.9 %gates.1 = (bf16[32,5376]{1,0:T(8,128)(2,1)}, bf16[32,5376]{1,0:T(8,128)(2,1)}, bf16[32,5376]{1,0:T(8,128)(2,1)}, bf16[32,5376]{1,0:T(8,128)(2,1)}) custom-call(s32[2]{0:T(128)} %pad_add_fusion.meta_ref, bf16[32,4096]{1,0:T(8,128)(2,1)} %bitcast.32, bf16[4096,128]{1,0:T(8,128)(2,1)} %router_ref.1, s32[32,8]{1,0:T(8,128)} %bitcast.27, bf16[32,4096]{1,0:T(8,128)(2,1)} %bitcast.33), custom_call_target="tpu_custom_call" | custom-call | flops 3220000000 | bytes 10080000 | tf_op jit(solution)/shard_map/gates/pallas_call | solution.py:93
  12.7 1.9 %collective-permute-done.2 = bf16[128,1024]{1,0:T(8,128)(2,1)S(1)} collective-permute-done((bf16[128,1024]{1,0:T(8,128)(2,1)}, bf16[128,1024]{1,0:T(8,128)(2,1)S(1)}, u32[]{:S(2)}, u32[]{:S(2)}) %collective-permute-start.2) | collective-permute-done | bytes 262176 | tf_op jit(solution)/shard_map/ppermute | solution.py:449
  14.6 15.4 %collective-permute-done.1 = bf16[128,1024]{1,0:T(8,128)(2,1)S(1)} collective-permute-done((bf16[128,1024]{1,0:T(8,128)(2,1)}, bf16[128,1024]{1,0:T(8,128)(2,1)S(1)}, u32[]{:S(2)}, u32[]{:S(2)}) %collective-permute-start.1) | collective-permute-done | bytes 262176 | tf_op jit(solution)/shard_map/ppermute | solution.py:449
  30.1 0.0 collective-permute-done
  30.1 0.0 copy-done.1
  30.2 0.0 copy-start.5
  30.2 0.1 collective-permute-start.3
  31.0 0.7 add_add_fusion.2
  31.6 1.0 collective-permute-start.4
  32.6 1.8 %collective-permute-start.5 = (bf16[32,5376]{1,0:T(8,128)(2,1)}, bf16[32,5376]{1,0:T(8,128)(2,1)S(1)}, u32[]{:S(2)}, u32[]{:S(2)}) collective-permute-start(bf16[32,5376]{1,0:T(8,128)(2,1)} %get-tuple-element.55), channel_id=1, source_target_pairs={{0,4},{1,5},{2,6},{3,7},{4,0},{5,1},{6,2},{7,3},{8,12},{9,13},{10,... | collective-permute-start | bytes 1032200 | tf_op jit(solution)/shard_map/ppermute | solution.py:449
  34.4 0.0 copy-done.9
  34.4 2.9 %collective-permute-start.6 = (bf16[32,5376]{1,0:T(8,128)(2,1)S(1)}, bf16[32,5376]{1,0:T(8,128)(2,1)S(1)}, u32[]{:S(2)}, u32[]{:S(2)}) collective-permute-start(bf16[32,5376]{1,0:T(8,128)(2,1)S(1)} %copy-done.9), channel_id=1, source_target_pairs={{0,6},{1,7},{2,0},{3,1},{4,2},{5,3},{6,4},{7,5},{8,14},{9,15},{10,... | collective-permute-start | bytes 1032200 | tf_op jit(solution)/shard_map/ppermute | solution.py:449
  37.4 0.0 collective-permute-done.3.refs_1_
  37.4 0.0 copy-start.8
  37.4 0.0 copy-done.5
  37.4 1.0 copy-done.8
  38.3 10.3 %attend.1 = (bf16[32,8192]{1,0:T(8,128)(2,1)}, f32[512,1024]{1,0:T(8,128)}, bf16[512,1024]{1,0:T(8,128)(2,1)}) custom-call(s32[9]{0:T(128)} %get-tuple-element.88.meta_ref, bf16[32,8192]{1,0:T(8,128)(2,1)} %bitcast.29, bf16[32,8192]{1,0:T(8,128)(2,1)} %bitcast.30, bf16[32,8192]{1,0:T(8,128)(2,1)} %bitcast.31, f32[1,128]{1,0:T(1,128)} %bitcast.37, ...), custom_call_target="tpu_custom_call" | custom-call | flops 11500000256 | bytes 36000000 | tf_op jit(solution)/shard_map/attend/pallas_call | solution.py:171
  48.6 0.0 collective-permute-done.4
  48.6 10.3 %collective-permute-done.5 = bf16[32,5376]{1,0:T(8,128)(2,1)S(1)} collective-permute-done((bf16[32,5376]{1,0:T(8,128)(2,1)}, bf16[32,5376]{1,0:T(8,128)(2,1)S(1)}, u32[]{:S(2)}, u32[]{:S(2)}) %collective-permute-start.5) | collective-permute-done | bytes 344096 | tf_op jit(solution)/shard_map/ppermute | solution.py:449
  58.9 0.0 collective-permute-done.6
  58.9 0.0 collective-permute-start.7
  59.0 2.9 %collective-permute-done.7 = bf16[512,1024]{1,0:T(8,128)(2,1)S(1)} collective-permute-done((bf16[512,1024]{1,0:T(8,128)(2,1)}, bf16[512,1024]{1,0:T(8,128)(2,1)S(1)}, u32[]{:S(2)}, u32[]{:S(2)}) %collective-permute-start.7) | collective-permute-done | bytes 1048608 | tf_op jit(solution)/shard_map/ppermute | solution.py:446
  61.8 2.7 %add_convert_fusion = (bf16[128,1024]{1,0:T(8,128)(2,1)S(1)}, bf16[128,1024]{1,0:T(8,128)(2,1)S(1)}, bf16[128,1024]{1,0:T(8,128)(2,1)S(1)}, f32[128,1024]{1,0:T(8,128)}) fusion(f32[512,1024]{1,0:T(8,128)} %get-tuple-element.63, bf16[512,1024]{1,0:T(8,128)(2,1)S(1)} %collective-permute-done.7), kind=kLoop, calls=%fused_computation | loop fusion | flops 1441792 | bytes 4456448 | tf_op jit(solution)/shard_map/convert_element_type | solution.py:488
  64.5 0.0 copy-done
  64.6 0.0 copy-start.4
  64.6 0.2 collective-permute-start.11
  64.8 9.1 %collective-permute-start.8 = (bf16[128,1024]{1,0:T(8,128)(2,1)S(1)}, bf16[128,1024]{1,0:T(8,128)(2,1)S(1)}, u32[]{:S(2)}, u32[]{:S(2)}) collective-permute-start(bf16[128,1024]{1,0:T(8,128)(2,1)S(1)} %get-tuple-element.66), channel_id=1, source_target_pairs={{0,6},{1,7},{2,0},{3,1},{4,2},{5,3},{6,4},{7,5},{8,14},{9,15},{10,... | collective-permute-start | bytes 786440 | tf_op jit(solution)/shard_map/ppermute | solution.py:452
  74.0 0.0 collective-permute-start.9
  74.0 0.6 collective-permute-start.10
  74.5 0.0 collective-permute-done.11.refs_1_.refs_3_
  74.6 0.0 copy-done.4
  74.6 1.1 copy-done.7
  75.6 6.3 %slot_terms.1 = (bf16[384,256]{1,0:T(8,128)(2,1)}, f32[24,128]{1,0:T(8,128)}) custom-call(s32[9]{0:T(128)} %get-tuple-element.87.meta_ref, s32[384,3]{1,0:T(8,128)} %constant.36.clone.table_ref, s32[1,384]{1,0:T(1,128)} %constant.37.clone.lanes_ref, bf16[128,5376]{1,0:T(8,128)(2,1)} %copy-done.4, bf16[128,5376]{1,0:T(8,128)(2,1)} %copy-done.7, ...), custom_call_target="tpu_custom_call" | custom-call | flops 7129999872 | bytes 22320000 | tf_op jit(solution)/shard_map/slot_terms/pallas_call | solution.py:297
  81.9 1.4 %broadcast_in_dim.31 = f32[8,24,128]{2,1,0:T(8,128)} broadcast(f32[24,128]{1,0:T(8,128)} %get-tuple-element.73), dimensions={1,2} | broadcast | bytes 110592 | tf_op jit(solution)/shard_map/broadcast_in_dim | solution.py:495
  83.3 4.5 %all-to-all-start = ((f32[8,24,128]{2,1,0:T(8,128)}), f32[8,24,128]{2,1,0:T(8,128)S(1)}, u32[]{:S(2)}, u32[]{:S(2)}) async-start(f32[8,24,128]{2,1,0:T(8,128)} %broadcast_in_dim.31), calls=%async_computation | async-start | bytes 196608 | tf_op jit(solution)/shard_map/all_to_all | solution.py:494
  87.8 4.7 %batch_grad.1 = bf16[384,4096]{1,0:T(8,128)(2,1)} custom-call(bf16[384,256]{1,0:T(8,128)(2,1)} %get-tuple-element.74.gated_ref, bf16[128,5376]{1,0:T(8,128)(2,1)} %copy-done.4, bf16[128,5376]{1,0:T(8,128)(2,1)} %copy-done.7), custom_call_target="tpu_custom_call" | custom-call | flops 5289999872 | bytes 16559999 | tf_op jit(solution)/shard_map/batch_grad/pallas_call | solution.py:335
  92.5 0.0 collective-permute-done.8.refs_1_
  92.5 6.4 %collective-permute-done.9.refs_2_ = bf16[128,1024]{1,0:T(8,128)(2,1)S(1)} collective-permute-done((bf16[128,1024]{1,0:T(8,128)(2,1)S(1)}, bf16[128,1024]{1,0:T(8,128)(2,1)S(1)}, u32[]{:S(2)}, u32[]{:S(2)}) %collective-permute-start.9) | collective-permute-done | bytes 262176 | tf_op jit(solution)/shard_map/ppermute | solution.py:452
  98.9 0.0 collective-permute-done.10.refs_3_
  98.9 0.5 all-to-all-done.refs_4_
  99.5 0.6 copy-done.3
  100.1 3.0 %router_grad.1 = bf16[512,128]{1,0:T(8,128)(2,1)} custom-call(s32[9]{0:T(128)} %get-tuple-element.87.meta_ref, bf16[128,5376]{1,0:T(8,128)(2,1)} %copy-done.4, bf16[128,5376]{1,0:T(8,128)(2,1)} %copy-done.7, bf16[128,5376]{1,0:T(8,128)(2,1)} %copy-done.4, bf16[128,5376]{1,0:T(8,128)(2,1)} %copy-done.7, f32[8,24,128]{2,1,0:T(8,128)} %copy-done.3), custom_call_target="tpu_custom_call" | custom-call | flops 3449999872 | bytes 10800000 | tf_op jit(solution)/shard_map/router_grad/pallas_call | solution.py:386
  103.1 0.0 copy-done.10
  103.1 0.0 copy-done.11
  103.1 0.0 copy-done.12
  103.1 0.0 copy-start.2
  103.1 2.5 %collective-permute-start.14 = (bf16[512,128]{1,0:T(8,128)(2,1)}, bf16[512,128]{1,0:T(8,128)(2,1)S(1)}, u32[]{:S(2)}, u32[]{:S(2)}) collective-permute-start(bf16[512,128]{1,0:T(8,128)(2,1)} %router_grad.1), channel_id=1, source_target_pairs={{0,24},{8,16},{16,8},{24,0},{1,25},{9,17},{17,9},{25,1},{2,26},{10... | collective-permute-start | bytes 393224 | tf_op jit(solution)/shard_map/ppermute | solution.py:403
  105.6 0.5 collective-permute-start.13
  106.1 0.5 collective-permute-start.12
  106.6 2.3 %finish_keys.1 = (bf16[128,512]{1,0:T(8,128)(2,1)}, bf16[128,512]{1,0:T(8,128)(2,1)}) custom-call(bf16[128,512]{1,0:T(8,128)(2,1)} %bitcast.36, f32[1,128]{1,0:T(1,128)} %bitcast.39, f32[128,1024]{1,0:T(8,128)} %get-tuple-element.75.refs_0_, bf16[128,1024]{1,0:T(8,128)(2,1)} %copy-done.10, bf16[128,1024]{1,0:T(8,128)(2,1)} %copy-done.11, ...), custom_call_target="tpu_custom_call" | custom-call | flops 2529999872 | bytes 7920000 | tf_op jit(solution)/shard_map/finish_keys/pallas_call | solution.py:213
  108.9 0.9 collective-permute-done.14
  109.9 2.3 %collective-permute-done.13 = bf16[512,128]{1,0:T(8,128)(2,1)S(1)} collective-permute-done((bf16[512,128]{1,0:T(8,128)(2,1)}, bf16[512,128]{1,0:T(8,128)(2,1)S(1)}, u32[]{:S(2)}, u32[]{:S(2)}) %collective-permute-start.13) | collective-permute-done | bytes 131104 | tf_op jit(solution)/shard_map/ppermute | solution.py:403
  112.2 0.1 collective-permute-done.12
  112.2 0.0 copy-done.2
  112.2 0.8 add_add_fusion
  (16 shorter events, 0.2 us)
Async XLA Ops:
  0.6 7.9 %copy-start.6 = (s32[1,32,8]{1,2,0:T(8,128)S(1)}, s32[1,32,8]{1,2,0:T(8,128)}, u32[]{:S(2)}) copy-start(s32[1,32,8]{1,2,0:T(8,128)} %param.25) | copy-start | bytes 3076
  2.5 12.1 %collective-permute-start.2 = (bf16[128,1024]{1,0:T(8,128)(2,1)}, bf16[128,1024]{1,0:T(8,128)(2,1)S(1)}, u32[]{:S(2)}, u32[]{:S(2)}) collective-permute-start(bf16[128,1024]{1,0:T(8,128)(2,1)} %pack_keys.1), channel_id=1, source_target_pairs={{0,6},{1,7},{2,0},{3,1},{4,2},{5,3},{6,4},{7,5},{8,14},{9,15},{10,... | collective-permute-start | bytes 786440 | tf_op jit(solution)/shard_map/ppermute | solution.py:449
  7.5 22.5 %collective-permute-start.1 = (bf16[128,1024]{1,0:T(8,128)(2,1)}, bf16[128,1024]{1,0:T(8,128)(2,1)S(1)}, u32[]{:S(2)}, u32[]{:S(2)}) collective-permute-start(bf16[128,1024]{1,0:T(8,128)(2,1)} %pack_keys.1), channel_id=1, source_target_pairs={{0,4},{1,5},{2,6},{3,7},{4,0},{5,1},{6,2},{7,3},{8,12},{9,13},{10,... | collective-permute-start | bytes 786440 | tf_op jit(solution)/shard_map/ppermute | solution.py:449
  7.5 22.5 %collective-permute-start = (bf16[128,1024]{1,0:T(8,128)(2,1)}, bf16[128,1024]{1,0:T(8,128)(2,1)S(1)}, u32[]{:S(2)}, u32[]{:S(2)}) collective-permute-start(bf16[128,1024]{1,0:T(8,128)(2,1)} %pack_keys.1), channel_id=1, source_target_pairs={{0,2},{1,3},{2,4},{3,5},{4,6},{5,7},{6,0},{7,1},{8,10},{9,11},{10,... | collective-permute-start | bytes 786440 | tf_op jit(solution)/shard_map/ppermute | solution.py:449
  9.8 20.2 %copy-start.1 = (bf16[128,1024]{1,0:T(8,128)(2,1)S(1)}, bf16[128,1024]{1,0:T(8,128)(2,1)}, u32[]{:S(2)}) copy-start(bf16[128,1024]{1,0:T(8,128)(2,1)} %pack_keys.1) | copy-start | bytes 786436
  12.7 21.8 %copy-start.9 = (bf16[32,5376]{1,0:T(8,128)(2,1)S(1)}, bf16[32,5376]{1,0:T(8,128)(2,1)}, u32[]{:S(2)}) copy-start(bf16[32,5376]{1,0:T(8,128)(2,1)} %get-tuple-element.56) | copy-start | bytes 1032196
  30.2 7.2 %copy-start.5 = (bf16[512,1024]{1,0:T(8,128)(2,1)}, bf16[512,1024]{1,0:T(8,128)(2,1)S(1)}, u32[]{:S(2)}) copy-start(bf16[512,1024]{1,0:T(8,128)(2,1)S(1)} %constant_dynamic-update-slice_fusion.refs_0_) | copy-start | bytes 3145732
  30.2 7.2 %collective-permute-start.3 = (bf16[512,1024]{1,0:T(8,128)(2,1)S(1)}, bf16[512,1024]{1,0:T(8,128)(2,1)S(1)}, u32[]{:S(2)}, u32[]{:S(2)}) collective-permute-start(bf16[512,1024]{1,0:T(8,128)(2,1)S(1)} %constant_dynamic-update-slice_fusion.refs_0_), channel_id=1, source_target_pairs={{0,1},{1,0},{2,3},{3,2},{4,5},{5,4},{6,7},{7,6},{8,9},{9,8},{10,11... | collective-permute-start | bytes 3145736 | tf_op jit(solution)/shard_map/ppermute | solution.py:446
  31.6 17.0 %collective-permute-start.4 = (bf16[32,5376]{1,0:T(8,128)(2,1)}, bf16[32,5376]{1,0:T(8,128)(2,1)S(1)}, u32[]{:S(2)}, u32[]{:S(2)}) collective-permute-start(bf16[32,5376]{1,0:T(8,128)(2,1)} %get-tuple-element.54), channel_id=1, source_target_pairs={{0,2},{1,3},{2,4},{3,5},{4,6},{5,7},{6,0},{7,1},{8,10},{9,11},{10,... | collective-permute-start | bytes 1032200 | tf_op jit(solution)/shard_map/ppermute | solution.py:449
  32.6 26.3 %collective-permute-start.5 = (bf16[32,5376]{1,0:T(8,128)(2,1)}, bf16[32,5376]{1,0:T(8,128)(2,1)S(1)}, u32[]{:S(2)}, u32[]{:S(2)}) collective-permute-start(bf16[32,5376]{1,0:T(8,128)(2,1)} %get-tuple-element.55), channel_id=1, source_target_pairs={{0,4},{1,5},{2,6},{3,7},{4,0},{5,1},{6,2},{7,3},{8,12},{9,13},{10,... | collective-permute-start | bytes 1032200 | tf_op jit(solution)/shard_map/ppermute | solution.py:449
  34.4 24.5 %collective-permute-start.6 = (bf16[32,5376]{1,0:T(8,128)(2,1)S(1)}, bf16[32,5376]{1,0:T(8,128)(2,1)S(1)}, u32[]{:S(2)}, u32[]{:S(2)}) collective-permute-start(bf16[32,5376]{1,0:T(8,128)(2,1)S(1)} %copy-done.9), channel_id=1, source_target_pairs={{0,6},{1,7},{2,0},{3,1},{4,2},{5,3},{6,4},{7,5},{8,14},{9,15},{10,... | collective-permute-start | bytes 1032200 | tf_op jit(solution)/shard_map/ppermute | solution.py:449
  37.4 1.0 copy-start.8
  58.9 5.5 %copy-start = (bf16[32,5376]{1,0:T(8,128)(2,1)S(1)}, bf16[32,5376]{1,0:T(8,128)(2,1)}, u32[]{:S(2)}) copy-start(bf16[32,5376]{1,0:T(8,128)(2,1)} %get-tuple-element.69) | copy-start | bytes 1032196
  58.9 2.9 %collective-permute-start.7 = (bf16[512,1024]{1,0:T(8,128)(2,1)}, bf16[512,1024]{1,0:T(8,128)(2,1)S(1)}, u32[]{:S(2)}, u32[]{:S(2)}) collective-permute-start(bf16[512,1024]{1,0:T(8,128)(2,1)} %get-tuple-element.64), channel_id=1, source_target_pairs={{0,1},{1,0},{2,3},{3,2},{4,5},{5,4},{6,7},{7,6},{8,9},{9,8},{10,11... | collective-permute-start | bytes 3145736 | tf_op jit(solution)/shard_map/ppermute | solution.py:446
  64.6 9.9 %copy-start.4 = (bf16[128,5376]{1,0:T(8,128)(2,1)}, bf16[128,5376]{1,0:T(8,128)(2,1)S(1)}, u32[]{:S(2)}) copy-start(bf16[128,5376]{1,0:T(8,128)(2,1)S(1)} %constant_dynamic-update-slice_fusion.4.refs_0_.refs_2_) | copy-start | bytes 4128772
  64.6 9.9 %collective-permute-start.11 = (bf16[128,5376]{1,0:T(8,128)(2,1)S(1)}, bf16[128,5376]{1,0:T(8,128)(2,1)S(1)}, u32[]{:S(2)}, u32[]{:S(2)}) collective-permute-start(bf16[128,5376]{1,0:T(8,128)(2,1)S(1)} %constant_dynamic-update-slice_fusion.4.refs_0_.refs_2_), channel_id=1, source_target_pairs={{0,1},{1,0},{2,3},{3,2},{4,5},{5,4},{6,7},{7,6},{8,9},{9,8},{10,11... | collective-permute-start | bytes 4128776 | tf_op jit(solution)/shard_map/ppermute | solution.py:446
  64.8 27.7 %collective-permute-start.8 = (bf16[128,1024]{1,0:T(8,128)(2,1)S(1)}, bf16[128,1024]{1,0:T(8,128)(2,1)S(1)}, u32[]{:S(2)}, u32[]{:S(2)}) collective-permute-start(bf16[128,1024]{1,0:T(8,128)(2,1)S(1)} %get-tuple-element.66), channel_id=1, source_target_pairs={{0,6},{1,7},{2,0},{3,1},{4,2},{5,3},{6,4},{7,5},{8,14},{9,15},{10,... | collective-permute-start | bytes 786440 | tf_op jit(solution)/shard_map/ppermute | solution.py:452
  74.0 24.9 %collective-permute-start.9 = (bf16[128,1024]{1,0:T(8,128)(2,1)S(1)}, bf16[128,1024]{1,0:T(8,128)(2,1)S(1)}, u32[]{:S(2)}, u32[]{:S(2)}) collective-permute-start(bf16[128,1024]{1,0:T(8,128)(2,1)S(1)} %get-tuple-element.67), channel_id=1, source_target_pairs={{0,4},{1,5},{2,6},{3,7},{4,0},{5,1},{6,2},{7,3},{8,12},{9,13},{10,... | collective-permute-start | bytes 786440 | tf_op jit(solution)/shard_map/ppermute | solution.py:452
  74.0 25.0 %collective-permute-start.10 = (bf16[128,1024]{1,0:T(8,128)(2,1)S(1)}, bf16[128,1024]{1,0:T(8,128)(2,1)S(1)}, u32[]{:S(2)}, u32[]{:S(2)}) collective-permute-start(bf16[128,1024]{1,0:T(8,128)(2,1)S(1)} %get-tuple-element.68), channel_id=1, source_target_pairs={{0,2},{1,3},{2,4},{3,5},{4,6},{5,7},{6,0},{7,1},{8,10},{9,11},{10,... | collective-permute-start | bytes 786440 | tf_op jit(solution)/shard_map/ppermute | solution.py:452
  74.5 1.1 copy-start.7
  83.3 16.2 %all-to-all-start = ((f32[8,24,128]{2,1,0:T(8,128)}), f32[8,24,128]{2,1,0:T(8,128)S(1)}, u32[]{:S(2)}, u32[]{:S(2)}) async-start(f32[8,24,128]{2,1,0:T(8,128)} %broadcast_in_dim.31), calls=%async_computation | async-start | bytes 196608 | tf_op jit(solution)/shard_map/all_to_all | solution.py:494
  92.5 10.6 %copy-start.10 = (bf16[128,1024]{1,0:T(8,128)(2,1)}, bf16[128,1024]{1,0:T(8,128)(2,1)S(1)}, u32[]{:S(2)}) copy-start(bf16[128,1024]{1,0:T(8,128)(2,1)S(1)} %collective-permute-done.8.refs_1_) | copy-start | bytes 786436
  98.9 4.2 %copy-start.11 = (bf16[128,1024]{1,0:T(8,128)(2,1)}, bf16[128,1024]{1,0:T(8,128)(2,1)S(1)}, u32[]{:S(2)}) copy-start(bf16[128,1024]{1,0:T(8,128)(2,1)S(1)} %collective-permute-done.9.refs_2_) | copy-start | bytes 786436
  98.9 4.1 %copy-start.12 = (bf16[128,1024]{1,0:T(8,128)(2,1)}, bf16[128,1024]{1,0:T(8,128)(2,1)S(1)}, u32[]{:S(2)}) copy-start(bf16[128,1024]{1,0:T(8,128)(2,1)S(1)} %collective-permute-done.10.refs_3_) | copy-start | bytes 786436
  99.5 0.6 copy-start.3
  103.1 9.1 %copy-start.2 = (bf16[512,128]{1,0:T(8,128)(2,1)S(1)}, bf16[512,128]{1,0:T(8,128)(2,1)}, u32[]{:S(2)}) copy-start(bf16[512,128]{1,0:T(8,128)(2,1)} %router_grad.1) | copy-start | bytes 393220
  103.1 6.8 %collective-permute-start.14 = (bf16[512,128]{1,0:T(8,128)(2,1)}, bf16[512,128]{1,0:T(8,128)(2,1)S(1)}, u32[]{:S(2)}, u32[]{:S(2)}) collective-permute-start(bf16[512,128]{1,0:T(8,128)(2,1)} %router_grad.1), channel_id=1, source_target_pairs={{0,24},{8,16},{16,8},{24,0},{1,25},{9,17},{17,9},{25,1},{2,26},{10... | collective-permute-start | bytes 393224 | tf_op jit(solution)/shard_map/ppermute | solution.py:403
  105.6 6.6 %collective-permute-start.13 = (bf16[512,128]{1,0:T(8,128)(2,1)}, bf16[512,128]{1,0:T(8,128)(2,1)S(1)}, u32[]{:S(2)}, u32[]{:S(2)}) collective-permute-start(bf16[512,128]{1,0:T(8,128)(2,1)} %router_grad.1), channel_id=1, source_target_pairs={{0,16},{8,24},{16,0},{24,8},{1,17},{9,25},{17,1},{25,9},{2,18},{10... | collective-permute-start | bytes 393224 | tf_op jit(solution)/shard_map/ppermute | solution.py:403
  106.1 6.1 %collective-permute-start.12 = (bf16[512,128]{1,0:T(8,128)(2,1)}, bf16[512,128]{1,0:T(8,128)(2,1)S(1)}, u32[]{:S(2)}, u32[]{:S(2)}) collective-permute-start(bf16[512,128]{1,0:T(8,128)(2,1)} %router_grad.1), channel_id=1, source_target_pairs={{0,8},{8,0},{16,24},{24,16},{1,9},{9,1},{17,25},{25,17},{2,10},{10... | collective-permute-start | bytes 393224 | tf_op jit(solution)/shard_map/ppermute | solution.py:403

commit v4 on v3

--- a/solution.py
+++ b/solution.py
@@ -56,10 +56,9 @@
     )(k_pre, values, k_gain)
 
 
-def gates_kernel(meta_ref, moe_ref, router_ref, ids_ref, dmoe_ref, *pack_refs):
+def gates_kernel(chips, meta_ref, moe_ref, router_ref, ids_ref, dmoe_ref, *pack_refs):
     tok, width = moe_ref.shape
     experts = router_ref.shape[1]
-    chips = len(pack_refs)
     logits = dot_nn(moe_ref[...], router_ref[...])
     lane = lax.broadcasted_iota(jnp.int32, (tok, experts), 1)
     chosen = lane == ids_ref[:, 0:1]
@@ -73,16 +72,14 @@
     share = width // (2 * chips)
     chip, core = meta_ref[0], meta_ref[1]
     d_all = dmoe_ref[...]
-    for k in range(chips):
-        to = lax.rem(chip + k, chips) * 2
-        pack_refs[k][:, :width] = d_all
+    for k, ref in enumerate(pack_refs):
+        ref[:, :width] = d_all
+        ref[:, width + 2 * share : width + 2 * share + experts] = coded
+        ref[:, width + 2 * share + experts : width + 2 * share + 2 * experts] = low
+        to = jnp.bitwise_xor(chip, k) * 2
         for i in range(2):
-            at = pl.multiple_of((to + lax.rem(core + i, 2)) * share, 128)
-            pack_refs[k][:, width + i * share : width + (i + 1) * share] = moe_ref[
-                :, pl.ds(at, share)
-            ]
-        pack_refs[k][:, width + 2 * share : width + 2 * share + experts] = coded
-        pack_refs[k][:, width + 2 * share + experts :] = low
+            at = pl.multiple_of((to + jnp.bitwise_xor(core, i)) * share, 128)
+            ref[:, width + i * share : width + (i + 1) * share] = moe_ref[:, pl.ds(at, share)]
 
 
 def gates(meta, moe_in, router, ids, d_moe, chips):
@@ -91,7 +88,7 @@
     vm = pl.BlockSpec(memory_space=pltpu.VMEM)
     packed = width + width // chips + 2 * experts
     return pl.pallas_call(
-        gates_kernel,
+        functools.partial(gates_kernel, chips),
         in_specs=[pl.BlockSpec(memory_space=pltpu.SMEM)] + [vm] * 4,
         out_shape=[jax.ShapeDtypeStruct((tok, packed), bf16)] * chips,
         compiler_params=pltpu.CompilerParams(vmem_limit_bytes=vmem_limit),
@@ -102,8 +99,8 @@
 
 def attend_kernel(blocks, meta_ref, q_ref, o_ref, do_ref, gain_ref, *refs):
     kv_refs = refs[:2]
-    dq_ref = refs[-3]
-    part_refs = refs[-2:]
+    dq_ref = refs[-5]
+    part_refs = refs[-4:]
     tok = q_ref.shape[0]
     hd = gain_ref.shape[1]
     heads = q_ref.shape[1] // hd
@@ -155,10 +152,12 @@
             dq_ref[:, h * hd : (h + 1) * hd] = dq_pre[i * tok : (i + 1) * tok, :]
         dk = dk_one if dk is None else dk + dk_one
         dv = dv_one if dv is None else dv + dv_one
-    half = keys // 2
-    for i, ref in enumerate(part_refs):
-        ref[:, :hd] = dk[i * half : (i + 1) * half, :].astype(ref.dtype)
-        ref[:, hd:] = dv[i * half : (i + 1) * half, :].astype(ref.dtype)
+    at = 0
+    for ref in part_refs:
+        size = ref.shape[0]
+        ref[:, :hd] = dk[at : at + size, :].astype(ref.dtype)
+        ref[:, hd:] = dv[at : at + size, :].astype(ref.dtype)
+        at += size
 
 
 def attend(meta, q, o, do, gain, kv_halves, blocks, kv_heads):
@@ -168,6 +167,8 @@
     step = width // kv_heads
     row_spec = pl.BlockSpec((tok, step), lambda g, m: (0, g))
     part_spec = pl.BlockSpec((half, 2 * hd), lambda g, m: (0, g))
+    own = 2 * half // blocks
+    sizes = (own, half - own) * 2
     return pl.pallas_call(
         functools.partial(attend_kernel, blocks),
         grid_spec=pltpu.PrefetchScalarGridSpec(
@@ -176,12 +177,14 @@
             in_specs=[row_spec] * 3
             + [whole((1, hd))]
             + [part_spec] * 2,
-            out_specs=[row_spec, part_spec, part_spec],
+            out_specs=[row_spec] + [pl.BlockSpec((n, 2 * hd), lambda g, m: (0, g)) for n in sizes],
         ),
         out_shape=[
             jax.ShapeDtypeStruct((tok, width), bf16),
-            jax.ShapeDtypeStruct((half, kv_width), f32),
-            jax.ShapeDtypeStruct((half, kv_width), bf16),
+            jax.ShapeDtypeStruct((sizes[0], kv_width), f32),
+            jax.ShapeDtypeStruct((sizes[1], kv_width), f32),
+            jax.ShapeDtypeStruct((sizes[2], kv_width), bf16),
+            jax.ShapeDtypeStruct((sizes[3], kv_width), bf16),
         ],
         compiler_params=pltpu.CompilerParams(vmem_limit_bytes=vmem_limit),
         cost_estimate=takes(10),
@@ -271,13 +274,15 @@
         placed = jnp.where(pick(), terms, 0.0)
         want = lax.broadcasted_iota(jnp.int32, (cap * sp, rows), 0)
         fold = jnp.where(want == lanes_ref[...], 1.0, 0.0)
-        terms_ref[...] = lax.dot_general(
+        folded = lax.dot_general(
             fold,
             placed,
             (((1,), (0,)), ((), ())),
             precision=lax.Precision.HIGHEST,
             preferred_element_type=f32,
         )
+        for to in range(terms_ref.shape[0]):
+            terms_ref[to] = folded
 
 
 def slot_terms(meta, packs, eout, experts, cap, sp):
@@ -303,7 +308,7 @@
             + [d_spec] * 2
             + [g_spec] * 2
             + [e_spec],
-            out_specs=[whole((rows, tokens)), whole((cap * sp, experts))],
+            out_specs=[whole((rows, tokens)), whole((sp, cap * sp, experts))],
             scratch_shapes=[
                 pltpu.VMEM((tokens, col), bf16),
                 pltpu.VMEM((rows, tokens), f32),
@@ -312,7 +317,7 @@
         ),
         out_shape=[
             jax.ShapeDtypeStruct((rows, tokens), bf16),
-            jax.ShapeDtypeStruct((cap * sp, experts), f32),
+            jax.ShapeDtypeStruct((sp, cap * sp, experts), f32),
         ],
         compiler_params=pltpu.CompilerParams(vmem_limit_bytes=vmem_limit),
         cost_estimate=takes(6.2),
@@ -445,18 +450,15 @@
     def exchange(x):
         return lax.ppermute(x, "sp", swap)
 
-    def ahead(x, k):
-        return lax.ppermute(x, "sp", [(i, (i + 2 * k) % sp) for i in range(sp)])
-
-    def back(x, k):
-        return lax.ppermute(x, "sp", [(i, (i - 2 * k) % sp) for i in range(sp)])
+    def to_chip(x, k):
+        return flipped(x, "sp", sp, 2 * k)
 
     def both(mine):
         mine = jnp.concatenate(mine, axis=0)
         return [mine, exchange(mine)]
 
     steps = 2 * jnp.arange(chips, dtype=jnp.int32)
-    owners = jnp.concatenate([lax.rem(me - steps + sp, sp), lax.rem(other - steps + sp, sp)])
+    owners = jnp.concatenate([jnp.bitwise_xor(me, steps), jnp.bitwise_xor(other, steps)])
     qg, kg = q_gain[None, :], k_gain[None, :]
     kv_heads = k_pre.shape[2] // q_gain.shape[0]
     width = moe_in.shape[2]
@@ -469,39 +471,37 @@
     meta = jnp.concatenate([offsets + me * q_pre.shape[1], owners])
 
     kv = pack_keys(k_pre[0], values[0], kg)
-    kv = [kv] + [ahead(kv, k) for k in range(1, chips)]
+    if chips == 4:
+        far = to_chip(kv, 2)
+        kv = [kv, to_chip(kv, 1), far, to_chip(far, 1)]
+    else:
+        kv = [kv] + [to_chip(kv, k) for k in range(1, chips)]
     packs = gates(place, moe_in[0], router, expert_ids[0], d_moe[0], chips)
     kv, packs = together(kv, packs)
 
-    packs = [packs[0]] + [ahead(packs[k], k) for k in range(1, chips)]
-    dq, keep, send = attend(
+    packs = [packs[0]] + [to_chip(packs[k], k) for k in range(1, chips)]
+    dq, own, keep, own_send, send = attend(
         meta, q_pre[0], attn_out[0], d_attn[0], qg, both(kv), sp, kv_heads
     )
-    packs, keep, send = together(packs, keep, send)
+    packs, own, keep, own_send, send = together(packs, own, keep, own_send, send)
 
     rows = k_pre.shape[1]
     arrived = exchange(send)
     sums = [
-        keep[k * rows : (k + 1) * rows] + arrived[k * rows : (k + 1) * rows].astype(f32)
-        for k in range(chips)
+        (keep[k * rows : (k + 1) * rows] + arrived[k * rows : (k + 1) * rows].astype(f32)).astype(bf16)
+        for k in range(chips - 1)
     ]
-    sums = [sums[0]] + [x.astype(bf16) for x in sums[1:]]
-    packs, sums = together(packs, sums)
-
-    sums = [sums[0]] + [back(sums[k], k) for k in range(1, chips)]
+    packs, sums, own_send = together(packs, sums, own_send)
+
+    sums = [to_chip(sums[k - 1], k) for k in range(1, chips)]
+    sums = [own, exchange(own_send)] + sums
     packs = both(packs)
     gated, terms = slot_terms(slot_meta, packs, eout, experts, cap, sp)
-    terms = lax.all_to_all(
-        jnp.broadcast_to(terms[None], (sp,) + terms.shape),
-        "sp",
-        split_axis=0,
-        concat_axis=0,
-        tiled=True,
-    )
+    terms = lax.all_to_all(terms, "sp", split_axis=0, concat_axis=0, tiled=True)
     batch = batch_grad(gated, packs, width)
-    sums, terms, batch = together(sums, terms, batch)
-
     routed = router_grad(slot_meta, packs, terms, width, experts, cap, sp)
+    sums, routed, batch = together(sums, routed, batch)
+
     routed = sent_over("dp", dp, routed)
     dk, dv = finish_keys(k_pre[0], kg, sums)
     batch = jnp.transpose(batch.reshape(experts_here, cap, sp, width), (0, 2, 1, 3))

time: 114 us -> 109 us (0.956)
  local copies, waits for them, and re-layouts: 4.94 us -> 3.57 us
    ppermute x9 -> x0, waiting for transfers between devices: 34.2 us -> none  [the longest x6 27.7 us: ahead(): return lax.ppermute(x, 'sp', [(i, (i + 2 * k) % sp) for i in range(sp)])]
    ppermute x3 -> x12, waiting for transfers between devices: 3.31 us -> 29.2 us  [flipped(): return lax.ppermute(x, axis, [(i, i ^ k) for i in range(size)])]
    ppermute x9 -> x0, starting transfers between devices: 21.5 us -> none  [the longest x6 11.8 us: ahead(): return lax.ppermute(x, 'sp', [(i, (i + 2 * k) % sp) for i in range(sp)])]
    ppermute x3 -> x12, starting transfers between devices: 3.55 us -> 24.5 us  [flipped(): return lax.ppermute(x, axis, [(i, i ^ k) for i in range(size)])]
    all_to_all x1, waiting for transfers between devices: 0.52 us -> 8.07 us  [on_device(): terms = lax.all_to_all(terms, 'sp', split_axis=0, concat_axis=0, tiled=True)]
    broadcast_in_dim x1 -> x0, local copies, waits for them, and re-layouts: 1.35 us -> none  [on_device(): jnp.broadcast_to(terms[None], (sp,) + terms.shape)]
    ppermute x3 -> x4, waiting for transfers between devices: 2.87 us -> 2.5 us  [exchange(): return lax.ppermute(x, 'sp', swap)]
    unnamed x33 -> x39, local copies, waits for them, and re-layouts: 3.54 us -> 3.53 us
  transfers between devices with their start and end apart: 16 -> 17, of which waited for: 9 -> 7; matrix products, arithmetic and copies ran while one was open for 3% -> 2% of each run, Pallas kernels for 23% -> 27%
where the time goes in v4:
time: 109 us
  waiting for transfers between devices  39.8 us (37%)
  Pallas kernels  31.3 us (29%)
  starting transfers between devices  29 us (27%)
  other arithmetic  3.61 us (3%)
  local copies, waits for them, and re-layouts  3.57 us (3%)
  between operations  1.58 us (1%)
    ppermute x12, waiting for transfers between devices, flipped(): return lax.ppermute(x, axis, [(i, i ^ k) for i in range(size)])  29.2 us
    ppermute x12, starting transfers between devices, flipped(): return lax.ppermute(x, axis, [(i, i ^ k) for i in range(size)])  24.5 us
    pallas_call x1, Pallas kernels, attend(): pl.pallas_call(functools.partial(attend_kernel, blocks), grid_spec=pltpu....  10.3 us
    all_to_all x1, waiting for transfers between devices, on_device(): terms = lax.all_to_all(terms, 'sp', split_axis=0, concat_axis=0, tiled=True)  8.07 us
    pallas_call x1, Pallas kernels, slot_terms(): pl.pallas_call(functools.partial(terms_kernel, blocks, sp, cap), grid_spe...  6.33 us
    pallas_call x1, Pallas kernels, batch_grad(): pl.pallas_call(batch_kernel, grid=(width // col,), in_specs=[whole((rows,...  4.68 us
    all_to_all x1, starting transfers between devices, on_device(): terms = lax.all_to_all(terms, 'sp', split_axis=0, concat_axis=0, tiled=True)  4.18 us
    unnamed x39, local copies, waits for them, and re-layouts  3.53 us
  transfers between devices with their start and end apart: 17, of which 7 were waited for; matrix products, arithmetic and copies ran while one was open for 2% of the time, Pallas kernels for 27%

profile of v4, /device:TPU:0, one launch (start us, length us, event | category | flops | bytes accessed | tf_op | source)
XLA Modules:
  0.0 108.9 jit_solution(13507413254880765352)
XLA Ops:
  0.6 0.0 copy-start.6
  0.6 1.8 %pack_keys.1 = bf16[128,1024]{1,0:T(8,128)(2,1)} custom-call(bf16[128,512]{1,0:T(8,128)(2,1)} %bitcast.35, bf16[128,512]{1,0:T(8,128)(2,1)} %bitcast.34, f32[1,128]{1,0:T(1,128)} %bitcast.38), custom_call_target="tpu_custom_call" | custom-call | flops 2070000000 | bytes 6480000 | tf_op jit(solution)/shard_map/pack_keys/pallas_call | solution.py:51
  2.5 4.0 %collective-permute-start.1 = (bf16[128,1024]{1,0:T(8,128)(2,1)}, bf16[128,1024]{1,0:T(8,128)(2,1)S(1)}, u32[]{:S(2)}, u32[]{:S(2)}) collective-permute-start(bf16[128,1024]{1,0:T(8,128)(2,1)} %pack_keys.1), channel_id=1, source_target_pairs={{0,4},{1,5},{2,6},{3,7},{4,0},{5,1},{6,2},{7,3},{8,12},{9,13},{10,... | collective-permute-start | bytes 786440 | tf_op jit(solution)/shard_map/ppermute | solution.py:408
  6.5 1.6 %collective-permute-start = (bf16[128,1024]{1,0:T(8,128)(2,1)}, bf16[128,1024]{1,0:T(8,128)(2,1)S(1)}, u32[]{:S(2)}, u32[]{:S(2)}) collective-permute-start(bf16[128,1024]{1,0:T(8,128)(2,1)} %pack_keys.1), channel_id=1, source_target_pairs={{0,2},{1,3},{2,0},{3,1},{4,6},{5,7},{6,4},{7,5},{8,10},{9,11},{10,... | collective-permute-start | bytes 786440 | tf_op jit(solution)/shard_map/ppermute | solution.py:408
  8.1 0.0 copy-done.6
  8.1 0.7 copy.20
  8.8 0.6 pad_add_fusion.meta_ref
  9.4 9.3 %collective-permute-done.1 = bf16[128,1024]{1,0:T(8,128)(2,1)S(1)} collective-permute-done((bf16[128,1024]{1,0:T(8,128)(2,1)}, bf16[128,1024]{1,0:T(8,128)(2,1)S(1)}, u32[]{:S(2)}, u32[]{:S(2)}) %collective-permute-start.1) | collective-permute-done | bytes 262176 | tf_op jit(solution)/shard_map/ppermute | solution.py:408
  18.8 0.7 collective-permute-start.2
  19.5 2.9 %gates.1 = (bf16[32,5376]{1,0:T(8,128)(2,1)}, bf16[32,5376]{1,0:T(8,128)(2,1)}, bf16[32,5376]{1,0:T(8,128)(2,1)}, bf16[32,5376]{1,0:T(8,128)(2,1)}) custom-call(s32[2]{0:T(128)} %pad_add_fusion.meta_ref, bf16[32,4096]{1,0:T(8,128)(2,1)} %bitcast.32, bf16[4096,128]{1,0:T(8,128)(2,1)} %router_ref.1, s32[32,8]{1,0:T(8,128)} %bitcast.27, bf16[32,4096]{1,0:T(8,128)(2,1)} %bitcast.33), custom_call_target="tpu_custom_call" | custom-call | flops 3220000000 | bytes 10080000 | tf_op jit(solution)/shard_map/gates/pallas_call | solution.py:90
  22.3 0.0 collective-permute-done
  22.3 3.8 %collective-permute-done.2 = bf16[128,1024]{1,0:T(8,128)(2,1)S(1)} collective-permute-done((bf16[128,1024]{1,0:T(8,128)(2,1)S(1)}, bf16[128,1024]{1,0:T(8,128)(2,1)S(1)}, u32[]{:S(2)}, u32[]{:S(2)}) %collective-permute-start.2) | collective-permute-done | bytes 262176 | tf_op jit(solution)/shard_map/ppermute | solution.py:408
  26.2 0.0 copy-done.1
  26.3 0.0 copy-start.5
  26.3 0.1 collective-permute-start.3
  27.1 0.6 add_add_fusion.2
  27.7 1.5 %collective-permute-start.4 = (bf16[32,5376]{1,0:T(8,128)(2,1)}, bf16[32,5376]{1,0:T(8,128)(2,1)S(1)}, u32[]{:S(2)}, u32[]{:S(2)}) collective-permute-start(bf16[32,5376]{1,0:T(8,128)(2,1)} %get-tuple-element.59), channel_id=1, source_target_pairs={{0,2},{1,3},{2,0},{3,1},{4,6},{5,7},{6,4},{7,5},{8,10},{9,11},{10,... | collective-permute-start | bytes 1032200 | tf_op jit(solution)/shard_map/ppermute | solution.py:408
  29.2 0.0 copy-done.10
  29.2 3.3 %collective-permute-start.5 = (bf16[32,5376]{1,0:T(8,128)(2,1)S(1)}, bf16[32,5376]{1,0:T(8,128)(2,1)S(1)}, u32[]{:S(2)}, u32[]{:S(2)}) collective-permute-start(bf16[32,5376]{1,0:T(8,128)(2,1)S(1)} %copy-done.10), channel_id=1, source_target_pairs={{0,4},{1,5},{2,6},{3,7},{4,0},{5,1},{6,2},{7,3},{8,12},{9,13},{10,... | collective-permute-start | bytes 1032200 | tf_op jit(solution)/shard_map/ppermute | solution.py:408
  32.5 0.0 copy-done.9
  32.5 0.0 collective-permute-start.6
  32.5 0.0 collective-permute-done.3.refs_1_
  32.5 0.0 copy-start.8
  32.5 0.0 copy-done.5
  32.5 1.0 copy-done.8
  33.5 10.3 %attend.1 = (bf16[32,8192]{1,0:T(8,128)(2,1)}, f32[128,1024]{1,0:T(8,128)}, f32[384,1024]{1,0:T(8,128)}, bf16[128,1024]{1,0:T(8,128)(2,1)}, bf16[384,1024]{1,0:T(8,128)(2,1)}) custom-call(s32[9]{0:T(128)} %get-tuple-element.97.meta_ref, bf16[32,8192]{1,0:T(8,128)(2,1)} %bitcast.29, bf16[32,8192]{1,0:T(8,128)(2,1)} %bitcast.30, bf16[32,8192]{1,0:T(8,128)(2,1)} %bitcast.31, ...), custom_call_target="tpu_custom_call" | custom-call | flops 11500000256 | bytes 36000000 | tf_op jit(solution)/shard_map/attend/pallas_call | solution.py:172
  43.7 1.7 %collective-permute-done.4 = bf16[32,5376]{1,0:T(8,128)(2,1)S(1)} collective-permute-done((bf16[32,5376]{1,0:T(8,128)(2,1)}, bf16[32,5376]{1,0:T(8,128)(2,1)S(1)}, u32[]{:S(2)}, u32[]{:S(2)}) %collective-permute-start.4) | collective-permute-done | bytes 344096 | tf_op jit(solution)/shard_map/ppermute | solution.py:408
  45.5 10.7 %collective-permute-done.5 = bf16[32,5376]{1,0:T(8,128)(2,1)S(1)} collective-permute-done((bf16[32,5376]{1,0:T(8,128)(2,1)S(1)}, bf16[32,5376]{1,0:T(8,128)(2,1)S(1)}, u32[]{:S(2)}, u32[]{:S(2)}) %collective-permute-start.5) | collective-permute-done | bytes 344096 | tf_op jit(solution)/shard_map/ppermute | solution.py:408
  56.1 0.0 collective-permute-done.6
  56.1 0.0 collective-permute-start.7
  56.1 2.5 %collective-permute-done.7 = bf16[384,1024]{1,0:T(8,128)(2,1)S(1)} collective-permute-done((bf16[384,1024]{1,0:T(8,128)(2,1)}, bf16[384,1024]{1,0:T(8,128)(2,1)S(1)}, u32[]{:S(2)}, u32[]{:S(2)}) %collective-permute-start.7) | collective-permute-done | bytes 786464 | tf_op jit(solution)/shard_map/ppermute | solution.py:451
  58.6 1.6 %add_convert_fusion = (bf16[128,1024]{1,0:T(8,128)(2,1)S(1)}, bf16[128,1024]{1,0:T(8,128)(2,1)S(1)}, bf16[128,1024]{1,0:T(8,128)(2,1)S(1)}) fusion(f32[384,1024]{1,0:T(8,128)} %get-tuple-element.71, bf16[384,1024]{1,0:T(8,128)(2,1)S(1)} %collective-permute-done.7), kind=kLoop, calls=%fused_computation | loop fusion | flops 1179648 | bytes 3145728 | tf_op jit(solution)/shard_map/convert_element_type | solution.py:491
  60.2 0.0 copy-done
  60.3 0.0 copy-start.11
  60.4 0.0 copy-start.4
  60.4 0.2 collective-permute-start.12
  60.6 8.4 %collective-permute-start.10 = (bf16[128,1024]{1,0:T(8,128)(2,1)S(1)}, bf16[128,1024]{1,0:T(8,128)(2,1)S(1)}, u32[]{:S(2)}, u32[]{:S(2)}) collective-permute-start(bf16[128,1024]{1,0:T(8,128)(2,1)S(1)} %get-tuple-element.76), channel_id=1, source_target_pairs={{0,4},{1,5},{2,6},{3,7},{4,0},{5,1},{6,2},{7,3},{8,12},{9,13},{10,... | collective-permute-start | bytes 786440 | tf_op jit(solution)/shard_map/ppermute | solution.py:408
  69.0 1.5 %collective-permute-start.11 = (bf16[128,1024]{1,0:T(8,128)(2,1)S(1)}, bf16[128,1024]{1,0:T(8,128)(2,1)S(1)}, u32[]{:S(2)}, u32[]{:S(2)}) collective-permute-start(bf16[128,1024]{1,0:T(8,128)(2,1)S(1)} %get-tuple-element.77), channel_id=1, source_target_pairs={{0,6},{1,7},{2,4},{3,5},{4,2},{5,3},{6,0},{7,1},{8,14},{9,15},{10,... | collective-permute-start | bytes 786440 | tf_op jit(solution)/shard_map/ppermute | solution.py:408
  70.5 0.0 copy-done.11
  70.5 0.0 collective-permute-start.8
  70.5 0.0 collective-permute-start.9
  70.5 0.0 collective-permute-done.12.refs_1_.refs_3_
  70.5 0.0 copy-start.7
  70.5 1.1 copy-done.7
  71.6 6.3 %slot_terms.1 = (bf16[384,256]{1,0:T(8,128)(2,1)}, f32[8,24,128]{2,1,0:T(8,128)}) custom-call(s32[9]{0:T(128)} %get-tuple-element.96.meta_ref, s32[384,3]{1,0:T(8,128)} %constant.29.clone.table_ref, s32[1,384]{1,0:T(1,128)} %constant.30.clone.lanes_ref, bf16[128,5376]{1,0:T(8,128)(2,1)} %copy-done.4, bf16[128,5376]{1,0:T(8,128)(2,1)} %copy-done.7, ...), custom_call_target="tpu_custom_call" | custom-call | flops 7129999872 | bytes 22320000 | tf_op jit(solution)/shard_map/slot_terms/pallas_call | solution.py:302
  77.9 4.2 %all-to-all-start = ((f32[8,24,128]{2,1,0:T(8,128)}), f32[8,24,128]{2,1,0:T(8,128)S(1)}, u32[]{:S(2)}, u32[]{:S(2)}) async-start(f32[8,24,128]{2,1,0:T(8,128)} %get-tuple-element.82), calls=%async_computation | async-start | bytes 196608 | tf_op jit(solution)/shard_map/all_to_all | solution.py:500
  82.1 4.7 %batch_grad.1 = bf16[384,4096]{1,0:T(8,128)(2,1)} custom-call(bf16[384,256]{1,0:T(8,128)(2,1)} %get-tuple-element.83.gated_ref, bf16[128,5376]{1,0:T(8,128)(2,1)} %copy-done.4, bf16[128,5376]{1,0:T(8,128)(2,1)} %copy-done.7), custom_call_target="tpu_custom_call" | custom-call | flops 5289999872 | bytes 16559999 | tf_op jit(solution)/shard_map/batch_grad/pallas_call | solution.py:340
  86.8 8.1 %all-to-all-done.refs_4_ = f32[8,24,128]{2,1,0:T(8,128)S(1)} async-done(((f32[8,24,128]{2,1,0:T(8,128)}), f32[8,24,128]{2,1,0:T(8,128)S(1)}, u32[]{:S(2)}, u32[]{:S(2)}) %all-to-all-start) | async-done | bytes 98336 | tf_op jit(solution)/shard_map/all_to_all | solution.py:500
  94.8 0.6 copy-done.3
  95.5 3.0 %router_grad.1 = bf16[512,128]{1,0:T(8,128)(2,1)} custom-call(s32[9]{0:T(128)} %get-tuple-element.96.meta_ref, bf16[128,5376]{1,0:T(8,128)(2,1)} %copy-done.4, bf16[128,5376]{1,0:T(8,128)(2,1)} %copy-done.7, bf16[128,5376]{1,0:T(8,128)(2,1)} %copy-done.4, bf16[128,5376]{1,0:T(8,128)(2,1)} %copy-done.7, f32[8,24,128]{2,1,0:T(8,128)} %copy-done.3), custom_call_target="tpu_custom_call" | custom-call | flops 3449999872 | bytes 10800000 | tf_op jit(solution)/shard_map/router_grad/pallas_call | solution.py:391
  98.5 0.0 collective-permute-done.10.refs_3_
  98.5 0.0 collective-permute-done.11.refs_4_
  98.5 0.0 collective-permute-done.8.refs_1_
  98.5 0.0 copy-start.14
  98.5 0.0 collective-permute-done.9.refs_2_
  98.5 1.6 %collective-permute-start.13 = (bf16[512,128]{1,0:T(8,128)(2,1)}, bf16[512,128]{1,0:T(8,128)(2,1)S(1)}, u32[]{:S(2)}, u32[]{:S(2)}) collective-permute-start(bf16[512,128]{1,0:T(8,128)(2,1)} %router_grad.1), channel_id=1, source_target_pairs={{0,8},{8,0},{16,24},{24,16},{1,9},{9,1},{17,25},{25,17},{2,10},{10... | collective-permute-start | bytes 393224 | tf_op jit(solution)/shard_map/ppermute | solution.py:408
  100.1 1.5 %collective-permute-start.14 = (bf16[512,128]{1,0:T(8,128)(2,1)}, bf16[512,128]{1,0:T(8,128)(2,1)S(1)}, u32[]{:S(2)}, u32[]{:S(2)}) collective-permute-start(bf16[512,128]{1,0:T(8,128)(2,1)} %router_grad.1), channel_id=1, source_target_pairs={{0,16},{8,24},{16,0},{24,8},{1,17},{9,25},{17,1},{25,9},{2,18},{10... | collective-permute-start | bytes 393224 | tf_op jit(solution)/shard_map/ppermute | solution.py:408
  101.6 0.5 collective-permute-start.15
  102.1 0.0 copy-done.15
  102.1 2.4 %finish_keys.1 = (bf16[128,512]{1,0:T(8,128)(2,1)}, bf16[128,512]{1,0:T(8,128)(2,1)}) custom-call(bf16[128,512]{1,0:T(8,128)(2,1)} %bitcast.36, f32[1,128]{1,0:T(1,128)} %bitcast.39, f32[128,1024]{1,0:T(8,128)} %get-tuple-element.84.refs_0_, bf16[128,1024]{1,0:T(8,128)(2,1)} %copy-done.14, bf16[128,1024]{1,0:T(8,128)(2,1)} %copy-done.15, ...), custom_call_target="tpu_custom_call" | custom-call | flops 2529999872 | bytes 7920000 | tf_op jit(solution)/shard_map/finish_keys/pallas_call | solution.py:216
  104.5 0.0 collective-permute-done.13
  104.5 3.6 %collective-permute-done.14 = bf16[512,128]{1,0:T(8,128)(2,1)S(1)} collective-permute-done((bf16[512,128]{1,0:T(8,128)(2,1)}, bf16[512,128]{1,0:T(8,128)(2,1)S(1)}, u32[]{:S(2)}, u32[]{:S(2)}) %collective-permute-start.14) | collective-permute-done | bytes 131104 | tf_op jit(solution)/shard_map/ppermute | solution.py:408
  108.1 0.0 collective-permute-done.15
  108.1 0.8 add_add_fusion
  (23 shorter events, 0.2 us)
Async XLA Ops:
  0.6 7.5 %copy-start.6 = (s32[1,32,8]{1,2,0:T(8,128)S(1)}, s32[1,32,8]{1,2,0:T(8,128)}, u32[]{:S(2)}) copy-start(s32[1,32,8]{1,2,0:T(8,128)} %param.25) | copy-start | bytes 3076
  2.5 16.3 %collective-permute-start.1 = (bf16[128,1024]{1,0:T(8,128)(2,1)}, bf16[128,1024]{1,0:T(8,128)(2,1)S(1)}, u32[]{:S(2)}, u32[]{:S(2)}) collective-permute-start(bf16[128,1024]{1,0:T(8,128)(2,1)} %pack_keys.1), channel_id=1, source_target_pairs={{0,4},{1,5},{2,6},{3,7},{4,0},{5,1},{6,2},{7,3},{8,12},{9,13},{10,... | collective-permute-start | bytes 786440 | tf_op jit(solution)/shard_map/ppermute | solution.py:408
  6.5 15.8 %collective-permute-start = (bf16[128,1024]{1,0:T(8,128)(2,1)}, bf16[128,1024]{1,0:T(8,128)(2,1)S(1)}, u32[]{:S(2)}, u32[]{:S(2)}) collective-permute-start(bf16[128,1024]{1,0:T(8,128)(2,1)} %pack_keys.1), channel_id=1, source_target_pairs={{0,2},{1,3},{2,0},{3,1},{4,6},{5,7},{6,4},{7,5},{8,10},{9,11},{10,... | collective-permute-start | bytes 786440 | tf_op jit(solution)/shard_map/ppermute | solution.py:408
  18.8 7.4 %collective-permute-start.2 = (bf16[128,1024]{1,0:T(8,128)(2,1)S(1)}, bf16[128,1024]{1,0:T(8,128)(2,1)S(1)}, u32[]{:S(2)}, u32[]{:S(2)}) collective-permute-start(bf16[128,1024]{1,0:T(8,128)(2,1)S(1)} %collective-permute-done.1), channel_id=1, source_target_pairs={{0,2},{1,3},{2,0},{3,1},{4,6},{5,7},{6,4},{7,5},{8,10},{9,11},{10,... | collective-permute-start | bytes 786440 | tf_op jit(solution)/shard_map/ppermute | solution.py:408
  19.5 6.7 %copy-start.1 = (bf16[128,1024]{1,0:T(8,128)(2,1)S(1)}, bf16[128,1024]{1,0:T(8,128)(2,1)}, u32[]{:S(2)}) copy-start(bf16[128,1024]{1,0:T(8,128)(2,1)} %pack_keys.1) | copy-start | bytes 786436
  22.3 6.9 %copy-start.10 = (bf16[32,5376]{1,0:T(8,128)(2,1)S(1)}, bf16[32,5376]{1,0:T(8,128)(2,1)}, u32[]{:S(2)}) copy-start(bf16[32,5376]{1,0:T(8,128)(2,1)} %get-tuple-element.60) | copy-start | bytes 1032196
  22.3 10.1 %copy-start.9 = (bf16[32,5376]{1,0:T(8,128)(2,1)S(1)}, bf16[32,5376]{1,0:T(8,128)(2,1)}, u32[]{:S(2)}) copy-start(bf16[32,5376]{1,0:T(8,128)(2,1)} %get-tuple-element.61) | copy-start | bytes 1032196
  26.3 6.2 %copy-start.5 = (bf16[512,1024]{1,0:T(8,128)(2,1)}, bf16[512,1024]{1,0:T(8,128)(2,1)S(1)}, u32[]{:S(2)}) copy-start(bf16[512,1024]{1,0:T(8,128)(2,1)S(1)} %constant_dynamic-update-slice_fusion.refs_0_) | copy-start | bytes 3145732
  26.3 6.2 %collective-permute-start.3 = (bf16[512,1024]{1,0:T(8,128)(2,1)S(1)}, bf16[512,1024]{1,0:T(8,128)(2,1)S(1)}, u32[]{:S(2)}, u32[]{:S(2)}) collective-permute-start(bf16[512,1024]{1,0:T(8,128)(2,1)S(1)} %constant_dynamic-update-slice_fusion.refs_0_), channel_id=1, source_target_pairs={{0,1},{1,0},{2,3},{3,2},{4,5},{5,4},{6,7},{7,6},{8,9},{9,8},{10,11... | collective-permute-start | bytes 3145736 | tf_op jit(solution)/shard_map/ppermute | solution.py:451
  27.7 17.8 %collective-permute-start.4 = (bf16[32,5376]{1,0:T(8,128)(2,1)}, bf16[32,5376]{1,0:T(8,128)(2,1)S(1)}, u32[]{:S(2)}, u32[]{:S(2)}) collective-permute-start(bf16[32,5376]{1,0:T(8,128)(2,1)} %get-tuple-element.59), channel_id=1, source_target_pairs={{0,2},{1,3},{2,0},{3,1},{4,6},{5,7},{6,4},{7,5},{8,10},{9,11},{10,... | collective-permute-start | bytes 1032200 | tf_op jit(solution)/shard_map/ppermute | solution.py:408
  29.2 26.9 %collective-permute-start.5 = (bf16[32,5376]{1,0:T(8,128)(2,1)S(1)}, bf16[32,5376]{1,0:T(8,128)(2,1)S(1)}, u32[]{:S(2)}, u32[]{:S(2)}) collective-permute-start(bf16[32,5376]{1,0:T(8,128)(2,1)S(1)} %copy-done.10), channel_id=1, source_target_pairs={{0,4},{1,5},{2,6},{3,7},{4,0},{5,1},{6,2},{7,3},{8,12},{9,13},{10,... | collective-permute-start | bytes 1032200 | tf_op jit(solution)/shard_map/ppermute | solution.py:408
  32.5 23.6 %collective-permute-start.6 = (bf16[32,5376]{1,0:T(8,128)(2,1)S(1)}, bf16[32,5376]{1,0:T(8,128)(2,1)S(1)}, u32[]{:S(2)}, u32[]{:S(2)}) collective-permute-start(bf16[32,5376]{1,0:T(8,128)(2,1)S(1)} %copy-done.9), channel_id=1, source_target_pairs={{0,6},{1,7},{2,4},{3,5},{4,2},{5,3},{6,0},{7,1},{8,14},{9,15},{10,... | collective-permute-start | bytes 1032200 | tf_op jit(solution)/shard_map/ppermute | solution.py:408
  32.5 1.0 copy-start.8
  56.1 4.1 %copy-start = (bf16[32,5376]{1,0:T(8,128)(2,1)S(1)}, bf16[32,5376]{1,0:T(8,128)(2,1)}, u32[]{:S(2)}) copy-start(bf16[32,5376]{1,0:T(8,128)(2,1)} %get-tuple-element.78) | copy-start | bytes 1032196
  56.1 2.5 %collective-permute-start.7 = (bf16[384,1024]{1,0:T(8,128)(2,1)}, bf16[384,1024]{1,0:T(8,128)(2,1)S(1)}, u32[]{:S(2)}, u32[]{:S(2)}) collective-permute-start(bf16[384,1024]{1,0:T(8,128)(2,1)} %get-tuple-element.72), channel_id=1, source_target_pairs={{0,1},{1,0},{2,3},{3,2},{4,5},{5,4},{6,7},{7,6},{8,9},{9,8},{10,11... | collective-permute-start | bytes 2359304 | tf_op jit(solution)/shard_map/ppermute | solution.py:451
  60.3 10.2 %copy-start.11 = (bf16[128,1024]{1,0:T(8,128)(2,1)S(1)}, bf16[128,1024]{1,0:T(8,128)(2,1)}, u32[]{:S(2)}) copy-start(bf16[128,1024]{1,0:T(8,128)(2,1)} %get-tuple-element.74) | copy-start | bytes 786436
  60.4 10.1 %copy-start.4 = (bf16[128,5376]{1,0:T(8,128)(2,1)}, bf16[128,5376]{1,0:T(8,128)(2,1)S(1)}, u32[]{:S(2)}) copy-start(bf16[128,5376]{1,0:T(8,128)(2,1)S(1)} %constant_dynamic-update-slice_fusion.4.refs_0_.refs_2_) | copy-start | bytes 4128772
  60.4 10.1 %collective-permute-start.12 = (bf16[128,5376]{1,0:T(8,128)(2,1)S(1)}, bf16[128,5376]{1,0:T(8,128)(2,1)S(1)}, u32[]{:S(2)}, u32[]{:S(2)}) collective-permute-start(bf16[128,5376]{1,0:T(8,128)(2,1)S(1)} %constant_dynamic-update-slice_fusion.4.refs_0_.refs_2_), channel_id=1, source_target_pairs={{0,1},{1,0},{2,3},{3,2},{4,5},{5,4},{6,7},{7,6},{8,9},{9,8},{10,11... | collective-permute-start | bytes 4128776 | tf_op jit(solution)/shard_map/ppermute | solution.py:451
  60.6 37.9 %collective-permute-start.10 = (bf16[128,1024]{1,0:T(8,128)(2,1)S(1)}, bf16[128,1024]{1,0:T(8,128)(2,1)S(1)}, u32[]{:S(2)}, u32[]{:S(2)}) collective-permute-start(bf16[128,1024]{1,0:T(8,128)(2,1)S(1)} %get-tuple-element.76), channel_id=1, source_target_pairs={{0,4},{1,5},{2,6},{3,7},{4,0},{5,1},{6,2},{7,3},{8,12},{9,13},{10,... | collective-permute-start | bytes 786440 | tf_op jit(solution)/shard_map/ppermute | solution.py:408
  69.0 29.5 %collective-permute-start.11 = (bf16[128,1024]{1,0:T(8,128)(2,1)S(1)}, bf16[128,1024]{1,0:T(8,128)(2,1)S(1)}, u32[]{:S(2)}, u32[]{:S(2)}) collective-permute-start(bf16[128,1024]{1,0:T(8,128)(2,1)S(1)} %get-tuple-element.77), channel_id=1, source_target_pairs={{0,6},{1,7},{2,4},{3,5},{4,2},{5,3},{6,0},{7,1},{8,14},{9,15},{10,... | collective-permute-start | bytes 786440 | tf_op jit(solution)/shard_map/ppermute | solution.py:408
  70.5 28.0 %collective-permute-start.8 = (bf16[128,1024]{1,0:T(8,128)(2,1)S(1)}, bf16[128,1024]{1,0:T(8,128)(2,1)S(1)}, u32[]{:S(2)}, u32[]{:S(2)}) collective-permute-start(bf16[128,1024]{1,0:T(8,128)(2,1)S(1)} %copy-done.11), channel_id=1, source_target_pairs={{0,1},{1,0},{2,3},{3,2},{4,5},{5,4},{6,7},{7,6},{8,9},{9,8},{10,11... | collective-permute-start | bytes 786440 | tf_op jit(solution)/shard_map/ppermute | solution.py:451
  70.5 28.1 %collective-permute-start.9 = (bf16[128,1024]{1,0:T(8,128)(2,1)S(1)}, bf16[128,1024]{1,0:T(8,128)(2,1)S(1)}, u32[]{:S(2)}, u32[]{:S(2)}) collective-permute-start(bf16[128,1024]{1,0:T(8,128)(2,1)S(1)} %get-tuple-element.75), channel_id=1, source_target_pairs={{0,2},{1,3},{2,0},{3,1},{4,6},{5,7},{6,4},{7,5},{8,10},{9,11},{10,... | collective-permute-start | bytes 786440 | tf_op jit(solution)/shard_map/ppermute | solution.py:408
  70.5 1.1 copy-start.7
  77.9 16.9 %all-to-all-start = ((f32[8,24,128]{2,1,0:T(8,128)}), f32[8,24,128]{2,1,0:T(8,128)S(1)}, u32[]{:S(2)}, u32[]{:S(2)}) async-start(f32[8,24,128]{2,1,0:T(8,128)} %get-tuple-element.82), calls=%async_computation | async-start | bytes 196608 | tf_op jit(solution)/shard_map/all_to_all | solution.py:500
  94.8 0.6 copy-start.3
  98.5 9.6 %copy-start.2 = (bf16[512,128]{1,0:T(8,128)(2,1)S(1)}, bf16[512,128]{1,0:T(8,128)(2,1)}, u32[]{:S(2)}) copy-start(bf16[512,128]{1,0:T(8,128)(2,1)} %router_grad.1) | copy-start | bytes 393220
  98.5 3.6 %copy-start.12 = (bf16[128,1024]{1,0:T(8,128)(2,1)}, bf16[128,1024]{1,0:T(8,128)(2,1)S(1)}, u32[]{:S(2)}) copy-start(bf16[128,1024]{1,0:T(8,128)(2,1)S(1)} %collective-permute-done.10.refs_3_) | copy-start | bytes 786436
  98.5 3.6 %copy-start.13 = (bf16[128,1024]{1,0:T(8,128)(2,1)}, bf16[128,1024]{1,0:T(8,128)(2,1)S(1)}, u32[]{:S(2)}) copy-start(bf16[128,1024]{1,0:T(8,128)(2,1)S(1)} %collective-permute-done.11.refs_4_) | copy-start | bytes 786436
  98.5 3.6 %copy-start.14 = (bf16[128,1024]{1,0:T(8,128)(2,1)}, bf16[128,1024]{1,0:T(8,128)(2,1)S(1)}, u32[]{:S(2)}) copy-start(bf16[128,1024]{1,0:T(8,128)(2,1)S(1)} %collective-permute-done.8.refs_1_) | copy-start | bytes 786436
  98.5 3.6 %copy-start.15 = (bf16[128,1024]{1,0:T(8,128)(2,1)}, bf16[128,1024]{1,0:T(8,128)(2,1)S(1)}, u32[]{:S(2)}) copy-start(bf16[128,1024]{1,0:T(8,128)(2,1)S(1)} %collective-permute-done.9.refs_2_) | copy-start | bytes 786436
  98.5 5.9 %collective-permute-start.13 = (bf16[512,128]{1,0:T(8,128)(2,1)}, bf16[512,128]{1,0:T(8,128)(2,1)S(1)}, u32[]{:S(2)}, u32[]{:S(2)}) collective-permute-start(bf16[512,128]{1,0:T(8,128)(2,1)} %router_grad.1), channel_id=1, source_target_pairs={{0,8},{8,0},{16,24},{24,16},{1,9},{9,1},{17,25},{25,17},{2,10},{10... | collective-permute-start | bytes 393224 | tf_op jit(solution)/shard_map/ppermute | solution.py:408
  100.1 8.0 %collective-permute-start.14 = (bf16[512,128]{1,0:T(8,128)(2,1)}, bf16[512,128]{1,0:T(8,128)(2,1)S(1)}, u32[]{:S(2)}, u32[]{:S(2)}) collective-permute-start(bf16[512,128]{1,0:T(8,128)(2,1)} %router_grad.1), channel_id=1, source_target_pairs={{0,16},{8,24},{16,0},{24,8},{1,17},{9,25},{17,1},{25,9},{2,18},{10... | collective-permute-start | bytes 393224 | tf_op jit(solution)/shard_map/ppermute | solution.py:408
  101.6 6.5 %collective-permute-start.15 = (bf16[512,128]{1,0:T(8,128)(2,1)}, bf16[512,128]{1,0:T(8,128)(2,1)S(1)}, u32[]{:S(2)}, u32[]{:S(2)}) collective-permute-start(bf16[512,128]{1,0:T(8,128)(2,1)} %router_grad.1), channel_id=1, source_target_pairs={{0,24},{8,16},{16,8},{24,0},{1,25},{9,17},{17,9},{25,1},{2,26},{10... | collective-permute-start | bytes 393224 | tf_op jit(solution)/shard_map/ppermute | solution.py:408

commit v5 on v4

--- a/solution.py
+++ b/solution.py
@@ -192,34 +192,36 @@
     )(meta, q, o, do, gain, *kv_halves)
 
 
-def finish_kernel(k_ref, gain_ref, *refs):
+def finish_kernel(chips, k_ref, gain_ref, own_ref, other_ref, *refs):
+    first, rest = refs[: chips - 1], refs[chips - 1 : -2]
     dk_ref, dv_ref = refs[-2:]
     hd = gain_ref.shape[1]
     gain = gain_ref[...]
-    total = refs[0][...].astype(f32)
-    for r in refs[1:-2]:
-        total = total + r[...].astype(f32)
+    cut = first[0].shape[1]
     for g in range(k_ref.shape[1] // hd):
+        at = 2 * g * hd
+        total = own_ref[:, at : at + 2 * hd] + other_ref[:, at : at + 2 * hd].astype(f32)
+        parts, start = (first, at) if at < cut else (rest, at - cut)
+        for r in parts:
+            total = total + r[:, start : start + 2 * hd].astype(f32)
         k = k_ref[:, g * hd : (g + 1) * hd].astype(f32)
         inv = lax.rsqrt(jnp.mean(k * k, axis=-1, keepdims=True) + norm_eps)
         unit = k * inv
-        c = total[:, 2 * g * hd : (2 * g + 1) * hd] * gain
+        c = total[:, :hd] * gain
         dk = inv * (c - unit * jnp.mean(c * unit, axis=-1, keepdims=True))
         dk_ref[:, g * hd : (g + 1) * hd] = dk.astype(bf16)
-        dv_ref[:, g * hd : (g + 1) * hd] = total[
-            :, (2 * g + 1) * hd : (2 * g + 2) * hd
-        ].astype(bf16)
-
-
-def finish_keys(k_pre, k_gain, sums):
+        dv_ref[:, g * hd : (g + 1) * hd] = total[:, hd:].astype(bf16)
+
+
+def finish_keys(k_pre, k_gain, own, first, rest):
     out = jax.ShapeDtypeStruct(k_pre.shape, bf16)
     return pl.pallas_call(
-        finish_kernel,
+        functools.partial(finish_kernel, len(first) + 1),
         out_shape=(out, out),
         compiler_params=pltpu.CompilerParams(vmem_limit_bytes=vmem_limit),
         cost_estimate=takes(2.2),
         name="finish_keys",
-    )(k_pre, k_gain, *sums)
+    )(k_pre, k_gain, *own, *first, *rest)
 
 
 def earlier_same_block(rows, block):
@@ -293,7 +295,7 @@
     e, c, s = r // (cap * sp), (r // sp) % cap, r % sp
     table = jnp.asarray(np.stack([e, c, s], axis=1), jnp.int32)
     lanes = jnp.asarray((c * sp + s)[None, :], jnp.int32)
-    col = min(width, 1024)
+    col = min(width, 2048)
     tokens = 2 * half
     gate_at = (packed - 2 * experts) // experts
     d_spec = pl.BlockSpec((half, col), lambda i, m: (0, i))
@@ -336,7 +338,7 @@
 def batch_grad(gated, packs, width):
     rows, tokens = gated.shape
     tok = packs[0].shape[0]
-    col = min(width, 1024)
+    col = min(width, 2048)
     return pl.pallas_call(
         batch_kernel,
         grid=(width // col,),
@@ -491,19 +493,23 @@
         (keep[k * rows : (k + 1) * rows] + arrived[k * rows : (k + 1) * rows].astype(f32)).astype(bf16)
         for k in range(chips - 1)
     ]
-    packs, sums, own_send = together(packs, sums, own_send)
-
-    sums = [to_chip(sums[k - 1], k) for k in range(1, chips)]
-    sums = [own, exchange(own_send)] + sums
+    cut = (kv_heads // 2) * 2 * q_gain.shape[0]
+    first, rest = [x[:, :cut] for x in sums], [x[:, cut:] for x in sums]
+    packs, first, rest, own_send = together(packs, first, rest, own_send)
+
+    own_arrived = exchange(own_send)
+    first = [to_chip(first[k - 1], k) for k in range(1, chips)]
     packs = both(packs)
     gated, terms = slot_terms(slot_meta, packs, eout, experts, cap, sp)
     terms = lax.all_to_all(terms, "sp", split_axis=0, concat_axis=0, tiled=True)
     batch = batch_grad(gated, packs, width)
+    own_arrived, first, rest, terms, batch = together(own_arrived, first, rest, terms, batch)
+
+    rest = [to_chip(rest[k - 1], k) for k in range(1, chips)]
     routed = router_grad(slot_meta, packs, terms, width, experts, cap, sp)
-    sums, routed, batch = together(sums, routed, batch)
-
     routed = sent_over("dp", dp, routed)
-    dk, dv = finish_keys(k_pre[0], kg, sums)
+    dk, dv = finish_keys(k_pre[0], kg, [own, own_arrived], first, rest)
+    dk, dv, routed = together(dk, dv, routed)
     batch = jnp.transpose(batch.reshape(experts_here, cap, sp, width), (0, 2, 1, 3))
     return (dq[None], dk[None], dv[None], batch[None], tree_sum(routed))
 

time: 109 us -> 106 us (0.972)
  waiting for transfers between devices: 39.8 us -> 33.2 us
  starting transfers between devices: 29 us -> 33 us
  Pallas kernels: 31.3 us -> 29.1 us
  local copies, waits for them, and re-layouts: 3.57 us -> 5.19 us
    all_to_all x1, waiting for transfers between devices: 8.07 us -> 2.69 us  [on_device(): terms = lax.all_to_all(terms, 'sp', split_axis=0, concat_axis=0, tiled=True)]
    ppermute x12 -> x15, starting transfers between devices: 24.5 us -> 28.9 us  [flipped(): return lax.ppermute(x, axis, [(i, i ^ k) for i in range(size)])]
    unnamed x39 -> x45, local copies, waits for them, and re-layouts: 3.53 us -> 5.09 us
    ppermute x12 -> x15, waiting for transfers between devices: 29.2 us -> 28 us  [flipped(): return lax.ppermute(x, axis, [(i, i ^ k) for i in range(size)])]
    pallas_call x1, Pallas kernels: 4.68 us -> 3.58 us  [batch_grad(): pl.pallas_call(batch_kernel, grid=(width // col,), in_specs=[whole((rows,...]
  transfers between devices with their start and end apart: 17 -> 20, of which waited for: 7 -> 7; matrix products, arithmetic and copies ran while one was open for 2% -> 2% of each run, Pallas kernels for 27% -> 26%
where the time goes in v5:
time: 106 us
  waiting for transfers between devices  33.2 us (31%)
  starting transfers between devices  33 us (31%)
  Pallas kernels  29.1 us (27%)
  local copies, waits for them, and re-layouts  5.19 us (5%)
  other arithmetic  3.6 us (3%)
  between operations  1.63 us (2%)
    ppermute x15, starting transfers between devices, flipped(): return lax.ppermute(x, axis, [(i, i ^ k) for i in range(size)])  28.9 us
    ppermute x15, waiting for transfers between devices, flipped(): return lax.ppermute(x, axis, [(i, i ^ k) for i in range(size)])  28 us
    pallas_call x1, Pallas kernels, attend(): pl.pallas_call(functools.partial(attend_kernel, blocks), grid_spec=pltpu....  10.2 us
    pallas_call x1, Pallas kernels, slot_terms(): pl.pallas_call(functools.partial(terms_kernel, blocks, sp, cap), grid_spe...  5.27 us
    unnamed x45, local copies, waits for them, and re-layouts  5.09 us
    all_to_all x1, starting transfers between devices, on_device(): terms = lax.all_to_all(terms, 'sp', split_axis=0, concat_axis=0, tiled=True)  3.74 us
    pallas_call x1, Pallas kernels, batch_grad(): pl.pallas_call(batch_kernel, grid=(width // col,), in_specs=[whole((rows,...  3.58 us
    pallas_call x1, Pallas kernels, router_grad(): pl.pallas_call(functools.partial(router_kernel, sp, cap), grid_spec=pltpu...  2.97 us
  transfers between devices with their start and end apart: 20, of which 7 were waited for; matrix products, arithmetic and copies ran while one was open for 2% of the time, Pallas kernels for 26%

profile of v5, /device:TPU:0, one launch (start us, length us, event | category | flops | bytes accessed | tf_op | source)
XLA Modules:
  0.0 105.7 jit_solution(7285194796353216864)
XLA Ops:
  0.6 0.0 copy-start.6
  0.6 1.8 %pack_keys.1 = bf16[128,1024]{1,0:T(8,128)(2,1)} custom-call(bf16[128,512]{1,0:T(8,128)(2,1)} %bitcast.35, bf16[128,512]{1,0:T(8,128)(2,1)} %bitcast.34, f32[1,128]{1,0:T(1,128)} %bitcast.38), custom_call_target="tpu_custom_call" | custom-call | flops 2070000000 | bytes 6480000 | tf_op jit(solution)/shard_map/pack_keys/pallas_call | solution.py:51
  2.5 4.0 %collective-permute-start.1 = (bf16[128,1024]{1,0:T(8,128)(2,1)}, bf16[128,1024]{1,0:T(8,128)(2,1)S(1)}, u32[]{:S(2)}, u32[]{:S(2)}) collective-permute-start(bf16[128,1024]{1,0:T(8,128)(2,1)} %pack_keys.1), channel_id=1, source_target_pairs={{0,4},{1,5},{2,6},{3,7},{4,0},{5,1},{6,2},{7,3},{8,12},{9,13},{10,... | collective-permute-start | bytes 786440 | tf_op jit(solution)/shard_map/ppermute | solution.py:410
  6.5 1.6 %collective-permute-start = (bf16[128,1024]{1,0:T(8,128)(2,1)}, bf16[128,1024]{1,0:T(8,128)(2,1)S(1)}, u32[]{:S(2)}, u32[]{:S(2)}) collective-permute-start(bf16[128,1024]{1,0:T(8,128)(2,1)} %pack_keys.1), channel_id=1, source_target_pairs={{0,2},{1,3},{2,0},{3,1},{4,6},{5,7},{6,4},{7,5},{8,10},{9,11},{10,... | collective-permute-start | bytes 786440 | tf_op jit(solution)/shard_map/ppermute | solution.py:410
  8.1 0.0 copy-done.6
  8.1 0.7 copy.20
  8.8 0.6 pad_add_fusion.meta_ref
  9.4 9.4 %collective-permute-done.1 = bf16[128,1024]{1,0:T(8,128)(2,1)S(1)} collective-permute-done((bf16[128,1024]{1,0:T(8,128)(2,1)}, bf16[128,1024]{1,0:T(8,128)(2,1)S(1)}, u32[]{:S(2)}, u32[]{:S(2)}) %collective-permute-start.1) | collective-permute-done | bytes 262176 | tf_op jit(solution)/shard_map/ppermute | solution.py:410
  18.8 0.7 collective-permute-start.2
  19.5 2.9 %gates.1 = (bf16[32,5376]{1,0:T(8,128)(2,1)}, bf16[32,5376]{1,0:T(8,128)(2,1)}, bf16[32,5376]{1,0:T(8,128)(2,1)}, bf16[32,5376]{1,0:T(8,128)(2,1)}) custom-call(s32[2]{0:T(128)} %pad_add_fusion.meta_ref, bf16[32,4096]{1,0:T(8,128)(2,1)} %bitcast.32, bf16[4096,128]{1,0:T(8,128)(2,1)} %router_ref.1, s32[32,8]{1,0:T(8,128)} %bitcast.27, bf16[32,4096]{1,0:T(8,128)(2,1)} %bitcast.33), custom_call_target="tpu_custom_call" | custom-call | flops 3220000000 | bytes 10080000 | tf_op jit(solution)/shard_map/gates/pallas_call | solution.py:90
  22.3 0.0 collective-permute-done
  22.3 3.8 %collective-permute-done.2 = bf16[128,1024]{1,0:T(8,128)(2,1)S(1)} collective-permute-done((bf16[128,1024]{1,0:T(8,128)(2,1)S(1)}, bf16[128,1024]{1,0:T(8,128)(2,1)S(1)}, u32[]{:S(2)}, u32[]{:S(2)}) %collective-permute-start.2) | collective-permute-done | bytes 262176 | tf_op jit(solution)/shard_map/ppermute | solution.py:410
  26.2 0.0 copy-done.1
  26.3 0.0 copy-start.5
  26.3 0.1 collective-permute-start.3
  27.1 0.6 add_add_fusion.2
  27.7 1.5 %collective-permute-start.4 = (bf16[32,5376]{1,0:T(8,128)(2,1)}, bf16[32,5376]{1,0:T(8,128)(2,1)S(1)}, u32[]{:S(2)}, u32[]{:S(2)}) collective-permute-start(bf16[32,5376]{1,0:T(8,128)(2,1)} %get-tuple-element.70), channel_id=1, source_target_pairs={{0,2},{1,3},{2,0},{3,1},{4,6},{5,7},{6,4},{7,5},{8,10},{9,11},{10,... | collective-permute-start | bytes 1032200 | tf_op jit(solution)/shard_map/ppermute | solution.py:410
  29.2 0.0 copy-done.10
  29.2 3.3 %collective-permute-start.5 = (bf16[32,5376]{1,0:T(8,128)(2,1)S(1)}, bf16[32,5376]{1,0:T(8,128)(2,1)S(1)}, u32[]{:S(2)}, u32[]{:S(2)}) collective-permute-start(bf16[32,5376]{1,0:T(8,128)(2,1)S(1)} %copy-done.10), channel_id=1, source_target_pairs={{0,4},{1,5},{2,6},{3,7},{4,0},{5,1},{6,2},{7,3},{8,12},{9,13},{10,... | collective-permute-start | bytes 1032200 | tf_op jit(solution)/shard_map/ppermute | solution.py:410
  32.5 0.0 copy-done.9
  32.5 0.0 collective-permute-start.6
  32.5 0.0 collective-permute-done.3.refs_1_
  32.5 1.0 copy-done.8
  33.5 10.2 %attend.1 = (bf16[32,8192]{1,0:T(8,128)(2,1)}, f32[128,1024]{1,0:T(8,128)}, f32[384,1024]{1,0:T(8,128)}, bf16[128,1024]{1,0:T(8,128)(2,1)}, bf16[384,1024]{1,0:T(8,128)(2,1)}) custom-call(s32[9]{0:T(128)} %get-tuple-element.125.meta_ref, bf16[32,8192]{1,0:T(8,128)(2,1)} %bitcast.29, bf16[32,8192]{1,0:T(8,128)(2,1)} %bitcast.30, bf16[32,8192]{1,0:T(8,128)(2,1)} %bitcast.31, ...), custom_call_target="tpu_custom_call" | custom-call | flops 11500000256 | bytes 36000000 | tf_op jit(solution)/shard_map/attend/pallas_call | solution.py:172
  43.7 1.7 %collective-permute-done.4 = bf16[32,5376]{1,0:T(8,128)(2,1)S(1)} collective-permute-done((bf16[32,5376]{1,0:T(8,128)(2,1)}, bf16[32,5376]{1,0:T(8,128)(2,1)S(1)}, u32[]{:S(2)}, u32[]{:S(2)}) %collective-permute-start.4) | collective-permute-done | bytes 344096 | tf_op jit(solution)/shard_map/ppermute | solution.py:410
  45.5 10.7 %collective-permute-done.5 = bf16[32,5376]{1,0:T(8,128)(2,1)S(1)} collective-permute-done((bf16[32,5376]{1,0:T(8,128)(2,1)S(1)}, bf16[32,5376]{1,0:T(8,128)(2,1)S(1)}, u32[]{:S(2)}, u32[]{:S(2)}) %collective-permute-start.5) | collective-permute-done | bytes 344096 | tf_op jit(solution)/shard_map/ppermute | solution.py:410
  56.1 0.0 collective-permute-done.6
  56.1 0.0 collective-permute-start.7
  56.1 2.5 %collective-permute-done.7 = bf16[384,1024]{1,0:T(8,128)(2,1)S(1)} collective-permute-done((bf16[384,1024]{1,0:T(8,128)(2,1)}, bf16[384,1024]{1,0:T(8,128)(2,1)S(1)}, u32[]{:S(2)}, u32[]{:S(2)}) %collective-permute-start.7) | collective-permute-done | bytes 786464 | tf_op jit(solution)/shard_map/ppermute | solution.py:453
  58.6 1.6 %add_convert_fusion = (bf16[128,1024]{1,0:T(8,128)(2,1)S(1)}, bf16[128,1024]{1,0:T(8,128)(2,1)S(1)}, bf16[128,1024]{1,0:T(8,128)(2,1)S(1)}) fusion(f32[384,1024]{1,0:T(8,128)} %get-tuple-element.82, bf16[384,1024]{1,0:T(8,128)(2,1)S(1)} %collective-permute-done.7), kind=kLoop, calls=%fused_computation | loop fusion | flops 1179648 | bytes 3145728 | tf_op jit(solution)/shard_map/convert_element_type | solution.py:493
  60.4 0.9 copy-done
  61.4 0.2 collective-permute-start.12
  61.6 7.5 %collective-permute-start.9 = (bf16[128,512]{1,0:T(8,128)(2,1)S(1)}, bf16[128,512]{1,0:T(8,128)(2,1)S(1)}, u32[]{:S(2)}, u32[]{:S(2)}) collective-permute-start(bf16[128,512]{1,0:T(8,128)(2,1)S(1)} %get-tuple-element.86), channel_id=1, source_target_pairs={{0,2},{1,3},{2,0},{3,1},{4,6},{5,7},{6,4},{7,5},{8,10},{9,11},{10,... | collective-permute-start | bytes 393224 | tf_op jit(solution)/shard_map/ppermute | solution.py:410
  69.1 0.9 collective-permute-start.10
  70.0 1.5 %collective-permute-start.11 = (bf16[128,512]{1,0:T(8,128)(2,1)S(1)}, bf16[128,512]{1,0:T(8,128)(2,1)S(1)}, u32[]{:S(2)}, u32[]{:S(2)}) collective-permute-start(bf16[128,512]{1,0:T(8,128)(2,1)S(1)} %get-tuple-element.88), channel_id=1, source_target_pairs={{0,6},{1,7},{2,4},{3,5},{4,2},{5,3},{6,0},{7,1},{8,14},{9,15},{10,... | collective-permute-start | bytes 393224 | tf_op jit(solution)/shard_map/ppermute | solution.py:410
  71.5 0.0 collective-permute-start.8
  71.5 0.0 collective-permute-done.12.refs_1_.refs_3_
  71.5 1.1 %copy-done.7 = bf16[128,5376]{1,0:T(8,128)(2,1)} copy-done((bf16[128,5376]{1,0:T(8,128)(2,1)}, bf16[128,5376]{1,0:T(8,128)(2,1)S(1)}, u32[]{:S(2)}) %copy-start.7) | copy-done | bytes 1376280
  72.5 5.3 %slot_terms.1 = (bf16[384,256]{1,0:T(8,128)(2,1)}, f32[8,24,128]{2,1,0:T(8,128)}) custom-call(s32[9]{0:T(128)} %get-tuple-element.124.meta_ref, s32[384,3]{1,0:T(8,128)} %constant.29.clone.table_ref, s32[1,384]{1,0:T(1,128)} %constant.30.clone.lanes_ref, bf16[128,5376]{1,0:T(8,128)(2,1)} %copy-done.4, bf16[128,5376]{1,0:T(8,128)(2,1)} %copy-done.7, ...), custom_call_target="tpu_custom_call" | custom-call | flops 7129999872 | bytes 22320000 | tf_op jit(solution)/shard_map/slot_terms/pallas_call | solution.py:304
  77.8 3.7 %all-to-all-start = ((f32[8,24,128]{2,1,0:T(8,128)}), f32[8,24,128]{2,1,0:T(8,128)S(1)}, u32[]{:S(2)}, u32[]{:S(2)}) async-start(f32[8,24,128]{2,1,0:T(8,128)} %get-tuple-element.96), calls=%async_computation | async-start | bytes 196608 | tf_op jit(solution)/shard_map/all_to_all | solution.py:504
  81.6 3.6 %batch_grad.1 = bf16[384,4096]{1,0:T(8,128)(2,1)} custom-call(bf16[384,256]{1,0:T(8,128)(2,1)} %get-tuple-element.97.gated_ref, bf16[128,5376]{1,0:T(8,128)(2,1)} %copy-done.4, bf16[128,5376]{1,0:T(8,128)(2,1)} %copy-done.7), custom_call_target="tpu_custom_call" | custom-call | flops 5289999872 | bytes 16559999 | tf_op jit(solution)/shard_map/batch_grad/pallas_call | solution.py:342
  85.1 0.0 collective-permute-done.9.refs_0_
  85.2 0.0 collective-permute-done.10.refs_1_
  85.2 0.0 collective-permute-done.11.refs_2_
  85.2 0.0 collective-permute-done.8.other_ref
  85.2 0.0 copy-start.12
  85.2 2.7 %all-to-all-done.refs_4_ = f32[8,24,128]{2,1,0:T(8,128)S(1)} async-done(((f32[8,24,128]{2,1,0:T(8,128)}), f32[8,24,128]{2,1,0:T(8,128)S(1)}, u32[]{:S(2)}, u32[]{:S(2)}) %all-to-all-start) | async-done | bytes 98336 | tf_op jit(solution)/shard_map/all_to_all | solution.py:504
  87.9 0.8 collective-permute-start.13
  88.7 0.9 collective-permute-start.14
  89.7 2.6 %collective-permute-start.15 = (bf16[128,512]{1,0:T(8,128)(2,1)S(1)}, bf16[128,512]{1,0:T(8,128)(2,1)S(1)}, u32[]{:S(2)}, u32[]{:S(2)}) collective-permute-start(bf16[128,512]{1,0:T(8,128)(2,1)S(1)} %get-tuple-element.104), channel_id=1, source_target_pairs={{0,6},{1,7},{2,4},{3,5},{4,2},{5,3},{6,0},{7,1},{8,14},{9,15},{10,... | collective-permute-start | bytes 393224 | tf_op jit(solution)/shard_map/ppermute | solution.py:410
  92.3 3.0 %router_grad.1 = bf16[512,128]{1,0:T(8,128)(2,1)} custom-call(s32[9]{0:T(128)} %get-tuple-element.124.meta_ref, bf16[128,5376]{1,0:T(8,128)(2,1)} %copy-done.4, bf16[128,5376]{1,0:T(8,128)(2,1)} %copy-done.7, bf16[128,5376]{1,0:T(8,128)(2,1)} %copy-done.4, bf16[128,5376]{1,0:T(8,128)(2,1)} %copy-done.7, f32[8,24,128]{2,1,0:T(8,128)} %copy-done.3), custom_call_target="tpu_custom_call" | custom-call | flops 3449999872 | bytes 10800000 | tf_op jit(solution)/shard_map/router_grad/pallas_call | solution.py:393
  95.3 2.5 %collective-permute-start.18 = (bf16[512,128]{1,0:T(8,128)(2,1)}, bf16[512,128]{1,0:T(8,128)(2,1)S(1)}, u32[]{:S(2)}, u32[]{:S(2)}) collective-permute-start(bf16[512,128]{1,0:T(8,128)(2,1)} %router_grad.1), channel_id=1, source_target_pairs={{0,24},{8,16},{16,8},{24,0},{1,25},{9,17},{17,9},{25,1},{2,26},{10... | collective-permute-start | bytes 393224 | tf_op jit(solution)/shard_map/ppermute | solution.py:410
  97.8 0.5 collective-permute-start.17
  98.3 0.0 collective-permute-done.13.refs_3_
  98.3 0.5 collective-permute-start.16
  98.9 2.4 %collective-permute-done.14.refs_4_ = bf16[128,512]{1,0:T(8,128)(2,1)S(1)} collective-permute-done((bf16[128,512]{1,0:T(8,128)(2,1)S(1)}, bf16[128,512]{1,0:T(8,128)(2,1)S(1)}, u32[]{:S(2)}, u32[]{:S(2)}) %collective-permute-start.14) | collective-permute-done | bytes 131104 | tf_op jit(solution)/shard_map/ppermute | solution.py:410
  101.2 0.0 collective-permute-done.15.refs_5_
  101.2 0.6 copy-done.17
  101.9 0.6 copy-done.18
  102.5 2.4 %finish_keys.1 = (bf16[128,512]{1,0:T(8,128)(2,1)}, bf16[128,512]{1,0:T(8,128)(2,1)}) custom-call(bf16[128,512]{1,0:T(8,128)(2,1)} %bitcast.36, f32[1,128]{1,0:T(1,128)} %bitcast.39, f32[128,1024]{1,0:T(8,128)} %get-tuple-element.77.own_ref, bf16[128,1024]{1,0:T(8,128)(2,1)} %copy-done.12, bf16[128,512]{1,0:T(8,128)(2,1)} %copy-done.13, ...), custom_call_target="tpu_custom_call" | custom-call | flops 2529999872 | bytes 7920000 | tf_op jit(solution)/shard_map/finish_keys/pallas_call | solution.py:218
  104.9 0.0 collective-permute-done.18
  104.9 0.0 collective-permute-done.17
  104.9 0.0 collective-permute-done.16
  104.9 0.8 add_add_fusion
  (38 shorter events, 0.3 us)
Async XLA Ops:
  0.6 7.5 %copy-start.6 = (s32[1,32,8]{1,2,0:T(8,128)S(1)}, s32[1,32,8]{1,2,0:T(8,128)}, u32[]{:S(2)}) copy-start(s32[1,32,8]{1,2,0:T(8,128)} %param.25) | copy-start | bytes 3076
  2.5 16.3 %collective-permute-start.1 = (bf16[128,1024]{1,0:T(8,128)(2,1)}, bf16[128,1024]{1,0:T(8,128)(2,1)S(1)}, u32[]{:S(2)}, u32[]{:S(2)}) collective-permute-start(bf16[128,1024]{1,0:T(8,128)(2,1)} %pack_keys.1), channel_id=1, source_target_pairs={{0,4},{1,5},{2,6},{3,7},{4,0},{5,1},{6,2},{7,3},{8,12},{9,13},{10,... | collective-permute-start | bytes 786440 | tf_op jit(solution)/shard_map/ppermute | solution.py:410
  6.5 15.8 %collective-permute-start = (bf16[128,1024]{1,0:T(8,128)(2,1)}, bf16[128,1024]{1,0:T(8,128)(2,1)S(1)}, u32[]{:S(2)}, u32[]{:S(2)}) collective-permute-start(bf16[128,1024]{1,0:T(8,128)(2,1)} %pack_keys.1), channel_id=1, source_target_pairs={{0,2},{1,3},{2,0},{3,1},{4,6},{5,7},{6,4},{7,5},{8,10},{9,11},{10,... | collective-permute-start | bytes 786440 | tf_op jit(solution)/shard_map/ppermute | solution.py:410
  18.8 7.4 %collective-permute-start.2 = (bf16[128,1024]{1,0:T(8,128)(2,1)S(1)}, bf16[128,1024]{1,0:T(8,128)(2,1)S(1)}, u32[]{:S(2)}, u32[]{:S(2)}) collective-permute-start(bf16[128,1024]{1,0:T(8,128)(2,1)S(1)} %collective-permute-done.1), channel_id=1, source_target_pairs={{0,2},{1,3},{2,0},{3,1},{4,6},{5,7},{6,4},{7,5},{8,10},{9,11},{10,... | collective-permute-start | bytes 786440 | tf_op jit(solution)/shard_map/ppermute | solution.py:410
  19.5 6.7 %copy-start.1 = (bf16[128,1024]{1,0:T(8,128)(2,1)S(1)}, bf16[128,1024]{1,0:T(8,128)(2,1)}, u32[]{:S(2)}) copy-start(bf16[128,1024]{1,0:T(8,128)(2,1)} %pack_keys.1) | copy-start | bytes 786436
  22.3 6.9 %copy-start.10 = (bf16[32,5376]{1,0:T(8,128)(2,1)S(1)}, bf16[32,5376]{1,0:T(8,128)(2,1)}, u32[]{:S(2)}) copy-start(bf16[32,5376]{1,0:T(8,128)(2,1)} %get-tuple-element.71) | copy-start | bytes 1032196
  22.3 10.1 %copy-start.9 = (bf16[32,5376]{1,0:T(8,128)(2,1)S(1)}, bf16[32,5376]{1,0:T(8,128)(2,1)}, u32[]{:S(2)}) copy-start(bf16[32,5376]{1,0:T(8,128)(2,1)} %get-tuple-element.72) | copy-start | bytes 1032196
  26.3 6.2 %copy-start.5 = (bf16[512,1024]{1,0:T(8,128)(2,1)}, bf16[512,1024]{1,0:T(8,128)(2,1)S(1)}, u32[]{:S(2)}) copy-start(bf16[512,1024]{1,0:T(8,128)(2,1)S(1)} %constant_dynamic-update-slice_fusion.refs_0_) | copy-start | bytes 3145732
  26.3 6.2 %collective-permute-start.3 = (bf16[512,1024]{1,0:T(8,128)(2,1)S(1)}, bf16[512,1024]{1,0:T(8,128)(2,1)S(1)}, u32[]{:S(2)}, u32[]{:S(2)}) collective-permute-start(bf16[512,1024]{1,0:T(8,128)(2,1)S(1)} %constant_dynamic-update-slice_fusion.refs_0_), channel_id=1, source_target_pairs={{0,1},{1,0},{2,3},{3,2},{4,5},{5,4},{6,7},{7,6},{8,9},{9,8},{10,11... | collective-permute-start | bytes 3145736 | tf_op jit(solution)/shard_map/ppermute | solution.py:453
  27.7 17.8 %collective-permute-start.4 = (bf16[32,5376]{1,0:T(8,128)(2,1)}, bf16[32,5376]{1,0:T(8,128)(2,1)S(1)}, u32[]{:S(2)}, u32[]{:S(2)}) collective-permute-start(bf16[32,5376]{1,0:T(8,128)(2,1)} %get-tuple-element.70), channel_id=1, source_target_pairs={{0,2},{1,3},{2,0},{3,1},{4,6},{5,7},{6,4},{7,5},{8,10},{9,11},{10,... | collective-permute-start | bytes 1032200 | tf_op jit(solution)/shard_map/ppermute | solution.py:410
  29.2 26.9 %collective-permute-start.5 = (bf16[32,5376]{1,0:T(8,128)(2,1)S(1)}, bf16[32,5376]{1,0:T(8,128)(2,1)S(1)}, u32[]{:S(2)}, u32[]{:S(2)}) collective-permute-start(bf16[32,5376]{1,0:T(8,128)(2,1)S(1)} %copy-done.10), channel_id=1, source_target_pairs={{0,4},{1,5},{2,6},{3,7},{4,0},{5,1},{6,2},{7,3},{8,12},{9,13},{10,... | collective-permute-start | bytes 1032200 | tf_op jit(solution)/shard_map/ppermute | solution.py:410
  32.5 23.6 %collective-permute-start.6 = (bf16[32,5376]{1,0:T(8,128)(2,1)S(1)}, bf16[32,5376]{1,0:T(8,128)(2,1)S(1)}, u32[]{:S(2)}, u32[]{:S(2)}) collective-permute-start(bf16[32,5376]{1,0:T(8,128)(2,1)S(1)} %copy-done.9), channel_id=1, source_target_pairs={{0,6},{1,7},{2,4},{3,5},{4,2},{5,3},{6,0},{7,1},{8,14},{9,15},{10,... | collective-permute-start | bytes 1032200 | tf_op jit(solution)/shard_map/ppermute | solution.py:410
  32.5 1.0 copy-start.8
  56.1 2.5 %collective-permute-start.7 = (bf16[384,1024]{1,0:T(8,128)(2,1)}, bf16[384,1024]{1,0:T(8,128)(2,1)S(1)}, u32[]{:S(2)}, u32[]{:S(2)}) collective-permute-start(bf16[384,1024]{1,0:T(8,128)(2,1)} %get-tuple-element.83), channel_id=1, source_target_pairs={{0,1},{1,0},{2,3},{3,2},{4,5},{5,4},{6,7},{7,6},{8,9},{9,8},{10,11... | collective-permute-start | bytes 2359304 | tf_op jit(solution)/shard_map/ppermute | solution.py:453
  60.3 1.0 copy-start
  61.2 10.2 %copy-start.11 = (bf16[128,1024]{1,0:T(8,128)(2,1)S(1)}, bf16[128,1024]{1,0:T(8,128)(2,1)}, u32[]{:S(2)}) copy-start(bf16[128,1024]{1,0:T(8,128)(2,1)} %get-tuple-element.85) | copy-start | bytes 786436
  61.4 10.1 %copy-start.4 = (bf16[128,5376]{1,0:T(8,128)(2,1)}, bf16[128,5376]{1,0:T(8,128)(2,1)S(1)}, u32[]{:S(2)}) copy-start(bf16[128,5376]{1,0:T(8,128)(2,1)S(1)} %constant_dynamic-update-slice_fusion.4.refs_0_.refs_2_) | copy-start | bytes 4128772
  61.4 10.1 %collective-permute-start.12 = (bf16[128,5376]{1,0:T(8,128)(2,1)S(1)}, bf16[128,5376]{1,0:T(8,128)(2,1)S(1)}, u32[]{:S(2)}, u32[]{:S(2)}) collective-permute-start(bf16[128,5376]{1,0:T(8,128)(2,1)S(1)} %constant_dynamic-update-slice_fusion.4.refs_0_.refs_2_), channel_id=1, source_target_pairs={{0,1},{1,0},{2,3},{3,2},{4,5},{5,4},{6,7},{7,6},{8,9},{9,8},{10,11... | collective-permute-start | bytes 4128776 | tf_op jit(solution)/shard_map/ppermute | solution.py:453
  61.6 23.6 %collective-permute-start.9 = (bf16[128,512]{1,0:T(8,128)(2,1)S(1)}, bf16[128,512]{1,0:T(8,128)(2,1)S(1)}, u32[]{:S(2)}, u32[]{:S(2)}) collective-permute-start(bf16[128,512]{1,0:T(8,128)(2,1)S(1)} %get-tuple-element.86), channel_id=1, source_target_pairs={{0,2},{1,3},{2,0},{3,1},{4,6},{5,7},{6,4},{7,5},{8,10},{9,11},{10,... | collective-permute-start | bytes 393224 | tf_op jit(solution)/shard_map/ppermute | solution.py:410
  69.1 16.1 %collective-permute-start.10 = (bf16[128,512]{1,0:T(8,128)(2,1)S(1)}, bf16[128,512]{1,0:T(8,128)(2,1)S(1)}, u32[]{:S(2)}, u32[]{:S(2)}) collective-permute-start(bf16[128,512]{1,0:T(8,128)(2,1)S(1)} %get-tuple-element.87), channel_id=1, source_target_pairs={{0,4},{1,5},{2,6},{3,7},{4,0},{5,1},{6,2},{7,3},{8,12},{9,13},{10,... | collective-permute-start | bytes 393224 | tf_op jit(solution)/shard_map/ppermute | solution.py:410
  70.0 15.2 %collective-permute-start.11 = (bf16[128,512]{1,0:T(8,128)(2,1)S(1)}, bf16[128,512]{1,0:T(8,128)(2,1)S(1)}, u32[]{:S(2)}, u32[]{:S(2)}) collective-permute-start(bf16[128,512]{1,0:T(8,128)(2,1)S(1)} %get-tuple-element.88), channel_id=1, source_target_pairs={{0,6},{1,7},{2,4},{3,5},{4,2},{5,3},{6,0},{7,1},{8,14},{9,15},{10,... | collective-permute-start | bytes 393224 | tf_op jit(solution)/shard_map/ppermute | solution.py:410
  71.5 13.7 %collective-permute-start.8 = (bf16[128,1024]{1,0:T(8,128)(2,1)S(1)}, bf16[128,1024]{1,0:T(8,128)(2,1)S(1)}, u32[]{:S(2)}, u32[]{:S(2)}) collective-permute-start(bf16[128,1024]{1,0:T(8,128)(2,1)S(1)} %copy-done.11), channel_id=1, source_target_pairs={{0,1},{1,0},{2,3},{3,2},{4,5},{5,4},{6,7},{7,6},{8,9},{9,8},{10,11... | collective-permute-start | bytes 786440 | tf_op jit(solution)/shard_map/ppermute | solution.py:453
  71.5 1.1 %copy-start.7 = (bf16[128,5376]{1,0:T(8,128)(2,1)}, bf16[128,5376]{1,0:T(8,128)(2,1)S(1)}, u32[]{:S(2)}) copy-start(bf16[128,5376]{1,0:T(8,128)(2,1)S(1)} %collective-permute-done.12.refs_1_.refs_3_) | copy-start | bytes 4128772
  77.8 10.1 %all-to-all-start = ((f32[8,24,128]{2,1,0:T(8,128)}), f32[8,24,128]{2,1,0:T(8,128)S(1)}, u32[]{:S(2)}, u32[]{:S(2)}) async-start(f32[8,24,128]{2,1,0:T(8,128)} %get-tuple-element.96), calls=%async_computation | async-start | bytes 196608 | tf_op jit(solution)/shard_map/all_to_all | solution.py:504
  85.1 10.1 %copy-start.13 = (bf16[128,512]{1,0:T(8,128)(2,1)}, bf16[128,512]{1,0:T(8,128)(2,1)S(1)}, u32[]{:S(2)}) copy-start(bf16[128,512]{1,0:T(8,128)(2,1)S(1)} %collective-permute-done.9.refs_0_) | copy-start | bytes 393220
  85.2 10.1 %copy-start.14 = (bf16[128,512]{1,0:T(8,128)(2,1)}, bf16[128,512]{1,0:T(8,128)(2,1)S(1)}, u32[]{:S(2)}) copy-start(bf16[128,512]{1,0:T(8,128)(2,1)S(1)} %collective-permute-done.10.refs_1_) | copy-start | bytes 393220
  85.2 10.1 %copy-start.15 = (bf16[128,512]{1,0:T(8,128)(2,1)}, bf16[128,512]{1,0:T(8,128)(2,1)S(1)}, u32[]{:S(2)}) copy-start(bf16[128,512]{1,0:T(8,128)(2,1)S(1)} %collective-permute-done.11.refs_2_) | copy-start | bytes 393220
  85.2 10.1 %copy-start.12 = (bf16[128,1024]{1,0:T(8,128)(2,1)}, bf16[128,1024]{1,0:T(8,128)(2,1)S(1)}, u32[]{:S(2)}) copy-start(bf16[128,1024]{1,0:T(8,128)(2,1)S(1)} %collective-permute-done.8.other_ref) | copy-start | bytes 786436
  87.9 4.4 %copy-start.3 = (f32[8,24,128]{2,1,0:T(8,128)}, f32[8,24,128]{2,1,0:T(8,128)S(1)}, u32[]{:S(2)}) copy-start(f32[8,24,128]{2,1,0:T(8,128)S(1)} %all-to-all-done.refs_4_) | copy-start | bytes 294916
  87.9 10.4 %collective-permute-start.13 = (bf16[128,512]{1,0:T(8,128)(2,1)S(1)}, bf16[128,512]{1,0:T(8,128)(2,1)S(1)}, u32[]{:S(2)}, u32[]{:S(2)}) collective-permute-start(bf16[128,512]{1,0:T(8,128)(2,1)S(1)} %get-tuple-element.102), channel_id=1, source_target_pairs={{0,2},{1,3},{2,0},{3,1},{4,6},{5,7},{6,4},{7,5},{8,10},{9,11},{10,... | collective-permute-start | bytes 393224 | tf_op jit(solution)/shard_map/ppermute | solution.py:410
  88.7 12.5 %collective-permute-start.14 = (bf16[128,512]{1,0:T(8,128)(2,1)S(1)}, bf16[128,512]{1,0:T(8,128)(2,1)S(1)}, u32[]{:S(2)}, u32[]{:S(2)}) collective-permute-start(bf16[128,512]{1,0:T(8,128)(2,1)S(1)} %get-tuple-element.103), channel_id=1, source_target_pairs={{0,4},{1,5},{2,6},{3,7},{4,0},{5,1},{6,2},{7,3},{8,12},{9,13},{10,... | collective-permute-start | bytes 393224 | tf_op jit(solution)/shard_map/ppermute | solution.py:410
  89.7 11.5 %collective-permute-start.15 = (bf16[128,512]{1,0:T(8,128)(2,1)S(1)}, bf16[128,512]{1,0:T(8,128)(2,1)S(1)}, u32[]{:S(2)}, u32[]{:S(2)}) collective-permute-start(bf16[128,512]{1,0:T(8,128)(2,1)S(1)} %get-tuple-element.104), channel_id=1, source_target_pairs={{0,6},{1,7},{2,4},{3,5},{4,2},{5,3},{6,0},{7,1},{8,14},{9,15},{10,... | collective-permute-start | bytes 393224 | tf_op jit(solution)/shard_map/ppermute | solution.py:410
  95.3 9.6 %copy-start.2 = (bf16[512,128]{1,0:T(8,128)(2,1)S(1)}, bf16[512,128]{1,0:T(8,128)(2,1)}, u32[]{:S(2)}) copy-start(bf16[512,128]{1,0:T(8,128)(2,1)} %router_grad.1) | copy-start | bytes 393220
  95.3 9.6 %collective-permute-start.18 = (bf16[512,128]{1,0:T(8,128)(2,1)}, bf16[512,128]{1,0:T(8,128)(2,1)S(1)}, u32[]{:S(2)}, u32[]{:S(2)}) collective-permute-start(bf16[512,128]{1,0:T(8,128)(2,1)} %router_grad.1), channel_id=1, source_target_pairs={{0,24},{8,16},{16,8},{24,0},{1,25},{9,17},{17,9},{25,1},{2,26},{10... | collective-permute-start | bytes 393224 | tf_op jit(solution)/shard_map/ppermute | solution.py:410
  97.8 7.1 %collective-permute-start.17 = (bf16[512,128]{1,0:T(8,128)(2,1)}, bf16[512,128]{1,0:T(8,128)(2,1)S(1)}, u32[]{:S(2)}, u32[]{:S(2)}) collective-permute-start(bf16[512,128]{1,0:T(8,128)(2,1)} %router_grad.1), channel_id=1, source_target_pairs={{0,16},{8,24},{16,0},{24,8},{1,17},{9,25},{17,1},{25,9},{2,18},{10... | collective-permute-start | bytes 393224 | tf_op jit(solution)/shard_map/ppermute | solution.py:410
  98.3 2.9 %copy-start.16 = (bf16[128,512]{1,0:T(8,128)(2,1)}, bf16[128,512]{1,0:T(8,128)(2,1)S(1)}, u32[]{:S(2)}) copy-start(bf16[128,512]{1,0:T(8,128)(2,1)S(1)} %collective-permute-done.13.refs_3_) | copy-start | bytes 393220
  98.3 6.6 %collective-permute-start.16 = (bf16[512,128]{1,0:T(8,128)(2,1)}, bf16[512,128]{1,0:T(8,128)(2,1)S(1)}, u32[]{:S(2)}, u32[]{:S(2)}) collective-permute-start(bf16[512,128]{1,0:T(8,128)(2,1)} %router_grad.1), channel_id=1, source_target_pairs={{0,8},{8,0},{16,24},{24,16},{1,9},{9,1},{17,25},{25,17},{2,10},{10... | collective-permute-start | bytes 393224 | tf_op jit(solution)/shard_map/ppermute | solution.py:410
  101.2 0.7 copy-start.17
  101.9 0.6 copy-start.18

commit v6 on v5

--- a/solution.py
+++ b/solution.py
@@ -12,7 +12,7 @@
 norm_eps = 1e-06
 f32 = jnp.float32
 bf16 = jnp.bfloat16
-vmem_limit = 56 * 1024 * 1024
+mib = 1024 * 1024
 
 
 def takes(us):
@@ -91,7 +91,7 @@
         functools.partial(gates_kernel, chips),
         in_specs=[pl.BlockSpec(memory_space=pltpu.SMEM)] + [vm] * 4,
         out_shape=[jax.ShapeDtypeStruct((tok, packed), bf16)] * chips,
-        compiler_params=pltpu.CompilerParams(vmem_limit_bytes=vmem_limit),
+        compiler_params=pltpu.CompilerParams(vmem_limit_bytes=8 * mib),
         cost_estimate=takes(2.8),
         name="gates",
     )(meta, moe_in, router, ids, d_moe)
@@ -186,10 +186,35 @@
             jax.ShapeDtypeStruct((sizes[2], kv_width), bf16),
             jax.ShapeDtypeStruct((sizes[3], kv_width), bf16),
         ],
-        compiler_params=pltpu.CompilerParams(vmem_limit_bytes=vmem_limit),
+        compiler_params=pltpu.CompilerParams(vmem_limit_bytes=32 * mib),
         cost_estimate=takes(10),
         name="attend",
     )(meta, q, o, do, gain, *kv_halves)
+
+
+def pair_kernel(keep_ref, other_ref, *out_refs):
+    rows, cut = out_refs[0].shape
+    blocks = len(out_refs) // 2
+    for k in range(blocks):
+        at = k * rows
+        total = keep_ref[at : at + rows, :] + other_ref[at : at + rows, :].astype(f32)
+        out_refs[k][...] = total[:, :cut].astype(bf16)
+        out_refs[blocks + k][...] = total[:, cut:].astype(bf16)
+
+
+def pair_sums(keep, other, rows, kv_heads):
+    blocks = keep.shape[0] // rows
+    width = keep.shape[1]
+    cut = (kv_heads // 2) * (width // kv_heads)
+    sums = pl.pallas_call(
+        pair_kernel,
+        out_shape=[jax.ShapeDtypeStruct((rows, cut), bf16)] * blocks
+        + [jax.ShapeDtypeStruct((rows, width - cut), bf16)] * blocks,
+        compiler_params=pltpu.CompilerParams(vmem_limit_bytes=32 * mib),
+        cost_estimate=takes(1),
+        name="pair_sums",
+    )(keep, other)
+    return sums[:blocks], sums[blocks:]
 
 
 def finish_kernel(chips, k_ref, gain_ref, own_ref, other_ref, *refs):
@@ -218,7 +243,7 @@
     return pl.pallas_call(
         functools.partial(finish_kernel, len(first) + 1),
         out_shape=(out, out),
-        compiler_params=pltpu.CompilerParams(vmem_limit_bytes=vmem_limit),
+        compiler_params=pltpu.CompilerParams(vmem_limit_bytes=8 * mib),
         cost_estimate=takes(2.2),
         name="finish_keys",
     )(k_pre, k_gain, *own, *first, *rest)
@@ -321,7 +346,7 @@
             jax.ShapeDtypeStruct((rows, tokens), bf16),
             jax.ShapeDtypeStruct((sp, cap * sp, experts), f32),
         ],
-        compiler_params=pltpu.CompilerParams(vmem_limit_bytes=vmem_limit),
+        compiler_params=pltpu.CompilerParams(vmem_limit_bytes=24 * mib),
         cost_estimate=takes(6.2),
         name="slot_terms",
     )(meta, table, lanes, *packs, *packs, eout)
@@ -347,7 +372,7 @@
         out_specs=pl.BlockSpec((rows, col), lambda i: (0, i)),
         out_shape=jax.ShapeDtypeStruct((rows, width), bf16),
         scratch_shapes=[pltpu.VMEM((tokens, col), bf16)],
-        compiler_params=pltpu.CompilerParams(vmem_limit_bytes=vmem_limit),
+        compiler_params=pltpu.CompilerParams(vmem_limit_bytes=16 * mib),
         cost_estimate=takes(4.6),
         name="batch_grad",
     )(gated, *packs)
@@ -400,7 +425,7 @@
             scratch_shapes=[pltpu.VMEM((cap * sp, experts), f32)],
         ),
         out_shape=jax.ShapeDtypeStruct((share, experts), bf16),
-        compiler_params=pltpu.CompilerParams(vmem_limit_bytes=vmem_limit),
+        compiler_params=pltpu.CompilerParams(vmem_limit_bytes=16 * mib),
         cost_estimate=takes(3),
         name="router_grad",
     )(meta, *packs, *packs, terms)
@@ -489,12 +514,7 @@
 
     rows = k_pre.shape[1]
     arrived = exchange(send)
-    sums = [
-        (keep[k * rows : (k + 1) * rows] + arrived[k * rows : (k + 1) * rows].astype(f32)).astype(bf16)
-        for k in range(chips - 1)
-    ]
-    cut = (kv_heads // 2) * 2 * q_gain.shape[0]
-    first, rest = [x[:, :cut] for x in sums], [x[:, cut:] for x in sums]
+    first, rest = pair_sums(keep, arrived, rows, kv_heads)
     packs, first, rest, own_send = together(packs, first, rest, own_send)
 
     own_arrived = exchange(own_send)

time: 106 us -> 101 us (0.953)
  Pallas kernels: 29.1 us -> 22.7 us
  waiting for transfers between devices: 33.2 us -> 37.1 us
  other arithmetic: 3.6 us -> 0.93 us
    ppermute x15, waiting for transfers between devices: 28 us -> 32 us  [flipped(): return lax.ppermute(x, axis, [(i, i ^ k) for i in range(size)])]
    pallas_call x1, Pallas kernels: 2.85 us -> 0.91 us  [gates(): pl.pallas_call(functools.partial(gates_kernel, chips), in_specs=[pl.Block...]
    pallas_call x1, Pallas kernels: 2.97 us -> 1.11 us  [router_grad(): pl.pallas_call(functools.partial(router_kernel, sp, cap), grid_spec=pltpu...]
    convert_element_type x1 -> x0, other arithmetic: 1.63 us -> none  [on_device(): (keep[k * rows:(k + 1) * rows] + arrived[k * rows:(k + 1) * rows].astype(...]
    pallas_call x1, Pallas kernels: 5.27 us -> 3.82 us  [slot_terms(): pl.pallas_call(functools.partial(terms_kernel, blocks, sp, cap), grid_spe...]
    unnamed x45 -> x47, local copies, waits for them, and re-layouts: 5.09 us -> 5.4 us
  transfers between devices with their start and end apart: 20 -> 20, of which waited for: 7 -> 7; matrix products, arithmetic and copies ran while one was open for 2% -> 0% of each run, Pallas kernels for 26% -> 20%
where the time goes in v6:
time: 101 us
  waiting for transfers between devices  37.1 us (37%)
  starting transfers between devices  33.1 us (33%)
  Pallas kernels  22.7 us (22%)
  local copies, waits for them, and re-layouts  5.45 us (5%)
  between operations  1.54 us (2%)
    ppermute x15, waiting for transfers between devices, flipped(): return lax.ppermute(x, axis, [(i, i ^ k) for i in range(size)])  32 us
    ppermute x15, starting transfers between devices, flipped(): return lax.ppermute(x, axis, [(i, i ^ k) for i in range(size)])  29.1 us
    pallas_call x1, Pallas kernels, attend(): pl.pallas_call(functools.partial(attend_kernel, blocks), grid_spec=pltpu....  9.33 us
    unnamed x47, local copies, waits for them, and re-layouts  5.4 us
    pallas_call x1, Pallas kernels, slot_terms(): pl.pallas_call(functools.partial(terms_kernel, blocks, sp, cap), grid_spe...  3.82 us
    all_to_all x1, starting transfers between devices, on_device(): terms = lax.all_to_all(terms, 'sp', split_axis=0, concat_axis=0, tiled=True)  3.74 us
    all_to_all x1, waiting for transfers between devices, on_device(): terms = lax.all_to_all(terms, 'sp', split_axis=0, concat_axis=0, tiled=True)  2.82 us
    pallas_call x1, Pallas kernels, batch_grad(): pl.pallas_call(batch_kernel, grid=(width // col,), in_specs=[whole((rows,...  2.56 us
  transfers between devices with their start and end apart: 20, of which 7 were waited for; matrix products, arithmetic and copies ran while one was open for 0% of the time, Pallas kernels for 20%

profile of v6, /device:TPU:0, one launch (start us, length us, event | category | flops | bytes accessed | tf_op | source)
XLA Modules:
  0.0 100.7 jit_solution(13080289258063668335)
XLA Ops:
  0.6 0.0 copy-start.19
  0.6 0.0 copy-start.1
  0.7 0.0 copy-start.7
  0.7 0.0 copy-start.8
  0.7 2.0 %pack_keys.1 = bf16[128,1024]{1,0:T(8,128)(2,1)} custom-call(bf16[128,512]{1,0:T(8,128)(2,1)} %bitcast.34, bf16[128,512]{1,0:T(8,128)(2,1)} %bitcast.39, f32[1,128]{1,0:T(1,128)} %bitcast.37), custom_call_target="tpu_custom_call" | custom-call | flops 2070000000 | bytes 6480000 | tf_op jit(solution)/shard_map/pack_keys/pallas_call | solution.py:51
  2.6 4.0 %collective-permute-start.1 = (bf16[128,1024]{1,0:T(8,128)(2,1)}, bf16[128,1024]{1,0:T(8,128)(2,1)S(1)}, u32[]{:S(2)}, u32[]{:S(2)}) collective-permute-start(bf16[128,1024]{1,0:T(8,128)(2,1)} %pack_keys.1), channel_id=1, source_target_pairs={{0,4},{1,5},{2,6},{3,7},{4,0},{5,1},{6,2},{7,3},{8,12},{9,13},{10,... | collective-permute-start | bytes 786440 | tf_op jit(solution)/shard_map/ppermute | solution.py:435
  6.7 1.6 %collective-permute-start = (bf16[128,1024]{1,0:T(8,128)(2,1)}, bf16[128,1024]{1,0:T(8,128)(2,1)S(1)}, u32[]{:S(2)}, u32[]{:S(2)}) collective-permute-start(bf16[128,1024]{1,0:T(8,128)(2,1)} %pack_keys.1), channel_id=1, source_target_pairs={{0,2},{1,3},{2,0},{3,1},{4,6},{5,7},{6,4},{7,5},{8,10},{9,11},{10,... | collective-permute-start | bytes 786440 | tf_op jit(solution)/shard_map/ppermute | solution.py:435
  8.2 0.0 copy-done.19
  8.2 0.1 copy.20
  8.3 0.1 pad_add_fusion.meta_ref
  8.4 10.5 %collective-permute-done.1 = bf16[128,1024]{1,0:T(8,128)(2,1)S(1)} collective-permute-done((bf16[128,1024]{1,0:T(8,128)(2,1)}, bf16[128,1024]{1,0:T(8,128)(2,1)S(1)}, u32[]{:S(2)}, u32[]{:S(2)}) %collective-permute-start.1) | collective-permute-done | bytes 262176 | tf_op jit(solution)/shard_map/ppermute | solution.py:435
  18.9 0.7 collective-permute-start.2
  19.6 0.9 gates.1
  20.6 0.7 copy-done.5
  21.3 0.7 copy-done.6
  22.0 0.0 collective-permute-done
  22.0 4.3 %collective-permute-done.2 = bf16[128,1024]{1,0:T(8,128)(2,1)S(1)} collective-permute-done((bf16[128,1024]{1,0:T(8,128)(2,1)S(1)}, bf16[128,1024]{1,0:T(8,128)(2,1)S(1)}, u32[]{:S(2)}, u32[]{:S(2)}) %collective-permute-start.2) | collective-permute-done | bytes 262176 | tf_op jit(solution)/shard_map/ppermute | solution.py:435
  26.4 0.1 collective-permute-start.3
  27.2 0.1 add_add_fusion.2
  27.3 1.5 %collective-permute-start.4 = (bf16[32,5376]{1,0:T(8,128)(2,1)}, bf16[32,5376]{1,0:T(8,128)(2,1)S(1)}, u32[]{:S(2)}, u32[]{:S(2)}) collective-permute-start(bf16[32,5376]{1,0:T(8,128)(2,1)} %copy-done.6), channel_id=1, source_target_pairs={{0,2},{1,3},{2,0},{3,1},{4,6},{5,7},{6,4},{7,5},{8,10},{9,11},{10,... | collective-permute-start | bytes 1032200 | tf_op jit(solution)/shard_map/ppermute | solution.py:435
  28.8 3.3 %collective-permute-start.5 = (bf16[32,5376]{1,0:T(8,128)(2,1)}, bf16[32,5376]{1,0:T(8,128)(2,1)S(1)}, u32[]{:S(2)}, u32[]{:S(2)}) collective-permute-start(bf16[32,5376]{1,0:T(8,128)(2,1)} %copy-done.5), channel_id=1, source_target_pairs={{0,4},{1,5},{2,6},{3,7},{4,0},{5,1},{6,2},{7,3},{8,12},{9,13},{10,... | collective-permute-start | bytes 1032200 | tf_op jit(solution)/shard_map/ppermute | solution.py:435
  32.1 0.0 collective-permute-start.6
  32.1 0.0 collective-permute-done.3.refs_1_
  32.1 0.0 copy-start.3
  32.1 1.0 %copy-done.3 = bf16[1,32,8192]{2,1,0:T(8,128)(2,1)S(1)} copy-done((bf16[1,32,8192]{2,1,0:T(8,128)(2,1)S(1)}, bf16[1,32,8192]{2,1,0:T(8,128)(2,1)}, u32[]{:S(2)}) %copy-start.3) | copy-done | bytes 524312
  33.1 1.0 %copy-done.4 = bf16[1,32,8192]{2,1,0:T(8,128)(2,1)S(1)} copy-done((bf16[1,32,8192]{2,1,0:T(8,128)(2,1)S(1)}, bf16[1,32,8192]{2,1,0:T(8,128)(2,1)}, u32[]{:S(2)}) %copy-start.4) | copy-done | bytes 524312
  34.2 9.3 %attend.1 = (bf16[32,8192]{1,0:T(8,128)(2,1)}, f32[128,1024]{1,0:T(8,128)S(1)}, f32[384,1024]{1,0:T(8,128)S(1)}, bf16[128,1024]{1,0:T(8,128)(2,1)}, bf16[384,1024]{1,0:T(8,128)(2,1)S(1)}) custom-call(s32[9]{0:T(128)S(1)} %get-tuple-element.128.meta_ref, bf16[32,8192]{1,0:T(8,128)(2,1)S(1)} %bitcast.29, bf16[32,8192]{1,0:T(8,128)(2,1)S(1)} %bitcast.30, ...), custom_call_target="tpu_custom_call" | custom-call | flops 11500000256 | bytes 36000000 | tf_op jit(solution)/shard_map/attend/pallas_call | solution.py:172
  43.5 1.5 %collective-permute-done.4 = bf16[32,5376]{1,0:T(8,128)(2,1)S(1)} collective-permute-done((bf16[32,5376]{1,0:T(8,128)(2,1)}, bf16[32,5376]{1,0:T(8,128)(2,1)S(1)}, u32[]{:S(2)}, u32[]{:S(2)}) %collective-permute-start.4) | collective-permute-done | bytes 344096 | tf_op jit(solution)/shard_map/ppermute | solution.py:435
  45.0 10.9 %collective-permute-done.5 = bf16[32,5376]{1,0:T(8,128)(2,1)S(1)} collective-permute-done((bf16[32,5376]{1,0:T(8,128)(2,1)}, bf16[32,5376]{1,0:T(8,128)(2,1)S(1)}, u32[]{:S(2)}, u32[]{:S(2)}) %collective-permute-start.5) | collective-permute-done | bytes 344096 | tf_op jit(solution)/shard_map/ppermute | solution.py:435
  55.9 0.0 collective-permute-done.6
  55.9 0.0 collective-permute-start.7
  55.9 2.3 %collective-permute-done.7.other_ref = bf16[384,1024]{1,0:T(8,128)(2,1)S(1)} collective-permute-done((bf16[384,1024]{1,0:T(8,128)(2,1)S(1)}, bf16[384,1024]{1,0:T(8,128)(2,1)S(1)}, u32[]{:S(2)}, u32[]{:S(2)}) %collective-permute-start.7) | collective-permute-done | bytes 786464 | tf_op jit(solution)/shard_map/ppermute | solution.py:478
  58.2 1.0 pair_sums.1
  59.3 0.2 collective-permute-start.12
  59.5 7.6 %collective-permute-start.9 = (bf16[128,512]{1,0:T(8,128)(2,1)}, bf16[128,512]{1,0:T(8,128)(2,1)}, u32[]{:S(2)}, u32[]{:S(2)}) collective-permute-start(bf16[128,512]{1,0:T(8,128)(2,1)} %get-tuple-element.98), channel_id=1, source_target_pairs={{0,2},{1,3},{2,0},{3,1},{4,6},{5,7},{6,4},{7,5},{8,10},{9,11},{10,... | collective-permute-start | bytes 393224 | tf_op jit(solution)/shard_map/ppermute | solution.py:435
  67.1 1.0 collective-permute-start.10
  68.0 1.5 %collective-permute-start.11 = (bf16[128,512]{1,0:T(8,128)(2,1)}, bf16[128,512]{1,0:T(8,128)(2,1)}, u32[]{:S(2)}, u32[]{:S(2)}) collective-permute-start(bf16[128,512]{1,0:T(8,128)(2,1)} %get-tuple-element.100), channel_id=1, source_target_pairs={{0,6},{1,7},{2,4},{3,5},{4,2},{5,3},{6,0},{7,1},{8,14},{9,15},{10,... | collective-permute-start | bytes 393224 | tf_op jit(solution)/shard_map/ppermute | solution.py:435
  69.5 0.0 collective-permute-start.8
  69.5 0.0 collective-permute-done.12.refs_1_.refs_3_
  69.5 3.8 %slot_terms.1 = (bf16[384,256]{1,0:T(8,128)(2,1)S(1)}, f32[8,24,128]{2,1,0:T(8,128)}) custom-call(s32[9]{0:T(128)S(1)} %get-tuple-element.127.meta_ref, s32[384,3]{1,0:T(8,128)S(1)} %copy-done.12, s32[1,384]{1,0:T(1,128)S(1)} %copy-done.13, bf16[128,5376]{1,0:T(8,128)(2,1)S(1)} %constant_dynamic-update-slice_fusion.4.refs_0_.refs_2_, ...), custom_call_target="tpu_custom_call" | custom-call | flops 7129999872 | bytes 22320000 | tf_op jit(solution)/shard_map/slot_terms/pallas_call | solution.py:329
  73.4 0.7 copy-done.16
  74.0 3.7 %all-to-all-start = ((f32[8,24,128]{2,1,0:T(8,128)}), f32[8,24,128]{2,1,0:T(8,128)S(1)}, u32[]{:S(2)}, u32[]{:S(2)}) async-start(f32[8,24,128]{2,1,0:T(8,128)} %get-tuple-element.108), calls=%async_computation | async-start | bytes 196608 | tf_op jit(solution)/shard_map/all_to_all | solution.py:524
  77.8 0.9 copy-done.17
  78.7 2.6 %batch_grad.1 = bf16[384,4096]{1,0:T(8,128)(2,1)} custom-call(bf16[384,256]{1,0:T(8,128)(2,1)S(1)} %copy-done.17, bf16[128,5376]{1,0:T(8,128)(2,1)S(1)} %constant_dynamic-update-slice_fusion.4.refs_0_.refs_2_, bf16[128,5376]{1,0:T(8,128)(2,1)S(1)} %collective-permute-done.12.refs_1_.refs_3_), custom_call_target="tpu_custom_call" | custom-call | flops 5289999872 | bytes 16559999 | tf_op jit(solution)/shard_map/batch_grad/pallas_call | solution.py:367
  81.3 0.0 collective-permute-done.9.refs_0_
  81.3 0.0 collective-permute-done.10.refs_1_
  81.3 0.0 collective-permute-done.11.refs_2_
  81.3 0.0 collective-permute-done.8.other_ref
  81.3 2.8 %all-to-all-done.refs_4_ = f32[8,24,128]{2,1,0:T(8,128)S(1)} async-done(((f32[8,24,128]{2,1,0:T(8,128)}), f32[8,24,128]{2,1,0:T(8,128)S(1)}, u32[]{:S(2)}, u32[]{:S(2)}) %all-to-all-start) | async-done | bytes 98336 | tf_op jit(solution)/shard_map/all_to_all | solution.py:524
  84.1 0.8 collective-permute-start.13
  84.9 2.3 %collective-permute-start.14 = (bf16[128,512]{1,0:T(8,128)(2,1)}, bf16[128,512]{1,0:T(8,128)(2,1)S(1)}, u32[]{:S(2)}, u32[]{:S(2)}) collective-permute-start(bf16[128,512]{1,0:T(8,128)(2,1)} %get-tuple-element.115), channel_id=1, source_target_pairs={{0,4},{1,5},{2,6},{3,7},{4,0},{5,1},{6,2},{7,3},{8,12},{9,13},{10,... | collective-permute-start | bytes 393224 | tf_op jit(solution)/shard_map/ppermute | solution.py:435
  87.2 1.3 %collective-permute-start.15 = (bf16[128,512]{1,0:T(8,128)(2,1)}, bf16[128,512]{1,0:T(8,128)(2,1)S(1)}, u32[]{:S(2)}, u32[]{:S(2)}) collective-permute-start(bf16[128,512]{1,0:T(8,128)(2,1)} %get-tuple-element.116), channel_id=1, source_target_pairs={{0,6},{1,7},{2,4},{3,5},{4,2},{5,3},{6,0},{7,1},{8,14},{9,15},{10,... | collective-permute-start | bytes 393224 | tf_op jit(solution)/shard_map/ppermute | solution.py:435
  88.5 1.1 %router_grad.1 = bf16[512,128]{1,0:T(8,128)(2,1)S(1)} custom-call(s32[9]{0:T(128)S(1)} %get-tuple-element.127.meta_ref, bf16[128,5376]{1,0:T(8,128)(2,1)S(1)} %constant_dynamic-update-slice_fusion.4.refs_0_.refs_2_, bf16[128,5376]{1,0:T(8,128)(2,1)S(1)} %collective-permute-done.12.refs_1_.refs_3_, ...), custom_call_target="tpu_custom_call" | custom-call | flops 3449999872 | bytes 10800000 | tf_op jit(solution)/shard_map/router_grad/pallas_call | solution.py:418
  89.6 2.5 %collective-permute-start.18 = (bf16[512,128]{1,0:T(8,128)(2,1)S(1)}, bf16[512,128]{1,0:T(8,128)(2,1)S(1)}, u32[]{:S(2)}, u32[]{:S(2)}) collective-permute-start(bf16[512,128]{1,0:T(8,128)(2,1)S(1)} %router_grad.1), channel_id=1, source_target_pairs={{0,24},{8,16},{16,8},{24,0},{1,25},{9,17},{17,9},{25,1},{2,26},{10... | collective-permute-start | bytes 393224 | tf_op jit(solution)/shard_map/ppermute | solution.py:435
  92.1 0.5 collective-permute-start.17
  92.6 0.0 collective-permute-done.13.refs_3_
  92.6 0.5 collective-permute-start.16
  93.2 4.7 %collective-permute-done.14.refs_4_ = bf16[128,512]{1,0:T(8,128)(2,1)S(1)} collective-permute-done((bf16[128,512]{1,0:T(8,128)(2,1)}, bf16[128,512]{1,0:T(8,128)(2,1)S(1)}, u32[]{:S(2)}, u32[]{:S(2)}) %collective-permute-start.14) | collective-permute-done | bytes 131104 | tf_op jit(solution)/shard_map/ppermute | solution.py:435
  97.9 0.0 collective-permute-done.15.refs_5_
  97.9 2.0 %finish_keys.1 = (bf16[128,512]{1,0:T(8,128)(2,1)}, bf16[128,512]{1,0:T(8,128)(2,1)}) custom-call(bf16[128,512]{1,0:T(8,128)(2,1)S(1)} %bitcast.35, f32[1,128]{1,0:T(1,128)S(1)} %bitcast.38, f32[128,1024]{1,0:T(8,128)S(1)} %copy-done.15, bf16[128,1024]{1,0:T(8,128)(2,1)S(1)} %collective-permute-done.8.other_ref, ...), custom_call_target="tpu_custom_call" | custom-call | flops 2529999872 | bytes 7920000 | tf_op jit(solution)/shard_map/finish_keys/pallas_call | solution.py:243
  99.9 0.0 collective-permute-done.18
  100.0 0.0 collective-permute-done.17
  100.0 0.0 collective-permute-done.16
  100.0 0.8 add_add_fusion
  (37 shorter events, 0.2 us)
Async XLA Ops:
  0.6 7.6 %copy-start.19 = (s32[1,32,8]{1,2,0:T(8,128)S(1)}, s32[1,32,8]{1,2,0:T(8,128)}, u32[]{:S(2)}) copy-start(s32[1,32,8]{1,2,0:T(8,128)} %param.25) | copy-start | bytes 3076
  0.6 19.0 %copy-start.1 = (bf16[4096,128]{1,0:T(8,128)(2,1)S(1)}, bf16[4096,128]{1,0:T(8,128)(2,1)}, u32[]{:S(2)}) copy-start(bf16[4096,128]{1,0:T(8,128)(2,1)} %router_ref.1) | copy-start | bytes 3145732
  0.7 19.0 %copy-start.7 = (bf16[1,32,4096]{2,1,0:T(8,128)(2,1)S(1)}, bf16[1,32,4096]{2,1,0:T(8,128)(2,1)}, u32[]{:S(2)}) copy-start(bf16[1,32,4096]{2,1,0:T(8,128)(2,1)} %param.23) | copy-start | bytes 786436
  0.7 19.0 %copy-start.8 = (bf16[1,32,4096]{2,1,0:T(8,128)(2,1)S(1)}, bf16[1,32,4096]{2,1,0:T(8,128)(2,1)}, u32[]{:S(2)}) copy-start(bf16[1,32,4096]{2,1,0:T(8,128)(2,1)} %param.26) | copy-start | bytes 786436
  2.6 16.3 %collective-permute-start.1 = (bf16[128,1024]{1,0:T(8,128)(2,1)}, bf16[128,1024]{1,0:T(8,128)(2,1)S(1)}, u32[]{:S(2)}, u32[]{:S(2)}) collective-permute-start(bf16[128,1024]{1,0:T(8,128)(2,1)} %pack_keys.1), channel_id=1, source_target_pairs={{0,4},{1,5},{2,6},{3,7},{4,0},{5,1},{6,2},{7,3},{8,12},{9,13},{10,... | collective-permute-start | bytes 786440 | tf_op jit(solution)/shard_map/ppermute | solution.py:435
  6.7 15.4 %collective-permute-start = (bf16[128,1024]{1,0:T(8,128)(2,1)}, bf16[128,1024]{1,0:T(8,128)(2,1)S(1)}, u32[]{:S(2)}, u32[]{:S(2)}) collective-permute-start(bf16[128,1024]{1,0:T(8,128)(2,1)} %pack_keys.1), channel_id=1, source_target_pairs={{0,2},{1,3},{2,0},{3,1},{4,6},{5,7},{6,4},{7,5},{8,10},{9,11},{10,... | collective-permute-start | bytes 786440 | tf_op jit(solution)/shard_map/ppermute | solution.py:435
  18.9 7.4 %collective-permute-start.2 = (bf16[128,1024]{1,0:T(8,128)(2,1)S(1)}, bf16[128,1024]{1,0:T(8,128)(2,1)S(1)}, u32[]{:S(2)}, u32[]{:S(2)}) collective-permute-start(bf16[128,1024]{1,0:T(8,128)(2,1)S(1)} %collective-permute-done.1), channel_id=1, source_target_pairs={{0,2},{1,3},{2,0},{3,1},{4,6},{5,7},{6,4},{7,5},{8,10},{9,11},{10,... | collective-permute-start | bytes 786440 | tf_op jit(solution)/shard_map/ppermute | solution.py:435
  19.6 6.7 %copy-start.18 = (bf16[128,1024]{1,0:T(8,128)(2,1)S(1)}, bf16[128,1024]{1,0:T(8,128)(2,1)}, u32[]{:S(2)}) copy-start(bf16[128,1024]{1,0:T(8,128)(2,1)} %pack_keys.1) | copy-start | bytes 786436
  20.6 0.7 copy-start.5
  21.3 0.7 copy-start.6
  22.0 10.0 %copy-start.2 = (bf16[1,32,8192]{2,1,0:T(8,128)(2,1)S(1)}, bf16[1,32,8192]{2,1,0:T(8,128)(2,1)}, u32[]{:S(2)}) copy-start(bf16[1,32,8192]{2,1,0:T(8,128)(2,1)} %param.15) | copy-start | bytes 1572868
  22.0 10.0 %copy-start.10 = (f32[128]{0:T(128)S(1)}, f32[128]{0:T(128)}, u32[]{:S(2)}) copy-start(f32[128]{0:T(128)} %param.20) | copy-start | bytes 1540
  26.4 5.6 %collective-permute-start.3 = (bf16[512,1024]{1,0:T(8,128)(2,1)S(1)}, bf16[512,1024]{1,0:T(8,128)(2,1)S(1)}, u32[]{:S(2)}, u32[]{:S(2)}) collective-permute-start(bf16[512,1024]{1,0:T(8,128)(2,1)S(1)} %constant_dynamic-update-slice_fusion.refs_0_), channel_id=1, source_target_pairs={{0,1},{1,0},{2,3},{3,2},{4,5},{5,4},{6,7},{7,6},{8,9},{9,8},{10,11... | collective-permute-start | bytes 3145736 | tf_op jit(solution)/shard_map/ppermute | solution.py:478
  27.3 17.7 %collective-permute-start.4 = (bf16[32,5376]{1,0:T(8,128)(2,1)}, bf16[32,5376]{1,0:T(8,128)(2,1)S(1)}, u32[]{:S(2)}, u32[]{:S(2)}) collective-permute-start(bf16[32,5376]{1,0:T(8,128)(2,1)} %copy-done.6), channel_id=1, source_target_pairs={{0,2},{1,3},{2,0},{3,1},{4,6},{5,7},{6,4},{7,5},{8,10},{9,11},{10,... | collective-permute-start | bytes 1032200 | tf_op jit(solution)/shard_map/ppermute | solution.py:435
  28.8 27.1 %collective-permute-start.5 = (bf16[32,5376]{1,0:T(8,128)(2,1)}, bf16[32,5376]{1,0:T(8,128)(2,1)S(1)}, u32[]{:S(2)}, u32[]{:S(2)}) collective-permute-start(bf16[32,5376]{1,0:T(8,128)(2,1)} %copy-done.5), channel_id=1, source_target_pairs={{0,4},{1,5},{2,6},{3,7},{4,0},{5,1},{6,2},{7,3},{8,12},{9,13},{10,... | collective-permute-start | bytes 1032200 | tf_op jit(solution)/shard_map/ppermute | solution.py:435
  32.1 23.8 %collective-permute-start.6 = (bf16[32,5376]{1,0:T(8,128)(2,1)S(1)}, bf16[32,5376]{1,0:T(8,128)(2,1)S(1)}, u32[]{:S(2)}, u32[]{:S(2)}) collective-permute-start(bf16[32,5376]{1,0:T(8,128)(2,1)S(1)} %get-tuple-element.78), channel_id=1, source_target_pairs={{0,6},{1,7},{2,4},{3,5},{4,2},{5,3},{6,0},{7,1},{8,14},{9,15},{10,... | collective-permute-start | bytes 1032200 | tf_op jit(solution)/shard_map/ppermute | solution.py:435
  32.1 1.0 %copy-start.3 = (bf16[1,32,8192]{2,1,0:T(8,128)(2,1)S(1)}, bf16[1,32,8192]{2,1,0:T(8,128)(2,1)}, u32[]{:S(2)}) copy-start(bf16[1,32,8192]{2,1,0:T(8,128)(2,1)} %param.16) | copy-start | bytes 1572868
  33.1 1.0 %copy-start.4 = (bf16[1,32,8192]{2,1,0:T(8,128)(2,1)S(1)}, bf16[1,32,8192]{2,1,0:T(8,128)(2,1)}, u32[]{:S(2)}) copy-start(bf16[1,32,8192]{2,1,0:T(8,128)(2,1)} %param.17) | copy-start | bytes 1572868
  43.5 15.7 %copy-start.14 = (f32[128,1024]{1,0:T(8,128)}, f32[128,1024]{1,0:T(8,128)S(1)}, u32[]{:S(2)}) copy-start(f32[128,1024]{1,0:T(8,128)S(1)} %get-tuple-element.83.own_ref) | copy-start | bytes 1572868
  55.9 2.3 %collective-permute-start.7 = (bf16[384,1024]{1,0:T(8,128)(2,1)S(1)}, bf16[384,1024]{1,0:T(8,128)(2,1)S(1)}, u32[]{:S(2)}, u32[]{:S(2)}) collective-permute-start(bf16[384,1024]{1,0:T(8,128)(2,1)S(1)} %get-tuple-element.89), channel_id=1, source_target_pairs={{0,1},{1,0},{2,3},{3,2},{4,5},{5,4},{6,7},{7,6},{8,9},{9,8},{10,11... | collective-permute-start | bytes 2359304 | tf_op jit(solution)/shard_map/ppermute | solution.py:478
  58.2 11.3 %copy-start = (bf16[1,16,8,3,4096]{4,2,3,1,0:T(8,128)(2,1)S(1)}, bf16[1,16,8,3,4096]{4,2,3,1,0:T(8,128)(2,1)}, u32[]{:S(2)}) copy-start(bf16[1,16,8,3,4096]{4,2,3,1,0:T(8,128)(2,1)} %param.27) | copy-start | bytes 9437188
  59.2 10.3 %copy-start.12 = (s32[384,3]{1,0:T(8,128)S(1)}, s32[384,3]{1,0:T(8,128)}, u32[]{:S(2)}) copy-start(s32[384,3]{1,0:T(8,128)} %constant.29.clone.table_ref) | copy-start | bytes 13828
  59.2 10.4 %copy-start.13 = (s32[1,384]{1,0:T(1,128)S(1)}, s32[1,384]{1,0:T(1,128)}, u32[]{:S(2)}) copy-start(s32[1,384]{1,0:T(1,128)} %constant.30.clone.lanes_ref) | copy-start | bytes 4612
  59.3 10.2 %collective-permute-start.12 = (bf16[128,5376]{1,0:T(8,128)(2,1)S(1)}, bf16[128,5376]{1,0:T(8,128)(2,1)S(1)}, u32[]{:S(2)}, u32[]{:S(2)}) collective-permute-start(bf16[128,5376]{1,0:T(8,128)(2,1)S(1)} %constant_dynamic-update-slice_fusion.4.refs_0_.refs_2_), channel_id=1, source_target_pairs={{0,1},{1,0},{2,3},{3,2},{4,5},{5,4},{6,7},{7,6},{8,9},{9,8},{10,11... | collective-permute-start | bytes 4128776 | tf_op jit(solution)/shard_map/ppermute | solution.py:478
  59.5 21.8 %collective-permute-start.9 = (bf16[128,512]{1,0:T(8,128)(2,1)}, bf16[128,512]{1,0:T(8,128)(2,1)}, u32[]{:S(2)}, u32[]{:S(2)}) collective-permute-start(bf16[128,512]{1,0:T(8,128)(2,1)} %get-tuple-element.98), channel_id=1, source_target_pairs={{0,2},{1,3},{2,0},{3,1},{4,6},{5,7},{6,4},{7,5},{8,10},{9,11},{10,... | collective-permute-start | bytes 393224 | tf_op jit(solution)/shard_map/ppermute | solution.py:435
  67.1 14.2 %collective-permute-start.10 = (bf16[128,512]{1,0:T(8,128)(2,1)}, bf16[128,512]{1,0:T(8,128)(2,1)}, u32[]{:S(2)}, u32[]{:S(2)}) collective-permute-start(bf16[128,512]{1,0:T(8,128)(2,1)} %get-tuple-element.99), channel_id=1, source_target_pairs={{0,4},{1,5},{2,6},{3,7},{4,0},{5,1},{6,2},{7,3},{8,12},{9,13},{10,... | collective-permute-start | bytes 393224 | tf_op jit(solution)/shard_map/ppermute | solution.py:435
  68.0 13.2 %collective-permute-start.11 = (bf16[128,512]{1,0:T(8,128)(2,1)}, bf16[128,512]{1,0:T(8,128)(2,1)}, u32[]{:S(2)}, u32[]{:S(2)}) collective-permute-start(bf16[128,512]{1,0:T(8,128)(2,1)} %get-tuple-element.100), channel_id=1, source_target_pairs={{0,6},{1,7},{2,4},{3,5},{4,2},{5,3},{6,0},{7,1},{8,14},{9,15},{10,... | collective-permute-start | bytes 393224 | tf_op jit(solution)/shard_map/ppermute | solution.py:435
  69.5 11.8 %collective-permute-start.8 = (bf16[128,1024]{1,0:T(8,128)(2,1)}, bf16[128,1024]{1,0:T(8,128)(2,1)S(1)}, u32[]{:S(2)}, u32[]{:S(2)}) collective-permute-start(bf16[128,1024]{1,0:T(8,128)(2,1)} %get-tuple-element.97), channel_id=1, source_target_pairs={{0,1},{1,0},{2,3},{3,2},{4,5},{5,4},{6,7},{7,6},{8,9},{9,8},{10,11... | collective-permute-start | bytes 786440 | tf_op jit(solution)/shard_map/ppermute | solution.py:478
  73.4 0.7 copy-start.16
  74.0 10.1 %all-to-all-start = ((f32[8,24,128]{2,1,0:T(8,128)}), f32[8,24,128]{2,1,0:T(8,128)S(1)}, u32[]{:S(2)}, u32[]{:S(2)}) async-start(f32[8,24,128]{2,1,0:T(8,128)} %get-tuple-element.108), calls=%async_computation | async-start | bytes 196608 | tf_op jit(solution)/shard_map/all_to_all | solution.py:524
  77.8 0.9 copy-start.17
  81.3 16.7 %copy-start.9 = (bf16[1,128,512]{2,1,0:T(8,128)(2,1)S(1)}, bf16[1,128,512]{2,1,0:T(8,128)(2,1)}, u32[]{:S(2)}) copy-start(bf16[1,128,512]{2,1,0:T(8,128)(2,1)} %param.18) | copy-start | bytes 393220
  81.3 16.7 %copy-start.11 = (f32[128]{0:T(128)S(1)}, f32[128]{0:T(128)}, u32[]{:S(2)}) copy-start(f32[128]{0:T(128)} %param.21) | copy-start | bytes 1540
  84.1 13.8 %copy-start.15 = (f32[128,1024]{1,0:T(8,128)S(1)}, f32[128,1024]{1,0:T(8,128)}, u32[]{:S(2)}) copy-start(f32[128,1024]{1,0:T(8,128)} %copy-done.14) | copy-start | bytes 1572868
  84.1 8.5 %collective-permute-start.13 = (bf16[128,512]{1,0:T(8,128)(2,1)}, bf16[128,512]{1,0:T(8,128)(2,1)S(1)}, u32[]{:S(2)}, u32[]{:S(2)}) collective-permute-start(bf16[128,512]{1,0:T(8,128)(2,1)} %get-tuple-element.114), channel_id=1, source_target_pairs={{0,2},{1,3},{2,0},{3,1},{4,6},{5,7},{6,4},{7,5},{8,10},{9,11},{10,... | collective-permute-start | bytes 393224 | tf_op jit(solution)/shard_map/ppermute | solution.py:435
  84.9 13.0 %collective-permute-start.14 = (bf16[128,512]{1,0:T(8,128)(2,1)}, bf16[128,512]{1,0:T(8,128)(2,1)S(1)}, u32[]{:S(2)}, u32[]{:S(2)}) collective-permute-start(bf16[128,512]{1,0:T(8,128)(2,1)} %get-tuple-element.115), channel_id=1, source_target_pairs={{0,4},{1,5},{2,6},{3,7},{4,0},{5,1},{6,2},{7,3},{8,12},{9,13},{10,... | collective-permute-start | bytes 393224 | tf_op jit(solution)/shard_map/ppermute | solution.py:435
  87.2 10.7 %collective-permute-start.15 = (bf16[128,512]{1,0:T(8,128)(2,1)}, bf16[128,512]{1,0:T(8,128)(2,1)S(1)}, u32[]{:S(2)}, u32[]{:S(2)}) collective-permute-start(bf16[128,512]{1,0:T(8,128)(2,1)} %get-tuple-element.116), channel_id=1, source_target_pairs={{0,6},{1,7},{2,4},{3,5},{4,2},{5,3},{6,0},{7,1},{8,14},{9,15},{10,... | collective-permute-start | bytes 393224 | tf_op jit(solution)/shard_map/ppermute | solution.py:435
  89.6 10.3 %collective-permute-start.18 = (bf16[512,128]{1,0:T(8,128)(2,1)S(1)}, bf16[512,128]{1,0:T(8,128)(2,1)S(1)}, u32[]{:S(2)}, u32[]{:S(2)}) collective-permute-start(bf16[512,128]{1,0:T(8,128)(2,1)S(1)} %router_grad.1), channel_id=1, source_target_pairs={{0,24},{8,16},{16,8},{24,0},{1,25},{9,17},{17,9},{25,1},{2,26},{10... | collective-permute-start | bytes 393224 | tf_op jit(solution)/shard_map/ppermute | solution.py:435
  92.1 7.8 %collective-permute-start.17 = (bf16[512,128]{1,0:T(8,128)(2,1)S(1)}, bf16[512,128]{1,0:T(8,128)(2,1)S(1)}, u32[]{:S(2)}, u32[]{:S(2)}) collective-permute-start(bf16[512,128]{1,0:T(8,128)(2,1)S(1)} %router_grad.1), channel_id=1, source_target_pairs={{0,16},{8,24},{16,0},{24,8},{1,17},{9,25},{17,1},{25,9},{2,18},{10... | collective-permute-start | bytes 393224 | tf_op jit(solution)/shard_map/ppermute | solution.py:435
  92.6 7.3 %collective-permute-start.16 = (bf16[512,128]{1,0:T(8,128)(2,1)S(1)}, bf16[512,128]{1,0:T(8,128)(2,1)S(1)}, u32[]{:S(2)}, u32[]{:S(2)}) collective-permute-start(bf16[512,128]{1,0:T(8,128)(2,1)S(1)} %router_grad.1), channel_id=1, source_target_pairs={{0,8},{8,0},{16,24},{24,16},{1,9},{9,1},{17,25},{25,17},{2,10},{10... | collective-permute-start | bytes 393224 | tf_op jit(solution)/shard_map/ppermute | solution.py:435

commit v7 on v6

--- a/solution.py
+++ b/solution.py
@@ -56,7 +56,7 @@
     )(k_pre, values, k_gain)
 
 
-def gates_kernel(chips, meta_ref, moe_ref, router_ref, ids_ref, dmoe_ref, *pack_refs):
+def gates_kernel(meta_ref, moe_ref, router_ref, ids_ref, dmoe_ref, pack_ref, *share_refs):
     tok, width = moe_ref.shape
     experts = router_ref.shape[1]
     logits = dot_nn(moe_ref[...], router_ref[...])
@@ -67,32 +67,29 @@
     weights = jnp.where(chosen, jnp.exp(logits), 0.0)
     probs = weights / jnp.sum(weights, axis=-1, keepdims=True)
     high = probs.astype(bf16)
-    low = (probs - high.astype(f32)).astype(bf16)
-    coded = jnp.where(chosen, high.astype(f32), -1.0).astype(bf16)
-    share = width // (2 * chips)
+    pack_ref[:, :width] = dmoe_ref[...]
+    pack_ref[:, width : width + experts] = jnp.where(chosen, high.astype(f32), -1.0).astype(bf16)
+    pack_ref[:, width + experts :] = (probs - high.astype(f32)).astype(bf16)
+    share = share_refs[0].shape[1] // 2
     chip, core = meta_ref[0], meta_ref[1]
-    d_all = dmoe_ref[...]
-    for k, ref in enumerate(pack_refs):
-        ref[:, :width] = d_all
-        ref[:, width + 2 * share : width + 2 * share + experts] = coded
-        ref[:, width + 2 * share + experts : width + 2 * share + 2 * experts] = low
+    for k, ref in enumerate(share_refs):
         to = jnp.bitwise_xor(chip, k) * 2
         for i in range(2):
             at = pl.multiple_of((to + jnp.bitwise_xor(core, i)) * share, 128)
-            ref[:, width + i * share : width + (i + 1) * share] = moe_ref[:, pl.ds(at, share)]
+            ref[:, i * share : (i + 1) * share] = moe_ref[:, pl.ds(at, share)]
 
 
 def gates(meta, moe_in, router, ids, d_moe, chips):
     tok, width = moe_in.shape
     experts = router.shape[1]
     vm = pl.BlockSpec(memory_space=pltpu.VMEM)
-    packed = width + width // chips + 2 * experts
-    return pl.pallas_call(
-        functools.partial(gates_kernel, chips),
+    return pl.pallas_call(
+        gates_kernel,
         in_specs=[pl.BlockSpec(memory_space=pltpu.SMEM)] + [vm] * 4,
-        out_shape=[jax.ShapeDtypeStruct((tok, packed), bf16)] * chips,
+        out_shape=[jax.ShapeDtypeStruct((tok, width + 2 * experts), bf16)]
+        + [jax.ShapeDtypeStruct((tok, width // chips), bf16)] * chips,
         compiler_params=pltpu.CompilerParams(vmem_limit_bytes=8 * mib),
-        cost_estimate=takes(2.8),
+        cost_estimate=takes(1),
         name="gates",
     )(meta, moe_in, router, ids, d_moe)
 
@@ -409,12 +406,12 @@
     out_ref[...] = total.astype(bf16)
 
 
-def router_grad(meta, packs, terms, width, experts, cap, sp):
+def router_grad(meta, packs, moe, terms, width, experts, cap, sp):
     half, packed = packs[0].shape
     share = width // sp
     info_at = packed // (2 * experts) - 1
     info_spec = pl.BlockSpec((half, 2 * experts), lambda i, m: (0, info_at))
-    moe_specs = [pl.BlockSpec((half, share), lambda i, m, c=c: (0, sp + c)) for c in range(2)]
+    moe_specs = [whole((half, share))] * 2
     return pl.pallas_call(
         functools.partial(router_kernel, sp, cap),
         grid_spec=pltpu.PrefetchScalarGridSpec(
@@ -428,7 +425,7 @@
         compiler_params=pltpu.CompilerParams(vmem_limit_bytes=16 * mib),
         cost_estimate=takes(3),
         name="router_grad",
-    )(meta, *packs, *packs, terms)
+    )(meta, *packs, *moe, terms)
 
 
 def flipped(x, axis, size, k):
@@ -503,14 +500,20 @@
         kv = [kv, to_chip(kv, 1), far, to_chip(far, 1)]
     else:
         kv = [kv] + [to_chip(kv, k) for k in range(1, chips)]
-    packs = gates(place, moe_in[0], router, expert_ids[0], d_moe[0], chips)
-    kv, packs = together(kv, packs)
-
-    packs = [packs[0]] + [to_chip(packs[k], k) for k in range(1, chips)]
+    pack, *shares = gates(place, moe_in[0], router, expert_ids[0], d_moe[0], chips)
+    shares = [shares[0]] + [to_chip(shares[k], k) for k in range(1, chips)]
+    kv, pack, shares = together(kv, pack, shares)
+
+    packs = [pack] + [to_chip(pack, k) for k in range(1, chips)]
+    share = width // sp
+    mine = jnp.concatenate([x[:, :share] for x in shares], axis=0)
+    theirs = exchange(jnp.concatenate([x[:, share:] for x in shares], axis=0))
     dq, own, keep, own_send, send = attend(
         meta, q_pre[0], attn_out[0], d_attn[0], qg, both(kv), sp, kv_heads
     )
-    packs, own, keep, own_send, send = together(packs, own, keep, own_send, send)
+    packs, mine, theirs, own, keep, own_send, send = together(
+        packs, mine, theirs, own, keep, own_send, send
+    )
 
     rows = k_pre.shape[1]
     arrived = exchange(send)
@@ -523,10 +526,10 @@
     gated, terms = slot_terms(slot_meta, packs, eout, experts, cap, sp)
     terms = lax.all_to_all(terms, "sp", split_axis=0, concat_axis=0, tiled=True)
     batch = batch_grad(gated, packs, width)
-    own_arrived, first, rest, terms, batch = together(own_arrived, first, rest, terms, batch)
+    own_arrived, first, rest, batch = together(own_arrived, first, rest, batch)
 
     rest = [to_chip(rest[k - 1], k) for k in range(1, chips)]
-    routed = router_grad(slot_meta, packs, terms, width, experts, cap, sp)
+    routed = router_grad(slot_meta, packs, (mine, theirs), terms, width, experts, cap, sp)
     routed = sent_over("dp", dp, routed)
     dk, dv = finish_keys(k_pre[0], kg, [own, own_arrived], first, rest)
     dk, dv, routed = together(dk, dv, routed)

time: 101 us -> 98.9 us (0.979)
  waiting for transfers between devices: 37.1 us -> 31.6 us
  starting transfers between devices: 33.1 us -> 36.9 us
    ppermute x15 -> x18, starting transfers between devices: 29.1 us -> 32.8 us  [flipped(): return lax.ppermute(x, axis, [(i, i ^ k) for i in range(size)])]
    all_to_all x1, waiting for transfers between devices: 2.82 us -> 0.01 us  [on_device(): terms = lax.all_to_all(terms, 'sp', split_axis=0, concat_axis=0, tiled=True)]
    ppermute x15 -> x18, waiting for transfers between devices: 32 us -> 29.3 us  [flipped(): return lax.ppermute(x, axis, [(i, i ^ k) for i in range(size)])]
    unnamed x47 -> x45, local copies, waits for them, and re-layouts: 5.4 us -> 3.93 us
    ppermute x4 -> x5, waiting for transfers between devices: 2.29 us -> 2.29 us  [exchange(): return lax.ppermute(x, 'sp', swap)]
  transfers between devices with their start and end apart: 20 -> 24, of which waited for: 7 -> 6; matrix products, arithmetic and copies ran while one was open for 0% -> 1% of each run, Pallas kernels for 20% -> 20%
where the time goes in v7:
time: 98.9 us; the launch traced here: 98.4 us
  starting transfers between devices  36.9 us (37%)
  waiting for transfers between devices  31.6 us (32%)
  Pallas kernels  22.6 us (23%)
  local copies, waits for them, and re-layouts  4.77 us (5%)
  between operations  1.65 us (2%)
    ppermute x18, starting transfers between devices, flipped(): return lax.ppermute(x, axis, [(i, i ^ k) for i in range(size)])  32.8 us
    ppermute x18, waiting for transfers between devices, flipped(): return lax.ppermute(x, axis, [(i, i ^ k) for i in range(size)])  29.3 us
    pallas_call x1, Pallas kernels, attend(): pl.pallas_call(functools.partial(attend_kernel, blocks), grid_spec=pltpu....  9.24 us
    unnamed x45, local copies, waits for them, and re-layouts  3.93 us
    pallas_call x1, Pallas kernels, slot_terms(): pl.pallas_call(functools.partial(terms_kernel, blocks, sp, cap), grid_spe...  3.81 us
    all_to_all x1, starting transfers between devices, on_device(): terms = lax.all_to_all(terms, 'sp', split_axis=0, concat_axis=0, tiled=True)  3.36 us
    pallas_call x1, Pallas kernels, batch_grad(): pl.pallas_call(batch_kernel, grid=(width // col,), in_specs=[whole((rows,...  2.56 us
    ppermute x5, waiting for transfers between devices, exchange(): return lax.ppermute(x, 'sp', swap)  2.29 us
  transfers between devices with their start and end apart: 24, of which 6 were waited for; matrix products, arithmetic and copies ran while one was open for 1% of the time, Pallas kernels for 20%

profile of v7, /device:TPU:0, one launch (start us, length us, event | category | flops | bytes accessed | tf_op | source)
XLA Modules:
  0.0 98.4 jit_solution(15918484821315863924)
XLA Ops:
  0.7 2.0 %pack_keys.1 = bf16[128,1024]{1,0:T(8,128)(2,1)} custom-call(bf16[128,512]{1,0:T(8,128)(2,1)} %bitcast.34, bf16[128,512]{1,0:T(8,128)(2,1)} %bitcast.39, f32[1,128]{1,0:T(1,128)} %bitcast.37), custom_call_target="tpu_custom_call" | custom-call | flops 2070000000 | bytes 6480000 | tf_op jit(solution)/shard_map/pack_keys/pallas_call | solution.py:51
  2.6 4.0 %collective-permute-start.1 = (bf16[128,1024]{1,0:T(8,128)(2,1)}, bf16[128,1024]{1,0:T(8,128)(2,1)S(1)}, u32[]{:S(2)}, u32[]{:S(2)}) collective-permute-start(bf16[128,1024]{1,0:T(8,128)(2,1)} %pack_keys.1), channel_id=1, source_target_pairs={{0,4},{1,5},{2,6},{3,7},{4,0},{5,1},{6,2},{7,3},{8,12},{9,13},{10,... | collective-permute-start | bytes 786440 | tf_op jit(solution)/shard_map/ppermute | solution.py:432
  6.7 1.6 %collective-permute-start = (bf16[128,1024]{1,0:T(8,128)(2,1)}, bf16[128,1024]{1,0:T(8,128)(2,1)S(1)}, u32[]{:S(2)}, u32[]{:S(2)}) collective-permute-start(bf16[128,1024]{1,0:T(8,128)(2,1)} %pack_keys.1), channel_id=1, source_target_pairs={{0,2},{1,3},{2,0},{3,1},{4,6},{5,7},{6,4},{7,5},{8,10},{9,11},{10,... | collective-permute-start | bytes 786440 | tf_op jit(solution)/shard_map/ppermute | solution.py:432
  8.2 0.1 copy.20
  8.3 10.6 %collective-permute-done.1 = bf16[128,1024]{1,0:T(8,128)(2,1)S(1)} collective-permute-done((bf16[128,1024]{1,0:T(8,128)(2,1)}, bf16[128,1024]{1,0:T(8,128)(2,1)S(1)}, u32[]{:S(2)}, u32[]{:S(2)}) %collective-permute-start.1) | collective-permute-done | bytes 262176 | tf_op jit(solution)/shard_map/ppermute | solution.py:432
  18.9 0.7 collective-permute-start.2
  19.6 0.1 pad_add_fusion.meta_ref
  19.7 0.9 gates.1
  20.6 1.4 %collective-permute-start.3 = (bf16[32,1024]{1,0:T(8,128)(2,1)S(1)}, bf16[32,1024]{1,0:T(8,128)(2,1)S(1)}, u32[]{:S(2)}, u32[]{:S(2)}) collective-permute-start(bf16[32,1024]{1,0:T(8,128)(2,1)S(1)} %get-tuple-element.71), channel_id=1, source_target_pairs={{0,2},{1,3},{2,0},{3,1},{4,6},{5,7},{6,4},{7,5},{8,10},{9,11},{10,... | collective-permute-start | bytes 196616 | tf_op jit(solution)/shard_map/ppermute | solution.py:432
  22.0 2.0 %collective-permute-start.4 = (bf16[32,1024]{1,0:T(8,128)(2,1)S(1)}, bf16[32,1024]{1,0:T(8,128)(2,1)S(1)}, u32[]{:S(2)}, u32[]{:S(2)}) collective-permute-start(bf16[32,1024]{1,0:T(8,128)(2,1)S(1)} %get-tuple-element.72), channel_id=1, source_target_pairs={{0,4},{1,5},{2,6},{3,7},{4,0},{5,1},{6,2},{7,3},{8,12},{9,13},{10,... | collective-permute-start | bytes 196616 | tf_op jit(solution)/shard_map/ppermute | solution.py:432
  24.0 1.4 %collective-permute-start.5 = (bf16[32,1024]{1,0:T(8,128)(2,1)S(1)}, bf16[32,1024]{1,0:T(8,128)(2,1)S(1)}, u32[]{:S(2)}, u32[]{:S(2)}) collective-permute-start(bf16[32,1024]{1,0:T(8,128)(2,1)S(1)} %get-tuple-element.73), channel_id=1, source_target_pairs={{0,6},{1,7},{2,4},{3,5},{4,2},{5,3},{6,0},{7,1},{8,14},{9,15},{10,... | collective-permute-start | bytes 196616 | tf_op jit(solution)/shard_map/ppermute | solution.py:432
  25.4 3.7 %collective-permute-done.3 = bf16[32,1024]{1,0:T(8,128)(2,1)S(1)} collective-permute-done((bf16[32,1024]{1,0:T(8,128)(2,1)S(1)}, bf16[32,1024]{1,0:T(8,128)(2,1)S(1)}, u32[]{:S(2)}, u32[]{:S(2)}) %collective-permute-start.3) | collective-permute-done | bytes 65568 | tf_op jit(solution)/shard_map/ppermute | solution.py:432
  29.1 0.0 collective-permute-done.4
  29.1 3.9 %collective-permute-done.5 = bf16[32,1024]{1,0:T(8,128)(2,1)S(1)} collective-permute-done((bf16[32,1024]{1,0:T(8,128)(2,1)S(1)}, bf16[32,1024]{1,0:T(8,128)(2,1)S(1)}, u32[]{:S(2)}, u32[]{:S(2)}) %collective-permute-start.5) | collective-permute-done | bytes 65568 | tf_op jit(solution)/shard_map/ppermute | solution.py:432
  33.0 0.0 collective-permute-done
  33.0 0.0 collective-permute-done.2
  33.1 0.0 copy-start.2
  33.1 0.0 copy-start.8
  33.2 0.1 collective-permute-start.6
  34.0 0.1 add_add_fusion.2
  34.0 0.0 collective-permute-start.7
  34.1 2.3 %collective-permute-start.8 = (bf16[32,4352]{1,0:T(8,128)(2,1)S(1)}, bf16[32,4352]{1,0:T(8,128)(2,1)S(1)}, u32[]{:S(2)}, u32[]{:S(2)}) collective-permute-start(bf16[32,4352]{1,0:T(8,128)(2,1)S(1)} %get-tuple-element.109), channel_id=1, source_target_pairs={{0,4},{1,5},{2,6},{3,7},{4,0},{5,1},{6,2},{7,3},{8,12},{9,13},{10,... | collective-permute-start | bytes 835592 | tf_op jit(solution)/shard_map/ppermute | solution.py:432
  36.4 2.1 %collective-permute-start.9 = (bf16[32,4352]{1,0:T(8,128)(2,1)S(1)}, bf16[32,4352]{1,0:T(8,128)(2,1)S(1)}, u32[]{:S(2)}, u32[]{:S(2)}) collective-permute-start(bf16[32,4352]{1,0:T(8,128)(2,1)S(1)} %get-tuple-element.109), channel_id=1, source_target_pairs={{0,6},{1,7},{2,4},{3,5},{4,2},{5,3},{6,0},{7,1},{8,14},{9,15},{10,... | collective-permute-start | bytes 835592 | tf_op jit(solution)/shard_map/ppermute | solution.py:432
  38.4 0.8 fusion.4
  39.3 0.1 collective-permute-start.10
  39.4 0.0 collective-permute-done.6.refs_1_
  39.4 0.0 copy-start.3
  39.4 1.0 %copy-done.3 = bf16[1,32,8192]{2,1,0:T(8,128)(2,1)S(1)} copy-done((bf16[1,32,8192]{2,1,0:T(8,128)(2,1)S(1)}, bf16[1,32,8192]{2,1,0:T(8,128)(2,1)}, u32[]{:S(2)}) %copy-start.3) | copy-done | bytes 524312
  40.4 1.0 %copy-done.4 = bf16[1,32,8192]{2,1,0:T(8,128)(2,1)S(1)} copy-done((bf16[1,32,8192]{2,1,0:T(8,128)(2,1)S(1)}, bf16[1,32,8192]{2,1,0:T(8,128)(2,1)}, u32[]{:S(2)}) %copy-start.4) | copy-done | bytes 524312
  41.5 9.2 %attend.1 = (bf16[32,8192]{1,0:T(8,128)(2,1)}, f32[128,1024]{1,0:T(8,128)S(1)}, f32[384,1024]{1,0:T(8,128)S(1)}, bf16[128,1024]{1,0:T(8,128)(2,1)S(1)}, bf16[384,1024]{1,0:T(8,128)(2,1)S(1)}) custom-call(s32[9]{0:T(128)S(1)} %get-tuple-element.142.meta_ref, bf16[32,8192]{1,0:T(8,128)(2,1)S(1)} %bitcast.29, bf16[32,8192]{1,0:T(8,128)(2,1)S(1)} %bitcast.30, ...), custom_call_target="tpu_custom_call" | custom-call | flops 11500000256 | bytes 36000000 | tf_op jit(solution)/shard_map/attend/pallas_call | solution.py:169
  50.7 0.0 collective-permute-done.10.refs_3_
  50.7 0.0 collective-permute-done.7
  50.7 5.7 %collective-permute-done.8 = bf16[32,4352]{1,0:T(8,128)(2,1)S(1)} collective-permute-done((bf16[32,4352]{1,0:T(8,128)(2,1)S(1)}, bf16[32,4352]{1,0:T(8,128)(2,1)S(1)}, u32[]{:S(2)}, u32[]{:S(2)}) %collective-permute-start.8) | collective-permute-done | bytes 278560 | tf_op jit(solution)/shard_map/ppermute | solution.py:432
  56.5 0.0 collective-permute-done.9
  56.5 0.0 collective-permute-start.11
  56.5 2.3 %collective-permute-done.11.other_ref = bf16[384,1024]{1,0:T(8,128)(2,1)S(1)} collective-permute-done((bf16[384,1024]{1,0:T(8,128)(2,1)S(1)}, bf16[384,1024]{1,0:T(8,128)(2,1)S(1)}, u32[]{:S(2)}, u32[]{:S(2)}) %collective-permute-start.11) | collective-permute-done | bytes 786464 | tf_op jit(solution)/shard_map/ppermute | solution.py:475
  58.8 0.9 pair_sums.1
  59.8 0.2 collective-permute-start.16
  60.0 0.4 collective-permute-start.12
  60.4 6.1 %collective-permute-start.13 = (bf16[128,512]{1,0:T(8,128)(2,1)}, bf16[128,512]{1,0:T(8,128)(2,1)}, u32[]{:S(2)}, u32[]{:S(2)}) collective-permute-start(bf16[128,512]{1,0:T(8,128)(2,1)} %get-tuple-element.103), channel_id=1, source_target_pairs={{0,2},{1,3},{2,0},{3,1},{4,6},{5,7},{6,4},{7,5},{8,10},{9,11},{10,... | collective-permute-start | bytes 393224 | tf_op jit(solution)/shard_map/ppermute | solution.py:432
  66.5 0.3 collective-permute-start.14
  66.8 2.1 %collective-permute-start.15 = (bf16[128,512]{1,0:T(8,128)(2,1)}, bf16[128,512]{1,0:T(8,128)(2,1)}, u32[]{:S(2)}, u32[]{:S(2)}) collective-permute-start(bf16[128,512]{1,0:T(8,128)(2,1)} %get-tuple-element.105), channel_id=1, source_target_pairs={{0,6},{1,7},{2,4},{3,5},{4,2},{5,3},{6,0},{7,1},{8,14},{9,15},{10,... | collective-permute-start | bytes 393224 | tf_op jit(solution)/shard_map/ppermute | solution.py:432
  68.8 0.0 collective-permute-done.16.refs_1_.refs_3_
  68.9 3.8 %slot_terms.1 = (bf16[384,256]{1,0:T(8,128)(2,1)S(1)}, f32[8,24,128]{2,1,0:T(8,128)}) custom-call(s32[9]{0:T(128)S(1)} %get-tuple-element.141.meta_ref, s32[384,3]{1,0:T(8,128)S(1)} %copy-done.10, s32[1,384]{1,0:T(1,128)S(1)} %copy-done.11, bf16[128,4352]{1,0:T(8,128)(2,1)S(1)} %constant_dynamic-update-slice_fusion.4.refs_0_.refs_2_, ...), custom_call_target="tpu_custom_call" | custom-call | flops 7129999872 | bytes 22320000 | tf_op jit(solution)/shard_map/slot_terms/pallas_call | solution.py:326
  72.7 0.7 copy-done.14
  73.4 3.4 %all-to-all-start = ((f32[8,24,128]{2,1,0:T(8,128)}), f32[8,24,128]{2,1,0:T(8,128)S(1)}, u32[]{:S(2)}, u32[]{:S(2)}) async-start(f32[8,24,128]{2,1,0:T(8,128)} %get-tuple-element.125), calls=%async_computation | async-start | bytes 196608 | tf_op jit(solution)/shard_map/all_to_all | solution.py:527
  76.7 0.0 copy-start.15
  76.7 0.9 copy-done.15
  77.7 2.6 %batch_grad.1 = bf16[384,4096]{1,0:T(8,128)(2,1)} custom-call(bf16[384,256]{1,0:T(8,128)(2,1)S(1)} %copy-done.15, bf16[128,4352]{1,0:T(8,128)(2,1)S(1)} %constant_dynamic-update-slice_fusion.4.refs_0_.refs_2_, bf16[128,4352]{1,0:T(8,128)(2,1)S(1)} %collective-permute-done.16.refs_1_.refs_3_), custom_call_target="tpu_custom_call" | custom-call | flops 5289999872 | bytes 16559999 | tf_op jit(solution)/shard_map/batch_grad/pallas_call | solution.py:364
  80.2 0.0 collective-permute-done.13.refs_0_
  80.2 0.0 collective-permute-done.15.refs_2_
  80.2 2.4 %collective-permute-start.17 = (bf16[128,512]{1,0:T(8,128)(2,1)}, bf16[128,512]{1,0:T(8,128)(2,1)S(1)}, u32[]{:S(2)}, u32[]{:S(2)}) collective-permute-start(bf16[128,512]{1,0:T(8,128)(2,1)} %get-tuple-element.118), channel_id=1, source_target_pairs={{0,2},{1,3},{2,0},{3,1},{4,6},{5,7},{6,4},{7,5},{8,10},{9,11},{10,... | collective-permute-start | bytes 393224 | tf_op jit(solution)/shard_map/ppermute | solution.py:432
  82.6 2.0 %collective-permute-start.18 = (bf16[128,512]{1,0:T(8,128)(2,1)}, bf16[128,512]{1,0:T(8,128)(2,1)S(1)}, u32[]{:S(2)}, u32[]{:S(2)}) collective-permute-start(bf16[128,512]{1,0:T(8,128)(2,1)} %get-tuple-element.119), channel_id=1, source_target_pairs={{0,4},{1,5},{2,6},{3,7},{4,0},{5,1},{6,2},{7,3},{8,12},{9,13},{10,... | collective-permute-start | bytes 393224 | tf_op jit(solution)/shard_map/ppermute | solution.py:432
  84.6 0.7 collective-permute-start.19
  85.3 0.0 all-to-all-done.refs_4_
  85.3 1.1 %router_grad.1 = bf16[512,128]{1,0:T(8,128)(2,1)S(1)} custom-call(s32[9]{0:T(128)S(1)} %get-tuple-element.141.meta_ref, bf16[128,4352]{1,0:T(8,128)(2,1)S(1)} %constant_dynamic-update-slice_fusion.4.refs_0_.refs_2_, bf16[128,4352]{1,0:T(8,128)(2,1)S(1)} %collective-permute-done.16.refs_1_.refs_3_, bf16[128,512]{1,0:T(8,128)(2,1)S(1)} %pad_maximum_fusion.refs_2_, ...), custom_call_target="tpu_custom_call" | custom-call | flops 3449999872 | bytes 10800000 | tf_op jit(solution)/shard_map/router_grad/pallas_call | solution.py:415
  86.5 1.6 %collective-permute-start.20 = (bf16[512,128]{1,0:T(8,128)(2,1)S(1)}, bf16[512,128]{1,0:T(8,128)(2,1)S(1)}, u32[]{:S(2)}, u32[]{:S(2)}) collective-permute-start(bf16[512,128]{1,0:T(8,128)(2,1)S(1)} %router_grad.1), channel_id=1, source_target_pairs={{0,8},{8,0},{16,24},{24,16},{1,9},{9,1},{17,25},{25,17},{2,10},{10... | collective-permute-start | bytes 393224 | tf_op jit(solution)/shard_map/ppermute | solution.py:432
  88.0 1.5 %collective-permute-start.21 = (bf16[512,128]{1,0:T(8,128)(2,1)S(1)}, bf16[512,128]{1,0:T(8,128)(2,1)S(1)}, u32[]{:S(2)}, u32[]{:S(2)}) collective-permute-start(bf16[512,128]{1,0:T(8,128)(2,1)S(1)} %router_grad.1), channel_id=1, source_target_pairs={{0,16},{8,24},{16,0},{24,8},{1,17},{9,25},{17,1},{25,9},{2,18},{10... | collective-permute-start | bytes 393224 | tf_op jit(solution)/shard_map/ppermute | solution.py:432
  89.5 0.0 collective-permute-done.17.refs_3_
  89.5 0.6 collective-permute-start.22
  90.2 5.3 %collective-permute-done.18.refs_4_ = bf16[128,512]{1,0:T(8,128)(2,1)S(1)} collective-permute-done((bf16[128,512]{1,0:T(8,128)(2,1)}, bf16[128,512]{1,0:T(8,128)(2,1)S(1)}, u32[]{:S(2)}, u32[]{:S(2)}) %collective-permute-start.18) | collective-permute-done | bytes 131104 | tf_op jit(solution)/shard_map/ppermute | solution.py:432
  95.6 2.1 %finish_keys.1 = (bf16[128,512]{1,0:T(8,128)(2,1)}, bf16[128,512]{1,0:T(8,128)(2,1)}) custom-call(bf16[128,512]{1,0:T(8,128)(2,1)S(1)} %bitcast.35, f32[1,128]{1,0:T(1,128)S(1)} %bitcast.38, f32[128,1024]{1,0:T(8,128)S(1)} %copy-done.13, bf16[128,1024]{1,0:T(8,128)(2,1)S(1)} %collective-permute-done.12.other_ref, ...), custom_call_target="tpu_custom_call" | custom-call | flops 2529999872 | bytes 7920000 | tf_op jit(solution)/shard_map/finish_keys/pallas_call | solution.py:240
  97.6 0.0 collective-permute-done.20
  97.6 0.8 add_add_fusion
  (47 shorter events, 0.3 us)
Async XLA Ops:
  0.6 7.6 %copy-start.18 = (s32[1,32,8]{1,2,0:T(8,128)S(1)}, s32[1,32,8]{1,2,0:T(8,128)}, u32[]{:S(2)}) copy-start(s32[1,32,8]{1,2,0:T(8,128)} %param.25) | copy-start | bytes 3076
  0.6 19.1 %copy-start.1 = (bf16[4096,128]{1,0:T(8,128)(2,1)S(1)}, bf16[4096,128]{1,0:T(8,128)(2,1)}, u32[]{:S(2)}) copy-start(bf16[4096,128]{1,0:T(8,128)(2,1)} %router_ref.1) | copy-start | bytes 3145732
  0.7 19.1 %copy-start.5 = (bf16[1,32,4096]{2,1,0:T(8,128)(2,1)S(1)}, bf16[1,32,4096]{2,1,0:T(8,128)(2,1)}, u32[]{:S(2)}) copy-start(bf16[1,32,4096]{2,1,0:T(8,128)(2,1)} %param.23) | copy-start | bytes 786436
  0.7 19.0 %copy-start.6 = (bf16[1,32,4096]{2,1,0:T(8,128)(2,1)S(1)}, bf16[1,32,4096]{2,1,0:T(8,128)(2,1)}, u32[]{:S(2)}) copy-start(bf16[1,32,4096]{2,1,0:T(8,128)(2,1)} %param.26) | copy-start | bytes 786436
  2.6 16.3 %collective-permute-start.1 = (bf16[128,1024]{1,0:T(8,128)(2,1)}, bf16[128,1024]{1,0:T(8,128)(2,1)S(1)}, u32[]{:S(2)}, u32[]{:S(2)}) collective-permute-start(bf16[128,1024]{1,0:T(8,128)(2,1)} %pack_keys.1), channel_id=1, source_target_pairs={{0,4},{1,5},{2,6},{3,7},{4,0},{5,1},{6,2},{7,3},{8,12},{9,13},{10,... | collective-permute-start | bytes 786440 | tf_op jit(solution)/shard_map/ppermute | solution.py:432
  6.7 26.4 %collective-permute-start = (bf16[128,1024]{1,0:T(8,128)(2,1)}, bf16[128,1024]{1,0:T(8,128)(2,1)S(1)}, u32[]{:S(2)}, u32[]{:S(2)}) collective-permute-start(bf16[128,1024]{1,0:T(8,128)(2,1)} %pack_keys.1), channel_id=1, source_target_pairs={{0,2},{1,3},{2,0},{3,1},{4,6},{5,7},{6,4},{7,5},{8,10},{9,11},{10,... | collective-permute-start | bytes 786440 | tf_op jit(solution)/shard_map/ppermute | solution.py:432
  18.9 14.1 %collective-permute-start.2 = (bf16[128,1024]{1,0:T(8,128)(2,1)S(1)}, bf16[128,1024]{1,0:T(8,128)(2,1)S(1)}, u32[]{:S(2)}, u32[]{:S(2)}) collective-permute-start(bf16[128,1024]{1,0:T(8,128)(2,1)S(1)} %collective-permute-done.1), channel_id=1, source_target_pairs={{0,2},{1,3},{2,0},{3,1},{4,6},{5,7},{6,4},{7,5},{8,10},{9,11},{10,... | collective-permute-start | bytes 786440 | tf_op jit(solution)/shard_map/ppermute | solution.py:432
  19.7 13.3 %copy-start.16 = (bf16[128,1024]{1,0:T(8,128)(2,1)S(1)}, bf16[128,1024]{1,0:T(8,128)(2,1)}, u32[]{:S(2)}) copy-start(bf16[128,1024]{1,0:T(8,128)(2,1)} %pack_keys.1) | copy-start | bytes 786436
  20.6 8.5 %collective-permute-start.3 = (bf16[32,1024]{1,0:T(8,128)(2,1)S(1)}, bf16[32,1024]{1,0:T(8,128)(2,1)S(1)}, u32[]{:S(2)}, u32[]{:S(2)}) collective-permute-start(bf16[32,1024]{1,0:T(8,128)(2,1)S(1)} %get-tuple-element.71), channel_id=1, source_target_pairs={{0,2},{1,3},{2,0},{3,1},{4,6},{5,7},{6,4},{7,5},{8,10},{9,11},{10,... | collective-permute-start | bytes 196616 | tf_op jit(solution)/shard_map/ppermute | solution.py:432
  22.0 7.1 %collective-permute-start.4 = (bf16[32,1024]{1,0:T(8,128)(2,1)S(1)}, bf16[32,1024]{1,0:T(8,128)(2,1)S(1)}, u32[]{:S(2)}, u32[]{:S(2)}) collective-permute-start(bf16[32,1024]{1,0:T(8,128)(2,1)S(1)} %get-tuple-element.72), channel_id=1, source_target_pairs={{0,4},{1,5},{2,6},{3,7},{4,0},{5,1},{6,2},{7,3},{8,12},{9,13},{10,... | collective-permute-start | bytes 196616 | tf_op jit(solution)/shard_map/ppermute | solution.py:432
  24.0 9.0 %collective-permute-start.5 = (bf16[32,1024]{1,0:T(8,128)(2,1)S(1)}, bf16[32,1024]{1,0:T(8,128)(2,1)S(1)}, u32[]{:S(2)}, u32[]{:S(2)}) collective-permute-start(bf16[32,1024]{1,0:T(8,128)(2,1)S(1)} %get-tuple-element.73), channel_id=1, source_target_pairs={{0,6},{1,7},{2,4},{3,5},{4,2},{5,3},{6,0},{7,1},{8,14},{9,15},{10,... | collective-permute-start | bytes 196616 | tf_op jit(solution)/shard_map/ppermute | solution.py:432
  33.0 3.3 %copy-start.17 = (bf16[32,1024]{1,0:T(8,128)(2,1)}, bf16[32,1024]{1,0:T(8,128)(2,1)S(1)}, u32[]{:S(2)}) copy-start(bf16[32,1024]{1,0:T(8,128)(2,1)S(1)} %collective-permute-done.5) | copy-start | bytes 196612
  33.1 6.3 %copy-start.2 = (bf16[1,32,8192]{2,1,0:T(8,128)(2,1)S(1)}, bf16[1,32,8192]{2,1,0:T(8,128)(2,1)}, u32[]{:S(2)}) copy-start(bf16[1,32,8192]{2,1,0:T(8,128)(2,1)} %param.15) | copy-start | bytes 1572868
  33.1 6.3 %copy-start.8 = (f32[128]{0:T(128)S(1)}, f32[128]{0:T(128)}, u32[]{:S(2)}) copy-start(f32[128]{0:T(128)} %param.20) | copy-start | bytes 1540
  33.2 6.2 %collective-permute-start.6 = (bf16[512,1024]{1,0:T(8,128)(2,1)S(1)}, bf16[512,1024]{1,0:T(8,128)(2,1)S(1)}, u32[]{:S(2)}, u32[]{:S(2)}) collective-permute-start(bf16[512,1024]{1,0:T(8,128)(2,1)S(1)} %constant_dynamic-update-slice_fusion.refs_0_), channel_id=1, source_target_pairs={{0,1},{1,0},{2,3},{3,2},{4,5},{5,4},{6,7},{7,6},{8,9},{9,8},{10,11... | collective-permute-start | bytes 3145736 | tf_op jit(solution)/shard_map/ppermute | solution.py:475
  34.0 16.7 %collective-permute-start.7 = (bf16[32,4352]{1,0:T(8,128)(2,1)S(1)}, bf16[32,4352]{1,0:T(8,128)(2,1)S(1)}, u32[]{:S(2)}, u32[]{:S(2)}) collective-permute-start(bf16[32,4352]{1,0:T(8,128)(2,1)S(1)} %get-tuple-element.109), channel_id=1, source_target_pairs={{0,2},{1,3},{2,0},{3,1},{4,6},{5,7},{6,4},{7,5},{8,10},{9,11},{10,... | collective-permute-start | bytes 835592 | tf_op jit(solution)/shard_map/ppermute | solution.py:432
  34.1 22.4 %collective-permute-start.8 = (bf16[32,4352]{1,0:T(8,128)(2,1)S(1)}, bf16[32,4352]{1,0:T(8,128)(2,1)S(1)}, u32[]{:S(2)}, u32[]{:S(2)}) collective-permute-start(bf16[32,4352]{1,0:T(8,128)(2,1)S(1)} %get-tuple-element.109), channel_id=1, source_target_pairs={{0,4},{1,5},{2,6},{3,7},{4,0},{5,1},{6,2},{7,3},{8,12},{9,13},{10,... | collective-permute-start | bytes 835592 | tf_op jit(solution)/shard_map/ppermute | solution.py:432
  36.4 20.1 %collective-permute-start.9 = (bf16[32,4352]{1,0:T(8,128)(2,1)S(1)}, bf16[32,4352]{1,0:T(8,128)(2,1)S(1)}, u32[]{:S(2)}, u32[]{:S(2)}) collective-permute-start(bf16[32,4352]{1,0:T(8,128)(2,1)S(1)} %get-tuple-element.109), channel_id=1, source_target_pairs={{0,6},{1,7},{2,4},{3,5},{4,2},{5,3},{6,0},{7,1},{8,14},{9,15},{10,... | collective-permute-start | bytes 835592 | tf_op jit(solution)/shard_map/ppermute | solution.py:432
  39.3 11.5 %collective-permute-start.10 = (bf16[128,512]{1,0:T(8,128)(2,1)S(1)}, bf16[128,512]{1,0:T(8,128)(2,1)S(1)}, u32[]{:S(2)}, u32[]{:S(2)}) collective-permute-start(bf16[128,512]{1,0:T(8,128)(2,1)S(1)} %pad_maximum_fusion.1), channel_id=1, source_target_pairs={{0,1},{1,0},{2,3},{3,2},{4,5},{5,4},{6,7},{7,6},{8,9},{9,8},{10,11... | collective-permute-start | bytes 393224 | tf_op jit(solution)/shard_map/ppermute | solution.py:475
  39.4 1.0 %copy-start.3 = (bf16[1,32,8192]{2,1,0:T(8,128)(2,1)S(1)}, bf16[1,32,8192]{2,1,0:T(8,128)(2,1)}, u32[]{:S(2)}) copy-start(bf16[1,32,8192]{2,1,0:T(8,128)(2,1)} %param.16) | copy-start | bytes 1572868
  40.4 1.0 %copy-start.4 = (bf16[1,32,8192]{2,1,0:T(8,128)(2,1)S(1)}, bf16[1,32,8192]{2,1,0:T(8,128)(2,1)}, u32[]{:S(2)}) copy-start(bf16[1,32,8192]{2,1,0:T(8,128)(2,1)} %param.17) | copy-start | bytes 1572868
  50.7 9.0 %copy-start.12 = (f32[128,1024]{1,0:T(8,128)}, f32[128,1024]{1,0:T(8,128)S(1)}, u32[]{:S(2)}) copy-start(f32[128,1024]{1,0:T(8,128)S(1)} %get-tuple-element.88.own_ref) | copy-start | bytes 1572868
  56.5 2.3 %collective-permute-start.11 = (bf16[384,1024]{1,0:T(8,128)(2,1)S(1)}, bf16[384,1024]{1,0:T(8,128)(2,1)S(1)}, u32[]{:S(2)}, u32[]{:S(2)}) collective-permute-start(bf16[384,1024]{1,0:T(8,128)(2,1)S(1)} %get-tuple-element.94), channel_id=1, source_target_pairs={{0,1},{1,0},{2,3},{3,2},{4,5},{5,4},{6,7},{7,6},{8,9},{9,8},{10,11... | collective-permute-start | bytes 2359304 | tf_op jit(solution)/shard_map/ppermute | solution.py:475
  58.8 10.1 %copy-start = (bf16[1,16,8,3,4096]{4,2,3,1,0:T(8,128)(2,1)S(1)}, bf16[1,16,8,3,4096]{4,2,3,1,0:T(8,128)(2,1)}, u32[]{:S(2)}) copy-start(bf16[1,16,8,3,4096]{4,2,3,1,0:T(8,128)(2,1)} %param.27) | copy-start | bytes 9437188
  59.7 9.2 %copy-start.10 = (s32[384,3]{1,0:T(8,128)S(1)}, s32[384,3]{1,0:T(8,128)}, u32[]{:S(2)}) copy-start(s32[384,3]{1,0:T(8,128)} %constant.29.clone.table_ref) | copy-start | bytes 13828
  59.7 9.2 %copy-start.11 = (s32[1,384]{1,0:T(1,128)S(1)}, s32[1,384]{1,0:T(1,128)}, u32[]{:S(2)}) copy-start(s32[1,384]{1,0:T(1,128)} %constant.30.clone.lanes_ref) | copy-start | bytes 4612
  59.8 9.0 %collective-permute-start.16 = (bf16[128,4352]{1,0:T(8,128)(2,1)S(1)}, bf16[128,4352]{1,0:T(8,128)(2,1)S(1)}, u32[]{:S(2)}, u32[]{:S(2)}) collective-permute-start(bf16[128,4352]{1,0:T(8,128)(2,1)S(1)} %constant_dynamic-update-slice_fusion.4.refs_0_.refs_2_), channel_id=1, source_target_pairs={{0,1},{1,0},{2,3},{3,2},{4,5},{5,4},{6,7},{7,6},{8,9},{9,8},{10,11... | collective-permute-start | bytes 3342344 | tf_op jit(solution)/shard_map/ppermute | solution.py:475
  60.0 20.2 %collective-permute-start.12 = (bf16[128,1024]{1,0:T(8,128)(2,1)S(1)}, bf16[128,1024]{1,0:T(8,128)(2,1)S(1)}, u32[]{:S(2)}, u32[]{:S(2)}) collective-permute-start(bf16[128,1024]{1,0:T(8,128)(2,1)S(1)} %get-tuple-element.102), channel_id=1, source_target_pairs={{0,1},{1,0},{2,3},{3,2},{4,5},{5,4},{6,7},{7,6},{8,9},{9,8},{10,11... | collective-permute-start | bytes 786440 | tf_op jit(solution)/shard_map/ppermute | solution.py:475
  60.4 19.8 %collective-permute-start.13 = (bf16[128,512]{1,0:T(8,128)(2,1)}, bf16[128,512]{1,0:T(8,128)(2,1)}, u32[]{:S(2)}, u32[]{:S(2)}) collective-permute-start(bf16[128,512]{1,0:T(8,128)(2,1)} %get-tuple-element.103), channel_id=1, source_target_pairs={{0,2},{1,3},{2,0},{3,1},{4,6},{5,7},{6,4},{7,5},{8,10},{9,11},{10,... | collective-permute-start | bytes 393224 | tf_op jit(solution)/shard_map/ppermute | solution.py:432
  66.5 13.7 %collective-permute-start.14 = (bf16[128,512]{1,0:T(8,128)(2,1)}, bf16[128,512]{1,0:T(8,128)(2,1)}, u32[]{:S(2)}, u32[]{:S(2)}) collective-permute-start(bf16[128,512]{1,0:T(8,128)(2,1)} %get-tuple-element.104), channel_id=1, source_target_pairs={{0,4},{1,5},{2,6},{3,7},{4,0},{5,1},{6,2},{7,3},{8,12},{9,13},{10,... | collective-permute-start | bytes 393224 | tf_op jit(solution)/shard_map/ppermute | solution.py:432
  66.8 13.4 %collective-permute-start.15 = (bf16[128,512]{1,0:T(8,128)(2,1)}, bf16[128,512]{1,0:T(8,128)(2,1)}, u32[]{:S(2)}, u32[]{:S(2)}) collective-permute-start(bf16[128,512]{1,0:T(8,128)(2,1)} %get-tuple-element.105), channel_id=1, source_target_pairs={{0,6},{1,7},{2,4},{3,5},{4,2},{5,3},{6,0},{7,1},{8,14},{9,15},{10,... | collective-permute-start | bytes 393224 | tf_op jit(solution)/shard_map/ppermute | solution.py:432
  72.7 0.7 copy-start.14
  73.4 12.0 %all-to-all-start = ((f32[8,24,128]{2,1,0:T(8,128)}), f32[8,24,128]{2,1,0:T(8,128)S(1)}, u32[]{:S(2)}, u32[]{:S(2)}) async-start(f32[8,24,128]{2,1,0:T(8,128)} %get-tuple-element.125), calls=%async_computation | async-start | bytes 196608 | tf_op jit(solution)/shard_map/all_to_all | solution.py:527
  76.7 0.9 copy-start.15
  80.2 15.3 %copy-start.7 = (bf16[1,128,512]{2,1,0:T(8,128)(2,1)S(1)}, bf16[1,128,512]{2,1,0:T(8,128)(2,1)}, u32[]{:S(2)}) copy-start(bf16[1,128,512]{2,1,0:T(8,128)(2,1)} %param.18) | copy-start | bytes 393220
  80.2 15.3 %copy-start.9 = (f32[128]{0:T(128)S(1)}, f32[128]{0:T(128)}, u32[]{:S(2)}) copy-start(f32[128]{0:T(128)} %param.21) | copy-start | bytes 1540
  80.2 9.3 %collective-permute-start.17 = (bf16[128,512]{1,0:T(8,128)(2,1)}, bf16[128,512]{1,0:T(8,128)(2,1)S(1)}, u32[]{:S(2)}, u32[]{:S(2)}) collective-permute-start(bf16[128,512]{1,0:T(8,128)(2,1)} %get-tuple-element.118), channel_id=1, source_target_pairs={{0,2},{1,3},{2,0},{3,1},{4,6},{5,7},{6,4},{7,5},{8,10},{9,11},{10,... | collective-permute-start | bytes 393224 | tf_op jit(solution)/shard_map/ppermute | solution.py:432
  82.6 12.9 %collective-permute-start.18 = (bf16[128,512]{1,0:T(8,128)(2,1)}, bf16[128,512]{1,0:T(8,128)(2,1)S(1)}, u32[]{:S(2)}, u32[]{:S(2)}) collective-permute-start(bf16[128,512]{1,0:T(8,128)(2,1)} %get-tuple-element.119), channel_id=1, source_target_pairs={{0,4},{1,5},{2,6},{3,7},{4,0},{5,1},{6,2},{7,3},{8,12},{9,13},{10,... | collective-permute-start | bytes 393224 | tf_op jit(solution)/shard_map/ppermute | solution.py:432
  84.6 10.9 %collective-permute-start.19 = (bf16[128,512]{1,0:T(8,128)(2,1)S(1)}, bf16[128,512]{1,0:T(8,128)(2,1)}, u32[]{:S(2)}, u32[]{:S(2)}) collective-permute-start(bf16[128,512]{1,0:T(8,128)(2,1)S(1)} %get-tuple-element.120), channel_id=1, source_target_pairs={{0,6},{1,7},{2,4},{3,5},{4,2},{5,3},{6,0},{7,1},{8,14},{9,15},{10,... | collective-permute-start | bytes 393224 | tf_op jit(solution)/shard_map/ppermute | solution.py:432
  85.3 10.2 %copy-start.13 = (f32[128,1024]{1,0:T(8,128)S(1)}, f32[128,1024]{1,0:T(8,128)}, u32[]{:S(2)}) copy-start(f32[128,1024]{1,0:T(8,128)} %copy-done.12) | copy-start | bytes 1572868
  86.5 11.2 %collective-permute-start.20 = (bf16[512,128]{1,0:T(8,128)(2,1)S(1)}, bf16[512,128]{1,0:T(8,128)(2,1)S(1)}, u32[]{:S(2)}, u32[]{:S(2)}) collective-permute-start(bf16[512,128]{1,0:T(8,128)(2,1)S(1)} %router_grad.1), channel_id=1, source_target_pairs={{0,8},{8,0},{16,24},{24,16},{1,9},{9,1},{17,25},{25,17},{2,10},{10... | collective-permute-start | bytes 393224 | tf_op jit(solution)/shard_map/ppermute | solution.py:432
  88.0 9.6 %collective-permute-start.21 = (bf16[512,128]{1,0:T(8,128)(2,1)S(1)}, bf16[512,128]{1,0:T(8,128)(2,1)S(1)}, u32[]{:S(2)}, u32[]{:S(2)}) collective-permute-start(bf16[512,128]{1,0:T(8,128)(2,1)S(1)} %router_grad.1), channel_id=1, source_target_pairs={{0,16},{8,24},{16,0},{24,8},{1,17},{9,25},{17,1},{25,9},{2,18},{10... | collective-permute-start | bytes 393224 | tf_op jit(solution)/shard_map/ppermute | solution.py:432
  89.5 8.1 %collective-permute-start.22 = (bf16[512,128]{1,0:T(8,128)(2,1)S(1)}, bf16[512,128]{1,0:T(8,128)(2,1)S(1)}, u32[]{:S(2)}, u32[]{:S(2)}) collective-permute-start(bf16[512,128]{1,0:T(8,128)(2,1)S(1)} %router_grad.1), channel_id=1, source_target_pairs={{0,24},{8,16},{16,8},{24,0},{1,25},{9,17},{17,9},{25,1},{2,26},{10... | collective-permute-start | bytes 393224 | tf_op jit(solution)/shard_map/ppermute | solution.py:432

commit v8 on v7

--- a/solution.py
+++ b/solution.py
@@ -214,36 +214,44 @@
     return sums[:blocks], sums[blocks:]
 
 
-def finish_kernel(chips, k_ref, gain_ref, own_ref, other_ref, *refs):
-    first, rest = refs[: chips - 1], refs[chips - 1 : -2]
+def finish_kernel(parts, k_ref, gain_ref, own_ref, other_ref, *refs):
     dk_ref, dv_ref = refs[-2:]
     hd = gain_ref.shape[1]
     gain = gain_ref[...]
-    cut = first[0].shape[1]
+    total = own_ref[...] + other_ref[...].astype(f32)
+    for r in refs[:parts]:
+        total = total + r[...].astype(f32)
     for g in range(k_ref.shape[1] // hd):
-        at = 2 * g * hd
-        total = own_ref[:, at : at + 2 * hd] + other_ref[:, at : at + 2 * hd].astype(f32)
-        parts, start = (first, at) if at < cut else (rest, at - cut)
-        for r in parts:
-            total = total + r[:, start : start + 2 * hd].astype(f32)
         k = k_ref[:, g * hd : (g + 1) * hd].astype(f32)
         inv = lax.rsqrt(jnp.mean(k * k, axis=-1, keepdims=True) + norm_eps)
         unit = k * inv
-        c = total[:, :hd] * gain
+        c = total[:, 2 * g * hd : (2 * g + 1) * hd] * gain
         dk = inv * (c - unit * jnp.mean(c * unit, axis=-1, keepdims=True))
         dk_ref[:, g * hd : (g + 1) * hd] = dk.astype(bf16)
-        dv_ref[:, g * hd : (g + 1) * hd] = total[:, hd:].astype(bf16)
-
-
-def finish_keys(k_pre, k_gain, own, first, rest):
+        dv_ref[:, g * hd : (g + 1) * hd] = total[
+            :, (2 * g + 1) * hd : (2 * g + 2) * hd
+        ].astype(bf16)
+
+
+def finish_keys(k_pre, k_gain, own, parts, half, filled):
+    rows, width = k_pre.shape
+    narrow = pl.BlockSpec((rows, width // 2), lambda i: (0, half))
+    wide = pl.BlockSpec((rows, width), lambda i: (0, half))
     out = jax.ShapeDtypeStruct(k_pre.shape, bf16)
-    return pl.pallas_call(
-        functools.partial(finish_kernel, len(first) + 1),
-        out_shape=(out, out),
+    before = 4 + len(parts)
+    return pl.pallas_call(
+        functools.partial(finish_kernel, len(parts)),
+        grid=(1,),
+        in_specs=[narrow, whole(k_gain.shape), wide, wide]
+        + [whole(p.shape) for p in parts]
+        + [pl.BlockSpec(memory_space=pl.ANY)] * len(filled),
+        out_specs=[narrow, narrow],
+        out_shape=[out, out],
+        input_output_aliases={before + i: i for i in range(len(filled))},
         compiler_params=pltpu.CompilerParams(vmem_limit_bytes=8 * mib),
-        cost_estimate=takes(2.2),
+        cost_estimate=takes(1.2),
         name="finish_keys",
-    )(k_pre, k_gain, *own, *first, *rest)
+    )(k_pre, k_gain, *own, *parts, *filled)
 
 
 def earlier_same_block(rows, block):
@@ -531,8 +539,8 @@
     rest = [to_chip(rest[k - 1], k) for k in range(1, chips)]
     routed = router_grad(slot_meta, packs, (mine, theirs), terms, width, experts, cap, sp)
     routed = sent_over("dp", dp, routed)
-    dk, dv = finish_keys(k_pre[0], kg, [own, own_arrived], first, rest)
-    dk, dv, routed = together(dk, dv, routed)
+    filled = finish_keys(k_pre[0], kg, [own, own_arrived], first, 0, [])
+    dk, dv = finish_keys(k_pre[0], kg, [own, own_arrived], rest, 1, filled)
     batch = jnp.transpose(batch.reshape(experts_here, cap, sp, width), (0, 2, 1, 3))
     return (dq[None], dk[None], dv[None], batch[None], tree_sum(routed))
 

time: 98.9 us -> 97.6 us (0.987)
  starting transfers between devices: 36.9 us -> 32 us
  waiting for transfers between devices: 31.6 us -> 34.5 us
  Pallas kernels: 22.6 us -> 24.1 us
    ppermute x18, starting transfers between devices: 32.8 us -> 28.3 us  [flipped(): return lax.ppermute(x, axis, [(i, i ^ k) for i in range(size)])]
    ppermute x18, waiting for transfers between devices: 29.3 us -> 32.2 us  [flipped(): return lax.ppermute(x, axis, [(i, i ^ k) for i in range(size)])]
    pallas_call x1 -> x2, Pallas kernels: 2.06 us -> 3.64 us  [finish_keys(): pl.pallas_call(functools.partial(finish_kernel, len(parts)), grid=(1,), i...]
    unnamed x45 -> x43, local copies, waits for them, and re-layouts: 3.93 us -> 3.93 us
  transfers between devices with their start and end apart: 24 -> 24, of which waited for: 6 -> 6; matrix products, arithmetic and copies ran while one was open for 1% -> 0% of each run, Pallas kernels for 20% -> 22%
where the time goes in v8:
time: 97.6 us; the launch traced here: 97.2 us
  waiting for transfers between devices  34.5 us (35%)
  starting transfers between devices  32 us (33%)
  Pallas kernels  24.1 us (25%)
  local copies, waits for them, and re-layouts  3.99 us (4%)
  between operations  1.63 us (2%)
    ppermute x18, waiting for transfers between devices, flipped(): return lax.ppermute(x, axis, [(i, i ^ k) for i in range(size)])  32.2 us
    ppermute x18, starting transfers between devices, flipped(): return lax.ppermute(x, axis, [(i, i ^ k) for i in range(size)])  28.3 us
    pallas_call x1, Pallas kernels, attend(): pl.pallas_call(functools.partial(attend_kernel, blocks), grid_spec=pltpu....  9.23 us
    unnamed x43, local copies, waits for them, and re-layouts  3.93 us
    pallas_call x1, Pallas kernels, slot_terms(): pl.pallas_call(functools.partial(terms_kernel, blocks, sp, cap), grid_spe...  3.81 us
    pallas_call x2, Pallas kernels, finish_keys(): pl.pallas_call(functools.partial(finish_kernel, len(parts)), grid=(1,), i...  3.64 us
    all_to_all x1, starting transfers between devices, on_device(): terms = lax.all_to_all(terms, 'sp', split_axis=0, concat_axis=0, tiled=True)  3.36 us
    pallas_call x1, Pallas kernels, batch_grad(): pl.pallas_call(batch_kernel, grid=(width // col,), in_specs=[whole((rows,...  2.56 us
  transfers between devices with their start and end apart: 24, of which 6 were waited for; matrix products, arithmetic and copies ran while one was open for 0% of the time, Pallas kernels for 22%

profile of v8, /device:TPU:0, one launch (start us, length us, event | category | flops | bytes accessed | tf_op | source)
XLA Modules:
  0.0 97.2 jit_solution(3067116093740638329)
XLA Ops:
  0.7 2.0 %pack_keys.1 = bf16[128,1024]{1,0:T(8,128)(2,1)} custom-call(bf16[128,512]{1,0:T(8,128)(2,1)} %bitcast.34, bf16[128,512]{1,0:T(8,128)(2,1)} %bitcast.41, f32[1,128]{1,0:T(1,128)} %bitcast.38), custom_call_target="tpu_custom_call" | custom-call | flops 2070000000 | bytes 6480000 | tf_op jit(solution)/shard_map/pack_keys/pallas_call | solution.py:51
  2.6 4.0 %collective-permute-start.1 = (bf16[128,1024]{1,0:T(8,128)(2,1)}, bf16[128,1024]{1,0:T(8,128)(2,1)S(1)}, u32[]{:S(2)}, u32[]{:S(2)}) collective-permute-start(bf16[128,1024]{1,0:T(8,128)(2,1)} %pack_keys.1), channel_id=1, source_target_pairs={{0,4},{1,5},{2,6},{3,7},{4,0},{5,1},{6,2},{7,3},{8,12},{9,13},{10,... | collective-permute-start | bytes 786440 | tf_op jit(solution)/shard_map/ppermute | solution.py:440
  6.7 1.6 %collective-permute-start = (bf16[128,1024]{1,0:T(8,128)(2,1)}, bf16[128,1024]{1,0:T(8,128)(2,1)S(1)}, u32[]{:S(2)}, u32[]{:S(2)}) collective-permute-start(bf16[128,1024]{1,0:T(8,128)(2,1)} %pack_keys.1), channel_id=1, source_target_pairs={{0,2},{1,3},{2,0},{3,1},{4,6},{5,7},{6,4},{7,5},{8,10},{9,11},{10,... | collective-permute-start | bytes 786440 | tf_op jit(solution)/shard_map/ppermute | solution.py:440
  8.2 0.1 copy.22
  8.3 10.6 %collective-permute-done.1 = bf16[128,1024]{1,0:T(8,128)(2,1)S(1)} collective-permute-done((bf16[128,1024]{1,0:T(8,128)(2,1)}, bf16[128,1024]{1,0:T(8,128)(2,1)S(1)}, u32[]{:S(2)}, u32[]{:S(2)}) %collective-permute-start.1) | collective-permute-done | bytes 262176 | tf_op jit(solution)/shard_map/ppermute | solution.py:440
  18.9 0.7 collective-permute-start.2
  19.6 0.1 pad_add_fusion.meta_ref
  19.7 0.9 gates.1
  20.6 1.4 %collective-permute-start.3 = (bf16[32,1024]{1,0:T(8,128)(2,1)S(1)}, bf16[32,1024]{1,0:T(8,128)(2,1)S(1)}, u32[]{:S(2)}, u32[]{:S(2)}) collective-permute-start(bf16[32,1024]{1,0:T(8,128)(2,1)S(1)} %get-tuple-element.67), channel_id=1, source_target_pairs={{0,2},{1,3},{2,0},{3,1},{4,6},{5,7},{6,4},{7,5},{8,10},{9,11},{10,... | collective-permute-start | bytes 196616 | tf_op jit(solution)/shard_map/ppermute | solution.py:440
  22.0 2.0 %collective-permute-start.4 = (bf16[32,1024]{1,0:T(8,128)(2,1)S(1)}, bf16[32,1024]{1,0:T(8,128)(2,1)S(1)}, u32[]{:S(2)}, u32[]{:S(2)}) collective-permute-start(bf16[32,1024]{1,0:T(8,128)(2,1)S(1)} %get-tuple-element.68), channel_id=1, source_target_pairs={{0,4},{1,5},{2,6},{3,7},{4,0},{5,1},{6,2},{7,3},{8,12},{9,13},{10,... | collective-permute-start | bytes 196616 | tf_op jit(solution)/shard_map/ppermute | solution.py:440
  24.0 1.4 %collective-permute-start.5 = (bf16[32,1024]{1,0:T(8,128)(2,1)S(1)}, bf16[32,1024]{1,0:T(8,128)(2,1)S(1)}, u32[]{:S(2)}, u32[]{:S(2)}) collective-permute-start(bf16[32,1024]{1,0:T(8,128)(2,1)S(1)} %get-tuple-element.69), channel_id=1, source_target_pairs={{0,6},{1,7},{2,4},{3,5},{4,2},{5,3},{6,0},{7,1},{8,14},{9,15},{10,... | collective-permute-start | bytes 196616 | tf_op jit(solution)/shard_map/ppermute | solution.py:440
  25.4 3.7 %collective-permute-done.3 = bf16[32,1024]{1,0:T(8,128)(2,1)S(1)} collective-permute-done((bf16[32,1024]{1,0:T(8,128)(2,1)S(1)}, bf16[32,1024]{1,0:T(8,128)(2,1)S(1)}, u32[]{:S(2)}, u32[]{:S(2)}) %collective-permute-start.3) | collective-permute-done | bytes 65568 | tf_op jit(solution)/shard_map/ppermute | solution.py:440
  29.1 0.0 collective-permute-done.4
  29.1 3.9 %collective-permute-done.5 = bf16[32,1024]{1,0:T(8,128)(2,1)S(1)} collective-permute-done((bf16[32,1024]{1,0:T(8,128)(2,1)S(1)}, bf16[32,1024]{1,0:T(8,128)(2,1)S(1)}, u32[]{:S(2)}, u32[]{:S(2)}) %collective-permute-start.5) | collective-permute-done | bytes 65568 | tf_op jit(solution)/shard_map/ppermute | solution.py:440
  33.0 0.0 collective-permute-done
  33.0 0.0 collective-permute-done.2
  33.1 0.0 copy-start.2
  33.1 0.0 copy-start.8
  33.2 0.1 collective-permute-start.6
  34.0 0.1 add_add_fusion.2
  34.0 1.8 %collective-permute-start.9 = (bf16[32,4352]{1,0:T(8,128)(2,1)S(1)}, bf16[32,4352]{1,0:T(8,128)(2,1)S(1)}, u32[]{:S(2)}, u32[]{:S(2)}) collective-permute-start(bf16[32,4352]{1,0:T(8,128)(2,1)S(1)} %get-tuple-element.105), channel_id=1, source_target_pairs={{0,6},{1,7},{2,4},{3,5},{4,2},{5,3},{6,0},{7,1},{8,14},{9,15},{10,... | collective-permute-start | bytes 835592 | tf_op jit(solution)/shard_map/ppermute | solution.py:440
  35.8 0.0 collective-permute-start.8
  35.8 2.6 %collective-permute-start.7 = (bf16[32,4352]{1,0:T(8,128)(2,1)S(1)}, bf16[32,4352]{1,0:T(8,128)(2,1)S(1)}, u32[]{:S(2)}, u32[]{:S(2)}) collective-permute-start(bf16[32,4352]{1,0:T(8,128)(2,1)S(1)} %get-tuple-element.105), channel_id=1, source_target_pairs={{0,2},{1,3},{2,0},{3,1},{4,6},{5,7},{6,4},{7,5},{8,10},{9,11},{10,... | collective-permute-start | bytes 835592 | tf_op jit(solution)/shard_map/ppermute | solution.py:440
  38.5 0.1 collective-permute-start.10
  38.6 0.0 collective-permute-done.6.refs_1_
  38.6 0.0 copy-start.3
  38.6 1.0 %copy-done.3 = bf16[1,32,8192]{2,1,0:T(8,128)(2,1)S(1)} copy-done((bf16[1,32,8192]{2,1,0:T(8,128)(2,1)S(1)}, bf16[1,32,8192]{2,1,0:T(8,128)(2,1)}, u32[]{:S(2)}) %copy-start.3) | copy-done | bytes 524312
  39.7 1.0 %copy-done.4 = bf16[1,32,8192]{2,1,0:T(8,128)(2,1)S(1)} copy-done((bf16[1,32,8192]{2,1,0:T(8,128)(2,1)S(1)}, bf16[1,32,8192]{2,1,0:T(8,128)(2,1)}, u32[]{:S(2)}) %copy-start.4) | copy-done | bytes 524312
  40.7 9.2 %attend.1 = (bf16[32,8192]{1,0:T(8,128)(2,1)}, f32[128,1024]{1,0:T(8,128)S(1)}, f32[384,1024]{1,0:T(8,128)S(1)}, bf16[128,1024]{1,0:T(8,128)(2,1)S(1)}, bf16[384,1024]{1,0:T(8,128)(2,1)S(1)}) custom-call(s32[9]{0:T(128)S(1)} %get-tuple-element.134.meta_ref, bf16[32,8192]{1,0:T(8,128)(2,1)S(1)} %bitcast.29, bf16[32,8192]{1,0:T(8,128)(2,1)S(1)} %bitcast.30, ...), custom_call_target="tpu_custom_call" | custom-call | flops 11500000256 | bytes 36000000 | tf_op jit(solution)/shard_map/attend/pallas_call | solution.py:169
  49.9 0.0 collective-permute-done.10.refs_3_
  49.9 0.0 collective-permute-done.9
  49.9 10.3 %collective-permute-done.8 = bf16[32,4352]{1,0:T(8,128)(2,1)S(1)} collective-permute-done((bf16[32,4352]{1,0:T(8,128)(2,1)S(1)}, bf16[32,4352]{1,0:T(8,128)(2,1)S(1)}, u32[]{:S(2)}, u32[]{:S(2)}) %collective-permute-start.8) | collective-permute-done | bytes 278560 | tf_op jit(solution)/shard_map/ppermute | solution.py:440
  60.2 0.0 collective-permute-done.7
  60.2 0.0 collective-permute-start.11
  60.2 2.3 %collective-permute-done.11.other_ref = bf16[384,1024]{1,0:T(8,128)(2,1)S(1)} collective-permute-done((bf16[384,1024]{1,0:T(8,128)(2,1)S(1)}, bf16[384,1024]{1,0:T(8,128)(2,1)S(1)}, u32[]{:S(2)}, u32[]{:S(2)}) %collective-permute-start.11) | collective-permute-done | bytes 786464 | tf_op jit(solution)/shard_map/ppermute | solution.py:483
  62.5 0.9 pair_sums.1
  63.5 0.2 collective-permute-start.16
  63.7 0.0 collective-permute-start.13
  63.7 2.4 %collective-permute-start.14 = (bf16[128,512]{1,0:T(8,128)(2,1)}, bf16[128,512]{1,0:T(8,128)(2,1)}, u32[]{:S(2)}, u32[]{:S(2)}) collective-permute-start(bf16[128,512]{1,0:T(8,128)(2,1)} %get-tuple-element.100), channel_id=1, source_target_pairs={{0,4},{1,5},{2,6},{3,7},{4,0},{5,1},{6,2},{7,3},{8,12},{9,13},{10,... | collective-permute-start | bytes 393224 | tf_op jit(solution)/shard_map/ppermute | solution.py:440
  66.2 2.0 %collective-permute-start.15 = (bf16[128,512]{1,0:T(8,128)(2,1)}, bf16[128,512]{1,0:T(8,128)(2,1)}, u32[]{:S(2)}, u32[]{:S(2)}) collective-permute-start(bf16[128,512]{1,0:T(8,128)(2,1)} %get-tuple-element.101), channel_id=1, source_target_pairs={{0,6},{1,7},{2,4},{3,5},{4,2},{5,3},{6,0},{7,1},{8,14},{9,15},{10,... | collective-permute-start | bytes 393224 | tf_op jit(solution)/shard_map/ppermute | solution.py:440
  68.1 0.0 collective-permute-done.16.refs_1_.refs_3_
  68.2 3.8 %slot_terms.1 = (bf16[384,256]{1,0:T(8,128)(2,1)S(1)}, f32[8,24,128]{2,1,0:T(8,128)}) custom-call(s32[9]{0:T(128)S(1)} %get-tuple-element.133.meta_ref, s32[384,3]{1,0:T(8,128)S(1)} %copy-done.10, s32[1,384]{1,0:T(1,128)S(1)} %copy-done.11, bf16[128,4352]{1,0:T(8,128)(2,1)S(1)} %constant_dynamic-update-slice_fusion.4.refs_0_.refs_2_, ...), custom_call_target="tpu_custom_call" | custom-call | flops 7129999872 | bytes 22320000 | tf_op jit(solution)/shard_map/slot_terms/pallas_call | solution.py:334
  72.0 0.7 copy-done.14
  72.7 3.4 %all-to-all-start = ((f32[8,24,128]{2,1,0:T(8,128)}), f32[8,24,128]{2,1,0:T(8,128)S(1)}, u32[]{:S(2)}, u32[]{:S(2)}) async-start(f32[8,24,128]{2,1,0:T(8,128)} %get-tuple-element.124), calls=%async_computation | async-start | bytes 196608 | tf_op jit(solution)/shard_map/all_to_all | solution.py:535
  76.0 0.0 copy-start.15
  76.0 0.9 copy-done.15
  77.0 2.6 %batch_grad.1 = bf16[384,4096]{1,0:T(8,128)(2,1)} custom-call(bf16[384,256]{1,0:T(8,128)(2,1)S(1)} %copy-done.15, bf16[128,4352]{1,0:T(8,128)(2,1)S(1)} %constant_dynamic-update-slice_fusion.4.refs_0_.refs_2_, bf16[128,4352]{1,0:T(8,128)(2,1)S(1)} %collective-permute-done.16.refs_1_.refs_3_), custom_call_target="tpu_custom_call" | custom-call | flops 5289999872 | bytes 16559999 | tf_op jit(solution)/shard_map/batch_grad/pallas_call | solution.py:372
  79.5 0.0 collective-permute-done.13.refs_0_
  79.5 0.0 collective-permute-done.14.refs_1_
  79.6 2.0 %collective-permute-start.17 = (bf16[128,512]{1,0:T(8,128)(2,1)}, bf16[128,512]{1,0:T(8,128)(2,1)S(1)}, u32[]{:S(2)}, u32[]{:S(2)}) collective-permute-start(bf16[128,512]{1,0:T(8,128)(2,1)} %get-tuple-element.111), channel_id=1, source_target_pairs={{0,2},{1,3},{2,0},{3,1},{4,6},{5,7},{6,4},{7,5},{8,10},{9,11},{10,... | collective-permute-start | bytes 393224 | tf_op jit(solution)/shard_map/ppermute | solution.py:440
  81.5 2.4 %collective-permute-start.18 = (bf16[128,512]{1,0:T(8,128)(2,1)}, bf16[128,512]{1,0:T(8,128)(2,1)S(1)}, u32[]{:S(2)}, u32[]{:S(2)}) collective-permute-start(bf16[128,512]{1,0:T(8,128)(2,1)} %get-tuple-element.112), channel_id=1, source_target_pairs={{0,4},{1,5},{2,6},{3,7},{4,0},{5,1},{6,2},{7,3},{8,12},{9,13},{10,... | collective-permute-start | bytes 393224 | tf_op jit(solution)/shard_map/ppermute | solution.py:440
  83.9 0.1 collective-permute-start.19
  84.0 0.0 all-to-all-done.refs_4_
  84.0 1.1 %router_grad.1 = bf16[512,128]{1,0:T(8,128)(2,1)S(1)} custom-call(s32[9]{0:T(128)S(1)} %get-tuple-element.133.meta_ref, bf16[128,4352]{1,0:T(8,128)(2,1)S(1)} %constant_dynamic-update-slice_fusion.4.refs_0_.refs_2_, bf16[128,4352]{1,0:T(8,128)(2,1)S(1)} %collective-permute-done.16.refs_1_.refs_3_, bf16[128,512]{1,0:T(8,128)(2,1)S(1)} %pad_maximum_fusion.refs_2_, ...), custom_call_target="tpu_custom_call" | custom-call | flops 3449999872 | bytes 10800000 | tf_op jit(solution)/shard_map/router_grad/pallas_call | solution.py:423
  85.1 2.5 %collective-permute-start.22 = (bf16[512,128]{1,0:T(8,128)(2,1)S(1)}, bf16[512,128]{1,0:T(8,128)(2,1)S(1)}, u32[]{:S(2)}, u32[]{:S(2)}) collective-permute-start(bf16[512,128]{1,0:T(8,128)(2,1)S(1)} %router_grad.1), channel_id=1, source_target_pairs={{0,24},{8,16},{16,8},{24,0},{1,25},{9,17},{17,9},{25,1},{2,26},{10... | collective-permute-start | bytes 393224 | tf_op jit(solution)/shard_map/ppermute | solution.py:440
  87.6 0.5 collective-permute-start.21
  88.2 0.9 collective-permute-start.20
  89.1 1.9 %finish_keys.2 = (bf16[128,512]{1,0:T(8,128)(2,1)}, bf16[128,512]{1,0:T(8,128)(2,1)}) custom-call(bf16[128,512]{1,0:T(8,128)(2,1)S(1)} %bitcast.35, f32[1,128]{1,0:T(1,128)S(1)} %bitcast.39, f32[128,1024]{1,0:T(8,128)S(1)} %copy-done.13, bf16[128,1024]{1,0:T(8,128)(2,1)S(1)} %collective-permute-done.12.other_ref, ...), custom_call_target="tpu_custom_call" | custom-call | flops 1380000000 | bytes 4320000 | tf_op jit(solution)/shard_map/finish_keys/pallas_call | solution.py:242
  91.0 3.7 %collective-permute-done.18.refs_1_ = bf16[128,512]{1,0:T(8,128)(2,1)S(1)} collective-permute-done((bf16[128,512]{1,0:T(8,128)(2,1)}, bf16[128,512]{1,0:T(8,128)(2,1)S(1)}, u32[]{:S(2)}, u32[]{:S(2)}) %collective-permute-start.18) | collective-permute-done | bytes 131104 | tf_op jit(solution)/shard_map/ppermute | solution.py:440
  94.6 0.0 collective-permute-done.19.refs_2_
  94.6 1.8 %finish_keys.3 = (bf16[128,512]{1,0:T(8,128)(2,1)}, bf16[128,512]{1,0:T(8,128)(2,1)}) custom-call(bf16[128,512]{1,0:T(8,128)(2,1)S(1)} %bitcast.36, f32[1,128]{1,0:T(1,128)S(1)} %bitcast.40, f32[128,1024]{1,0:T(8,128)S(1)} %copy-done.13, bf16[128,1024]{1,0:T(8,128)(2,1)S(1)} %collective-permute-done.12.other_ref, ...), custom_call_target="tpu_custom_call", output_to_operand_aliasing={{0}: (7, {}), {1}: (8, {})} | custom-call | flops 1380000000 | bytes 4320000 | tf_op jit(solution)/shard_map/finish_keys/pallas_call | solution.py:242
  96.4 0.0 collective-permute-done.22
  96.4 0.0 collective-permute-done.21
  96.4 0.8 add_add_fusion
  (46 shorter events, 0.3 us)
Async XLA Ops:
  0.6 7.6 %copy-start.17 = (s32[1,32,8]{1,2,0:T(8,128)S(1)}, s32[1,32,8]{1,2,0:T(8,128)}, u32[]{:S(2)}) copy-start(s32[1,32,8]{1,2,0:T(8,128)} %param.25) | copy-start | bytes 3076
  0.6 19.1 %copy-start.1 = (bf16[4096,128]{1,0:T(8,128)(2,1)S(1)}, bf16[4096,128]{1,0:T(8,128)(2,1)}, u32[]{:S(2)}) copy-start(bf16[4096,128]{1,0:T(8,128)(2,1)} %router_ref.1) | copy-start | bytes 3145732
  0.7 19.1 %copy-start.5 = (bf16[1,32,4096]{2,1,0:T(8,128)(2,1)S(1)}, bf16[1,32,4096]{2,1,0:T(8,128)(2,1)}, u32[]{:S(2)}) copy-start(bf16[1,32,4096]{2,1,0:T(8,128)(2,1)} %param.23) | copy-start | bytes 786436
  0.7 19.0 %copy-start.6 = (bf16[1,32,4096]{2,1,0:T(8,128)(2,1)S(1)}, bf16[1,32,4096]{2,1,0:T(8,128)(2,1)}, u32[]{:S(2)}) copy-start(bf16[1,32,4096]{2,1,0:T(8,128)(2,1)} %param.26) | copy-start | bytes 786436
  2.6 16.3 %collective-permute-start.1 = (bf16[128,1024]{1,0:T(8,128)(2,1)}, bf16[128,1024]{1,0:T(8,128)(2,1)S(1)}, u32[]{:S(2)}, u32[]{:S(2)}) collective-permute-start(bf16[128,1024]{1,0:T(8,128)(2,1)} %pack_keys.1), channel_id=1, source_target_pairs={{0,4},{1,5},{2,6},{3,7},{4,0},{5,1},{6,2},{7,3},{8,12},{9,13},{10,... | collective-permute-start | bytes 786440 | tf_op jit(solution)/shard_map/ppermute | solution.py:440
  6.7 26.4 %collective-permute-start = (bf16[128,1024]{1,0:T(8,128)(2,1)}, bf16[128,1024]{1,0:T(8,128)(2,1)S(1)}, u32[]{:S(2)}, u32[]{:S(2)}) collective-permute-start(bf16[128,1024]{1,0:T(8,128)(2,1)} %pack_keys.1), channel_id=1, source_target_pairs={{0,2},{1,3},{2,0},{3,1},{4,6},{5,7},{6,4},{7,5},{8,10},{9,11},{10,... | collective-permute-start | bytes 786440 | tf_op jit(solution)/shard_map/ppermute | solution.py:440
  18.9 14.1 %collective-permute-start.2 = (bf16[128,1024]{1,0:T(8,128)(2,1)S(1)}, bf16[128,1024]{1,0:T(8,128)(2,1)S(1)}, u32[]{:S(2)}, u32[]{:S(2)}) collective-permute-start(bf16[128,1024]{1,0:T(8,128)(2,1)S(1)} %collective-permute-done.1), channel_id=1, source_target_pairs={{0,2},{1,3},{2,0},{3,1},{4,6},{5,7},{6,4},{7,5},{8,10},{9,11},{10,... | collective-permute-start | bytes 786440 | tf_op jit(solution)/shard_map/ppermute | solution.py:440
  19.7 13.3 %copy-start.16 = (bf16[128,1024]{1,0:T(8,128)(2,1)S(1)}, bf16[128,1024]{1,0:T(8,128)(2,1)}, u32[]{:S(2)}) copy-start(bf16[128,1024]{1,0:T(8,128)(2,1)} %pack_keys.1) | copy-start | bytes 786436
  20.6 8.5 %collective-permute-start.3 = (bf16[32,1024]{1,0:T(8,128)(2,1)S(1)}, bf16[32,1024]{1,0:T(8,128)(2,1)S(1)}, u32[]{:S(2)}, u32[]{:S(2)}) collective-permute-start(bf16[32,1024]{1,0:T(8,128)(2,1)S(1)} %get-tuple-element.67), channel_id=1, source_target_pairs={{0,2},{1,3},{2,0},{3,1},{4,6},{5,7},{6,4},{7,5},{8,10},{9,11},{10,... | collective-permute-start | bytes 196616 | tf_op jit(solution)/shard_map/ppermute | solution.py:440
  22.0 7.1 %collective-permute-start.4 = (bf16[32,1024]{1,0:T(8,128)(2,1)S(1)}, bf16[32,1024]{1,0:T(8,128)(2,1)S(1)}, u32[]{:S(2)}, u32[]{:S(2)}) collective-permute-start(bf16[32,1024]{1,0:T(8,128)(2,1)S(1)} %get-tuple-element.68), channel_id=1, source_target_pairs={{0,4},{1,5},{2,6},{3,7},{4,0},{5,1},{6,2},{7,3},{8,12},{9,13},{10,... | collective-permute-start | bytes 196616 | tf_op jit(solution)/shard_map/ppermute | solution.py:440
  24.0 9.0 %collective-permute-start.5 = (bf16[32,1024]{1,0:T(8,128)(2,1)S(1)}, bf16[32,1024]{1,0:T(8,128)(2,1)S(1)}, u32[]{:S(2)}, u32[]{:S(2)}) collective-permute-start(bf16[32,1024]{1,0:T(8,128)(2,1)S(1)} %get-tuple-element.69), channel_id=1, source_target_pairs={{0,6},{1,7},{2,4},{3,5},{4,2},{5,3},{6,0},{7,1},{8,14},{9,15},{10,... | collective-permute-start | bytes 196616 | tf_op jit(solution)/shard_map/ppermute | solution.py:440
  33.1 5.5 %copy-start.2 = (bf16[1,32,8192]{2,1,0:T(8,128)(2,1)S(1)}, bf16[1,32,8192]{2,1,0:T(8,128)(2,1)}, u32[]{:S(2)}) copy-start(bf16[1,32,8192]{2,1,0:T(8,128)(2,1)} %param.15) | copy-start | bytes 1572868
  33.1 5.5 %copy-start.8 = (f32[128]{0:T(128)S(1)}, f32[128]{0:T(128)}, u32[]{:S(2)}) copy-start(f32[128]{0:T(128)} %param.20) | copy-start | bytes 1540
  33.2 5.4 %collective-permute-start.6 = (bf16[512,1024]{1,0:T(8,128)(2,1)S(1)}, bf16[512,1024]{1,0:T(8,128)(2,1)S(1)}, u32[]{:S(2)}, u32[]{:S(2)}) collective-permute-start(bf16[512,1024]{1,0:T(8,128)(2,1)S(1)} %constant_dynamic-update-slice_fusion.refs_0_), channel_id=1, source_target_pairs={{0,1},{1,0},{2,3},{3,2},{4,5},{5,4},{6,7},{7,6},{8,9},{9,8},{10,11... | collective-permute-start | bytes 3145736 | tf_op jit(solution)/shard_map/ppermute | solution.py:483
  34.0 15.9 %collective-permute-start.9 = (bf16[32,4352]{1,0:T(8,128)(2,1)S(1)}, bf16[32,4352]{1,0:T(8,128)(2,1)S(1)}, u32[]{:S(2)}, u32[]{:S(2)}) collective-permute-start(bf16[32,4352]{1,0:T(8,128)(2,1)S(1)} %get-tuple-element.105), channel_id=1, source_target_pairs={{0,6},{1,7},{2,4},{3,5},{4,2},{5,3},{6,0},{7,1},{8,14},{9,15},{10,... | collective-permute-start | bytes 835592 | tf_op jit(solution)/shard_map/ppermute | solution.py:440
  35.8 24.4 %collective-permute-start.8 = (bf16[32,4352]{1,0:T(8,128)(2,1)S(1)}, bf16[32,4352]{1,0:T(8,128)(2,1)S(1)}, u32[]{:S(2)}, u32[]{:S(2)}) collective-permute-start(bf16[32,4352]{1,0:T(8,128)(2,1)S(1)} %get-tuple-element.105), channel_id=1, source_target_pairs={{0,4},{1,5},{2,6},{3,7},{4,0},{5,1},{6,2},{7,3},{8,12},{9,13},{10,... | collective-permute-start | bytes 835592 | tf_op jit(solution)/shard_map/ppermute | solution.py:440
  35.8 24.4 %collective-permute-start.7 = (bf16[32,4352]{1,0:T(8,128)(2,1)S(1)}, bf16[32,4352]{1,0:T(8,128)(2,1)S(1)}, u32[]{:S(2)}, u32[]{:S(2)}) collective-permute-start(bf16[32,4352]{1,0:T(8,128)(2,1)S(1)} %get-tuple-element.105), channel_id=1, source_target_pairs={{0,2},{1,3},{2,0},{3,1},{4,6},{5,7},{6,4},{7,5},{8,10},{9,11},{10,... | collective-permute-start | bytes 835592 | tf_op jit(solution)/shard_map/ppermute | solution.py:440
  38.5 11.5 %collective-permute-start.10 = (bf16[128,512]{1,0:T(8,128)(2,1)S(1)}, bf16[128,512]{1,0:T(8,128)(2,1)S(1)}, u32[]{:S(2)}, u32[]{:S(2)}) collective-permute-start(bf16[128,512]{1,0:T(8,128)(2,1)S(1)} %pad_maximum_fusion.1), channel_id=1, source_target_pairs={{0,1},{1,0},{2,3},{3,2},{4,5},{5,4},{6,7},{7,6},{8,9},{9,8},{10,11... | collective-permute-start | bytes 393224 | tf_op jit(solution)/shard_map/ppermute | solution.py:483
  38.6 1.0 %copy-start.3 = (bf16[1,32,8192]{2,1,0:T(8,128)(2,1)S(1)}, bf16[1,32,8192]{2,1,0:T(8,128)(2,1)}, u32[]{:S(2)}) copy-start(bf16[1,32,8192]{2,1,0:T(8,128)(2,1)} %param.16) | copy-start | bytes 1572868
  39.7 1.0 %copy-start.4 = (bf16[1,32,8192]{2,1,0:T(8,128)(2,1)S(1)}, bf16[1,32,8192]{2,1,0:T(8,128)(2,1)}, u32[]{:S(2)}) copy-start(bf16[1,32,8192]{2,1,0:T(8,128)(2,1)} %param.17) | copy-start | bytes 1572868
  49.9 13.5 %copy-start.12 = (f32[128,1024]{1,0:T(8,128)}, f32[128,1024]{1,0:T(8,128)S(1)}, u32[]{:S(2)}) copy-start(f32[128,1024]{1,0:T(8,128)S(1)} %get-tuple-element.84.own_ref) | copy-start | bytes 1572868
  60.2 2.3 %collective-permute-start.11 = (bf16[384,1024]{1,0:T(8,128)(2,1)S(1)}, bf16[384,1024]{1,0:T(8,128)(2,1)S(1)}, u32[]{:S(2)}, u32[]{:S(2)}) collective-permute-start(bf16[384,1024]{1,0:T(8,128)(2,1)S(1)} %get-tuple-element.90), channel_id=1, source_target_pairs={{0,1},{1,0},{2,3},{3,2},{4,5},{5,4},{6,7},{7,6},{8,9},{9,8},{10,11... | collective-permute-start | bytes 2359304 | tf_op jit(solution)/shard_map/ppermute | solution.py:483
  62.5 5.7 %copy-start = (bf16[1,16,8,3,4096]{4,2,3,1,0:T(8,128)(2,1)S(1)}, bf16[1,16,8,3,4096]{4,2,3,1,0:T(8,128)(2,1)}, u32[]{:S(2)}) copy-start(bf16[1,16,8,3,4096]{4,2,3,1,0:T(8,128)(2,1)} %param.27) | copy-start | bytes 9437188
  63.4 4.7 %copy-start.10 = (s32[384,3]{1,0:T(8,128)S(1)}, s32[384,3]{1,0:T(8,128)}, u32[]{:S(2)}) copy-start(s32[384,3]{1,0:T(8,128)} %constant.29.clone.table_ref) | copy-start | bytes 13828
  63.4 4.7 %copy-start.11 = (s32[1,384]{1,0:T(1,128)S(1)}, s32[1,384]{1,0:T(1,128)}, u32[]{:S(2)}) copy-start(s32[1,384]{1,0:T(1,128)} %constant.30.clone.lanes_ref) | copy-start | bytes 4612
  63.5 4.6 %collective-permute-start.16 = (bf16[128,4352]{1,0:T(8,128)(2,1)S(1)}, bf16[128,4352]{1,0:T(8,128)(2,1)S(1)}, u32[]{:S(2)}, u32[]{:S(2)}) collective-permute-start(bf16[128,4352]{1,0:T(8,128)(2,1)S(1)} %constant_dynamic-update-slice_fusion.4.refs_0_.refs_2_), channel_id=1, source_target_pairs={{0,1},{1,0},{2,3},{3,2},{4,5},{5,4},{6,7},{7,6},{8,9},{9,8},{10,11... | collective-permute-start | bytes 3342344 | tf_op jit(solution)/shard_map/ppermute | solution.py:483
  63.7 15.8 %collective-permute-start.13 = (bf16[128,512]{1,0:T(8,128)(2,1)}, bf16[128,512]{1,0:T(8,128)(2,1)}, u32[]{:S(2)}, u32[]{:S(2)}) collective-permute-start(bf16[128,512]{1,0:T(8,128)(2,1)} %get-tuple-element.99), channel_id=1, source_target_pairs={{0,2},{1,3},{2,0},{3,1},{4,6},{5,7},{6,4},{7,5},{8,10},{9,11},{10,... | collective-permute-start | bytes 393224 | tf_op jit(solution)/shard_map/ppermute | solution.py:440
  63.7 15.8 %collective-permute-start.14 = (bf16[128,512]{1,0:T(8,128)(2,1)}, bf16[128,512]{1,0:T(8,128)(2,1)}, u32[]{:S(2)}, u32[]{:S(2)}) collective-permute-start(bf16[128,512]{1,0:T(8,128)(2,1)} %get-tuple-element.100), channel_id=1, source_target_pairs={{0,4},{1,5},{2,6},{3,7},{4,0},{5,1},{6,2},{7,3},{8,12},{9,13},{10,... | collective-permute-start | bytes 393224 | tf_op jit(solution)/shard_map/ppermute | solution.py:440
  66.2 13.4 %collective-permute-start.15 = (bf16[128,512]{1,0:T(8,128)(2,1)}, bf16[128,512]{1,0:T(8,128)(2,1)}, u32[]{:S(2)}, u32[]{:S(2)}) collective-permute-start(bf16[128,512]{1,0:T(8,128)(2,1)} %get-tuple-element.101), channel_id=1, source_target_pairs={{0,6},{1,7},{2,4},{3,5},{4,2},{5,3},{6,0},{7,1},{8,14},{9,15},{10,... | collective-permute-start | bytes 393224 | tf_op jit(solution)/shard_map/ppermute | solution.py:440
  68.1 11.4 %collective-permute-start.12 = (bf16[128,1024]{1,0:T(8,128)(2,1)S(1)}, bf16[128,1024]{1,0:T(8,128)(2,1)S(1)}, u32[]{:S(2)}, u32[]{:S(2)}) collective-permute-start(bf16[128,1024]{1,0:T(8,128)(2,1)S(1)} %get-tuple-element.98), channel_id=1, source_target_pairs={{0,1},{1,0},{2,3},{3,2},{4,5},{5,4},{6,7},{7,6},{8,9},{9,8},{10,11... | collective-permute-start | bytes 786440 | tf_op jit(solution)/shard_map/ppermute | solution.py:483
  72.0 0.7 copy-start.14
  72.7 11.4 %all-to-all-start = ((f32[8,24,128]{2,1,0:T(8,128)}), f32[8,24,128]{2,1,0:T(8,128)S(1)}, u32[]{:S(2)}, u32[]{:S(2)}) async-start(f32[8,24,128]{2,1,0:T(8,128)} %get-tuple-element.124), calls=%async_computation | async-start | bytes 196608 | tf_op jit(solution)/shard_map/all_to_all | solution.py:535
  76.0 0.9 copy-start.15
  79.5 9.6 %copy-start.7 = (bf16[1,128,512]{2,1,0:T(8,128)(2,1)S(1)}, bf16[1,128,512]{2,1,0:T(8,128)(2,1)}, u32[]{:S(2)}) copy-start(bf16[1,128,512]{2,1,0:T(8,128)(2,1)} %param.18) | copy-start | bytes 393220
  79.5 9.6 %copy-start.9 = (f32[128]{0:T(128)S(1)}, f32[128]{0:T(128)}, u32[]{:S(2)}) copy-start(f32[128]{0:T(128)} %param.21) | copy-start | bytes 1540
  79.6 8.6 %collective-permute-start.17 = (bf16[128,512]{1,0:T(8,128)(2,1)}, bf16[128,512]{1,0:T(8,128)(2,1)S(1)}, u32[]{:S(2)}, u32[]{:S(2)}) collective-permute-start(bf16[128,512]{1,0:T(8,128)(2,1)} %get-tuple-element.111), channel_id=1, source_target_pairs={{0,2},{1,3},{2,0},{3,1},{4,6},{5,7},{6,4},{7,5},{8,10},{9,11},{10,... | collective-permute-start | bytes 393224 | tf_op jit(solution)/shard_map/ppermute | solution.py:440
  81.5 13.1 %collective-permute-start.18 = (bf16[128,512]{1,0:T(8,128)(2,1)}, bf16[128,512]{1,0:T(8,128)(2,1)S(1)}, u32[]{:S(2)}, u32[]{:S(2)}) collective-permute-start(bf16[128,512]{1,0:T(8,128)(2,1)} %get-tuple-element.112), channel_id=1, source_target_pairs={{0,4},{1,5},{2,6},{3,7},{4,0},{5,1},{6,2},{7,3},{8,12},{9,13},{10,... | collective-permute-start | bytes 393224 | tf_op jit(solution)/shard_map/ppermute | solution.py:440
  83.9 10.7 %collective-permute-start.19 = (bf16[128,512]{1,0:T(8,128)(2,1)S(1)}, bf16[128,512]{1,0:T(8,128)(2,1)}, u32[]{:S(2)}, u32[]{:S(2)}) collective-permute-start(bf16[128,512]{1,0:T(8,128)(2,1)S(1)} %get-tuple-element.113), channel_id=1, source_target_pairs={{0,6},{1,7},{2,4},{3,5},{4,2},{5,3},{6,0},{7,1},{8,14},{9,15},{10,... | collective-permute-start | bytes 393224 | tf_op jit(solution)/shard_map/ppermute | solution.py:440
  84.0 5.1 %copy-start.13 = (f32[128,1024]{1,0:T(8,128)S(1)}, f32[128,1024]{1,0:T(8,128)}, u32[]{:S(2)}) copy-start(f32[128,1024]{1,0:T(8,128)} %copy-done.12) | copy-start | bytes 1572868
  85.1 11.3 %collective-permute-start.22 = (bf16[512,128]{1,0:T(8,128)(2,1)S(1)}, bf16[512,128]{1,0:T(8,128)(2,1)S(1)}, u32[]{:S(2)}, u32[]{:S(2)}) collective-permute-start(bf16[512,128]{1,0:T(8,128)(2,1)S(1)} %router_grad.1), channel_id=1, source_target_pairs={{0,24},{8,16},{16,8},{24,0},{1,25},{9,17},{17,9},{25,1},{2,26},{10... | collective-permute-start | bytes 393224 | tf_op jit(solution)/shard_map/ppermute | solution.py:440
  87.6 8.8 %collective-permute-start.21 = (bf16[512,128]{1,0:T(8,128)(2,1)S(1)}, bf16[512,128]{1,0:T(8,128)(2,1)S(1)}, u32[]{:S(2)}, u32[]{:S(2)}) collective-permute-start(bf16[512,128]{1,0:T(8,128)(2,1)S(1)} %router_grad.1), channel_id=1, source_target_pairs={{0,16},{8,24},{16,0},{24,8},{1,17},{9,25},{17,1},{25,9},{2,18},{10... | collective-permute-start | bytes 393224 | tf_op jit(solution)/shard_map/ppermute | solution.py:440
  88.2 8.3 %collective-permute-start.20 = (bf16[512,128]{1,0:T(8,128)(2,1)S(1)}, bf16[512,128]{1,0:T(8,128)(2,1)S(1)}, u32[]{:S(2)}, u32[]{:S(2)}) collective-permute-start(bf16[512,128]{1,0:T(8,128)(2,1)S(1)} %router_grad.1), channel_id=1, source_target_pairs={{0,8},{8,0},{16,24},{24,16},{1,9},{9,1},{17,25},{25,17},{2,10},{10... | collective-permute-start | bytes 393224 | tf_op jit(solution)/shard_map/ppermute | solution.py:440
